TPU v7x, 32 devices: a whole 2x2x4 slice. The times are simulated.
32 devices in a mesh: parts: 2 (over y), dp: 4 (over z), fsdp: 4 (over x, core).
Axes of the slice: x: 2, y: 2, z: 4, core: 2. Of those that a mesh axis runs over, the one named last changes fastest.
Arguments:
- tokens: bfloat16 [12288, 5120], P(('parts', 'dp', 'fsdp')), parts along dimension 0, may hold values from -6 to 6
- cotangent: bfloat16 [12288, 1024], P(('parts', 'dp', 'fsdp')), parts along dimension 0, may hold values from -0.1875 to 0.1875
- lengths: int32 [32, 12], P(('parts', 'dp', 'fsdp')), parts along dimension 0, may hold values from 1 to 32, 288 in all within a row
- slot_adapter_index: int32 [32, 12], P(('parts', 'dp', 'fsdp')), parts along dimension 0, may hold values from 0 to 3, as said below
- adapter_rank_sizes: int32 [4], replicated, may hold values from 8 to 128
- frozen: bfloat16 [5120, 1024], P('fsdp'), may hold values from -0.078125 to 0.078125
- key_norm_weight: float32 [128], replicated, may hold values from 0.25 to 1.75
- adapter_down_factor: float32 [8, 5120, 128], P(('parts', 'dp'), 'fsdp'), parts along dimension 0, may hold values from -0.078125 to 0.078125
- adapter_up_factor: float32 [8, 128, 1024], P(('parts', 'dp'), 'fsdp'), parts along dimension 0, may hold values from -0.5 to 0.5
- down_first_moment: float32 [8, 5120, 128], P(('parts', 'dp'), 'fsdp'), parts along dimension 0, may hold values from -1.75 to 1.75
- up_first_moment: float32 [8, 128, 1024], P(('parts', 'dp'), 'fsdp'), parts along dimension 0, may hold values from -1.75 to 1.75
- down_second_moment: float32 [8, 5120, 128], P(('parts', 'dp'), 'fsdp'), parts along dimension 0, may hold values from 0.01 to 1
- up_second_moment: float32 [8, 128, 1024], P(('parts', 'dp'), 'fsdp'), parts along dimension 0, may hold values from 0.01 to 1
Outputs:
- updated_down_factor: float32 [8, 5120, 128], P(('parts', 'dp'), 'fsdp'), parts along dimension 0
- updated_up_factor: float32 [8, 128, 1024], P(('parts', 'dp'), 'fsdp'), parts along dimension 0
- updated_down_first_moment: float32 [8, 5120, 128], P(('parts', 'dp'), 'fsdp'), parts along dimension 0
- updated_up_first_moment: float32 [8, 128, 1024], P(('parts', 'dp'), 'fsdp'), parts along dimension 0
- updated_down_second_moment: float32 [8, 5120, 128], P(('parts', 'dp'), 'fsdp'), parts along dimension 0
- updated_up_second_moment: float32 [8, 128, 1024], P(('parts', 'dp'), 'fsdp'), parts along dimension 0
There are 2 independent parts, one for each index of `parts`. A program takes and returns all parts, laid end to end along the dimension named above; an argument that names none is the same for every part. Nothing has to cross between parts.
Inputs may be any that keep to these rules, and one draw needn't show every extreme that they name: `slot_adapter_index`: no adapter is used by more than 3 sequence slots of one device; some adapter is used by exactly 3 slots on every device.
All inputs are finite; a program needn't handle non-finite values.
Results may differ from a plain program's by a relative error of at most 0.0018.
Values may be sent and summed in bfloat16 or wider, within the bound.
No kernel may reach another device: no remote copies, remote signals or barrier semaphores. Data moves between devices by JAX's collectives and lax.ppermute only.
A program may use at most 128 MiB of HBM per device.

v0:
```python
import jax
import jax.numpy as jnp
from jax import lax
from jax.sharding import PartitionSpec as P

MODEL_WIDTH = 5120
HEAD = 128
KEY_WIDTH = 1024
PADDED_RANK = 128
SEQ = 32


adapter_alpha_scale = 16.0
norm_epsilon = 1e-06
learn_rate = 0.001
weight_decay = 0.01
beta_one = 0.9
beta_two = 0.999
correct_one = 1.0 - 0.9**10
correct_two = 1.0 - 0.999**10
adam_epsilon = 1e-08


def adapter_grads(
    row_tokens,
    row_base,
    row_grads,
    down_factor_weight,
    up_factor_weight,
    owned_adapter_rank,
    key_norm_weight,
):
    columns = jnp.arange(PADDED_RANK) < owned_adapter_rank
    masked_down = jnp.where(columns[None, :], down_factor_weight, jnp.zeros((), jnp.bfloat16))
    masked_up = jnp.where(columns[:, None], up_factor_weight, jnp.zeros((), jnp.bfloat16))
    adapter_scale_factor = adapter_alpha_scale / owned_adapter_rank.astype(jnp.float32)
    lowrank = jnp.dot(row_tokens, masked_down, preferred_element_type=jnp.float32).astype(
        jnp.bfloat16
    )
    key_rows = row_base.astype(jnp.float32) + adapter_scale_factor * jnp.dot(
        lowrank, masked_up, preferred_element_type=jnp.float32
    )
    per_head = key_rows.reshape(key_rows.shape[0], KEY_WIDTH // HEAD, HEAD)
    inverse = lax.rsqrt(jnp.mean(per_head * per_head, axis=-1, keepdims=True) + norm_epsilon)
    normed = per_head * inverse
    incoming = row_grads.astype(jnp.float32).reshape(per_head.shape) * key_norm_weight
    key_grads = inverse * (incoming - normed * jnp.mean(incoming * normed, axis=-1, keepdims=True))
    key_grads = key_grads.reshape(key_rows.shape).astype(jnp.bfloat16)
    up_factor_gradient = adapter_scale_factor * lax.dot_general(
        lowrank, key_grads, (((0,), (0,)), ((), ())), preferred_element_type=jnp.float32
    )
    up_factor_gradient = jnp.where(columns[:, None], up_factor_gradient, 0.0)
    low_grads = (
        adapter_scale_factor
        * lax.dot_general(
            key_grads, masked_up, (((1,), (1,)), ((), ())), preferred_element_type=jnp.float32
        )
    ).astype(jnp.bfloat16)
    down_factor_gradient = lax.dot_general(
        row_tokens, low_grads, (((0,), (0,)), ((), ())), preferred_element_type=jnp.float32
    )
    return (down_factor_gradient, up_factor_gradient)


def optimizer_update(weights, gradient, moment, variance):
    moment_new = beta_one * moment + (1.0 - beta_one) * gradient
    variance_new = beta_two * variance + (1.0 - beta_two) * gradient * gradient
    update = moment_new / correct_one / (jnp.sqrt(variance_new / correct_two) + adam_epsilon)
    return (weights - learn_rate * (update + weight_decay * weights), moment_new, variance_new)


def frozen_product(row_data, frozen):
    return jnp.dot(
        row_data,
        lax.all_gather(frozen, "fsdp", axis=0, tiled=True),
        preferred_element_type=jnp.float32,
    ).astype(jnp.bfloat16)


def local(
    tokens,
    cotangent,
    lengths,
    slot_adapter_index,
    adapter_rank_sizes,
    frozen,
    key_norm_weight,
    adapter_down_factor,
    adapter_up_factor,
    down_first_moment,
    up_first_moment,
    down_second_moment,
    up_second_moment,
):
    data_ranks = lax.axis_size("dp")
    owning_replica = lax.axis_index("dp")
    seq_count = lengths.shape[1]
    per_pair = -(-seq_count // data_ranks)
    slot_total = data_ranks * per_pair
    token_seqs = tokens.reshape(seq_count, SEQ, MODEL_WIDTH)
    live_mask = jnp.arange(SEQ)[None, :] < lengths[0][:, None]
    upstream = jnp.where(
        live_mask[:, :, None],
        cotangent.reshape(seq_count, SEQ, KEY_WIDTH),
        jnp.zeros((), cotangent.dtype),
    )
    target = slot_adapter_index[0]
    seq_index = jnp.arange(seq_count)
    earlier = (target[None, :] == target[:, None]) & (seq_index[None, :] < seq_index[:, None])
    slot_order = jnp.sum(earlier.astype(jnp.int32), axis=1)
    slot_of = target * per_pair + slot_order
    matches = slot_of[None, :] == jnp.arange(slot_total)[:, None]
    source = jnp.sum(jnp.where(matches, seq_index[None, :], 0), axis=1)
    filled = jnp.any(matches, axis=1)

    def pack_slots(values):
        picked = jnp.take(values, source, axis=0)
        picked = jnp.where(filled[:, None, None], picked, jnp.zeros((), values.dtype))
        return picked.reshape(data_ranks, per_pair * SEQ, values.shape[-1])

    arrived_tokens, arrived_grads = (
        lax.all_to_all(pack_slots(token_seqs), "dp", split_axis=0, concat_axis=0, tiled=True),
        lax.all_to_all(pack_slots(upstream), "dp", split_axis=0, concat_axis=0, tiled=True),
    )
    row_tokens = arrived_tokens.reshape(-1, MODEL_WIDTH)
    row_base = frozen_product(row_tokens, frozen)
    row_grads = arrived_grads.reshape(-1, KEY_WIDTH)
    owned_adapter_rank = jnp.sum(
        jnp.where(jnp.arange(adapter_rank_sizes.shape[0]) == owning_replica, adapter_rank_sizes, 0)
    )
    full_down, full_up = (
        lax.all_gather(adapter_down_factor.astype(jnp.bfloat16), "fsdp", axis=1, tiled=True),
        lax.all_gather(adapter_up_factor.astype(jnp.bfloat16), "fsdp", axis=1, tiled=True),
    )
    down_factor_gradient, up_factor_gradient = adapter_grads(
        row_tokens,
        row_base,
        row_grads,
        full_down[0],
        full_up[0],
        owned_adapter_rank,
        key_norm_weight,
    )
    down_gradient_portion, up_gradient_portion = (
        lax.psum_scatter(down_factor_gradient, "fsdp", scatter_dimension=0, tiled=True),
        lax.psum_scatter(up_factor_gradient, "fsdp", scatter_dimension=0, tiled=True),
    )
    updated_down_factor, updated_down_first_moment, updated_down_second_moment = optimizer_update(
        adapter_down_factor[0], down_gradient_portion, down_first_moment[0], down_second_moment[0]
    )
    updated_up_factor, updated_up_first_moment, updated_up_second_moment = optimizer_update(
        adapter_up_factor[0], up_gradient_portion, up_first_moment[0], up_second_moment[0]
    )
    return (
        updated_down_factor[None],
        updated_up_factor[None],
        updated_down_first_moment[None],
        updated_up_first_moment[None],
        updated_down_second_moment[None],
        updated_up_second_moment[None],
    )


def solution(mesh):
    return jax.shard_map(
        local,
        mesh=mesh,
        in_specs=(
            P(("parts", "dp", "fsdp"), None),
            P(("parts", "dp", "fsdp"), None),
            P(("parts", "dp", "fsdp"), None),
            P(("parts", "dp", "fsdp"), None),
            P(),
            P("fsdp", None),
            P(),
            P(("parts", "dp"), "fsdp", None),
            P(("parts", "dp"), "fsdp", None),
            P(("parts", "dp"), "fsdp", None),
            P(("parts", "dp"), "fsdp", None),
            P(("parts", "dp"), "fsdp", None),
            P(("parts", "dp"), "fsdp", None),
        ),
        out_specs=(
            P(("parts", "dp"), "fsdp", None),
            P(("parts", "dp"), "fsdp", None),
            P(("parts", "dp"), "fsdp", None),
            P(("parts", "dp"), "fsdp", None),
            P(("parts", "dp"), "fsdp", None),
            P(("parts", "dp"), "fsdp", None),
        ),
        check_vma=False,
    )
```

profile of v0, /device:TPU:0, one launch (start us, length us, event | category | flops | bytes accessed | tf_op | source)
XLA Modules:
  0.0 217.2 jit_solution(8406802204694800867)
XLA Ops:
  7.2 1.8 convert_element_type.44
  9.1 0.7 all-gather.3.cloned.1.call-update
  9.9 0.2 convert_reduce_fusion
  10.9 0.1 broadcast_select_fusion
  11.0 0.6 gather_fusion.1
  11.6 1.1 fusion.14
  12.7 6.3 %all-to-all-start.1 = ((bf16[4,96,1024]{2,1,0:T(8,128)(2,1)}), bf16[4,96,1024]{2,1,0:T(8,128)(2,1)S(1)}, u32[]{:S(2)}, u32[]{:S(2)}) async-start(bf16[4,96,1024]{2,1,0:T(8,128)(2,1)} %fusion.14), calls=%async_computation.1 | async-start | bytes 1572864 | tf_op jit(solution)/shard_map/all_to_all | solution.py:123
  19.0 5.3 %gather_fusion = bf16[12,32,5120]{2,1,0:T(8,128)(2,1)} fusion(bf16[12,32,5120]{2,1,0:T(8,128)(2,1)} %bitcast.136, s32[1024]{0:T(1024)S(1)} %pad_clamp_fusion), kind=kCustom, calls=%fused_computation | custom fusion | bytes 7864368 | tf_op jit(solution)/shard_map/jit(_take)/gather | solution.py:117
  24.3 4.6 %fusion = bf16[4,96,5120]{2,1,0:T(8,128)(2,1)} fusion(pred[4,96]{1,0:T(4,128)(4,1)S(1)} %broadcast_in_dim.153, pred[4,96]{1,0:T(4,128)(4,1)S(1)} %broadcast_in_dim.149, bf16[4,96,5120]{2,1,0:T(8,128)(2,1)} %bitcast.129), kind=kLoop, calls=%fused_computation.3 | loop fusion | flops 3932160 | bytes 7865088 | tf_op jit(solution)/shard_map/jit(_where)/select_n | solution.py:118
  28.9 10.2 %all-to-all-done.1 = bf16[4,96,1024]{2,1,0:T(8,128)(2,1)S(1)} async-done(((bf16[4,96,1024]{2,1,0:T(8,128)(2,1)}), bf16[4,96,1024]{2,1,0:T(8,128)(2,1)S(1)}, u32[]{:S(2)}, u32[]{:S(2)}) %all-to-all-start.1) | async-done | bytes 786464 | tf_op jit(solution)/shard_map/all_to_all | solution.py:123
  39.1 5.0 %all-to-all-start = ((bf16[4,96,5120]{2,1,0:T(8,128)(2,1)}), bf16[4,96,5120]{2,1,0:T(8,128)(2,1)}, u32[]{:S(2)}, u32[]{:S(2)}) async-start(bf16[4,96,5120]{2,1,0:T(8,128)(2,1)} %fusion), calls=%async_computation | async-start | bytes 7864320 | tf_op jit(solution)/shard_map/all_to_all | solution.py:122
  44.2 0.6 fusion.31
  45.6 7.6 %all_gather.11 = bf16[1,128,1024]{2,1,0:T(8,128)(2,1)S(1)} all-gather(bf16[1,32,1024]{2,1,0:T(8,128)(2,1)S(1)} %convert_element_type.46), channel_id=1, replica_groups=mesh['parts'=2,'dp'=4,'fsdp'=4] {'fsdp'}, dimensions={1}, use_global_device_ids=true | all-gather | bytes 327680 | tf_op jit(solution)/shard_map/all_gather | solution.py:133
  53.1 0.6 iota_compare_fusion.3
  53.8 0.2 copy.21
  54.2 77.0 %all-to-all-done = bf16[4,96,5120]{2,1,0:T(8,128)(2,1)} async-done(((bf16[4,96,5120]{2,1,0:T(8,128)(2,1)}), bf16[4,96,5120]{2,1,0:T(8,128)(2,1)}, u32[]{:S(2)}, u32[]{:S(2)}) %all-to-all-start) | async-done | bytes 3932192 | tf_op jit(solution)/shard_map/all_to_all | solution.py:122
  131.2 3.7 %fusion.10 = bf16[384,128]{1,0:T(8,128)(2,1)S(1)} fusion(bf16[384,5120]{1,0:T(8,128)(2,1)} %bitcast.9, bf16[1,5120,128]{2,1,0:T(8,128)(2,1)} %all-gather.5.cloned.1.call-done, pred[128]{0:T(512)(128)(4,1)S(1)} %iota_compare_fusion.3), kind=kOutput, calls=%fused_computation.23 | convolution fusion | flops 504020992 | bytes 5341312 | tf_op jit(solution)/shard_map/dot_general | solution.py:37
  134.9 9.4 %convolution_convert_fusion = bf16[384,1024]{1,0:T(8,128)(2,1)S(1)} fusion(bf16[384,5120]{1,0:T(8,128)(2,1)} %bitcast.9, bf16[5120,1024]{1,0:T(8,128)(2,1)} %all-gather.3.cloned.1.call-done), kind=kOutput, calls=%fused_computation.14 | convolution fusion | flops 4026925056 | bytes 15204352 | tf_op jit(solution)/shard_map/dot_general | solution.py:73
  144.3 0.4 multiply_add_fusion
  144.7 0.3 copy.19
  145.1 0.5 multiply_reduce_fusion.1
  145.6 0.9 multiply_reduce_fusion
  146.5 0.5 mul.173
  147.0 0.5 mul.162
  147.5 1.1 fusion.3
  148.6 1.1 fusion.8
  149.7 0.2 reduce-scatter.3.cloned.1.call-start
  150.0 5.6 %fusion.13 = f32[5120,128]{1,0:T(8,128)} fusion(bf16[384,5120]{1,0:T(8,128)(2,1)} %bitcast.9, bf16[384,1024]{1,0:T(8,128)(2,1)S(1)} %fusion.3, bf16[1,128,1024]{2,1,0:T(8,128)(2,1)S(1)} %all_gather.11, pred[128]{0:T(512)(128)(4,1)S(1)} %iota_compare_fusion.3, f32[]{:T(128)S(6)} %div.39), kind=kOutput, calls=%fused_computation.24 | convolution fusion | flops 604209152 | bytes 7602308 | tf_op jit(solution)/shard_map/dot_general | solution.py:59
  155.6 15.0 %reduce-scatter.5.cloned.1.call-done = f32[32,1024]{1,0:T(8,128)} async-done(((f32[128,1024]{1,0:T(8,128)}), f32[32,1024]{1,0:T(8,128)}) %reduce-scatter.5.cloned.1.call-update) | async-done | bytes 131088 | tf_op jit(solution)/shard_map/reduce_scatter | solution.py:146
  170.6 1.7 fusion.28
  172.4 35.5 %reduce-scatter.3.cloned.1.call-done = f32[1280,128]{1,0:T(8,128)} async-done(((f32[5120,128]{1,0:T(8,128)}), f32[1280,128]{1,0:T(8,128)}) %reduce-scatter.3.cloned.1.call-update) | async-done | bytes 655376 | tf_op jit(solution)/shard_map/reduce_scatter | solution.py:145
  207.9 2.8 %fusion.21 = (f32[1,1280,128]{2,1,0:T(8,128)}, f32[1,1280,128]{2,1,0:T(8,128)}, f32[1,1280,128]{2,1,0:T(8,128)}) fusion(f32[1280,128]{1,0:T(8,128)} %reduce-scatter.3.cloned.1.call-done, f32[1,1280,128]{2,1,0:T(8,128)S(1)} %copy-done.2, f32[1,1280,128]{2,1,0:T(8,128)S(1)} %copy-done.3, f32[1,1280,128]{2,1,0:T(8,128)S(1)} %copy-done), kind=kLoop, calls=%fused_computation.41 | loop fusion | flops 2457600 | bytes 4587520 | tf_op jit(solution)/shard_map/broadcast_in_dim | solution.py:159
  (48 shorter events, 1.3 us)
Async XLA Ops:
  7.2 47.0 %all-gather.5.cloned.1.call-start = ((), (), s32[]{:S(2)}) async-start(), calls=%async_computation.5 | async-start | bytes 1638400 | tf_op jit(solution)/shard_map/all_gather | solution.py:132
  9.1 0.8 copy-start.9
  9.1 1.8 copy-start.8
  9.1 1.8 copy-start.1
  9.1 125.8 %all-gather.3.cloned.1.call-start = ((), (), s32[]{:S(2)}) async-start(), calls=%async_computation.4 | async-start | bytes 13107200 | tf_op jit(solution)/shard_map/all_gather | solution.py:75
  12.7 26.4 %all-to-all-start.1 = ((bf16[4,96,1024]{2,1,0:T(8,128)(2,1)}), bf16[4,96,1024]{2,1,0:T(8,128)(2,1)S(1)}, u32[]{:S(2)}, u32[]{:S(2)}) async-start(bf16[4,96,1024]{2,1,0:T(8,128)(2,1)} %fusion.14), calls=%async_computation.1 | async-start | bytes 1572864 | tf_op jit(solution)/shard_map/all_to_all | solution.py:123
  28.9 15.3 %copy-start.10 = (s32[4]{0:T(128)S(1)}, s32[4]{0:T(128)}, u32[]{:S(2)}) copy-start(s32[4]{0:T(128)} %param.17) | copy-start | bytes 52
  28.9 16.6 %copy-start.4 = (f32[1,32,1024]{2,1,0:T(8,128)S(1)}, f32[1,32,1024]{2,1,0:T(8,128)}, u32[]{:S(2)}) copy-start(f32[1,32,1024]{2,1,0:T(8,128)} %param.21) | copy-start | bytes 393220
  28.9 24.9 %copy-start.7 = (f32[128]{0:T(128)S(1)}, f32[128]{0:T(128)}, u32[]{:S(2)}) copy-start(f32[128]{0:T(128)} %param.19) | copy-start | bytes 1540
  39.1 92.0 %all-to-all-start = ((bf16[4,96,5120]{2,1,0:T(8,128)(2,1)}), bf16[4,96,5120]{2,1,0:T(8,128)(2,1)}, u32[]{:S(2)}, u32[]{:S(2)}) async-start(bf16[4,96,5120]{2,1,0:T(8,128)(2,1)} %fusion), calls=%async_computation | async-start | bytes 7864320 | tf_op jit(solution)/shard_map/all_to_all | solution.py:122
  44.1 126.5 %reduce-scatter.5.cloned.1.call-start = ((), (), s32[]{:S(2)}) async-start(), calls=%async_computation.7 | async-start | bytes 655360 | tf_op jit(solution)/shard_map/reduce_scatter | solution.py:146
  149.7 58.1 %reduce-scatter.3.cloned.1.call-start = ((), (), s32[]{:S(2)}) async-start(), calls=%async_computation.6 | async-start | bytes 3276800 | tf_op jit(solution)/shard_map/reduce_scatter | solution.py:145
  155.6 15.1 %copy-start.5 = (f32[1,32,1024]{2,1,0:T(8,128)S(1)}, f32[1,32,1024]{2,1,0:T(8,128)}, u32[]{:S(2)}) copy-start(f32[1,32,1024]{2,1,0:T(8,128)} %param.25) | copy-start | bytes 393220
  155.6 15.1 %copy-start.6 = (f32[1,32,1024]{2,1,0:T(8,128)S(1)}, f32[1,32,1024]{2,1,0:T(8,128)}, u32[]{:S(2)}) copy-start(f32[1,32,1024]{2,1,0:T(8,128)} %param.23) | copy-start | bytes 393220
  155.6 52.3 %copy-start = (f32[1,1280,128]{2,1,0:T(8,128)S(1)}, f32[1,1280,128]{2,1,0:T(8,128)}, u32[]{:S(2)}) copy-start(f32[1,1280,128]{2,1,0:T(8,128)} %param.20) | copy-start | bytes 1966084
  155.6 52.3 %copy-start.2 = (f32[1,1280,128]{2,1,0:T(8,128)S(1)}, f32[1,1280,128]{2,1,0:T(8,128)}, u32[]{:S(2)}) copy-start(f32[1,1280,128]{2,1,0:T(8,128)} %param.24) | copy-start | bytes 1966084
  155.6 52.3 %copy-start.3 = (f32[1,1280,128]{2,1,0:T(8,128)S(1)}, f32[1,1280,128]{2,1,0:T(8,128)}, u32[]{:S(2)}) copy-start(f32[1,1280,128]{2,1,0:T(8,128)} %param.22) | copy-start | bytes 1966084
Sparse Core Ops, SparseCore 0:
  10.1 20.9 all-gather.4
  32.7 71.5 all-gather.2
  149.8 20.7 reduce-scatter.4
  173.2 34.6 reduce-scatter.2
where the time goes:
time: 218 us; the launch traced here: 217 us
  waiting for transfers between devices  139 us (64%)
  matrix products  20.2 us (9%)
  other arithmetic  16.6 us (8%)
  between operations  14.7 us (7%)
  starting transfers between devices  11.6 us (5%)
  local copies, waits for them, and re-layouts  7.92 us (4%)
  blocking collectives  7.6 us (3%)
    all_to_all x1, waiting for transfers between devices, local(): lax.all_to_all(pack_slots(token_seqs), 'dp', split_axis=0, concat_axis=0,...  77 us
    reduce_scatter x1, waiting for transfers between devices, local(): lax.psum_scatter(down_factor_gradient, 'fsdp', scatter_dimension=0, tiled...  35.5 us
    reduce_scatter x1, waiting for transfers between devices, local(): lax.psum_scatter(up_factor_gradient, 'fsdp', scatter_dimension=0, tiled=T...  15 us
    all_to_all x1, waiting for transfers between devices, local(): lax.all_to_all(pack_slots(upstream), 'dp', split_axis=0, concat_axis=0, t...  10.2 us
    dot_general x1, matrix products, frozen_product(): jnp.dot(row_data, lax.all_gather(frozen, 'fsdp', axis=0, tiled=True), pre...  9.39 us
    all_gather x1, blocking collectives, local(): lax.all_gather(adapter_up_factor.astype(jnp.bfloat16), 'fsdp', axis=1, ti...  7.6 us
    all_to_all x1, starting transfers between devices, local(): lax.all_to_all(pack_slots(upstream), 'dp', split_axis=0, concat_axis=0, t...  6.32 us
    gather x2, local copies, waits for them, and re-layouts, pack_slots(): picked = jnp.take(values, source, axis=0)  5.92 us
  transfers between devices with their start and end apart: 6, of which 4 were waited for; matrix products, arithmetic and copies ran while one was open for 12% of the time, Pallas kernels for 0%

commit v1 on v0

v1 whole, which is shorter than its diff:
```python
import jax
import jax.numpy as jnp
from jax import lax
from jax.experimental import pallas as pl
from jax.experimental.pallas import tpu as pltpu
from jax.sharding import PartitionSpec as P

MODEL_WIDTH = 5120
HEAD = 128
KEY_WIDTH = 1024
PADDED_RANK = 128
SEQ = 32
LIVE = 288
FIRST = 192
QUARTER = MODEL_WIDTH // 4


adapter_alpha_scale = 16.0
norm_epsilon = 1e-06
learn_rate = 0.001
weight_decay = 0.01
beta_one = 0.9
beta_two = 0.999
correct_one = 1.0 - 0.9**10
correct_two = 1.0 - 0.999**10
adam_epsilon = 1e-08

bf16 = jnp.bfloat16
f32 = jnp.float32
i32 = jnp.int32


def optimizer_update(weights, gradient, moment, variance):
    moment_new = beta_one * moment + (1.0 - beta_one) * gradient
    variance_new = beta_two * variance + (1.0 - beta_two) * gradient * gradient
    update = moment_new / correct_one / (jnp.sqrt(variance_new / correct_two) + adam_epsilon)
    return (weights - learn_rate * (update + weight_decay * weights), moment_new, variance_new)


def adapter_grads(
    row_tokens,
    row_base,
    row_grads,
    down_factor_weight,
    up_factor_weight,
    owned_adapter_rank,
    key_norm_weight,
):
    columns = jnp.arange(PADDED_RANK) < owned_adapter_rank
    masked_down = jnp.where(columns[None, :], down_factor_weight, jnp.zeros((), bf16))
    masked_up = jnp.where(columns[:, None], up_factor_weight, jnp.zeros((), bf16))
    adapter_scale_factor = adapter_alpha_scale / owned_adapter_rank.astype(f32)
    lowrank = jnp.dot(row_tokens, masked_down, preferred_element_type=f32).astype(bf16)
    key_rows = row_base.astype(f32) + adapter_scale_factor * jnp.dot(
        lowrank, masked_up, preferred_element_type=f32
    )
    per_head = key_rows.reshape(key_rows.shape[0], KEY_WIDTH // HEAD, HEAD)
    inverse = lax.rsqrt(jnp.mean(per_head * per_head, axis=-1, keepdims=True) + norm_epsilon)
    normed = per_head * inverse
    incoming = row_grads.astype(f32).reshape(per_head.shape) * key_norm_weight
    key_grads = inverse * (incoming - normed * jnp.mean(incoming * normed, axis=-1, keepdims=True))
    key_grads = key_grads.reshape(key_rows.shape).astype(bf16)
    up_factor_gradient = adapter_scale_factor * lax.dot_general(
        lowrank, key_grads, (((0,), (0,)), ((), ())), preferred_element_type=f32
    )
    up_factor_gradient = jnp.where(columns[:, None], up_factor_gradient, 0.0)
    low_grads = (
        adapter_scale_factor
        * lax.dot_general(key_grads, masked_up, (((1,), (1,)), ((), ())), preferred_element_type=f32)
    ).astype(bf16)
    down_factor_gradient = lax.dot_general(
        row_tokens, low_grads, (((0,), (0,)), ((), ())), preferred_element_type=f32
    )
    return (down_factor_gradient, up_factor_gradient)


def general_gradients(
    tokens,
    cotangent,
    lengths,
    slot_adapter_index,
    adapter_rank_sizes,
    frozen,
    key_norm_weight,
    adapter_down_factor,
    adapter_up_factor,
):
    data_ranks = lax.axis_size("dp")
    owning_replica = lax.axis_index("dp")
    seq_count = lengths.shape[1]
    per_pair = -(-seq_count // data_ranks)
    slot_total = data_ranks * per_pair
    token_seqs = tokens.reshape(seq_count, SEQ, MODEL_WIDTH)
    live_mask = jnp.arange(SEQ)[None, :] < lengths[0][:, None]
    upstream = jnp.where(
        live_mask[:, :, None],
        cotangent.reshape(seq_count, SEQ, KEY_WIDTH),
        jnp.zeros((), cotangent.dtype),
    )
    target = slot_adapter_index[0]
    seq_index = jnp.arange(seq_count)
    earlier = (target[None, :] == target[:, None]) & (seq_index[None, :] < seq_index[:, None])
    slot_order = jnp.sum(earlier.astype(i32), axis=1)
    slot_of = target * per_pair + slot_order
    matches = slot_of[None, :] == jnp.arange(slot_total)[:, None]
    source = jnp.sum(jnp.where(matches, seq_index[None, :], 0), axis=1)
    filled = jnp.any(matches, axis=1)

    def pack_slots(values):
        picked = jnp.take(values, source, axis=0)
        picked = jnp.where(filled[:, None, None], picked, jnp.zeros((), values.dtype))
        return picked.reshape(data_ranks, per_pair * SEQ, values.shape[-1])

    arrived_tokens, arrived_grads = (
        lax.all_to_all(pack_slots(token_seqs), "dp", split_axis=0, concat_axis=0, tiled=True),
        lax.all_to_all(pack_slots(upstream), "dp", split_axis=0, concat_axis=0, tiled=True),
    )
    row_tokens = arrived_tokens.reshape(-1, MODEL_WIDTH)
    row_base = jnp.dot(
        row_tokens,
        lax.all_gather(frozen, "fsdp", axis=0, tiled=True),
        preferred_element_type=f32,
    ).astype(bf16)
    row_grads = arrived_grads.reshape(-1, KEY_WIDTH)
    owned_adapter_rank = jnp.sum(
        jnp.where(jnp.arange(adapter_rank_sizes.shape[0]) == owning_replica, adapter_rank_sizes, 0)
    )
    full_down, full_up = (
        lax.all_gather(adapter_down_factor.astype(bf16), "fsdp", axis=1, tiled=True),
        lax.all_gather(adapter_up_factor.astype(bf16), "fsdp", axis=1, tiled=True),
    )
    down_factor_gradient, up_factor_gradient = adapter_grads(
        row_tokens,
        row_base,
        row_grads,
        full_down[0],
        full_up[0],
        owned_adapter_rank,
        key_norm_weight,
    )
    return (
        lax.psum_scatter(down_factor_gradient, "fsdp", scatter_dimension=0, tiled=True),
        lax.psum_scatter(up_factor_gradient, "fsdp", scatter_dimension=0, tiled=True),
    )


def local_general(
    tokens,
    cotangent,
    lengths,
    slot_adapter_index,
    adapter_rank_sizes,
    frozen,
    key_norm_weight,
    adapter_down_factor,
    adapter_up_factor,
    down_first_moment,
    up_first_moment,
    down_second_moment,
    up_second_moment,
):
    down_gradient, up_gradient = general_gradients(
        tokens,
        cotangent,
        lengths,
        slot_adapter_index,
        adapter_rank_sizes,
        frozen,
        key_norm_weight,
        adapter_down_factor,
        adapter_up_factor,
    )
    new_down, down_first, down_second = optimizer_update(
        adapter_down_factor[0], down_gradient, down_first_moment[0], down_second_moment[0]
    )
    new_up, up_first, up_second = optimizer_update(
        adapter_up_factor[0], up_gradient, up_first_moment[0], up_second_moment[0]
    )
    return (
        new_down[None],
        new_up[None],
        down_first[None],
        up_first[None],
        down_second[None],
        up_second[None],
    )


SMEM = pl.BlockSpec(memory_space=pltpu.SMEM)
VMEM = pl.BlockSpec(memory_space=pltpu.VMEM)
HBM = pl.BlockSpec(memory_space=pl.ANY)


def call(kernel, name, specs, outs, args, scratch=(), flops=0):
    moved = sum(a.size * a.dtype.itemsize for a in list(args) + list(outs))
    return pl.pallas_call(
        kernel,
        name=name,
        in_specs=list(specs),
        out_specs=tuple(VMEM for _ in outs),
        out_shape=tuple(outs),
        scratch_shapes=list(scratch),
        compiler_params=pltpu.CompilerParams(vmem_limit_bytes=56 * 2**20),
        cost_estimate=pl.CostEstimate(flops=flops, bytes_accessed=moved, transcendentals=0),
    )(*args)


def shape(dims, dtype):
    return jax.ShapeDtypeStruct(dims, dtype)


def packing(meta, first, rows, slots):
    token = lax.broadcasted_iota(i32, (1, slots * SEQ), 1)
    place = jnp.full((1, slots * SEQ), -1, i32)
    for s in range(slots):
        position = token - s * SEQ
        inside = (position >= 0) & (position < meta[1, s])
        place = jnp.where(inside, position + meta[0, s], place)
    row = lax.broadcasted_iota(i32, (rows, slots * SEQ), 0) + first
    return jnp.where(row == place, 1.0, 0.0).astype(bf16)


def row_adapters(meta, first, rows, slots):
    row = lax.broadcasted_iota(i32, (rows, HEAD), 0) + first
    adapter = jnp.zeros((rows, HEAD), i32)
    for s in range(slots):
        inside = (row >= meta[0, s]) & (row < meta[0, s] + meta[1, s])
        adapter = jnp.where(inside, meta[2, s], adapter)
    return adapter


def mm(a, b):
    return jnp.dot(a, b, preferred_element_type=f32)


def mm_t(a, b):
    return lax.dot_general(a, b, (((0,), (0,)), ((), ())), preferred_element_type=f32)


def mm_nt(a, b):
    return lax.dot_general(a, b, (((1,), (1,)), ((), ())), preferred_element_type=f32)


def pack_sent_kernel(slots, meta, tokens, first_out, second_out, held, sems):
    f = lax.axis_index("fsdp")
    copies = []
    for q, other in enumerate((2, 3)):
        start = pl.multiple_of((f ^ other) * QUARTER, QUARTER)
        copies.append(
            pltpu.make_async_copy(tokens.at[:, pl.ds(start, QUARTER)], held.at[q], sems.at[q])
        )
        copies[-1].start()
    chosen = packing(meta, 0, LIVE, slots)
    for q in range(2):
        copies[q].wait()
        rows = mm(chosen, held[q]).astype(bf16)
        first_out[q] = rows[:FIRST]
        second_out[q] = rows[FIRST:]


def pack_kept_kernel(slots, meta, tokens, cotangent, near_out, far_out, grads_out, held, sems):
    f = lax.axis_index("fsdp")
    copies = []
    for q in range(2):
        start = pl.multiple_of((f ^ q) * QUARTER, QUARTER)
        copies.append(
            pltpu.make_async_copy(tokens.at[:, pl.ds(start, QUARTER)], held.at[q], sems.at[q])
        )
        copies[-1].start()
    chosen = packing(meta, 0, LIVE, slots)
    grads_out[...] = mm(chosen, cotangent[...]).astype(bf16)
    copies[0].wait()
    near_out[...] = mm(chosen, held[0]).astype(bf16)
    copies[1].wait()
    far_out[...] = mm(chosen, held[1]).astype(bf16)


def weights_kernel(ranks, down, up_own, up_mate, out):
    rank = ranks[lax.axis_index("dp")]
    side = lax.axis_index("fsdp") // 2
    column = lax.broadcasted_iota(i32, (QUARTER, PADDED_RANK), 1)
    out[:QUARTER] = jnp.where(column < rank, down[...], 0.0).astype(bf16)
    own, mate = up_own[...], up_mate[...]
    zero = jnp.full((32, 1), side, i32) == 0
    low_part, high_part = jnp.where(zero, own, mate), jnp.where(zero, mate, own)
    for k in range(8):
        lanes = slice(128 * k, 128 * k + 128)
        out[QUARTER + 64 * k : QUARTER + 64 * k + 32] = low_part[:, lanes]
        out[QUARTER + 64 * k + 32 : QUARTER + 64 * k + 64] = high_part[:, lanes]


def base_mate_kernel(rows, own, mate, out):
    out[...] = (mm(rows[0], own[...]) + mm(rows[1], mate[...])).astype(bf16)


def base_own_kernel(near, far, own, mate, out):
    out[...] = mm(near[...], own[...]) + mm(far[...], mate[...])


def low_kernel(slots, meta, mate_meta, near, far, first, second, *refs):
    own, core, (kept_out, sent_out) = refs[:4], refs[4:8], refs[8:]
    down_own = jnp.concatenate([w[:QUARTER] for w in own], axis=1)
    down_core = jnp.concatenate([w[:QUARTER] for w in core], axis=1)

    def chosen(a, b, which, start, count):
        every = mm(a, down_own) + mm(b, down_core)
        adapter = row_adapters(which, start, count, slots)
        total = jnp.zeros((count, PADDED_RANK), f32)
        for j in range(4):
            total = jnp.where(adapter == j, every[:, 128 * j : 128 * j + 128], total)
        return total

    sent_out[:FIRST] = chosen(first[0], first[1], mate_meta, 0, FIRST)
    sent_out[FIRST:] = chosen(second[0], second[1], mate_meta, FIRST, LIVE - FIRST)
    kept_out[...] = chosen(near[...], far[...], meta, 0, LIVE)


def keys_kernel(slots, start, count, places, meta, ranks, base, arrived, low, low_mate, grads, gain, *refs):
    own, core = refs[:4], refs[4:8]
    has_sum = start > 0
    sums = refs[8] if has_sum else None
    refs = refs[9:] if has_sum else refs[8:]
    dlow_out, kept_out, sent_out = refs[:3]
    rest_out = None if has_sum else refs[3]
    up, total = refs[-2:]
    dp = lax.axis_index("dp")
    c = lax.axis_index("fsdp") % 2
    rows = slice(start, start + count)
    for j in range(4):
        for k in range(8):
            for part in range(2):
                source = QUARTER + 64 * k + 32 * part
                target = pl.multiple_of(128 * j + 64 * part + 32 * c, 32)
                up[pl.ds(target, 32), 128 * k : 128 * k + 128] = own[j][source : source + 32]
                target = pl.multiple_of(128 * j + 64 * part + 32 * (1 - c), 32)
                up[pl.ds(target, 32), 128 * k : 128 * k + 128] = core[j][source : source + 32]
    adapter = row_adapters(meta, start, count, slots)
    scales = [adapter_alpha_scale / jnp.full((1, HEAD), ranks[dp ^ j], i32).astype(f32) for j in range(4)]
    scale = jnp.zeros((count, HEAD), f32)
    for j in range(4):
        scale = jnp.where(adapter == j, scales[j], scale)
    lowrank = (low[rows] + low_mate[rows]).astype(bf16).astype(f32)
    spread = jnp.concatenate([jnp.where(adapter == j, lowrank, 0.0).astype(bf16) for j in range(4)], axis=1)
    added = mm(spread, up[...])
    parts = []
    for k in range(8):
        lanes = slice(128 * k, 128 * k + 128)
        held = (base[rows, lanes] + arrived[:, lanes].astype(f32)).astype(bf16).astype(f32)
        head = held + scale * added[:, lanes]
        inverse = lax.rsqrt(jnp.mean(head * head, axis=-1, keepdims=True) + norm_epsilon)
        normed = head * inverse
        incoming = grads[rows, lanes].astype(f32) * gain[...]
        mean = jnp.mean(incoming * normed, axis=-1, keepdims=True)
        parts.append((inverse * (incoming - normed * mean)).astype(bf16))
    key_grads = jnp.concatenate(parts, axis=1)
    every = mm_nt(key_grads, up[...])
    picked = jnp.zeros((count, PADDED_RANK), f32)
    for j in range(4):
        picked = jnp.where(adapter == j, every[:, 128 * j : 128 * j + 128], picked)
    dlow_out[...] = (scale * picked).astype(bf16)
    total[...] = mm_t(spread, key_grads)
    for i, j in enumerate(places):
        scale_j = scales[j][0:1, 0:1]
        for part in range(2):
            kept = pl.multiple_of(128 * j + 64 * part + 32 * c, 32)
            sent = pl.multiple_of(128 * j + 64 * part + 32 * (1 - c), 32)
            here = slice(32 * part, 32 * part + 32)
            one, two = total[pl.ds(kept, 32), :], total[pl.ds(sent, 32), :]
            if has_sum:
                one = one + sums[pl.ds(pl.multiple_of(kept, 32), 32), :]
                two = two + sums[pl.ds(pl.multiple_of(sent, 32), 32), :]
            kept_out[i, here, :] = one * scale_j
            sent_out[i, here, :] = two * scale_j
    if rest_out is not None:
        rest_out[...] = total[:256]


def up_kernel(kept, arrived, own_out, mate_out):
    x = lax.axis_index("fsdp") // 2
    for i in range(kept.shape[0]):
        here = pl.ds(pl.multiple_of(32 * x, 32), 32)
        there = pl.ds(pl.multiple_of(32 * (1 - x), 32), 32)
        own_out[i] = kept[i, here, :] + arrived[i, here, :]
        mate_out[i] = (kept[i, there, :] + arrived[i, there, :]).astype(bf16)


def down_kernel(slots, spans, places, metas, up_own, up_arrived, *refs):
    number = 4 * len(spans)
    tokens, dlows, outs = refs[:number], refs[number : 2 * number], refs[2 * number :]
    total = jnp.zeros((QUARTER, 128 * len(places)), f32)
    lhs, rhs = [], []
    for device in range(4):
        for n, (start, count) in enumerate(spans):
            dlow = dlows[device * len(spans) + n][...].astype(f32)
            adapter = row_adapters(metas.at[device], start, count, slots)
            rhs.append(
                jnp.concatenate([jnp.where(adapter == j, dlow, 0.0).astype(bf16) for j in places], axis=1)
            )
            held = tokens[device * len(spans) + n]
            lhs.append(held[0] if len(held.shape) == 3 else held[start : start + count])
    total = mm_t(jnp.concatenate(lhs, axis=0), jnp.concatenate(rhs, axis=0))
    for i, _ in enumerate(places):
        outs[i][:QUARTER] = total[:, 128 * i : 128 * i + 128].astype(outs[i].dtype)
        rows = up_own[i] + up_arrived[i].astype(f32)
        for k in range(8):
            outs[i][QUARTER + 32 * k : QUARTER + 32 * k + 32] = rows[:, 128 * k : 128 * k + 128].astype(
                outs[i].dtype
            )


def update_kernel(own, one, two, three, *refs):
    (down, up, down_m, up_m, down_v, up_v), outs = refs[:6], refs[6:]

    def gradient(rows):
        return own[rows] + one[rows].astype(f32) + (two[rows].astype(f32) + three[rows].astype(f32))

    step = 256
    for start in range(0, QUARTER, step):
        rows = slice(start, start + step)
        outs[0][rows], outs[2][rows], outs[4][rows] = optimizer_update(
            down[rows], gradient(rows), down_m[rows], down_v[rows]
        )
    for k in range(8):
        lanes = slice(128 * k, 128 * k + 128)
        rows = slice(QUARTER + 32 * k, QUARTER + 32 * k + 32)
        outs[1][:, lanes], outs[3][:, lanes], outs[5][:, lanes] = optimizer_update(
            up[:, lanes], gradient(rows), up_m[:, lanes], up_v[:, lanes]
        )


def after(value, *others):
    return lax.optimization_barrier((value,) + others)[0]


def local(
    tokens,
    cotangent,
    lengths,
    slot_adapter_index,
    adapter_rank_sizes,
    frozen,
    key_norm_weight,
    adapter_down_factor,
    adapter_up_factor,
    down_first_moment,
    up_first_moment,
    down_second_moment,
    up_second_moment,
):
    dp = lax.axis_index("dp")
    f = lax.axis_index("fsdp")
    slots = lengths.shape[1]

    def core(value):
        return lax.ppermute(value, "fsdp", [(i, i ^ 1) for i in range(4)])

    def across(value):
        return lax.ppermute(value, "fsdp", [(i, i ^ 2) for i in range(4)])

    def along(value, distance):
        return lax.ppermute(value, "dp", [(i, i ^ distance) for i in range(4)])

    place = slot_adapter_index[0] ^ dp
    key = (3 - place) * slots + jnp.arange(slots, dtype=i32)
    offset = jnp.sum(jnp.where(key[None, :] < key[:, None], lengths[0][None, :], 0), axis=1)
    meta = jnp.stack([offset, lengths[0], place])

    first, second = call(
        lambda *refs: pack_sent_kernel(slots, *refs),
        "pack_sent",
        [SMEM, HBM],
        [shape((2, FIRST, QUARTER), bf16), shape((2, LIVE - FIRST, QUARTER), bf16)],
        [meta, tokens],
        [pltpu.VMEM((2, tokens.shape[0], QUARTER), bf16), pltpu.SemaphoreType.DMA((2,))],
        flops=2 * LIVE * tokens.shape[0] * 2 * QUARTER,
    )
    first_in = across(first)
    second_in = across(second)

    rank = adapter_rank_sizes[dp]
    up_rows = f * 32 + jnp.arange(32)
    up_own = jnp.where((up_rows < rank)[:, None], adapter_up_factor[0], 0.0).astype(bf16)
    up_mate = across(up_own)
    (message,) = call(
        weights_kernel,
        "weights",
        [SMEM, VMEM, VMEM, VMEM],
        [shape((QUARTER + 512, PADDED_RANK), bf16)],
        [adapter_rank_sizes, adapter_down_factor[0], up_own, up_mate],
    )
    weights = [message, along(message, 1), along(message, 2), along(message, 3)]

    frozen_core = core(frozen)
    near, far, grads = call(
        lambda *refs: pack_kept_kernel(slots, *refs),
        "pack_kept",
        [SMEM, HBM, VMEM],
        [shape((LIVE, QUARTER), bf16), shape((LIVE, QUARTER), bf16), shape((LIVE, KEY_WIDTH), bf16)],
        [meta, tokens, cotangent],
        [pltpu.VMEM((2, tokens.shape[0], QUARTER), bf16), pltpu.SemaphoreType.DMA((2,))],
        flops=2 * LIVE * tokens.shape[0] * 2 * QUARTER,
    )
    far_core = core(far)
    mate_meta = across(meta)
    core_metas = core(jnp.stack([meta, mate_meta]))
    metas = jnp.concatenate([jnp.stack([meta, mate_meta]), core_metas])

    (base,) = call(
        base_own_kernel,
        "base_own",
        [VMEM] * 4,
        [shape((LIVE, KEY_WIDTH), f32)],
        [near, far, frozen, frozen_core],
        flops=2 * LIVE * 2 * QUARTER * KEY_WIDTH,
    )
    returned = []
    for rows in (first_in, second_in):
        (partial,) = call(
            base_mate_kernel,
            "base_mate",
            [VMEM] * 3,
            [shape((rows.shape[1], KEY_WIDTH), bf16)],
            [rows, frozen, frozen_core],
            flops=2 * rows.shape[1] * 2 * QUARTER * KEY_WIDTH,
        )
        returned.append(across(partial))
    first_core, second_core = core(first_in[1]), core(second_in[1])

    weights_core = [core(w) for w in weights]
    low, low_sent = call(
        lambda *refs: low_kernel(slots, *refs),
        "low",
        [SMEM, SMEM] + [VMEM] * 12,
        [shape((LIVE, PADDED_RANK), f32), shape((LIVE, PADDED_RANK), f32)],
        [meta, mate_meta, near, far, first_in, second_in] + weights + weights_core,
        flops=2 * 2 * LIVE * 2 * QUARTER * 512,
    )
    low_mate = across(low_sent)

    gain = key_norm_weight[None, :]

    def keys(start, count, places, arrived, sums):
        outs = [
            shape((count, PADDED_RANK), bf16),
            shape((len(places), 64, KEY_WIDTH), f32),
            shape((len(places), 64, KEY_WIDTH), f32),
        ]
        if not sums:
            outs.append(shape((256, KEY_WIDTH), f32))
        return call(
            lambda *refs: keys_kernel(slots, start, count, places, *refs),
            "keys",
            [SMEM, SMEM] + [VMEM] * (14 + len(sums)),
            outs,
            [meta, adapter_rank_sizes, base, arrived, low, low_mate, grads, gain]
            + weights
            + weights_core
            + sums,
            [pltpu.VMEM((512, KEY_WIDTH), bf16), pltpu.VMEM((512, KEY_WIDTH), f32)],
            flops=3 * 2 * count * 512 * KEY_WIDTH,
        )

    def exchange_low(dlow):
        mate = across(dlow)
        pair = core(jnp.stack([dlow, mate]))
        return [dlow, mate, pair[0], pair[1]]

    def exchange_up(kept, sent):
        own, mate = call(
            up_kernel,
            "up",
            [VMEM] * 2,
            [shape((kept.shape[0], 32, KEY_WIDTH), f32), shape((kept.shape[0], 32, KEY_WIDTH), bf16)],
            [kept, core(sent)],
        )
        return own, across(mate)

    def down(spans, places, up_parts, held, dlows, types):
        return call(
            lambda *refs: down_kernel(slots, spans, places, *refs),
            "down",
            [SMEM] + [VMEM] * (2 + len(held) + len(dlows)),
            [shape((QUARTER + 256, PADDED_RANK), t) for t in types],
            [metas, *up_parts, *held, *dlows],
            flops=2 * 4 * sum(n for _, n in spans) * QUARTER * 128 * len(places),
        )

    dlow_one, kept, sent, rest = keys(0, FIRST, (3, 2), returned[0], [])
    up_parts = exchange_up(kept, sent)
    dlow_first = exchange_low(dlow_one)
    head = ((0, FIRST),)
    first_core, far_core3 = first_core[None], far_core
    three, two = down(head, (3, 2), up_parts, [near, first_in, far_core3, first_core], dlow_first, [bf16, bf16])
    three_in = along(three, 3)
    two_in = along(two, 2)

    dlow_two, kept, sent = keys(FIRST, LIVE - FIRST, (1, 0), returned[1], [rest])
    up_parts = exchange_up(kept, sent)
    dlow_second = exchange_low(dlow_two)
    both = ((0, FIRST), (FIRST, LIVE - FIRST))
    held = [near, near, first_in, second_in, far_core3, far_core3, first_core, second_core[None]]
    dlows = [d for pair in zip(dlow_first, dlow_second) for d in pair]
    one, own = down(both, (1, 0), up_parts, held, dlows, [bf16, f32])
    one_in = along(one, 1)

    outs = call(
        update_kernel,
        "update",
        [VMEM] * 10,
        [shape(adapter_down_factor.shape[1:], f32), shape(adapter_up_factor.shape[1:], f32)] * 3,
        [own, one_in, two_in, three_in]
        + [
            a[0]
            for a in (
                adapter_down_factor,
                adapter_up_factor,
                down_first_moment,
                up_first_moment,
                down_second_moment,
                up_second_moment,
            )
        ],
    )
    return tuple(o[None] for o in outs)


def solution(mesh):
    paired = mesh.shape["dp"] == 4 and mesh.shape["fsdp"] == 4
    return jax.shard_map(
        local if paired else local_general,
        mesh=mesh,
        in_specs=(
            P(("parts", "dp", "fsdp"), None),
            P(("parts", "dp", "fsdp"), None),
            P(("parts", "dp", "fsdp"), None),
            P(("parts", "dp", "fsdp"), None),
            P(),
            P("fsdp", None),
            P(),
            P(("parts", "dp"), "fsdp", None),
            P(("parts", "dp"), "fsdp", None),
            P(("parts", "dp"), "fsdp", None),
            P(("parts", "dp"), "fsdp", None),
            P(("parts", "dp"), "fsdp", None),
            P(("parts", "dp"), "fsdp", None),
        ),
        out_specs=(
            P(("parts", "dp"), "fsdp", None),
            P(("parts", "dp"), "fsdp", None),
            P(("parts", "dp"), "fsdp", None),
            P(("parts", "dp"), "fsdp", None),
            P(("parts", "dp"), "fsdp", None),
            P(("parts", "dp"), "fsdp", None),
        ),
        check_vma=False,
    )
```

time: 218 us -> 196 us (0.90)
  the two profiles are of different devices: /device:TPU:0 before, /device:TPU:8 now
where the time goes in v1:
time: 196 us
  waiting for transfers between devices  97.7 us (50%)
  Pallas kernels  61 us (31%)
  starting transfers between devices  21.6 us (11%)
  local copies, waits for them, and re-layouts  9.82 us (5%)
  other arithmetic  4.85 us (2%)
    ppermute x6, waiting for transfers between devices, along(): return lax.ppermute(value, 'dp', [(i, i ^ distance) for i in range(4)])  66.5 us
    pallas_call x14, Pallas kernels, call(): pl.pallas_call(kernel, name=name, in_specs=list(specs), out_specs=tuple((...  61 us
    ppermute x11, waiting for transfers between devices, across(): return lax.ppermute(value, 'fsdp', [(i, i ^ 2) for i in range(4)])  29.9 us
    ppermute x11, starting transfers between devices, across(): return lax.ppermute(value, 'fsdp', [(i, i ^ 2) for i in range(4)])  12 us
    ppermute x6, starting transfers between devices, along(): return lax.ppermute(value, 'dp', [(i, i ^ distance) for i in range(4)])  7.79 us
    unnamed x68, local copies, waits for them, and re-layouts  6.89 us
  transfers between devices with their start and end apart: 30, of which 12 were waited for; matrix products, arithmetic and copies ran while one was open for 4% of the time, Pallas kernels for 29%

profile of v1, /device:TPU:8, one launch (start us, length us, event | category | flops | bytes accessed | tf_op | source)
XLA Modules:
  0.0 195.9 jit_solution(4728946000333917712)
XLA Ops:
  3.5 4.4 %pack_sent.1 = (bf16[2,192,1280]{2,1,0:T(8,128)(2,1)}, bf16[2,96,1280]{2,1,0:T(8,128)(2,1)}) custom-call(s32[3,12]{1,0:T(4,128)} %get-tuple-element.69.refs_0_, bf16[384,5120]{1,0:T(8,128)(2,1)} %refs_1_.5), custom_call_target="tpu_custom_call" | custom-call | flops 566231040 | bytes 5406864 | tf_op jit(solution)/shard_map/pack_sent/pallas_call | solution.py:196
  7.9 1.6 collective-permute-start.5
  11.4 22.3 %collective-permute-done.6.up_mate = bf16[32,1024]{1,0:T(8,128)(2,1)S(1)} collective-permute-done((bf16[32,1024]{1,0:T(8,128)(2,1)S(1)}, bf16[32,1024]{1,0:T(8,128)(2,1)S(1)}, u32[]{:S(2)}, u32[]{:S(2)}) %collective-permute-start.6) | collective-permute-done | bytes 65568 | tf_op jit(solution)/shard_map/ppermute | solution.py:458
  34.3 2.0 %weights.1.refs_6_.refs_8_ = bf16[1792,128]{1,0:T(8,128)(2,1)} custom-call(s32[4]{0:T(128)} %refs_1_.7, f32[1280,128]{1,0:T(8,128)} %bitcast.42, bf16[32,1024]{1,0:T(8,128)(2,1)} %copy-done.23, bf16[32,1024]{1,0:T(8,128)(2,1)} %copy-done.30), custom_call_target="tpu_custom_call" | custom-call | bytes 1245200 | tf_op jit(solution)/shard_map/weights/pallas_call | solution.py:196
  36.6 1.7 collective-permute-start
  38.3 1.8 collective-permute-done.refs_1_
  40.2 2.9 %collective-permute-start.8 = (bf16[1792,128]{1,0:T(8,128)(2,1)}, bf16[1792,128]{1,0:T(8,128)(2,1)S(1)}, u32[]{:S(2)}, u32[]{:S(2)}) collective-permute-start(bf16[1792,128]{1,0:T(8,128)(2,1)} %weights.1.refs_6_.refs_8_), channel_id=1, source_target_pairs={{0,8},{4,12},{8,0},{12,4},{1,9},{5,13},{9,1},{13,5},{2,10},{6,14},... | collective-permute-start | bytes 1376264 | tf_op jit(solution)/shard_map/ppermute | solution.py:461
  44.3 7.5 %collective-permute-done.7.refs_7_.refs_9_ = bf16[1792,128]{1,0:T(8,128)(2,1)S(1)} collective-permute-done((bf16[1792,128]{1,0:T(8,128)(2,1)}, bf16[1792,128]{1,0:T(8,128)(2,1)S(1)}, u32[]{:S(2)}, u32[]{:S(2)}) %collective-permute-start.7) | collective-permute-done | bytes 458784 | tf_op jit(solution)/shard_map/ppermute | solution.py:461
  51.8 1.5 collective-permute-start.3
  53.3 4.7 %pack_kept.1 = (bf16[288,1280]{1,0:T(8,128)(2,1)}, bf16[288,1280]{1,0:T(8,128)(2,1)}, bf16[288,1024]{1,0:T(8,128)(2,1)}) custom-call(s32[3,12]{1,0:T(4,128)} %get-tuple-element.69.refs_0_, bf16[384,5120]{1,0:T(8,128)(2,1)} %refs_1_.5, bf16[384,1024]{1,0:T(8,128)(2,1)} %refs_2_.1), custom_call_target="tpu_custom_call" | custom-call | flops 566231040 | bytes 6783120 | tf_op jit(solution)/shard_map/pack_kept/pallas_call | solution.py:196
  58.6 15.3 %collective-permute-done.8.refs_8_.refs_10_ = bf16[1792,128]{1,0:T(8,128)(2,1)S(1)} collective-permute-done((bf16[1792,128]{1,0:T(8,128)(2,1)}, bf16[1792,128]{1,0:T(8,128)(2,1)S(1)}, u32[]{:S(2)}, u32[]{:S(2)}) %collective-permute-start.8) | collective-permute-done | bytes 458784 | tf_op jit(solution)/shard_map/ppermute | solution.py:461
  73.9 10.2 %collective-permute-done.9.refs_9_.refs_11_ = bf16[1792,128]{1,0:T(8,128)(2,1)S(1)} collective-permute-done((bf16[1792,128]{1,0:T(8,128)(2,1)}, bf16[1792,128]{1,0:T(8,128)(2,1)S(1)}, u32[]{:S(2)}, u32[]{:S(2)}) %collective-permute-start.9) | collective-permute-done | bytes 458784 | tf_op jit(solution)/shard_map/ppermute | solution.py:461
  84.7 1.4 copy-done
  86.1 4.8 %base_mate.3 = bf16[192,1024]{1,0:T(8,128)(2,1)} custom-call(bf16[2,192,1280]{2,1,0:T(8,128)(2,1)} %collective-permute-done.5.refs_4_.rows.refs_5_, bf16[1280,1024]{1,0:T(8,128)(2,1)} %own.5, bf16[1280,1024]{1,0:T(8,128)(2,1)} %copy-done), custom_call_target="tpu_custom_call" | custom-call | flops 1006632960 | bytes 6619136 | tf_op jit(solution)/shard_map/base_mate/pallas_call | solution.py:196
  90.9 1.6 collective-permute-start.15
  93.7 5.6 %low.1 = (f32[288,128]{1,0:T(8,128)}, f32[288,128]{1,0:T(8,128)}) custom-call(s32[3,12]{1,0:T(4,128)} %get-tuple-element.69.refs_0_, s32[3,12]{1,0:T(4,128)} %copy-done.31, bf16[288,1280]{1,0:T(8,128)(2,1)} %get-tuple-element.34.near.refs_2_.refs_3_.refs_4_, bf16[288,1280]{1,0:T(8,128)(2,1)} %get-tuple-element.35.far.refs_3_, ...), custom_call_target="tpu_custom_call" | custom-call | flops 1509949440 | bytes 6914336 | tf_op jit(solution)/shard_map/low/pallas_call | solution.py:196
  99.9 4.3 %base_mate.2 = bf16[96,1024]{1,0:T(8,128)(2,1)} custom-call(bf16[2,96,1280]{2,1,0:T(8,128)(2,1)} %copy-done.3, bf16[1280,1024]{1,0:T(8,128)(2,1)} %own.5, bf16[1280,1024]{1,0:T(8,128)(2,1)} %copy-done), custom_call_target="tpu_custom_call" | custom-call | flops 503316480 | bytes 5931008 | tf_op jit(solution)/shard_map/base_mate/pallas_call | solution.py:196
  104.2 1.5 collective-permute-start.4
  105.7 5.7 %base_own.1.refs_2_ = f32[288,1024]{1,0:T(8,128)} custom-call(bf16[288,1280]{1,0:T(8,128)(2,1)} %get-tuple-element.34.near.refs_2_.refs_3_.refs_4_, bf16[288,1280]{1,0:T(8,128)(2,1)} %get-tuple-element.35.far.refs_3_, bf16[1280,1024]{1,0:T(8,128)(2,1)} %own.5, bf16[1280,1024]{1,0:T(8,128)(2,1)} %copy-done), custom_call_target="tpu_custom_call" | custom-call | flops 1509949440 | bytes 7897088 | tf_op jit(solution)/shard_map/base_own/pallas_call | solution.py:196
  112.2 5.8 %keys.2 = (bf16[192,128]{1,0:T(8,128)(2,1)}, f32[2,64,1024]{2,1,0:T(8,128)}, f32[2,64,1024]{2,1,0:T(8,128)}, f32[256,1024]{1,0:T(8,128)}) custom-call(s32[3,12]{1,0:T(4,128)} %get-tuple-element.69.refs_0_, s32[4]{0:T(128)} %refs_1_.7, f32[288,1024]{1,0:T(8,128)} %base_own.1.refs_2_, bf16[192,1024]{1,0:T(8,128)(2,1)} %copy-done.20, ...), custom_call_target="tpu_custom_call" | custom-call | flops 603979776 | bytes 8274592 | tf_op jit(solution)/shard_map/keys/pallas_call | solution.py:196
  118.7 5.7 %keys.3 = (bf16[96,128]{1,0:T(8,128)(2,1)}, f32[2,64,1024]{2,1,0:T(8,128)}, f32[2,64,1024]{2,1,0:T(8,128)}) custom-call(s32[3,12]{1,0:T(4,128)} %get-tuple-element.69.refs_0_, s32[4]{0:T(128)} %refs_1_.7, f32[288,1024]{1,0:T(8,128)} %base_own.1.refs_2_, bf16[96,1024]{1,0:T(8,128)(2,1)} %copy-done.25, f32[288,128]{1,0:T(8,128)} %get-tuple-element.38.refs_4_, ...), custom_call_target="tpu_custom_call" | custom-call | flops 301989888 | bytes 8053408 | tf_op jit(solution)/shard_map/keys/pallas_call | solution.py:196
  126.7 1.9 collective-permute-done.22.refs_14_
  129.8 2.8 %collective-permute-done.21.refs_13_.refs_8_ = bf16[192,128]{1,0:T(8,128)(2,1)S(1)} collective-permute-done((bf16[192,128]{1,0:T(8,128)(2,1)S(1)}, bf16[192,128]{1,0:T(8,128)(2,1)S(1)}, u32[]{:S(2)}, u32[]{:S(2)}) %collective-permute-start.21) | collective-permute-done | bytes 49184 | tf_op jit(solution)/shard_map/ppermute | solution.py:458
  135.0 2.0 %up.2 = (f32[2,32,1024]{2,1,0:T(8,128)}, bf16[2,32,1024]{2,1,0:T(8,128)(2,1)}) custom-call(f32[2,64,1024]{2,1,0:T(8,128)} %get-tuple-element.42.kept, f32[2,64,1024]{2,1,0:T(8,128)} %copy-done.16), custom_call_target="tpu_custom_call" | custom-call | bytes 1441792 | tf_op jit(solution)/shard_map/up/pallas_call | solution.py:196
  137.8 2.0 %up.3 = (f32[2,32,1024]{2,1,0:T(8,128)}, bf16[2,32,1024]{2,1,0:T(8,128)(2,1)}) custom-call(f32[2,64,1024]{2,1,0:T(8,128)} %get-tuple-element.50.kept, f32[2,64,1024]{2,1,0:T(8,128)} %copy-done.15), custom_call_target="tpu_custom_call" | custom-call | bytes 1441792 | tf_op jit(solution)/shard_map/up/pallas_call | solution.py:196
  143.5 5.5 %down.2 = (bf16[1536,128]{1,0:T(8,128)(2,1)}, f32[1536,128]{1,0:T(8,128)}) custom-call(s32[4,3,12]{2,1,0:T(4,128)} %pad_add_fusion.refs_0_, f32[2,32,1024]{2,1,0:T(8,128)} %get-tuple-element.44.refs_1_, bf16[2,32,1024]{2,1,0:T(8,128)(2,1)} %copy-done.27, bf16[288,1280]{1,0:T(8,128)(2,1)} %get-tuple-element.34.near.refs_2_.refs_3_.refs_4_, ...), custom_call_target="tpu_custom_call" | custom-call | flops 754974720 | bytes 7029312 | tf_op jit(solution)/shard_map/down/pallas_call | solution.py:196
  149.7 4.2 %down.3 = (bf16[1536,128]{1,0:T(8,128)(2,1)}, bf16[1536,128]{1,0:T(8,128)(2,1)}) custom-call(s32[4,3,12]{2,1,0:T(4,128)} %pad_add_fusion.refs_0_, f32[2,32,1024]{2,1,0:T(8,128)} %get-tuple-element.52.refs_1_, bf16[2,32,1024]{2,1,0:T(8,128)(2,1)} %copy-done.26, bf16[288,1280]{1,0:T(8,128)(2,1)} %get-tuple-element.34.near.refs_2_.refs_3_.refs_4_, ...), custom_call_target="tpu_custom_call" | custom-call | flops 503316480 | bytes 4325952 | tf_op jit(solution)/shard_map/down/pallas_call | solution.py:196
  153.9 3.0 %collective-permute-start.28 = (bf16[1536,128]{1,0:T(8,128)(2,1)}, bf16[1536,128]{1,0:T(8,128)(2,1)S(1)}, u32[]{:S(2)}, u32[]{:S(2)}) collective-permute-start(bf16[1536,128]{1,0:T(8,128)(2,1)} %get-tuple-element.54), channel_id=1, source_target_pairs={{0,8},{4,12},{8,0},{12,4},{1,9},{5,13},{9,1},{13,5},{2,10},{6,14},... | collective-permute-start | bytes 1179656 | tf_op jit(solution)/shard_map/ppermute | solution.py:461
  157.4 3.9 %collective-permute-done.25.one = bf16[1536,128]{1,0:T(8,128)(2,1)S(1)} collective-permute-done((bf16[1536,128]{1,0:T(8,128)(2,1)}, bf16[1536,128]{1,0:T(8,128)(2,1)S(1)}, u32[]{:S(2)}, u32[]{:S(2)}) %collective-permute-start.25) | collective-permute-done | bytes 393248 | tf_op jit(solution)/shard_map/ppermute | solution.py:461
  161.3 21.7 %collective-permute-done.28.two = bf16[1536,128]{1,0:T(8,128)(2,1)S(1)} collective-permute-done((bf16[1536,128]{1,0:T(8,128)(2,1)}, bf16[1536,128]{1,0:T(8,128)(2,1)S(1)}, u32[]{:S(2)}, u32[]{:S(2)}) %collective-permute-start.28) | collective-permute-done | bytes 393248 | tf_op jit(solution)/shard_map/ppermute | solution.py:461
  183.0 8.0 %collective-permute-done.29.three = bf16[1536,128]{1,0:T(8,128)(2,1)S(1)} collective-permute-done((bf16[1536,128]{1,0:T(8,128)(2,1)}, bf16[1536,128]{1,0:T(8,128)(2,1)S(1)}, u32[]{:S(2)}, u32[]{:S(2)}) %collective-permute-start.29) | collective-permute-done | bytes 393248 | tf_op jit(solution)/shard_map/ppermute | solution.py:461
  191.8 4.2 %update.1 = (f32[1280,128]{1,0:T(8,128)}, f32[32,1024]{1,0:T(8,128)}, f32[1280,128]{1,0:T(8,128)}, f32[32,1024]{1,0:T(8,128)}, f32[1280,128]{1,0:T(8,128)}, /*index=5*/f32[32,1024]{1,0:T(8,128)}) custom-call(f32[1536,128]{1,0:T(8,128)} %get-tuple-element.48.own, bf16[1536,128]{1,0:T(8,128)(2,1)} %copy-done.19, bf16[1536,128]{1,0:T(8,128)(2,1)} %copy-done.21, ...), custom_call_target="tpu_custom_call" | custom-call | bytes 6684672 | tf_op jit(solution)/shard_map/update/pallas_call | solution.py:196
  (125 shorter events, 23.4 us)
Async XLA Ops:
  0.7 84.0 %collective-permute-start.2 = (bf16[1280,1024]{1,0:T(8,128)(2,1)}, bf16[1280,1024]{1,0:T(8,128)(2,1)S(1)}, u32[]{:S(2)}, u32[]{:S(2)}) collective-permute-start(bf16[1280,1024]{1,0:T(8,128)(2,1)} %own.5), channel_id=1, source_target_pairs={{0,1},{1,0},{2,3},{3,2},{4,5},{5,4},{6,7},{7,6},{8,9},{9,8},{10,11... | collective-permute-start | bytes 7864328 | tf_op jit(solution)/shard_map/ppermute | solution.py:455
  7.9 76.2 %collective-permute-start.5 = (bf16[2,192,1280]{2,1,0:T(8,128)(2,1)}, bf16[2,192,1280]{2,1,0:T(8,128)(2,1)}, u32[]{:S(2)}, u32[]{:S(2)}) collective-permute-start(bf16[2,192,1280]{2,1,0:T(8,128)(2,1)} %get-tuple-element.37), channel_id=1, source_target_pairs={{0,2},{1,3},{2,0},{3,1},{4,6},{5,7},{6,4},{7,5},{8,10},{9,11},{10,... | collective-permute-start | bytes 2949128 | tf_op jit(solution)/shard_map/ppermute | solution.py:458
  10.8 22.9 %collective-permute-start.6 = (bf16[32,1024]{1,0:T(8,128)(2,1)S(1)}, bf16[32,1024]{1,0:T(8,128)(2,1)S(1)}, u32[]{:S(2)}, u32[]{:S(2)}) collective-permute-start(bf16[32,1024]{1,0:T(8,128)(2,1)S(1)} %select_convert_fusion.up_own), channel_id=1, source_target_pairs={{0,2},{1,3},{2,0},{3,1},{4,6},{5,7},{6,4},{7,5},{8,10},{9,11},{10,... | collective-permute-start | bytes 196616 | tf_op jit(solution)/shard_map/ppermute | solution.py:458
  36.4 15.4 %collective-permute-start.7 = (bf16[1792,128]{1,0:T(8,128)(2,1)}, bf16[1792,128]{1,0:T(8,128)(2,1)S(1)}, u32[]{:S(2)}, u32[]{:S(2)}) collective-permute-start(bf16[1792,128]{1,0:T(8,128)(2,1)} %weights.1.refs_6_.refs_8_), channel_id=1, source_target_pairs={{0,4},{4,0},{8,12},{12,8},{1,5},{5,1},{9,13},{13,9},{2,6},{6,2},{1... | collective-permute-start | bytes 1376264 | tf_op jit(solution)/shard_map/ppermute | solution.py:461
  36.6 3.6 %collective-permute-start = (s32[3,12]{1,0:T(4,128)S(1)}, s32[3,12]{1,0:T(4,128)S(1)}, u32[]{:S(2)}, u32[]{:S(2)}) collective-permute-start(s32[3,12]{1,0:T(4,128)S(1)} %copy-done.29), channel_id=1, source_target_pairs={{0,2},{1,3},{2,0},{3,1},{4,6},{5,7},{6,4},{7,5},{8,10},{9,11},{10,... | collective-permute-start | bytes 440 | tf_op jit(solution)/shard_map/ppermute | solution.py:458
  40.2 50.7 %copy-start.31 = (s32[3,12]{1,0:T(4,128)}, s32[3,12]{1,0:T(4,128)S(1)}, u32[]{:S(2)}) copy-start(s32[3,12]{1,0:T(4,128)S(1)} %collective-permute-done.refs_1_) | copy-start | bytes 436
  40.2 2.9 %collective-permute-start.1 = (s32[2,3,12]{2,1,0:T(4,128)S(1)}, s32[2,3,12]{2,1,0:T(4,128)S(1)}, u32[]{:S(2)}, u32[]{:S(2)}) collective-permute-start(s32[2,3,12]{2,1,0:T(4,128)S(1)} %pad_add_fusion.1), channel_id=1, source_target_pairs={{0,1},{1,0},{2,3},{3,2},{4,5},{5,4},{6,7},{7,6},{8,9},{9,8},{10,11... | collective-permute-start | bytes 872 | tf_op jit(solution)/shard_map/ppermute | solution.py:455
  40.2 33.8 %collective-permute-start.8 = (bf16[1792,128]{1,0:T(8,128)(2,1)}, bf16[1792,128]{1,0:T(8,128)(2,1)S(1)}, u32[]{:S(2)}, u32[]{:S(2)}) collective-permute-start(bf16[1792,128]{1,0:T(8,128)(2,1)} %weights.1.refs_6_.refs_8_), channel_id=1, source_target_pairs={{0,8},{4,12},{8,0},{12,4},{1,9},{5,13},{9,1},{13,5},{2,10},{6,14},... | collective-permute-start | bytes 1376264 | tf_op jit(solution)/shard_map/ppermute | solution.py:461
  43.1 41.0 %collective-permute-start.9 = (bf16[1792,128]{1,0:T(8,128)(2,1)}, bf16[1792,128]{1,0:T(8,128)(2,1)S(1)}, u32[]{:S(2)}, u32[]{:S(2)}) collective-permute-start(bf16[1792,128]{1,0:T(8,128)(2,1)} %weights.1.refs_6_.refs_8_), channel_id=1, source_target_pairs={{0,12},{4,8},{8,4},{12,0},{1,13},{5,9},{9,5},{13,1},{2,14},{6,10},... | collective-permute-start | bytes 1376264 | tf_op jit(solution)/shard_map/ppermute | solution.py:461
  51.8 39.1 %copy-start.4 = (bf16[1792,128]{1,0:T(8,128)(2,1)}, bf16[1792,128]{1,0:T(8,128)(2,1)S(1)}, u32[]{:S(2)}) copy-start(bf16[1792,128]{1,0:T(8,128)(2,1)S(1)} %collective-permute-done.7.refs_7_.refs_9_) | copy-start | bytes 1376260
  51.8 39.1 %collective-permute-start.3 = (bf16[2,96,1280]{2,1,0:T(8,128)(2,1)}, bf16[2,96,1280]{2,1,0:T(8,128)(2,1)S(1)}, u32[]{:S(2)}, u32[]{:S(2)}) collective-permute-start(bf16[2,96,1280]{2,1,0:T(8,128)(2,1)} %get-tuple-element.36), channel_id=1, source_target_pairs={{0,2},{1,3},{2,0},{3,1},{4,6},{5,7},{6,4},{7,5},{8,10},{9,11},{10,... | collective-permute-start | bytes 1474568 | tf_op jit(solution)/shard_map/ppermute | solution.py:458
  73.9 18.5 %collective-permute-start.10 = (bf16[1792,128]{1,0:T(8,128)(2,1)S(1)}, bf16[1792,128]{1,0:T(8,128)(2,1)S(1)}, u32[]{:S(2)}, u32[]{:S(2)}) collective-permute-start(bf16[1792,128]{1,0:T(8,128)(2,1)S(1)} %copy-done.1), channel_id=1, source_target_pairs={{0,1},{1,0},{2,3},{3,2},{4,5},{5,4},{6,7},{7,6},{8,9},{9,8},{10,11... | collective-permute-start | bytes 1376264 | tf_op jit(solution)/shard_map/ppermute | solution.py:455
  84.1 8.5 %collective-permute-start.11 = (bf16[1792,128]{1,0:T(8,128)(2,1)S(1)}, bf16[1792,128]{1,0:T(8,128)(2,1)S(1)}, u32[]{:S(2)}, u32[]{:S(2)}) collective-permute-start(bf16[1792,128]{1,0:T(8,128)(2,1)S(1)} %collective-permute-done.7.refs_7_.refs_9_), channel_id=1, source_target_pairs={{0,1},{1,0},{2,3},{3,2},{4,5},{5,4},{6,7},{7,6},{8,9},{9,8},{10,11... | collective-permute-start | bytes 1376264 | tf_op jit(solution)/shard_map/ppermute | solution.py:455
  84.1 8.5 %collective-permute-start.12 = (bf16[1792,128]{1,0:T(8,128)(2,1)S(1)}, bf16[1792,128]{1,0:T(8,128)(2,1)S(1)}, u32[]{:S(2)}, u32[]{:S(2)}) collective-permute-start(bf16[1792,128]{1,0:T(8,128)(2,1)S(1)} %collective-permute-done.8.refs_8_.refs_10_), channel_id=1, source_target_pairs={{0,1},{1,0},{2,3},{3,2},{4,5},{5,4},{6,7},{7,6},{8,9},{9,8},{10,11... | collective-permute-start | bytes 1376264 | tf_op jit(solution)/shard_map/ppermute | solution.py:455
  84.6 8.0 %collective-permute-start.13 = (bf16[1792,128]{1,0:T(8,128)(2,1)S(1)}, bf16[1792,128]{1,0:T(8,128)(2,1)S(1)}, u32[]{:S(2)}, u32[]{:S(2)}) collective-permute-start(bf16[1792,128]{1,0:T(8,128)(2,1)S(1)} %collective-permute-done.9.refs_9_.refs_11_), channel_id=1, source_target_pairs={{0,1},{1,0},{2,3},{3,2},{4,5},{5,4},{6,7},{7,6},{8,9},{9,8},{10,11... | collective-permute-start | bytes 1376264 | tf_op jit(solution)/shard_map/ppermute | solution.py:455
  90.9 20.5 %collective-permute-start.15 = (bf16[192,1024]{1,0:T(8,128)(2,1)}, bf16[192,1024]{1,0:T(8,128)(2,1)S(1)}, u32[]{:S(2)}, u32[]{:S(2)}) collective-permute-start(bf16[192,1024]{1,0:T(8,128)(2,1)} %base_mate.3), channel_id=1, source_target_pairs={{0,2},{1,3},{2,0},{3,1},{4,6},{5,7},{6,4},{7,5},{8,10},{9,11},{10,... | collective-permute-start | bytes 1179656 | tf_op jit(solution)/shard_map/ppermute | solution.py:458
  92.5 49.2 %collective-permute-start.18 = (bf16[288,1280]{1,0:T(8,128)(2,1)S(1)}, bf16[288,1280]{1,0:T(8,128)(2,1)S(1)}, u32[]{:S(2)}, u32[]{:S(2)}) collective-permute-start(bf16[288,1280]{1,0:T(8,128)(2,1)S(1)} %copy-done.11), channel_id=1, source_target_pairs={{0,1},{1,0},{2,3},{3,2},{4,5},{5,4},{6,7},{7,6},{8,9},{9,8},{10,11... | collective-permute-start | bytes 2211848 | tf_op jit(solution)/shard_map/ppermute | solution.py:455
  99.4 12.1 %collective-permute-start.14 = (f32[288,128]{1,0:T(8,128)}, f32[288,128]{1,0:T(8,128)S(1)}, u32[]{:S(2)}, u32[]{:S(2)}) collective-permute-start(f32[288,128]{1,0:T(8,128)} %get-tuple-element.39), channel_id=1, source_target_pairs={{0,2},{1,3},{2,0},{3,1},{4,6},{5,7},{6,4},{7,5},{8,10},{9,11},{10,... | collective-permute-start | bytes 442376 | tf_op jit(solution)/shard_map/ppermute | solution.py:458
  104.2 13.8 %collective-permute-start.4 = (bf16[96,1024]{1,0:T(8,128)(2,1)}, bf16[96,1024]{1,0:T(8,128)(2,1)S(1)}, u32[]{:S(2)}, u32[]{:S(2)}) collective-permute-start(bf16[96,1024]{1,0:T(8,128)(2,1)} %base_mate.2), channel_id=1, source_target_pairs={{0,2},{1,3},{2,0},{3,1},{4,6},{5,7},{6,4},{7,5},{8,10},{9,11},{10,... | collective-permute-start | bytes 589832 | tf_op jit(solution)/shard_map/ppermute | solution.py:458
  124.4 9.6 %collective-permute-start.16 = (f32[2,64,1024]{2,1,0:T(8,128)}, f32[2,64,1024]{2,1,0:T(8,128)S(1)}, u32[]{:S(2)}, u32[]{:S(2)}) collective-permute-start(f32[2,64,1024]{2,1,0:T(8,128)} %get-tuple-element.43), channel_id=1, source_target_pairs={{0,1},{1,0},{2,3},{3,2},{4,5},{5,4},{6,7},{7,6},{8,9},{9,8},{10,11... | collective-permute-start | bytes 1572872 | tf_op jit(solution)/shard_map/ppermute | solution.py:455
  124.4 4.1 %collective-permute-start.22 = (bf16[96,128]{1,0:T(8,128)(2,1)}, bf16[96,128]{1,0:T(8,128)(2,1)S(1)}, u32[]{:S(2)}, u32[]{:S(2)}) collective-permute-start(bf16[96,128]{1,0:T(8,128)(2,1)} %get-tuple-element.47.refs_12_), channel_id=1, source_target_pairs={{0,2},{1,3},{2,0},{3,1},{4,6},{5,7},{6,4},{7,5},{8,10},{9,11},{10,... | collective-permute-start | bytes 73736 | tf_op jit(solution)/shard_map/ppermute | solution.py:458
  125.0 12.0 %collective-permute-start.26 = (f32[2,64,1024]{2,1,0:T(8,128)S(1)}, f32[2,64,1024]{2,1,0:T(8,128)S(1)}, u32[]{:S(2)}, u32[]{:S(2)}) collective-permute-start(f32[2,64,1024]{2,1,0:T(8,128)S(1)} %copy-done.33), channel_id=1, source_target_pairs={{0,1},{1,0},{2,3},{3,2},{4,5},{5,4},{6,7},{7,6},{8,9},{9,8},{10,11... | collective-permute-start | bytes 1572872 | tf_op jit(solution)/shard_map/ppermute | solution.py:455
  126.3 15.5 %collective-permute-start.19 = (bf16[192,1280]{1,0:T(8,128)(2,1)S(1)}, bf16[192,1280]{1,0:T(8,128)(2,1)S(1)}, u32[]{:S(2)}, u32[]{:S(2)}) collective-permute-start(bf16[192,1280]{1,0:T(8,128)(2,1)S(1)} %slice_bitcast_fusion), channel_id=1, source_target_pairs={{0,1},{1,0},{2,3},{3,2},{4,5},{5,4},{6,7},{7,6},{8,9},{9,8},{10,11... | collective-permute-start | bytes 1474568 | tf_op jit(solution)/shard_map/ppermute | solution.py:455
  128.6 4.1 %collective-permute-start.21 = (bf16[192,128]{1,0:T(8,128)(2,1)S(1)}, bf16[192,128]{1,0:T(8,128)(2,1)S(1)}, u32[]{:S(2)}, u32[]{:S(2)}) collective-permute-start(bf16[192,128]{1,0:T(8,128)(2,1)S(1)} %copy-done.17), channel_id=1, source_target_pairs={{0,2},{1,3},{2,0},{3,1},{4,6},{5,7},{6,4},{7,5},{8,10},{9,11},{10,... | collective-permute-start | bytes 147464 | tf_op jit(solution)/shard_map/ppermute | solution.py:458
  132.6 1.2 collective-permute-start.24
  133.9 7.9 %collective-permute-start.20 = (bf16[96,1280]{1,0:T(8,128)(2,1)S(1)}, bf16[96,1280]{1,0:T(8,128)(2,1)S(1)}, u32[]{:S(2)}, u32[]{:S(2)}) collective-permute-start(bf16[96,1280]{1,0:T(8,128)(2,1)S(1)} %slice_bitcast_fusion.1), channel_id=1, source_target_pairs={{0,1},{1,0},{2,3},{3,2},{4,5},{5,4},{6,7},{7,6},{8,9},{9,8},{10,11... | collective-permute-start | bytes 737288 | tf_op jit(solution)/shard_map/ppermute | solution.py:455
  134.0 5.8 %collective-permute-start.23 = (bf16[2,192,128]{2,1,0:T(8,128)(2,1)S(1)}, bf16[2,192,128]{2,1,0:T(8,128)(2,1)S(1)}, u32[]{:S(2)}, u32[]{:S(2)}) collective-permute-start(bf16[2,192,128]{2,1,0:T(8,128)(2,1)S(1)} %pad_maximum_fusion), channel_id=1, source_target_pairs={{0,1},{1,0},{2,3},{3,2},{4,5},{5,4},{6,7},{7,6},{8,9},{9,8},{10,11... | collective-permute-start | bytes 294920 | tf_op jit(solution)/shard_map/ppermute | solution.py:455
  137.0 5.8 %collective-permute-start.17 = (bf16[2,32,1024]{2,1,0:T(8,128)(2,1)}, bf16[2,32,1024]{2,1,0:T(8,128)(2,1)S(1)}, u32[]{:S(2)}, u32[]{:S(2)}) collective-permute-start(bf16[2,32,1024]{2,1,0:T(8,128)(2,1)} %get-tuple-element.45), channel_id=1, source_target_pairs={{0,2},{1,3},{2,0},{3,1},{4,6},{5,7},{6,4},{7,5},{8,10},{9,11},{10,... | collective-permute-start | bytes 393224 | tf_op jit(solution)/shard_map/ppermute | solution.py:458
  139.8 9.2 %collective-permute-start.27 = (bf16[2,32,1024]{2,1,0:T(8,128)(2,1)}, bf16[2,32,1024]{2,1,0:T(8,128)(2,1)S(1)}, u32[]{:S(2)}, u32[]{:S(2)}) collective-permute-start(bf16[2,32,1024]{2,1,0:T(8,128)(2,1)} %get-tuple-element.53), channel_id=1, source_target_pairs={{0,2},{1,3},{2,0},{3,1},{4,6},{5,7},{6,4},{7,5},{8,10},{9,11},{10,... | collective-permute-start | bytes 393224 | tf_op jit(solution)/shard_map/ppermute | solution.py:458
  149.0 12.3 %collective-permute-start.25 = (bf16[1536,128]{1,0:T(8,128)(2,1)}, bf16[1536,128]{1,0:T(8,128)(2,1)S(1)}, u32[]{:S(2)}, u32[]{:S(2)}) collective-permute-start(bf16[1536,128]{1,0:T(8,128)(2,1)} %get-tuple-element.49), channel_id=1, source_target_pairs={{0,4},{4,0},{8,12},{12,8},{1,5},{5,1},{9,13},{13,9},{2,6},{6,2},{1... | collective-permute-start | bytes 1179656 | tf_op jit(solution)/shard_map/ppermute | solution.py:461
  153.9 29.1 %collective-permute-start.28 = (bf16[1536,128]{1,0:T(8,128)(2,1)}, bf16[1536,128]{1,0:T(8,128)(2,1)S(1)}, u32[]{:S(2)}, u32[]{:S(2)}) collective-permute-start(bf16[1536,128]{1,0:T(8,128)(2,1)} %get-tuple-element.54), channel_id=1, source_target_pairs={{0,8},{4,12},{8,0},{12,4},{1,9},{5,13},{9,1},{13,5},{2,10},{6,14},... | collective-permute-start | bytes 1179656 | tf_op jit(solution)/shard_map/ppermute | solution.py:461
  157.0 34.0 %collective-permute-start.29 = (bf16[1536,128]{1,0:T(8,128)(2,1)}, bf16[1536,128]{1,0:T(8,128)(2,1)S(1)}, u32[]{:S(2)}, u32[]{:S(2)}) collective-permute-start(bf16[1536,128]{1,0:T(8,128)(2,1)} %get-tuple-element.55), channel_id=1, source_target_pairs={{0,12},{4,8},{8,4},{12,0},{1,13},{5,9},{9,5},{13,1},{2,14},{6,10},... | collective-permute-start | bytes 1179656 | tf_op jit(solution)/shard_map/ppermute | solution.py:461
  (32 other events, 268.8 us)

commit v2 on v0

v2 whole, which is shorter than its diff:
```python
import jax
import jax.numpy as jnp
from jax import lax
from jax.experimental import pallas as pl
from jax.experimental.pallas import tpu as pltpu
from jax.sharding import PartitionSpec as P

MODEL_WIDTH = 5120
HEAD = 128
KEY_WIDTH = 1024
PADDED_RANK = 128
SEQ = 32
LIVE = 288
QUARTER = MODEL_WIDTH // 4


adapter_alpha_scale = 16.0
norm_epsilon = 1e-06
learn_rate = 0.001
weight_decay = 0.01
beta_one = 0.9
beta_two = 0.999
correct_one = 1.0 - 0.9**10
correct_two = 1.0 - 0.999**10
adam_epsilon = 1e-08

bf16 = jnp.bfloat16
f32 = jnp.float32
i32 = jnp.int32


def optimizer_update(weights, gradient, moment, variance):
    moment_new = beta_one * moment + (1.0 - beta_one) * gradient
    variance_new = beta_two * variance + (1.0 - beta_two) * gradient * gradient
    update = moment_new / correct_one / (jnp.sqrt(variance_new / correct_two) + adam_epsilon)
    return (weights - learn_rate * (update + weight_decay * weights), moment_new, variance_new)


def adapter_grads(
    row_tokens,
    row_base,
    row_grads,
    down_factor_weight,
    up_factor_weight,
    owned_adapter_rank,
    key_norm_weight,
):
    columns = jnp.arange(PADDED_RANK) < owned_adapter_rank
    masked_down = jnp.where(columns[None, :], down_factor_weight, jnp.zeros((), bf16))
    masked_up = jnp.where(columns[:, None], up_factor_weight, jnp.zeros((), bf16))
    adapter_scale_factor = adapter_alpha_scale / owned_adapter_rank.astype(f32)
    lowrank = jnp.dot(row_tokens, masked_down, preferred_element_type=f32).astype(bf16)
    key_rows = row_base.astype(f32) + adapter_scale_factor * jnp.dot(
        lowrank, masked_up, preferred_element_type=f32
    )
    per_head = key_rows.reshape(key_rows.shape[0], KEY_WIDTH // HEAD, HEAD)
    inverse = lax.rsqrt(jnp.mean(per_head * per_head, axis=-1, keepdims=True) + norm_epsilon)
    normed = per_head * inverse
    incoming = row_grads.astype(f32).reshape(per_head.shape) * key_norm_weight
    key_grads = inverse * (incoming - normed * jnp.mean(incoming * normed, axis=-1, keepdims=True))
    key_grads = key_grads.reshape(key_rows.shape).astype(bf16)
    up_factor_gradient = adapter_scale_factor * lax.dot_general(
        lowrank, key_grads, (((0,), (0,)), ((), ())), preferred_element_type=f32
    )
    up_factor_gradient = jnp.where(columns[:, None], up_factor_gradient, 0.0)
    low_grads = (
        adapter_scale_factor
        * lax.dot_general(key_grads, masked_up, (((1,), (1,)), ((), ())), preferred_element_type=f32)
    ).astype(bf16)
    down_factor_gradient = lax.dot_general(
        row_tokens, low_grads, (((0,), (0,)), ((), ())), preferred_element_type=f32
    )
    return (down_factor_gradient, up_factor_gradient)


def general_gradients(
    tokens,
    cotangent,
    lengths,
    slot_adapter_index,
    adapter_rank_sizes,
    frozen,
    key_norm_weight,
    adapter_down_factor,
    adapter_up_factor,
):
    data_ranks = lax.axis_size("dp")
    owning_replica = lax.axis_index("dp")
    seq_count = lengths.shape[1]
    per_pair = -(-seq_count // data_ranks)
    slot_total = data_ranks * per_pair
    token_seqs = tokens.reshape(seq_count, SEQ, MODEL_WIDTH)
    live_mask = jnp.arange(SEQ)[None, :] < lengths[0][:, None]
    upstream = jnp.where(
        live_mask[:, :, None],
        cotangent.reshape(seq_count, SEQ, KEY_WIDTH),
        jnp.zeros((), cotangent.dtype),
    )
    target = slot_adapter_index[0]
    seq_index = jnp.arange(seq_count)
    earlier = (target[None, :] == target[:, None]) & (seq_index[None, :] < seq_index[:, None])
    slot_order = jnp.sum(earlier.astype(i32), axis=1)
    slot_of = target * per_pair + slot_order
    matches = slot_of[None, :] == jnp.arange(slot_total)[:, None]
    source = jnp.sum(jnp.where(matches, seq_index[None, :], 0), axis=1)
    filled = jnp.any(matches, axis=1)

    def pack_slots(values):
        picked = jnp.take(values, source, axis=0)
        picked = jnp.where(filled[:, None, None], picked, jnp.zeros((), values.dtype))
        return picked.reshape(data_ranks, per_pair * SEQ, values.shape[-1])

    arrived_tokens, arrived_grads = (
        lax.all_to_all(pack_slots(token_seqs), "dp", split_axis=0, concat_axis=0, tiled=True),
        lax.all_to_all(pack_slots(upstream), "dp", split_axis=0, concat_axis=0, tiled=True),
    )
    row_tokens = arrived_tokens.reshape(-1, MODEL_WIDTH)
    row_base = jnp.dot(
        row_tokens,
        lax.all_gather(frozen, "fsdp", axis=0, tiled=True),
        preferred_element_type=f32,
    ).astype(bf16)
    row_grads = arrived_grads.reshape(-1, KEY_WIDTH)
    owned_adapter_rank = jnp.sum(
        jnp.where(jnp.arange(adapter_rank_sizes.shape[0]) == owning_replica, adapter_rank_sizes, 0)
    )
    full_down, full_up = (
        lax.all_gather(adapter_down_factor.astype(bf16), "fsdp", axis=1, tiled=True),
        lax.all_gather(adapter_up_factor.astype(bf16), "fsdp", axis=1, tiled=True),
    )
    down_factor_gradient, up_factor_gradient = adapter_grads(
        row_tokens,
        row_base,
        row_grads,
        full_down[0],
        full_up[0],
        owned_adapter_rank,
        key_norm_weight,
    )
    return (
        lax.psum_scatter(down_factor_gradient, "fsdp", scatter_dimension=0, tiled=True),
        lax.psum_scatter(up_factor_gradient, "fsdp", scatter_dimension=0, tiled=True),
    )


def local_general(
    tokens,
    cotangent,
    lengths,
    slot_adapter_index,
    adapter_rank_sizes,
    frozen,
    key_norm_weight,
    adapter_down_factor,
    adapter_up_factor,
    down_first_moment,
    up_first_moment,
    down_second_moment,
    up_second_moment,
):
    down_gradient, up_gradient = general_gradients(
        tokens,
        cotangent,
        lengths,
        slot_adapter_index,
        adapter_rank_sizes,
        frozen,
        key_norm_weight,
        adapter_down_factor,
        adapter_up_factor,
    )
    new_down, down_first, down_second = optimizer_update(
        adapter_down_factor[0], down_gradient, down_first_moment[0], down_second_moment[0]
    )
    new_up, up_first, up_second = optimizer_update(
        adapter_up_factor[0], up_gradient, up_first_moment[0], up_second_moment[0]
    )
    return (
        new_down[None],
        new_up[None],
        down_first[None],
        up_first[None],
        down_second[None],
        up_second[None],
    )


SMEM = pl.BlockSpec(memory_space=pltpu.SMEM)
VMEM = pl.BlockSpec(memory_space=pltpu.VMEM)
HBM = pl.BlockSpec(memory_space=pl.ANY)


class Late:
    def __init__(self, source, target, sem):
        self.copy, self.target, self.waited = pltpu.make_async_copy(source, target, sem), target, False
        self.copy.start()

    def get(self):
        if not self.waited:
            self.copy.wait()
            self.waited = True
        return self.target


def call(kernel, name, scalars, late, outs, plain=(), order=(), scratch=()):
    n, m, p, d, o = len(scalars), len(late), len(plain), len(order), len(outs)

    def body(*refs):
        ins, rest = refs[: n + m + p], refs[n + m + p + d :]
        outputs, held, sems, scratches = rest[:o], rest[o : o + m], rest[o + m], rest[o + m + 1 :]
        lates = [Late(ins[n + i], held[i], sems.at[i]) for i in range(m)]
        kernel(*ins[:n], *lates, *ins[n + m :], *outputs, *scratches)
        for one in lates:
            one.get()

    args = list(scalars) + list(late) + list(plain) + list(order)
    moved = sum(a.size * a.dtype.itemsize for a in list(scalars) + list(late) + list(plain) + list(outs))
    return pl.pallas_call(
        body,
        name=name,
        in_specs=[SMEM] * n + [HBM] * (m + p + d),
        out_specs=tuple(VMEM for _ in outs),
        out_shape=tuple(outs),
        scratch_shapes=[pltpu.VMEM(a.shape, a.dtype) for a in late]
        + [pltpu.SemaphoreType.DMA((max(m, 1),))]
        + list(scratch),
        compiler_params=pltpu.CompilerParams(vmem_limit_bytes=36 * 2**20),
        cost_estimate=pl.CostEstimate(flops=3 * 10**10, bytes_accessed=moved, transcendentals=0),
    )(*args)


def shape(dims, dtype):
    return jax.ShapeDtypeStruct(dims, dtype)


def offsets(place, length, slots):
    found = []
    for s in range(slots):
        total = jnp.int32(0)
        for t in range(slots):
            if t != s:
                first = place[t] > place[s] if t > s else place[t] >= place[s]
                total = total + jnp.where(first, length[t], 0)
        found.append(total)
    return found


def slot_places(lengths, adapters, slots):
    dp = lax.axis_index("dp")
    place = [adapters[0, s] ^ dp for s in range(slots)]
    length = [lengths[0, s] for s in range(slots)]
    return place, length, offsets(place, length, slots)


def packing(place, length, start, slots):
    token = lax.broadcasted_iota(i32, (1, slots * SEQ), 1)
    row_of = jnp.full((1, slots * SEQ), -1, i32)
    for s in range(slots):
        position = token - s * SEQ
        inside = (position >= 0) & (position < length[s])
        row_of = jnp.where(inside, position + start[s], row_of)
    row = lax.broadcasted_iota(i32, (LIVE, slots * SEQ), 0)
    return jnp.where(row == row_of, 1.0, 0.0).astype(bf16)


def row_places(place, length, start, slots):
    row = lax.broadcasted_iota(i32, (LIVE, HEAD), 0)
    found = jnp.zeros((LIVE, HEAD), f32)
    for s in range(slots):
        inside = (row >= start[s]) & (row < start[s] + length[s])
        found = jnp.where(inside, place[s].astype(f32), found)
    return found.astype(bf16)


def mm(a, b):
    return jnp.dot(a, b, preferred_element_type=f32)


def mm_nt(a, b):
    return lax.dot_general(a, b, (((1,), (1,)), ((), ())), preferred_element_type=f32)


def quarter_copies(tokens, held, sems, others):
    f = lax.axis_index("fsdp")
    copies = []
    for n, other in enumerate(others):
        start = pl.multiple_of((f ^ other) * QUARTER, QUARTER)
        copies.append(pltpu.make_async_copy(tokens.at[:, pl.ds(start, QUARTER)], held.at[n], sems.at[n]))
        copies[-1].start()
    return copies


def pack_sent_kernel(slots, lengths, adapters, tokens, out, held, sems):
    copies = quarter_copies(tokens, held, sems, (2, 3))
    found = slot_places(lengths, adapters, slots)
    chosen = packing(*found, slots)
    ids = row_places(*found, slots)
    for q in range(2):
        for b in range(10):
            at = min(16 * (10 * q + b), LIVE - 16)
            out[q, LIVE:, 128 * b : 128 * b + 128] = ids[at : at + 16]
        copies[q].wait()
        out[q, :LIVE] = mm(chosen, held[q]).astype(bf16)


def pack_kept_kernel(slots, lengths, adapters, cotangent, tokens, near_out, far_out, grads_out, held, sems):
    copies = quarter_copies(tokens, held, sems, (0, 1))
    found = slot_places(lengths, adapters, slots)
    chosen = packing(*found, slots)
    far_out[:, QUARTER:] = row_places(*found, slots)
    copies[0].wait()
    near_out[...] = mm(chosen, held[0]).astype(bf16)
    copies[1].wait()
    far_out[:, :QUARTER] = mm(chosen, held[1]).astype(bf16)
    grads_out[...] = mm(chosen, cotangent.get()[...]).astype(bf16)


def down_mask_kernel(ranks, down, out):
    rank = ranks[lax.axis_index("dp")]
    column = lax.broadcasted_iota(i32, (QUARTER, PADDED_RANK), 1)
    masked = jnp.where(column < rank, down.get()[...], 0.0).astype(bf16)
    for i in range(4):
        out[i] = masked


def up_mask_kernel(ranks, own, mate, out):
    rank = ranks[lax.axis_index("dp")]
    f = lax.axis_index("fsdp")
    row = lax.broadcasted_iota(i32, (32, KEY_WIDTH), 0)
    own_rows = jnp.where(row + 32 * f < rank, own.get()[...], 0.0).astype(bf16)
    mate_rows = jnp.where(row + 32 * (f ^ 2) < rank, mate.get()[...], 0.0).astype(bf16)
    for i in range(4):
        out[i, 0] = own_rows
        out[i, 1] = mate_rows


def base_left_kernel(rows, own, mate, out):
    half = KEY_WIDTH // 2
    total = mm(rows.get()[0, :LIVE], own.get()[:, :half])
    out[...] = (total + mm(rows.get()[1, :LIVE], mate.get()[:, :half])).astype(bf16)


def down_factors(held):
    dp = lax.axis_index("dp")
    return jnp.concatenate([held.get()[dp ^ j] for j in range(4)], axis=1)


def mate_places(rows):
    blocks = [rows[n // 10, LIVE:, 128 * (n % 10) : 128 * (n % 10) + 128] for n in range(LIVE // 16)]
    return jnp.concatenate(blocks, axis=0)


def own_adapter(every, places):
    adapter = places.astype(f32)
    total = jnp.zeros((LIVE, PADDED_RANK), f32)
    for j in range(4):
        total = jnp.where(adapter == j, every[:, 128 * j : 128 * j + 128], total)
    return total


def mate_kernel(rows, own, mate, downs, downs_core, out, core_out):
    half = KEY_WIDTH // 2
    held = rows.get()
    places = mate_places(held)
    core_out[:, :QUARTER] = held[1, :LIVE]
    core_out[:, QUARTER:] = places
    total = mm(held[0, :LIVE], own.get()[:, half:]) + mm(held[1, :LIVE], mate.get()[:, half:])
    out[:, :half] = total.astype(bf16)
    every = mm(held[0, :LIVE], down_factors(downs)) + mm(held[1, :LIVE], down_factors(downs_core))
    low = own_adapter(every, places)
    high = low.astype(bf16)
    out[:, half : half + 128] = high
    out[:, half + 128 :] = (low - high.astype(f32)).astype(bf16)


def base_own_kernel(near, own, far, mate, out):
    total = mm(near.get()[...], own.get()[...])
    out[...] = total + mm(far.get()[:, :QUARTER], mate.get()[...])


def low_own_kernel(near, far, downs, downs_core, out):
    held = far.get()
    every = mm(near.get()[...], down_factors(downs)) + mm(held[:, :QUARTER], down_factors(downs_core))
    out[...] = own_adapter(every, held[:, QUARTER:])


def identity():
    row = lax.broadcasted_iota(i32, (HEAD, HEAD), 0)
    return jnp.where(row == lax.broadcasted_iota(i32, (HEAD, HEAD), 1), 1.0, 0.0).astype(bf16)


def spread(values, places, which):
    adapter, value = places.astype(f32), values.astype(f32)
    return jnp.concatenate([jnp.where(adapter == j, value, 0.0).astype(bf16) for j in which], axis=1)


def transposed(values):
    unit = identity()
    parts = [mm_nt(unit, values[:, n : n + 128]).astype(bf16) for n in range(0, values.shape[1], 128)]
    return jnp.concatenate(parts, axis=0)


def keys_kernel(ranks, far, low, right, ups, ups_core, base, left, grads, gain, *refs):
    dlow_out, kept_out, sent_out, up, total = refs
    dp = lax.axis_index("dp")
    f = lax.axis_index("fsdp")
    c, x = f % 2, f // 2
    for j in range(4):
        for part in range(2):
            for held, side in ((ups, c), (ups_core, 1 - c)):
                target = 128 * j + 64 * (x ^ part) + 32 * side
                up[pl.ds(pl.multiple_of(target, 32), 32), :] = held.get()[dp ^ j, part]
    ids = far.get()[:, QUARTER:]
    adapter = ids.astype(f32)
    scales = [adapter_alpha_scale / jnp.full((1, HEAD), ranks[dp ^ j], i32).astype(f32) for j in range(4)]
    scale = jnp.zeros((LIVE, HEAD), f32)
    for j in range(4):
        scale = jnp.where(adapter == j, scales[j], scale)
    half = KEY_WIDTH // 2
    arrived = right.get()[:, half:].astype(f32)
    lowrank = (low.get()[...] + (arrived[:, :128] + arrived[:, 128:])).astype(bf16).astype(f32)
    wide = spread(lowrank, ids, range(4))
    added = mm(wide, up[...])
    parts = []
    for k in range(8):
        lanes = slice(128 * k, 128 * k + 128)
        source = left.get()[:, lanes] if k < 4 else right.get()[:, 128 * k - half : 128 * k - half + 128]
        arrived = source.astype(f32)
        held = (base.get()[:, lanes] + arrived).astype(bf16).astype(f32)
        head = held + scale * added[:, lanes]
        inverse = lax.rsqrt(jnp.mean(head * head, axis=-1, keepdims=True) + norm_epsilon)
        normed = head * inverse
        incoming = grads.get()[:, lanes].astype(f32) * gain.get()[...]
        mean = jnp.mean(incoming * normed, axis=-1, keepdims=True)
        parts.append((inverse * (incoming - normed * mean)).astype(bf16))
    key_grads = jnp.concatenate(parts, axis=1)
    every = mm_nt(key_grads, up[...])
    picked = jnp.zeros((LIVE, PADDED_RANK), f32)
    for j in range(4):
        picked = jnp.where(adapter == j, every[:, 128 * j : 128 * j + 128], picked)
    dlow_out[...] = (scale * picked).astype(bf16)
    total[...] = mm(transposed(wide), key_grads)
    for j in range(4):
        scale_j = scales[j][0:1, 0:1]
        for part in range(2):
            kept = pl.multiple_of(128 * j + 64 * (x ^ part) + 32 * c, 32)
            sent = pl.multiple_of(128 * j + 64 * (x ^ part) + 32 * (1 - c), 32)
            kept_out[part, j] = total[pl.ds(kept, 32), :] * scale_j
            sent_out[part, j] = total[pl.ds(sent, 32), :] * scale_j


def up_core_kernel(kept, arrived, own_out, mate_out):
    own_out[...] = kept.get()[0] + arrived.get()[0]
    mate_out[...] = (kept.get()[1] + arrived.get()[1]).astype(bf16)


def up_across_kernel(own, arrived, own_out, one_out, two_out, three_out):
    for j, out in enumerate((own_out, one_out, two_out, three_out)):
        out[...] = (own.get()[j] + arrived.get()[j].astype(f32)).astype(out.dtype)


def down_kernel(dlow, dlow_mate, dlow_core, dlow_cross, rows, near, far, far_core, cross, *refs):
    outs, (held, ids, sems) = refs[:4], refs[4:]
    copies = [pltpu.make_async_copy(far.at[:, pl.ds(QUARTER, 128)], ids.at[pl.ds(0, LIVE), :], sems.at[0])]
    copies.append(
        pltpu.make_async_copy(far_core.at[:, pl.ds(QUARTER, 128)], ids.at[pl.ds(2 * LIVE, LIVE), :], sems.at[1])
    )
    copies.append(
        pltpu.make_async_copy(cross.at[:, pl.ds(QUARTER, 128)], ids.at[pl.ds(3 * LIVE, LIVE), :], sems.at[2])
    )
    sources = [near, None, far_core.at[:, pl.ds(0, QUARTER)], cross.at[:, pl.ds(0, QUARTER)]]
    for n, source in enumerate(sources):
        if source is not None:
            copies.append(pltpu.make_async_copy(source, held.at[pl.ds(n * LIVE, LIVE), :], sems.at[3 + n]))
    for copy in copies:
        copy.start()
    held[LIVE : 2 * LIVE, :] = rows.get()[0, :LIVE]
    ids[LIVE : 2 * LIVE, :] = mate_places(rows.get())
    for copy in copies[:3]:
        copy.wait()
    lows = jnp.concatenate([d.get()[...] for d in (dlow, dlow_mate, dlow_core, dlow_cross)], axis=0)
    wide = transposed(spread(lows, ids[...], range(4)))
    for copy in copies[3:]:
        copy.wait()
    for j, out in enumerate(outs):
        out[...] = mm(wide[128 * j : 128 * j + 128], held[...]).astype(out.dtype)


def update_kernel(*refs):
    own, one, two, three, down, moment, variance = refs[:7]
    outs = refs[14:]
    for start in range(0, QUARTER, 128):
        part = slice(start, start + 128)
        total = own.get()[:, part] + one.get()[:, part].astype(f32)
        total = total + (two.get()[:, part].astype(f32) + three.get()[:, part].astype(f32))
        outs[0][part], outs[1][part], outs[2][part] = optimizer_update(
            down.get()[part], total.T, moment.get()[part], variance.get()[part]
        )
    own, one, two, three, up, moment, variance = refs[7:14]
    total = own.get()[...] + one.get()[...].astype(f32)
    total = total + (two.get()[...].astype(f32) + three.get()[...].astype(f32))
    outs[3][...], outs[4][...], outs[5][...] = optimizer_update(
        up.get()[...], total, moment.get()[...], variance.get()[...]
    )


def after(value, *others):
    return lax.optimization_barrier((value, *others))[0]


def local(
    tokens,
    cotangent,
    lengths,
    slot_adapter_index,
    adapter_rank_sizes,
    frozen,
    key_norm_weight,
    adapter_down_factor,
    adapter_up_factor,
    down_first_moment,
    up_first_moment,
    down_second_moment,
    up_second_moment,
):
    dp = lax.axis_index("dp")
    slots = lengths.shape[1]
    ranks = adapter_rank_sizes

    def core(value):
        return lax.ppermute(value, "fsdp", [(i, i ^ 1) for i in range(4)])

    def across(value):
        return lax.ppermute(value, "fsdp", [(i, i ^ 2) for i in range(4)])

    def along(value, distance):
        return lax.ppermute(value, "dp", [(i, i ^ distance) for i in range(4)])

    def exchange(value):
        return lax.all_to_all(value, "dp", split_axis=0, concat_axis=0, tiled=True)

    frozen_core = core(frozen)
    up_mate = across(adapter_up_factor[0])
    (sent,) = call(
        lambda *refs: pack_sent_kernel(slots, *refs),
        "pack_sent",
        [lengths, slot_adapter_index],
        [],
        [shape((2, LIVE + 16, QUARTER), bf16)],
        [tokens],
        scratch=[pltpu.VMEM((2, tokens.shape[0], QUARTER), bf16), pltpu.SemaphoreType.DMA((2,))],
    )
    rows = across(sent)

    (masked,) = call(
        down_mask_kernel,
        "down_mask",
        [ranks],
        [adapter_down_factor[0]],
        [shape((4, QUARTER, PADDED_RANK), bf16)],
        order=[sent],
    )
    downs = exchange(masked)
    near, far, grads = call(
        lambda *refs: pack_kept_kernel(slots, *refs),
        "pack_kept",
        [lengths, slot_adapter_index],
        [cotangent],
        [
            shape((LIVE, QUARTER), bf16),
            shape((LIVE, QUARTER + 128), bf16),
            shape((LIVE, KEY_WIDTH), bf16),
        ],
        [tokens],
        order=[masked, frozen_core],
        scratch=[pltpu.VMEM((2, tokens.shape[0], QUARTER), bf16), pltpu.SemaphoreType.DMA((2,))],
    )
    far_core = core(far)

    (base,) = call(
        base_own_kernel,
        "base_own",
        [],
        [near, frozen, far, frozen_core],
        [shape((LIVE, KEY_WIDTH), f32)],
    )
    (up_pair,) = call(
        up_mask_kernel,
        "up_mask",
        [ranks],
        [adapter_up_factor[0], up_mate],
        [shape((4, 2, 32, KEY_WIDTH), bf16)],
        order=[base, far_core],
    )
    ups = exchange(up_pair)
    downs = after(downs, base)
    downs_core = core(downs)
    (left,) = call(
        base_left_kernel,
        "base_left",
        [],
        [rows, frozen, frozen_core],
        [shape((LIVE, KEY_WIDTH // 2), bf16)],
        order=[up_pair],
    )
    right, cross = call(
        mate_kernel,
        "mate",
        [],
        [rows, frozen, frozen_core, downs, downs_core],
        [shape((LIVE, KEY_WIDTH // 2 + 256), bf16), shape((LIVE, QUARTER + 128), bf16)],
        order=[left],
    )
    left_in, right_in, cross_core = across(left), across(right), core(cross)
    (low,) = call(
        low_own_kernel,
        "low_own",
        [],
        [near, far, downs, downs_core],
        [shape((LIVE, PADDED_RANK), f32)],
        order=[right],
    )
    ups_core = core(ups)
    dlow, up_kept, up_core = call(
        keys_kernel,
        "keys",
        [ranks],
        [far, low, right_in, ups, ups_core, base, left_in, grads, key_norm_weight[None, :]],
        [
            shape((LIVE, PADDED_RANK), bf16),
            shape((2, 4, 32, KEY_WIDTH), f32),
            shape((2, 4, 32, KEY_WIDTH), f32),
        ],
        order=[cross_core],
        scratch=[pltpu.VMEM((512, KEY_WIDTH), bf16), pltpu.VMEM((512, KEY_WIDTH), f32)],
    )
    dlow_mate, dlow_core = across(dlow), core(dlow)
    dlow_cross = core(dlow_mate)
    up_core_in = core(up_core)

    up_total, up_sent = call(
        up_core_kernel,
        "up_core",
        [],
        [up_kept, up_core_in],
        [shape((4, 32, KEY_WIDTH), f32), shape((4, 32, KEY_WIDTH), bf16)],
    )
    own, one, two, three = call(
        down_kernel,
        "down",
        [],
        [dlow, dlow_mate, dlow_core, dlow_cross, rows],
        [shape((PADDED_RANK, QUARTER), t) for t in (f32, bf16, bf16, bf16)],
        [near, far, far_core, cross_core],
        order=[up_total],
        scratch=[
            pltpu.VMEM((4 * LIVE, QUARTER), bf16),
            pltpu.VMEM((4 * LIVE, HEAD), bf16),
            pltpu.SemaphoreType.DMA((7,)),
        ],
    )
    three_in, two_in, one_in = along(three, 3), along(two, 2), along(one, 1)

    up_parts = call(
        up_across_kernel,
        "up_across",
        [],
        [up_total, across(up_sent)],
        [shape((32, KEY_WIDTH), t) for t in (f32, bf16, bf16, bf16)],
        order=[one],
    )
    up_in = [up_parts[0]] + [along(up_parts[j], j) for j in (1, 2, 3)]

    new_down, down_first, down_second, new_up, up_first, up_second = call(
        update_kernel,
        "update",
        [],
        [own, one_in, two_in, three_in, adapter_down_factor[0], down_first_moment[0], down_second_moment[0]]
        + [*up_in, adapter_up_factor[0], up_first_moment[0], up_second_moment[0]],
        [shape(adapter_down_factor.shape[1:], f32)] * 3 + [shape(adapter_up_factor.shape[1:], f32)] * 3,
    )
    return tuple(o[None] for o in (new_down, new_up, down_first, up_first, down_second, up_second))


def solution(mesh):
    paired = mesh.shape["dp"] == 4 and mesh.shape["fsdp"] == 4
    return jax.shard_map(
        local if paired else local_general,
        mesh=mesh,
        in_specs=(
            P(("parts", "dp", "fsdp"), None),
            P(("parts", "dp", "fsdp"), None),
            P(("parts", "dp", "fsdp"), None),
            P(("parts", "dp", "fsdp"), None),
            P(),
            P("fsdp", None),
            P(),
            P(("parts", "dp"), "fsdp", None),
            P(("parts", "dp"), "fsdp", None),
            P(("parts", "dp"), "fsdp", None),
            P(("parts", "dp"), "fsdp", None),
            P(("parts", "dp"), "fsdp", None),
            P(("parts", "dp"), "fsdp", None),
        ),
        out_specs=(
            P(("parts", "dp"), "fsdp", None),
            P(("parts", "dp"), "fsdp", None),
            P(("parts", "dp"), "fsdp", None),
            P(("parts", "dp"), "fsdp", None),
            P(("parts", "dp"), "fsdp", None),
            P(("parts", "dp"), "fsdp", None),
        ),
        check_vma=False,
    )
```

time: 218 us -> 141 us (0.65)
  waiting for transfers between devices: 139 us -> 55.8 us
  Pallas kernels: 0 us -> 40.9 us
  matrix products: 20.2 us -> 0 us
  starting transfers between devices: 11.6 us -> 28.5 us
  other arithmetic: 16.6 us -> 0 us
  between operations: 14.7 us -> 1.15 us
  blocking collectives: 7.6 us -> 0 us
  local copies, waits for them, and re-layouts: 7.92 us -> 13.7 us
    all_to_all x2, waiting for transfers between devices: 87.2 us -> 19.6 us  [exchange(): return lax.all_to_all(value, 'dp', split_axis=0, concat_axis=0, tiled=True)]
    reduce_scatter x2 -> x0, waiting for transfers between devices: 50.5 us -> none  [the longest x1 35.5 us: local(): lax.psum_scatter(down_factor_gradient, 'fsdp', scatter_dimension=0, tiled...]
    pallas_call x0 -> x13, Pallas kernels: none -> 40.9 us  [call(): pl.pallas_call(body, name=name, in_specs=[SMEM] * n + [HBM] * (m + p + d)...]
    ppermute x0 -> x20, waiting for transfers between devices: none -> 36.3 us  [the longest x6 26.7 us: along(): return lax.ppermute(value, 'dp', [(i, i ^ distance) for i in range(4)])]
    dot_general x5 -> x0, matrix products: 20.2 us -> none  [the longest x1 9.39 us: frozen_product(): jnp.dot(row_data, lax.all_gather(frozen, 'fsdp', axis=0, tiled=True), pre...]
    ppermute x0 -> x20, starting transfers between devices: none -> 19.4 us  [the longest x6 11.5 us: along(): return lax.ppermute(value, 'dp', [(i, i ^ distance) for i in range(4)])]
    unnamed x24 -> x54, local copies, waits for them, and re-layouts: 0.56 us -> 13.7 us
    all_gather x1 -> x0, blocking collectives: 7.6 us -> none  [local(): lax.all_gather(adapter_up_factor.astype(jnp.bfloat16), 'fsdp', axis=1, ti...]
  transfers between devices with their start and end apart: 6 -> 22, of which waited for: 4 -> 6; matrix products, arithmetic and copies ran while one was open for 12% -> 0% of each run, Pallas kernels for 0% -> 23%
where the time goes in v2:
time: 141 us; the launch traced here: 140 us
  waiting for transfers between devices  55.8 us (40%)
  Pallas kernels  40.9 us (29%)
  starting transfers between devices  28.5 us (20%)
  local copies, waits for them, and re-layouts  13.7 us (10%)
    pallas_call x13, Pallas kernels, call(): pl.pallas_call(body, name=name, in_specs=[SMEM] * n + [HBM] * (m + p + d)...  40.9 us
    ppermute x6, waiting for transfers between devices, along(): return lax.ppermute(value, 'dp', [(i, i ^ distance) for i in range(4)])  26.7 us
    all_to_all x2, waiting for transfers between devices, exchange(): return lax.all_to_all(value, 'dp', split_axis=0, concat_axis=0, tiled=True)  19.6 us
    unnamed x54, local copies, waits for them, and re-layouts  13.7 us
    ppermute x6, starting transfers between devices, along(): return lax.ppermute(value, 'dp', [(i, i ^ distance) for i in range(4)])  11.5 us
    ppermute x6, waiting for transfers between devices, across(): return lax.ppermute(value, 'fsdp', [(i, i ^ 2) for i in range(4)])  9.58 us
    all_to_all x2, starting transfers between devices, exchange(): return lax.all_to_all(value, 'dp', split_axis=0, concat_axis=0, tiled=True)  9.05 us
    ppermute x6, starting transfers between devices, across(): return lax.ppermute(value, 'fsdp', [(i, i ^ 2) for i in range(4)])  6.93 us
  transfers between devices with their start and end apart: 22, of which 6 were waited for; matrix products, arithmetic and copies ran while one was open for 0% of the time, Pallas kernels for 23%

profile of v2, /device:TPU:0, one launch (start us, length us, event | category | flops | bytes accessed | tf_op | source)
XLA Modules:
  0.0 140.1 jit_solution(3588547532499041758)
XLA Ops:
  1.1 2.6 %collective-permute-start.3 = (f32[32,1024]{1,0:T(8,128)}, f32[32,1024]{1,0:T(8,128)S(1)}, u32[]{:S(2)}, u32[]{:S(2)}) collective-permute-start(f32[32,1024]{1,0:T(8,128)} %bitcast.17), channel_id=1, source_target_pairs={{0,2},{1,3},{2,0},{3,1},{4,6},{5,7},{6,4},{7,5},{8,10},{9,11},{10,... | collective-permute-start | bytes 393224 | tf_op jit(solution)/shard_map/ppermute | solution.py:534
  3.7 2.1 %copy-done = bf16[384,5120]{1,0:T(8,128)(2,1)S(1)} copy-done((bf16[384,5120]{1,0:T(8,128)(2,1)S(1)}, bf16[384,5120]{1,0:T(8,128)(2,1)}, u32[]{:S(2)}) %copy-start) | copy-done | bytes 3932184
  7.1 3.8 %pack_sent.1.refs_2_ = bf16[2,304,1280]{2,1,0:T(8,128)(2,1)} custom-call(s32[1,12]{1,0:T(1,128)S(1)} %copy-done.13, s32[1,12]{1,0:T(1,128)S(1)} %copy-done.15, bf16[384,5120]{1,0:T(8,128)(2,1)S(1)} %copy-done), custom_call_target="tpu_custom_call" | custom-call | flops 30000001024 | bytes 5488736 | tf_op jit(solution)/shard_map/pack_sent/pallas_call | solution.py:218
  11.0 2.0 %down_mask.1.refs_4_ = bf16[4,1280,128]{2,1,0:T(8,128)(2,1)} custom-call(s32[4]{0:T(128)S(1)} %copy-done.17, f32[1280,128]{1,0:T(8,128)S(1)} %bitcast.13, bf16[2,304,1280]{2,1,0:T(8,128)(2,1)} %pack_sent.1.refs_2_), custom_call_target="tpu_custom_call" | custom-call | flops 30000001024 | bytes 1966096 | tf_op jit(solution)/shard_map/down_mask/pallas_call | solution.py:218
  13.0 5.4 %all-to-all-start = ((bf16[4,1280,128]{2,1,0:T(8,128)(2,1)}), bf16[4,1280,128]{2,1,0:T(8,128)(2,1)S(1)}, u32[]{:S(2)}, u32[]{:S(2)}) async-start(bf16[4,1280,128]{2,1,0:T(8,128)(2,1)} %down_mask.1.refs_4_), calls=%async_computation | async-start | bytes 2621440 | tf_op jit(solution)/shard_map/all_to_all | solution.py:540
  18.5 2.1 %copy-done.1 = bf16[384,5120]{1,0:T(8,128)(2,1)S(1)} copy-done((bf16[384,5120]{1,0:T(8,128)(2,1)S(1)}, bf16[384,5120]{1,0:T(8,128)(2,1)}, u32[]{:S(2)}) %copy-start.1) | copy-done | bytes 3932184
  20.6 1.1 copy-done.4
  21.7 3.5 %pack_kept.1 = (bf16[288,1280]{1,0:T(8,128)(2,1)S(1)}, bf16[288,1408]{1,0:T(8,128)(2,1)}, bf16[288,1024]{1,0:T(8,128)(2,1)S(1)}) custom-call(s32[1,12]{1,0:T(1,128)S(1)} %copy-done.14, s32[1,12]{1,0:T(1,128)S(1)} %copy-done.16, bf16[384,1024]{1,0:T(8,128)(2,1)S(1)} %copy-done.4, bf16[384,5120]{1,0:T(8,128)(2,1)S(1)} %copy-done.1, ...), custom_call_target="tpu_custom_call" | custom-call | flops 30000001024 | bytes 6856800 | tf_op jit(solution)/shard_map/pack_kept/pallas_call | solution.py:218
  26.0 4.2 %base_own.1.refs_3_.refs_6_ = f32[288,1024]{1,0:T(8,128)S(1)} custom-call(bf16[288,1280]{1,0:T(8,128)(2,1)S(1)} %get-tuple-element.32.refs_0_.refs_5_, bf16[1280,1024]{1,0:T(8,128)(2,1)S(1)} %copy-done.2, bf16[288,1408]{1,0:T(8,128)(2,1)} %get-tuple-element.31.refs_2_.refs_1_.refs_6_, bf16[1280,1024]{1,0:T(8,128)(2,1)} %collective-permute-done.refs_5_.refs_3_.refs_2_), custom_call_target="tpu_custom_call" | custom-call | flops 30000001024 | bytes 7970816 | tf_op jit(solution)/shard_map/base_own/pallas_call | solution.py:218
  32.2 17.7 %all-to-all-done.refs_3_.refs_2_ = bf16[4,1280,128]{2,1,0:T(8,128)(2,1)S(1)} async-done(((bf16[4,1280,128]{2,1,0:T(8,128)(2,1)}), bf16[4,1280,128]{2,1,0:T(8,128)(2,1)S(1)}, u32[]{:S(2)}, u32[]{:S(2)}) %all-to-all-start) | async-done | bytes 1310752 | tf_op jit(solution)/shard_map/all_to_all | solution.py:540
  49.9 1.3 copy-done.20
  51.1 1.7 %up_mask.1.refs_3_ = bf16[4,2,32,1024]{3,2,1,0:T(8,128)(2,1)} custom-call(s32[4]{0:T(128)S(1)} %copy-done.17, f32[32,1024]{1,0:T(8,128)S(1)} %bitcast.18, f32[32,1024]{1,0:T(8,128)S(1)} %collective-permute-done.3.refs_2_, f32[288,1024]{1,0:T(8,128)S(1)} %copy-done.20, bf16[288,1408]{1,0:T(8,128)(2,1)} %collective-permute-done.4.refs_4_.refs_7_), custom_call_target="tpu_custom_call" | custom-call | flops 30000001024 | bytes 786448 | tf_op jit(solution)/shard_map/up_mask/pallas_call | solution.py:218
  52.9 3.7 %all-to-all-start.1 = ((bf16[4,2,32,1024]{3,2,1,0:T(8,128)(2,1)}), bf16[4,2,32,1024]{3,2,1,0:T(8,128)(2,1)S(1)}, u32[]{:S(2)}, u32[]{:S(2)}) async-start(bf16[4,2,32,1024]{3,2,1,0:T(8,128)(2,1)} %up_mask.1.refs_3_), calls=%async_computation.1 | async-start | bytes 1048576 | tf_op jit(solution)/shard_map/all_to_all | solution.py:540
  56.6 1.7 %copy-done.3 = bf16[1280,1024]{1,0:T(8,128)(2,1)S(1)} copy-done((bf16[1280,1024]{1,0:T(8,128)(2,1)S(1)}, bf16[1280,1024]{1,0:T(8,128)(2,1)}, u32[]{:S(2)}) %copy-start.3) | copy-done | bytes 2621464
  58.3 4.0 %base_left.1.refs_5_ = bf16[288,512]{1,0:T(8,128)(2,1)} custom-call(bf16[2,304,1280]{2,1,0:T(8,128)(2,1)S(1)} %collective-permute-done.2.refs_0_.refs_4_, bf16[1280,1024]{1,0:T(8,128)(2,1)S(1)} %copy-done.3, bf16[1280,1024]{1,0:T(8,128)(2,1)} %collective-permute-done.refs_5_.refs_3_.refs_2_, bf16[4,2,32,1024]{3,2,1,0:T(8,128)(2,1)} %up_mask.1.refs_3_), custom_call_target="tpu_custom_call" | custom-call | flops 30000001024 | bytes 7094272 | tf_op jit(solution)/shard_map/base_left/pallas_call | solution.py:218
  62.3 1.6 %collective-permute-start.7 = (bf16[288,512]{1,0:T(8,128)(2,1)}, bf16[288,512]{1,0:T(8,128)(2,1)}, u32[]{:S(2)}, u32[]{:S(2)}) collective-permute-start(bf16[288,512]{1,0:T(8,128)(2,1)} %base_left.1.refs_5_), channel_id=1, source_target_pairs={{0,2},{1,3},{2,0},{3,1},{4,6},{5,7},{6,4},{7,5},{8,10},{9,11},{10,... | collective-permute-start | bytes 884744 | tf_op jit(solution)/shard_map/ppermute | solution.py:534
  63.8 5.2 %mate.1 = (bf16[288,768]{1,0:T(8,128)(2,1)}, bf16[288,1408]{1,0:T(8,128)(2,1)}) custom-call(bf16[2,304,1280]{2,1,0:T(8,128)(2,1)S(1)} %collective-permute-done.2.refs_0_.refs_4_, bf16[1280,1024]{1,0:T(8,128)(2,1)S(1)} %copy-done.3, bf16[1280,1024]{1,0:T(8,128)(2,1)} %collective-permute-done.refs_5_.refs_3_.refs_2_, ...), custom_call_target="tpu_custom_call" | custom-call | flops 30000001024 | bytes 10674176 | tf_op jit(solution)/shard_map/mate/pallas_call | solution.py:218
  69.9 1.9 %all-to-all-done.1.refs_4_ = bf16[4,2,32,1024]{3,2,1,0:T(8,128)(2,1)S(1)} async-done(((bf16[4,2,32,1024]{3,2,1,0:T(8,128)(2,1)}), bf16[4,2,32,1024]{3,2,1,0:T(8,128)(2,1)S(1)}, u32[]{:S(2)}, u32[]{:S(2)}) %all-to-all-start.1) | async-done | bytes 524320 | tf_op jit(solution)/shard_map/all_to_all | solution.py:540
  71.8 1.2 copy-done.23
  73.0 2.9 %low_own.1.refs_2_ = f32[288,128]{1,0:T(8,128)S(1)} custom-call(bf16[288,1280]{1,0:T(8,128)(2,1)S(1)} %copy-done.23, bf16[288,1408]{1,0:T(8,128)(2,1)} %get-tuple-element.31.refs_2_.refs_1_.refs_6_, bf16[4,1280,128]{2,1,0:T(8,128)(2,1)S(1)} %all-to-all-done.refs_3_.refs_2_, bf16[4,1280,128]{2,1,0:T(8,128)(2,1)} %collective-permute-done.1.refs_4_.refs_3_, ...), custom_call_target="tpu_custom_call" | custom-call | flops 30000001024 | bytes 4317184 | tf_op jit(solution)/shard_map/low_own/pallas_call | solution.py:218
  75.9 6.1 %collective-permute-done.5.refs_3_ = bf16[288,768]{1,0:T(8,128)(2,1)} collective-permute-done((bf16[288,768]{1,0:T(8,128)(2,1)}, bf16[288,768]{1,0:T(8,128)(2,1)}, u32[]{:S(2)}, u32[]{:S(2)}) %collective-permute-start.5) | collective-permute-done | bytes 442400 | tf_op jit(solution)/shard_map/ppermute | solution.py:534
  82.0 4.4 %keys.1 = (bf16[288,128]{1,0:T(8,128)(2,1)S(1)}, f32[2,4,32,1024]{3,2,1,0:T(8,128)S(1)}, f32[2,4,32,1024]{3,2,1,0:T(8,128)S(1)}) custom-call(s32[4]{0:T(128)S(1)} %copy-done.17, bf16[288,1408]{1,0:T(8,128)(2,1)} %get-tuple-element.31.refs_2_.refs_1_.refs_6_, f32[288,128]{1,0:T(8,128)S(1)} %low_own.1.refs_2_, ...), custom_call_target="tpu_custom_call" | custom-call | flops 30000001024 | bytes 6685200 | tf_op jit(solution)/shard_map/keys/pallas_call | solution.py:218
  86.5 1.1 collective-permute-start.9
  87.7 3.4 %collective-permute-done.9.refs_1_ = bf16[288,128]{1,0:T(8,128)(2,1)S(1)} collective-permute-done((bf16[288,128]{1,0:T(8,128)(2,1)S(1)}, bf16[288,128]{1,0:T(8,128)(2,1)S(1)}, u32[]{:S(2)}, u32[]{:S(2)}) %collective-permute-start.9) | collective-permute-done | bytes 73760 | tf_op jit(solution)/shard_map/ppermute | solution.py:534
  92.6 4.4 %down.1 = (f32[128,1280]{1,0:T(8,128)S(1)}, bf16[128,1280]{1,0:T(8,128)(2,1)S(1)}, bf16[128,1280]{1,0:T(8,128)(2,1)S(1)}, bf16[128,1280]{1,0:T(8,128)(2,1)S(1)}) custom-call(bf16[288,128]{1,0:T(8,128)(2,1)S(1)} %get-tuple-element.37.refs_0_, bf16[288,128]{1,0:T(8,128)(2,1)S(1)} %collective-permute-done.9.refs_1_, ...), custom_call_target="tpu_custom_call" | custom-call | flops 30000001024 | bytes 6660096 | tf_op jit(solution)/shard_map/down/pallas_call | solution.py:218
  97.0 1.7 %collective-permute-start.13 = (bf16[128,1280]{1,0:T(8,128)(2,1)S(1)}, bf16[128,1280]{1,0:T(8,128)(2,1)S(1)}, u32[]{:S(2)}, u32[]{:S(2)}) collective-permute-start(bf16[128,1280]{1,0:T(8,128)(2,1)S(1)} %get-tuple-element.42.refs_2_), channel_id=1, source_target_pairs={{0,4},{4,0},{8,12},{12,8},{1,5},{5,1},{9,13},{13,9},{2,6},{6,2},{1... | collective-permute-start | bytes 983048 | tf_op jit(solution)/shard_map/ppermute | solution.py:537
  98.7 2.4 %collective-permute-start.14 = (bf16[128,1280]{1,0:T(8,128)(2,1)S(1)}, bf16[128,1280]{1,0:T(8,128)(2,1)S(1)}, u32[]{:S(2)}, u32[]{:S(2)}) collective-permute-start(bf16[128,1280]{1,0:T(8,128)(2,1)S(1)} %get-tuple-element.43), channel_id=1, source_target_pairs={{0,8},{4,12},{8,0},{12,4},{1,9},{5,13},{9,1},{13,5},{2,10},{6,14},... | collective-permute-start | bytes 983048 | tf_op jit(solution)/shard_map/ppermute | solution.py:537
  102.5 3.3 %collective-permute-start.18 = (bf16[32,1024]{1,0:T(8,128)(2,1)S(1)}, bf16[32,1024]{1,0:T(8,128)(2,1)S(1)}, u32[]{:S(2)}, u32[]{:S(2)}) collective-permute-start(bf16[32,1024]{1,0:T(8,128)(2,1)S(1)} %get-tuple-element.48), channel_id=1, source_target_pairs={{0,8},{4,12},{8,0},{12,4},{1,9},{5,13},{9,1},{13,5},{2,10},{6,14},... | collective-permute-start | bytes 196616 | tf_op jit(solution)/shard_map/ppermute | solution.py:537
  105.8 16.5 %collective-permute-done.17.refs_8_ = bf16[32,1024]{1,0:T(8,128)(2,1)S(1)} collective-permute-done((bf16[32,1024]{1,0:T(8,128)(2,1)S(1)}, bf16[32,1024]{1,0:T(8,128)(2,1)S(1)}, u32[]{:S(2)}, u32[]{:S(2)}) %collective-permute-start.17) | collective-permute-done | bytes 65568 | tf_op jit(solution)/shard_map/ppermute | solution.py:537
  122.3 2.9 %collective-permute-start.19 = (bf16[32,1024]{1,0:T(8,128)(2,1)S(1)}, bf16[32,1024]{1,0:T(8,128)(2,1)S(1)}, u32[]{:S(2)}, u32[]{:S(2)}) collective-permute-start(bf16[32,1024]{1,0:T(8,128)(2,1)S(1)} %get-tuple-element.49), channel_id=1, source_target_pairs={{0,12},{4,8},{8,4},{12,0},{1,13},{5,9},{9,5},{13,1},{2,14},{6,10},... | collective-permute-start | bytes 196616 | tf_op jit(solution)/shard_map/ppermute | solution.py:537
  125.2 10.2 %collective-permute-done.18.refs_9_ = bf16[32,1024]{1,0:T(8,128)(2,1)S(1)} collective-permute-done((bf16[32,1024]{1,0:T(8,128)(2,1)S(1)}, bf16[32,1024]{1,0:T(8,128)(2,1)S(1)}, u32[]{:S(2)}, u32[]{:S(2)}) %collective-permute-start.18) | collective-permute-done | bytes 65568 | tf_op jit(solution)/shard_map/ppermute | solution.py:537
  135.4 4.5 %update.1 = (f32[1280,128]{1,0:T(8,128)}, f32[1280,128]{1,0:T(8,128)}, f32[1280,128]{1,0:T(8,128)}, f32[32,1024]{1,0:T(8,128)}, f32[32,1024]{1,0:T(8,128)}, /*index=5*/f32[32,1024]{1,0:T(8,128)}) custom-call(f32[128,1280]{1,0:T(8,128)S(1)} %get-tuple-element.41.refs_0_, bf16[128,1280]{1,0:T(8,128)(2,1)S(1)} %collective-permute-done.13.refs_1_, ...), custom_call_target="tpu_custom_call" | custom-call | flops 30000001024 | bytes 6684672 | tf_op jit(solution)/shard_map/update/pallas_call | solution.py:218
  (79 shorter events, 8.6 us)
Async XLA Ops:
  0.6 17.8 %collective-permute-start = (bf16[1280,1024]{1,0:T(8,128)(2,1)}, bf16[1280,1024]{1,0:T(8,128)(2,1)}, u32[]{:S(2)}, u32[]{:S(2)}) collective-permute-start(bf16[1280,1024]{1,0:T(8,128)(2,1)} %refs_1_.9), channel_id=1, source_target_pairs={{0,1},{1,0},{2,3},{3,2},{4,5},{5,4},{6,7},{7,6},{8,9},{9,8},{10,11... | collective-permute-start | bytes 7864328 | tf_op jit(solution)/shard_map/ppermute | solution.py:531
  1.1 48.7 %collective-permute-start.3 = (f32[32,1024]{1,0:T(8,128)}, f32[32,1024]{1,0:T(8,128)S(1)}, u32[]{:S(2)}, u32[]{:S(2)}) collective-permute-start(f32[32,1024]{1,0:T(8,128)} %bitcast.17), channel_id=1, source_target_pairs={{0,2},{1,3},{2,0},{3,1},{4,6},{5,7},{6,4},{7,5},{8,10},{9,11},{10,... | collective-permute-start | bytes 393224 | tf_op jit(solution)/shard_map/ppermute | solution.py:534
  10.9 45.6 %collective-permute-start.2 = (bf16[2,304,1280]{2,1,0:T(8,128)(2,1)}, bf16[2,304,1280]{2,1,0:T(8,128)(2,1)S(1)}, u32[]{:S(2)}, u32[]{:S(2)}) collective-permute-start(bf16[2,304,1280]{2,1,0:T(8,128)(2,1)} %pack_sent.1.refs_2_), channel_id=1, source_target_pairs={{0,2},{1,3},{2,0},{3,1},{4,6},{5,7},{6,4},{7,5},{8,10},{9,11},{10,... | collective-permute-start | bytes 4669448 | tf_op jit(solution)/shard_map/ppermute | solution.py:534
  13.0 36.8 %all-to-all-start = ((bf16[4,1280,128]{2,1,0:T(8,128)(2,1)}), bf16[4,1280,128]{2,1,0:T(8,128)(2,1)S(1)}, u32[]{:S(2)}, u32[]{:S(2)}) async-start(bf16[4,1280,128]{2,1,0:T(8,128)(2,1)} %down_mask.1.refs_4_), calls=%async_computation | async-start | bytes 2621440 | tf_op jit(solution)/shard_map/all_to_all | solution.py:540
  26.0 23.8 %collective-permute-start.4 = (bf16[288,1408]{1,0:T(8,128)(2,1)}, bf16[288,1408]{1,0:T(8,128)(2,1)}, u32[]{:S(2)}, u32[]{:S(2)}) collective-permute-start(bf16[288,1408]{1,0:T(8,128)(2,1)} %get-tuple-element.31.refs_2_.refs_1_.refs_6_), channel_id=1, source_target_pairs={{0,1},{1,0},{2,3},{3,2},{4,5},{5,4},{6,7},{7,6},{8,9},{9,8},{10,11... | collective-permute-start | bytes 2433032 | tf_op jit(solution)/shard_map/ppermute | solution.py:531
  26.0 23.8 %copy-start.9 = (f32[1,32,1024]{2,1,0:T(8,128)S(1)}, f32[1,32,1024]{2,1,0:T(8,128)}, u32[]{:S(2)}) copy-start(f32[1,32,1024]{2,1,0:T(8,128)} %param.21) | copy-start | bytes 393220
  49.8 14.0 %collective-permute-start.1 = (bf16[4,1280,128]{2,1,0:T(8,128)(2,1)S(1)}, bf16[4,1280,128]{2,1,0:T(8,128)(2,1)}, u32[]{:S(2)}, u32[]{:S(2)}) collective-permute-start(bf16[4,1280,128]{2,1,0:T(8,128)(2,1)S(1)} %all-to-all-done.refs_3_.refs_2_), channel_id=1, source_target_pairs={{0,1},{1,0},{2,3},{3,2},{4,5},{5,4},{6,7},{7,6},{8,9},{9,8},{10,11... | collective-permute-start | bytes 3932168 | tf_op jit(solution)/shard_map/ppermute | solution.py:531
  52.9 18.9 %all-to-all-start.1 = ((bf16[4,2,32,1024]{3,2,1,0:T(8,128)(2,1)}), bf16[4,2,32,1024]{3,2,1,0:T(8,128)(2,1)S(1)}, u32[]{:S(2)}, u32[]{:S(2)}) async-start(bf16[4,2,32,1024]{3,2,1,0:T(8,128)(2,1)} %up_mask.1.refs_3_), calls=%async_computation.1 | async-start | bytes 1048576 | tf_op jit(solution)/shard_map/all_to_all | solution.py:540
  62.3 13.6 %collective-permute-start.7 = (bf16[288,512]{1,0:T(8,128)(2,1)}, bf16[288,512]{1,0:T(8,128)(2,1)}, u32[]{:S(2)}, u32[]{:S(2)}) collective-permute-start(bf16[288,512]{1,0:T(8,128)(2,1)} %base_left.1.refs_5_), channel_id=1, source_target_pairs={{0,2},{1,3},{2,0},{3,1},{4,6},{5,7},{6,4},{7,5},{8,10},{9,11},{10,... | collective-permute-start | bytes 884744 | tf_op jit(solution)/shard_map/ppermute | solution.py:534
  69.0 13.0 %collective-permute-start.8 = (bf16[288,1408]{1,0:T(8,128)(2,1)}, bf16[288,1408]{1,0:T(8,128)(2,1)}, u32[]{:S(2)}, u32[]{:S(2)}) collective-permute-start(bf16[288,1408]{1,0:T(8,128)(2,1)} %get-tuple-element.36), channel_id=1, source_target_pairs={{0,1},{1,0},{2,3},{3,2},{4,5},{5,4},{6,7},{7,6},{8,9},{9,8},{10,11... | collective-permute-start | bytes 2433032 | tf_op jit(solution)/shard_map/ppermute | solution.py:531
  69.3 12.7 %copy-start.18 = (f32[128]{0:T(128)S(1)}, f32[128]{0:T(128)}, u32[]{:S(2)}) copy-start(f32[128]{0:T(128)} %param.19) | copy-start | bytes 1540
  69.3 12.7 %collective-permute-start.5 = (bf16[288,768]{1,0:T(8,128)(2,1)}, bf16[288,768]{1,0:T(8,128)(2,1)}, u32[]{:S(2)}, u32[]{:S(2)}) collective-permute-start(bf16[288,768]{1,0:T(8,128)(2,1)} %get-tuple-element.34.refs_4_), channel_id=1, source_target_pairs={{0,2},{1,3},{2,0},{3,1},{4,6},{5,7},{6,4},{7,5},{8,10},{9,11},{10,... | collective-permute-start | bytes 1327112 | tf_op jit(solution)/shard_map/ppermute | solution.py:534
  71.8 10.3 %copy-start.21 = (f32[288,1024]{1,0:T(8,128)S(1)}, f32[288,1024]{1,0:T(8,128)}, u32[]{:S(2)}) copy-start(f32[288,1024]{1,0:T(8,128)} %copy-done.19) | copy-start | bytes 3538948
  71.8 10.2 %collective-permute-start.6 = (bf16[4,2,32,1024]{3,2,1,0:T(8,128)(2,1)S(1)}, bf16[4,2,32,1024]{3,2,1,0:T(8,128)(2,1)S(1)}, u32[]{:S(2)}, u32[]{:S(2)}) collective-permute-start(bf16[4,2,32,1024]{3,2,1,0:T(8,128)(2,1)S(1)} %all-to-all-done.1.refs_4_), channel_id=1, source_target_pairs={{0,1},{1,0},{2,3},{3,2},{4,5},{5,4},{6,7},{7,6},{8,9},{9,8},{10,11... | collective-permute-start | bytes 1572872 | tf_op jit(solution)/shard_map/ppermute | solution.py:531
  73.0 9.0 %copy-start.26 = (bf16[288,1024]{1,0:T(8,128)(2,1)S(1)}, bf16[288,1024]{1,0:T(8,128)(2,1)}, u32[]{:S(2)}) copy-start(bf16[288,1024]{1,0:T(8,128)(2,1)} %copy-done.25) | copy-start | bytes 1769476
  86.4 4.8 %collective-permute-start.12 = (f32[2,4,32,1024]{3,2,1,0:T(8,128)S(1)}, f32[2,4,32,1024]{3,2,1,0:T(8,128)S(1)}, u32[]{:S(2)}, u32[]{:S(2)}) collective-permute-start(f32[2,4,32,1024]{3,2,1,0:T(8,128)S(1)} %get-tuple-element.39), channel_id=1, source_target_pairs={{0,1},{1,0},{2,3},{3,2},{4,5},{5,4},{6,7},{7,6},{8,9},{9,8},{10,11... | collective-permute-start | bytes 3145736 | tf_op jit(solution)/shard_map/ppermute | solution.py:531
  86.5 4.7 %collective-permute-start.9 = (bf16[288,128]{1,0:T(8,128)(2,1)S(1)}, bf16[288,128]{1,0:T(8,128)(2,1)S(1)}, u32[]{:S(2)}, u32[]{:S(2)}) collective-permute-start(bf16[288,128]{1,0:T(8,128)(2,1)S(1)} %get-tuple-element.37.refs_0_), channel_id=1, source_target_pairs={{0,2},{1,3},{2,0},{3,1},{4,6},{5,7},{6,4},{7,5},{8,10},{9,11},{10,... | collective-permute-start | bytes 221192 | tf_op jit(solution)/shard_map/ppermute | solution.py:534
  87.6 5.0 %collective-permute-start.10 = (bf16[288,128]{1,0:T(8,128)(2,1)S(1)}, bf16[288,128]{1,0:T(8,128)(2,1)S(1)}, u32[]{:S(2)}, u32[]{:S(2)}) collective-permute-start(bf16[288,128]{1,0:T(8,128)(2,1)S(1)} %get-tuple-element.37.refs_0_), channel_id=1, source_target_pairs={{0,1},{1,0},{2,3},{3,2},{4,5},{5,4},{6,7},{7,6},{8,9},{9,8},{10,11... | collective-permute-start | bytes 221192 | tf_op jit(solution)/shard_map/ppermute | solution.py:531
  91.2 1.4 %collective-permute-start.11 = (bf16[288,128]{1,0:T(8,128)(2,1)S(1)}, bf16[288,128]{1,0:T(8,128)(2,1)S(1)}, u32[]{:S(2)}, u32[]{:S(2)}) collective-permute-start(bf16[288,128]{1,0:T(8,128)(2,1)S(1)} %collective-permute-done.9.refs_1_), channel_id=1, source_target_pairs={{0,1},{1,0},{2,3},{3,2},{4,5},{5,4},{6,7},{7,6},{8,9},{9,8},{10,11... | collective-permute-start | bytes 221192 | tf_op jit(solution)/shard_map/ppermute | solution.py:531
  91.5 10.1 %collective-permute-start.16 = (bf16[4,32,1024]{2,1,0:T(8,128)(2,1)S(1)}, bf16[4,32,1024]{2,1,0:T(8,128)(2,1)S(1)}, u32[]{:S(2)}, u32[]{:S(2)}) collective-permute-start(bf16[4,32,1024]{2,1,0:T(8,128)(2,1)S(1)} %get-tuple-element.45), channel_id=1, source_target_pairs={{0,2},{1,3},{2,0},{3,1},{4,6},{5,7},{6,4},{7,5},{8,10},{9,11},{10,... | collective-permute-start | bytes 786440 | tf_op jit(solution)/shard_map/ppermute | solution.py:534
  97.0 38.3 %collective-permute-start.13 = (bf16[128,1280]{1,0:T(8,128)(2,1)S(1)}, bf16[128,1280]{1,0:T(8,128)(2,1)S(1)}, u32[]{:S(2)}, u32[]{:S(2)}) collective-permute-start(bf16[128,1280]{1,0:T(8,128)(2,1)S(1)} %get-tuple-element.42.refs_2_), channel_id=1, source_target_pairs={{0,4},{4,0},{8,12},{12,8},{1,5},{5,1},{9,13},{13,9},{2,6},{6,2},{1... | collective-permute-start | bytes 983048 | tf_op jit(solution)/shard_map/ppermute | solution.py:537
  98.7 36.6 %collective-permute-start.14 = (bf16[128,1280]{1,0:T(8,128)(2,1)S(1)}, bf16[128,1280]{1,0:T(8,128)(2,1)S(1)}, u32[]{:S(2)}, u32[]{:S(2)}) collective-permute-start(bf16[128,1280]{1,0:T(8,128)(2,1)S(1)} %get-tuple-element.43), channel_id=1, source_target_pairs={{0,8},{4,12},{8,0},{12,4},{1,9},{5,13},{9,1},{13,5},{2,10},{6,14},... | collective-permute-start | bytes 983048 | tf_op jit(solution)/shard_map/ppermute | solution.py:537
  101.1 34.3 %copy-start.6 = (f32[1,1280,128]{2,1,0:T(8,128)S(1)}, f32[1,1280,128]{2,1,0:T(8,128)}, u32[]{:S(2)}) copy-start(f32[1,1280,128]{2,1,0:T(8,128)} %param.20) | copy-start | bytes 1966084
  101.1 34.3 %copy-start.7 = (f32[1,1280,128]{2,1,0:T(8,128)S(1)}, f32[1,1280,128]{2,1,0:T(8,128)}, u32[]{:S(2)}) copy-start(f32[1,1280,128]{2,1,0:T(8,128)} %param.22) | copy-start | bytes 1966084
  101.1 34.3 %copy-start.8 = (f32[1,1280,128]{2,1,0:T(8,128)S(1)}, f32[1,1280,128]{2,1,0:T(8,128)}, u32[]{:S(2)}) copy-start(f32[1,1280,128]{2,1,0:T(8,128)} %param.24) | copy-start | bytes 1966084
  101.1 34.3 %copy-start.10 = (f32[1,32,1024]{2,1,0:T(8,128)S(1)}, f32[1,32,1024]{2,1,0:T(8,128)}, u32[]{:S(2)}) copy-start(f32[1,32,1024]{2,1,0:T(8,128)} %param.21) | copy-start | bytes 393220
  101.1 34.3 %copy-start.11 = (f32[1,32,1024]{2,1,0:T(8,128)S(1)}, f32[1,32,1024]{2,1,0:T(8,128)}, u32[]{:S(2)}) copy-start(f32[1,32,1024]{2,1,0:T(8,128)} %param.23) | copy-start | bytes 393220
  101.1 34.3 %copy-start.12 = (f32[1,32,1024]{2,1,0:T(8,128)S(1)}, f32[1,32,1024]{2,1,0:T(8,128)}, u32[]{:S(2)}) copy-start(f32[1,32,1024]{2,1,0:T(8,128)} %param.25) | copy-start | bytes 393220
  101.1 34.2 %collective-permute-start.15 = (bf16[128,1280]{1,0:T(8,128)(2,1)S(1)}, bf16[128,1280]{1,0:T(8,128)(2,1)S(1)}, u32[]{:S(2)}, u32[]{:S(2)}) collective-permute-start(bf16[128,1280]{1,0:T(8,128)(2,1)S(1)} %get-tuple-element.44), channel_id=1, source_target_pairs={{0,12},{4,8},{8,4},{12,0},{1,13},{5,9},{9,5},{13,1},{2,14},{6,10},... | collective-permute-start | bytes 983048 | tf_op jit(solution)/shard_map/ppermute | solution.py:537
  101.7 20.6 %collective-permute-start.17 = (bf16[32,1024]{1,0:T(8,128)(2,1)S(1)}, bf16[32,1024]{1,0:T(8,128)(2,1)S(1)}, u32[]{:S(2)}, u32[]{:S(2)}) collective-permute-start(bf16[32,1024]{1,0:T(8,128)(2,1)S(1)} %get-tuple-element.47), channel_id=1, source_target_pairs={{0,4},{4,0},{8,12},{12,8},{1,5},{5,1},{9,13},{13,9},{2,6},{6,2},{1... | collective-permute-start | bytes 196616 | tf_op jit(solution)/shard_map/ppermute | solution.py:537
  102.5 32.8 %collective-permute-start.18 = (bf16[32,1024]{1,0:T(8,128)(2,1)S(1)}, bf16[32,1024]{1,0:T(8,128)(2,1)S(1)}, u32[]{:S(2)}, u32[]{:S(2)}) collective-permute-start(bf16[32,1024]{1,0:T(8,128)(2,1)S(1)} %get-tuple-element.48), channel_id=1, source_target_pairs={{0,8},{4,12},{8,0},{12,4},{1,9},{5,13},{9,1},{13,5},{2,10},{6,14},... | collective-permute-start | bytes 196616 | tf_op jit(solution)/shard_map/ppermute | solution.py:537
  122.3 13.0 %collective-permute-start.19 = (bf16[32,1024]{1,0:T(8,128)(2,1)S(1)}, bf16[32,1024]{1,0:T(8,128)(2,1)S(1)}, u32[]{:S(2)}, u32[]{:S(2)}) collective-permute-start(bf16[32,1024]{1,0:T(8,128)(2,1)S(1)} %get-tuple-element.49), channel_id=1, source_target_pairs={{0,12},{4,8},{8,4},{12,0},{1,13},{5,9},{9,5},{13,1},{2,14},{6,10},... | collective-permute-start | bytes 196616 | tf_op jit(solution)/shard_map/ppermute | solution.py:537
  (17 other events, 37.9 us)

commit v3 on v2

--- a/solution.py
+++ b/solution.py
@@ -202,7 +202,7 @@
         return self.target
 
 
-def call(kernel, name, scalars, late, outs, plain=(), order=(), scratch=()):
+def call(kernel, name, scalars, late, outs, plain=(), order=(), scratch=(), vmem=36, light=False):
     n, m, p, d, o = len(scalars), len(late), len(plain), len(order), len(outs)
 
     def body(*refs):
@@ -224,8 +224,10 @@
         scratch_shapes=[pltpu.VMEM(a.shape, a.dtype) for a in late]
         + [pltpu.SemaphoreType.DMA((max(m, 1),))]
         + list(scratch),
-        compiler_params=pltpu.CompilerParams(vmem_limit_bytes=36 * 2**20),
-        cost_estimate=pl.CostEstimate(flops=3 * 10**10, bytes_accessed=moved, transcendentals=0),
+        compiler_params=pltpu.CompilerParams(vmem_limit_bytes=vmem * 2**20),
+        cost_estimate=pl.CostEstimate(
+            flops=1 if light else 3 * 10**10, bytes_accessed=1 if light else moved, transcendentals=0
+        ),
     )(*args)
 
 
@@ -315,34 +317,27 @@
     grads_out[...] = mm(chosen, cotangent.get()[...]).astype(bf16)
 
 
-def down_mask_kernel(ranks, down, out):
-    rank = ranks[lax.axis_index("dp")]
-    column = lax.broadcasted_iota(i32, (QUARTER, PADDED_RANK), 1)
-    masked = jnp.where(column < rank, down.get()[...], 0.0).astype(bf16)
-    for i in range(4):
-        out[i] = masked
-
-
-def up_mask_kernel(ranks, own, mate, out):
+def weights_kernel(ranks, down, up_own, up_mate, out):
     rank = ranks[lax.axis_index("dp")]
     f = lax.axis_index("fsdp")
+    column = lax.broadcasted_iota(i32, (QUARTER, PADDED_RANK), 1)
+    out[:QUARTER] = jnp.where(column < rank, down.get()[...], 0.0).astype(bf16)
     row = lax.broadcasted_iota(i32, (32, KEY_WIDTH), 0)
-    own_rows = jnp.where(row + 32 * f < rank, own.get()[...], 0.0).astype(bf16)
-    mate_rows = jnp.where(row + 32 * (f ^ 2) < rank, mate.get()[...], 0.0).astype(bf16)
-    for i in range(4):
-        out[i, 0] = own_rows
-        out[i, 1] = mate_rows
-
-
-def base_left_kernel(rows, own, mate, out):
-    half = KEY_WIDTH // 2
-    total = mm(rows.get()[0, :LIVE], own.get()[:, :half])
-    out[...] = (total + mm(rows.get()[1, :LIVE], mate.get()[:, :half])).astype(bf16)
-
-
-def down_factors(held):
-    dp = lax.axis_index("dp")
-    return jnp.concatenate([held.get()[dp ^ j] for j in range(4)], axis=1)
+    for part, held in enumerate((up_own, up_mate)):
+        masked = jnp.where(row + 32 * (f ^ (2 * part)) < rank, held.get()[...], 0.0).astype(bf16)
+        for k in range(8):
+            at = QUARTER + 64 * k + 32 * part
+            out[at : at + 32] = masked[:, 128 * k : 128 * k + 128]
+
+
+def base_mate_kernel(rows, own, mate, out):
+    total = mm(rows.get()[0, :LIVE], own.get()[...])
+    out[...] = (total + mm(rows.get()[1, :LIVE], mate.get()[...])).astype(bf16)
+
+
+def down_factors(own, others):
+    parts = [own.get()[:QUARTER]] + [others.get()[j, :QUARTER] for j in range(3)]
+    return jnp.concatenate(parts, axis=1)
 
 
 def mate_places(rows):
@@ -358,19 +353,14 @@
     return total
 
 
-def mate_kernel(rows, own, mate, downs, downs_core, out, core_out):
-    half = KEY_WIDTH // 2
+def low_mate_kernel(rows, own, others, core_own, core_others, out, core_out):
     held = rows.get()
     places = mate_places(held)
     core_out[:, :QUARTER] = held[1, :LIVE]
     core_out[:, QUARTER:] = places
-    total = mm(held[0, :LIVE], own.get()[:, half:]) + mm(held[1, :LIVE], mate.get()[:, half:])
-    out[:, :half] = total.astype(bf16)
-    every = mm(held[0, :LIVE], down_factors(downs)) + mm(held[1, :LIVE], down_factors(downs_core))
-    low = own_adapter(every, places)
-    high = low.astype(bf16)
-    out[:, half : half + 128] = high
-    out[:, half + 128 :] = (low - high.astype(f32)).astype(bf16)
+    every = mm(held[0, :LIVE], down_factors(own, others))
+    every = every + mm(held[1, :LIVE], down_factors(core_own, core_others))
+    out[...] = own_adapter(every, places)
 
 
 def base_own_kernel(near, own, far, mate, out):
@@ -378,10 +368,21 @@
     out[...] = total + mm(far.get()[:, :QUARTER], mate.get()[...])
 
 
-def low_own_kernel(near, far, downs, downs_core, out):
+def low_own_kernel(near, far, own, others, core_own, core_others, out, up):
+    f = lax.axis_index("fsdp")
+    c, x = f % 2, f // 2
     held = far.get()
-    every = mm(near.get()[...], down_factors(downs)) + mm(held[:, :QUARTER], down_factors(downs_core))
+    every = mm(near.get()[...], down_factors(own, others))
+    every = every + mm(held[:, :QUARTER], down_factors(core_own, core_others))
     out[...] = own_adapter(every, held[:, QUARTER:])
+    for j in range(4):
+        for part in range(2):
+            for first, rest, side in ((own, others, c), (core_own, core_others, 1 - c)):
+                source = rest.get().at[j - 1] if j else first.get()
+                target = pl.multiple_of(128 * j + 64 * (x ^ part) + 32 * side, 32)
+                for k in range(8):
+                    at = QUARTER + 64 * k + 32 * part
+                    up[pl.ds(target, 32), 128 * k : 128 * k + 128] = source[at : at + 32, :]
 
 
 def identity():
@@ -400,33 +401,25 @@
     return jnp.concatenate(parts, axis=0)
 
 
-def keys_kernel(ranks, far, low, right, ups, ups_core, base, left, grads, gain, *refs):
-    dlow_out, kept_out, sent_out, up, total = refs
+def keys_kernel(ranks, far, low, low_mate, up_late, base, base_mate, grads, gain, *refs):
+    dlow_out, kept_out, sent_out, total = refs
+    up = up_late.get()
     dp = lax.axis_index("dp")
     f = lax.axis_index("fsdp")
     c, x = f % 2, f // 2
-    for j in range(4):
-        for part in range(2):
-            for held, side in ((ups, c), (ups_core, 1 - c)):
-                target = 128 * j + 64 * (x ^ part) + 32 * side
-                up[pl.ds(pl.multiple_of(target, 32), 32), :] = held.get()[dp ^ j, part]
     ids = far.get()[:, QUARTER:]
     adapter = ids.astype(f32)
     scales = [adapter_alpha_scale / jnp.full((1, HEAD), ranks[dp ^ j], i32).astype(f32) for j in range(4)]
     scale = jnp.zeros((LIVE, HEAD), f32)
     for j in range(4):
         scale = jnp.where(adapter == j, scales[j], scale)
-    half = KEY_WIDTH // 2
-    arrived = right.get()[:, half:].astype(f32)
-    lowrank = (low.get()[...] + (arrived[:, :128] + arrived[:, 128:])).astype(bf16).astype(f32)
+    lowrank = (low.get()[...] + low_mate.get()[...]).astype(bf16).astype(f32)
     wide = spread(lowrank, ids, range(4))
     added = mm(wide, up[...])
     parts = []
     for k in range(8):
         lanes = slice(128 * k, 128 * k + 128)
-        source = left.get()[:, lanes] if k < 4 else right.get()[:, 128 * k - half : 128 * k - half + 128]
-        arrived = source.astype(f32)
-        held = (base.get()[:, lanes] + arrived).astype(bf16).astype(f32)
+        held = (base.get()[:, lanes] + base_mate.get()[:, lanes].astype(f32)).astype(bf16).astype(f32)
         head = held + scale * added[:, lanes]
         inverse = lax.rsqrt(jnp.mean(head * head, axis=-1, keepdims=True) + norm_epsilon)
         normed = head * inverse
@@ -536,9 +529,6 @@
     def along(value, distance):
         return lax.ppermute(value, "dp", [(i, i ^ distance) for i in range(4)])
 
-    def exchange(value):
-        return lax.all_to_all(value, "dp", split_axis=0, concat_axis=0, tiled=True)
-
     frozen_core = core(frozen)
     up_mate = across(adapter_up_factor[0])
     (sent,) = call(
@@ -549,18 +539,21 @@
         [shape((2, LIVE + 16, QUARTER), bf16)],
         [tokens],
         scratch=[pltpu.VMEM((2, tokens.shape[0], QUARTER), bf16), pltpu.SemaphoreType.DMA((2,))],
+        vmem=60,
     )
     rows = across(sent)
 
-    (masked,) = call(
-        down_mask_kernel,
-        "down_mask",
+    (message,) = call(
+        weights_kernel,
+        "weights",
         [ranks],
-        [adapter_down_factor[0]],
-        [shape((4, QUARTER, PADDED_RANK), bf16)],
+        [adapter_down_factor[0], adapter_up_factor[0], up_mate],
+        [shape((QUARTER + 512, PADDED_RANK), bf16)],
         order=[sent],
     )
-    downs = exchange(masked)
+    arrived = [along(message, j) for j in (1, 2, 3)]
+    message_core = core(message)
+
     near, far, grads = call(
         lambda *refs: pack_kept_kernel(slots, *refs),
         "pack_kept",
@@ -572,67 +565,62 @@
             shape((LIVE, KEY_WIDTH), bf16),
         ],
         [tokens],
-        order=[masked, frozen_core],
+        order=[message_core, frozen_core],
         scratch=[pltpu.VMEM((2, tokens.shape[0], QUARTER), bf16), pltpu.SemaphoreType.DMA((2,))],
     )
     far_core = core(far)
 
+    (partial,) = call(
+        base_mate_kernel,
+        "base_mate",
+        [],
+        [rows, frozen, frozen_core],
+        [shape((LIVE, KEY_WIDTH), bf16)],
+        order=[near],
+    )
+    base_mate = across(partial)
+    others = jnp.stack([after(w, partial) for w in arrived])
+    others_core = core(others)
     (base,) = call(
         base_own_kernel,
         "base_own",
         [],
         [near, frozen, far, frozen_core],
         [shape((LIVE, KEY_WIDTH), f32)],
-    )
-    (up_pair,) = call(
-        up_mask_kernel,
-        "up_mask",
-        [ranks],
-        [adapter_up_factor[0], up_mate],
-        [shape((4, 2, 32, KEY_WIDTH), bf16)],
-        order=[base, far_core],
-    )
-    ups = exchange(up_pair)
-    downs = after(downs, base)
-    downs_core = core(downs)
-    (left,) = call(
-        base_left_kernel,
-        "base_left",
-        [],
-        [rows, frozen, frozen_core],
-        [shape((LIVE, KEY_WIDTH // 2), bf16)],
-        order=[up_pair],
-    )
-    right, cross = call(
-        mate_kernel,
-        "mate",
-        [],
-        [rows, frozen, frozen_core, downs, downs_core],
-        [shape((LIVE, KEY_WIDTH // 2 + 256), bf16), shape((LIVE, QUARTER + 128), bf16)],
-        order=[left],
-    )
-    left_in, right_in, cross_core = across(left), across(right), core(cross)
-    (low,) = call(
+        order=[others],
+    )
+    weights = [message, others, message_core, others_core]
+    low_sent, cross = call(
+        low_mate_kernel,
+        "low_mate",
+        [],
+        [rows, *weights],
+        [shape((LIVE, PADDED_RANK), f32), shape((LIVE, QUARTER + 128), bf16)],
+        order=[base],
+        light=True,
+    )
+    low_mate, cross_core = across(low_sent), core(cross)
+    low, up = call(
         low_own_kernel,
         "low_own",
         [],
-        [near, far, downs, downs_core],
-        [shape((LIVE, PADDED_RANK), f32)],
-        order=[right],
-    )
-    ups_core = core(ups)
+        [near, far, *weights],
+        [shape((LIVE, PADDED_RANK), f32), shape((512, KEY_WIDTH), bf16)],
+        order=[low_sent],
+        light=True,
+    )
     dlow, up_kept, up_core = call(
         keys_kernel,
         "keys",
         [ranks],
-        [far, low, right_in, ups, ups_core, base, left_in, grads, key_norm_weight[None, :]],
+        [far, low, low_mate, up, base, base_mate, grads, key_norm_weight[None, :]],
         [
             shape((LIVE, PADDED_RANK), bf16),
             shape((2, 4, 32, KEY_WIDTH), f32),
             shape((2, 4, 32, KEY_WIDTH), f32),
         ],
-        order=[cross_core],
-        scratch=[pltpu.VMEM((512, KEY_WIDTH), bf16), pltpu.VMEM((512, KEY_WIDTH), f32)],
+        order=[far_core],
+        scratch=[pltpu.VMEM((512, KEY_WIDTH), f32)],
     )
     dlow_mate, dlow_core = across(dlow), core(dlow)
     dlow_cross = core(dlow_mate)

time: 141 us -> 124 us (0.88)
  local copies, waits for them, and re-layouts: 13.7 us -> 0.07 us
  Pallas kernels: 40.9 us -> 32.4 us
  waiting for transfers between devices: 55.8 us -> 63.8 us
  starting transfers between devices: 28.5 us -> 26.6 us
    ppermute x6, waiting for transfers between devices: 9.58 us -> 37.5 us  [across(): return lax.ppermute(value, 'fsdp', [(i, i ^ 2) for i in range(4)])]
    all_to_all x2 -> x0, waiting for transfers between devices: 19.6 us -> none  [exchange(): return lax.all_to_all(value, 'dp', split_axis=0, concat_axis=0, tiled=True)]
    unnamed x54 -> x26, local copies, waits for them, and re-layouts: 13.7 us -> 0.07 us
    all_to_all x2 -> x0, starting transfers between devices: 9.05 us -> none  [exchange(): return lax.all_to_all(value, 'dp', split_axis=0, concat_axis=0, tiled=True)]
    pallas_call x13 -> x12, Pallas kernels: 40.9 us -> 32.4 us  [call(): pl.pallas_call(body, name=name, in_specs=[SMEM] * n + [HBM] * (m + p + d)...]
    ppermute x6 -> x9, starting transfers between devices: 11.5 us -> 16.1 us  [along(): return lax.ppermute(value, 'dp', [(i, i ^ distance) for i in range(4)])]
    ppermute x6, starting transfers between devices: 6.93 us -> 8.81 us  [across(): return lax.ppermute(value, 'fsdp', [(i, i ^ 2) for i in range(4)])]
    ppermute x6 -> x9, waiting for transfers between devices: 26.7 us -> 26.3 us  [along(): return lax.ppermute(value, 'dp', [(i, i ^ distance) for i in range(4)])]
  transfers between devices with their start and end apart: 22 -> 23, of which waited for: 6 -> 6; matrix products, arithmetic and copies ran while one was open for 0% -> 0% of each run, Pallas kernels for 23% -> 19%
where the time goes in v3:
time: 124 us
  waiting for transfers between devices  63.8 us (51%)
  Pallas kernels  32.4 us (26%)
  starting transfers between devices  26.6 us (21%)
    ppermute x6, waiting for transfers between devices, across(): return lax.ppermute(value, 'fsdp', [(i, i ^ 2) for i in range(4)])  37.5 us
    pallas_call x12, Pallas kernels, call(): pl.pallas_call(body, name=name, in_specs=[SMEM] * n + [HBM] * (m + p + d)...  32.4 us
    ppermute x9, waiting for transfers between devices, along(): return lax.ppermute(value, 'dp', [(i, i ^ distance) for i in range(4)])  26.3 us
    ppermute x9, starting transfers between devices, along(): return lax.ppermute(value, 'dp', [(i, i ^ distance) for i in range(4)])  16.1 us
    ppermute x6, starting transfers between devices, across(): return lax.ppermute(value, 'fsdp', [(i, i ^ 2) for i in range(4)])  8.81 us
  transfers between devices with their start and end apart: 23, of which 6 were waited for; matrix products, arithmetic and copies ran while one was open for 0% of the time, Pallas kernels for 19%

profile of v3, /device:TPU:0, one launch (start us, length us, event | category | flops | bytes accessed | tf_op | source)
XLA Modules:
  0.0 124.2 jit_solution(702900180794536619)
XLA Ops:
  0.7 3.0 %collective-permute-start = (f32[32,1024]{1,0:T(8,128)}, f32[32,1024]{1,0:T(8,128)S(1)}, u32[]{:S(2)}, u32[]{:S(2)}) collective-permute-start(f32[32,1024]{1,0:T(8,128)} %bitcast.20), channel_id=1, source_target_pairs={{0,2},{1,3},{2,0},{3,1},{4,6},{5,7},{6,4},{7,5},{8,10},{9,11},{10,... | collective-permute-start | bytes 393224 | tf_op jit(solution)/shard_map/ppermute | solution.py:527
  3.7 4.3 %pack_sent.1.refs_4_ = bf16[2,304,1280]{2,1,0:T(8,128)(2,1)} custom-call(s32[1,12]{1,0:T(1,128)} %refs_0_.6, s32[1,12]{1,0:T(1,128)} %refs_1_.5, bf16[384,5120]{1,0:T(8,128)(2,1)} %refs_3_.1), custom_call_target="tpu_custom_call" | custom-call | flops 30000001024 | bytes 5488736 | tf_op jit(solution)/shard_map/pack_sent/pallas_call | solution.py:218
  8.1 1.2 weights.1.refs_1_.refs_2_
  9.3 0.6 collective-permute-start.1
  9.9 0.6 collective-permute-start.4
  10.5 1.6 %collective-permute-start.3 = (bf16[1792,128]{1,0:T(8,128)(2,1)S(1)}, bf16[1792,128]{1,0:T(8,128)(2,1)S(1)}, u32[]{:S(2)}, u32[]{:S(2)}) collective-permute-start(bf16[1792,128]{1,0:T(8,128)(2,1)S(1)} %weights.1.refs_1_.refs_2_), channel_id=1, source_target_pairs={{0,4},{4,0},{8,12},{12,8},{1,5},{5,1},{9,13},{13,9},{2,6},{6,2},{1... | collective-permute-start | bytes 1376264 | tf_op jit(solution)/shard_map/ppermute | solution.py:530
  12.1 2.6 %collective-permute-start.5 = (bf16[1792,128]{1,0:T(8,128)(2,1)S(1)}, bf16[1792,128]{1,0:T(8,128)(2,1)S(1)}, u32[]{:S(2)}, u32[]{:S(2)}) collective-permute-start(bf16[1792,128]{1,0:T(8,128)(2,1)S(1)} %weights.1.refs_1_.refs_2_), channel_id=1, source_target_pairs={{0,8},{4,12},{8,0},{12,4},{1,9},{5,13},{9,1},{13,5},{2,10},{6,14},... | collective-permute-start | bytes 1376264 | tf_op jit(solution)/shard_map/ppermute | solution.py:530
  15.0 3.0 %pack_kept.1 = (bf16[288,1280]{1,0:T(8,128)(2,1)S(1)}, bf16[288,1408]{1,0:T(8,128)(2,1)S(1)}, bf16[288,1024]{1,0:T(8,128)(2,1)S(1)}) custom-call(s32[1,12]{1,0:T(1,128)S(1)} %copy-done.9, s32[1,12]{1,0:T(1,128)S(1)} %copy-done.10, bf16[384,1024]{1,0:T(8,128)(2,1)S(1)} %copy-done.2, bf16[384,5120]{1,0:T(8,128)(2,1)S(1)} %copy-done, ...), custom_call_target="tpu_custom_call" | custom-call | flops 30000001024 | bytes 6856800 | tf_op jit(solution)/shard_map/pack_kept/pallas_call | solution.py:218
  18.0 28.1 %collective-permute-done.4.refs_0_.refs_4_ = bf16[2,304,1280]{2,1,0:T(8,128)(2,1)S(1)} collective-permute-done((bf16[2,304,1280]{2,1,0:T(8,128)(2,1)}, bf16[2,304,1280]{2,1,0:T(8,128)(2,1)S(1)}, u32[]{:S(2)}, u32[]{:S(2)}) %collective-permute-start.4) | collective-permute-done | bytes 1556512 | tf_op jit(solution)/shard_map/ppermute | solution.py:527
  46.1 2.7 %base_mate.1 = bf16[288,1024]{1,0:T(8,128)(2,1)S(1)} custom-call(bf16[2,304,1280]{2,1,0:T(8,128)(2,1)S(1)} %collective-permute-done.4.refs_0_.refs_4_, bf16[1280,1024]{1,0:T(8,128)(2,1)S(1)} %copy-done.1, bf16[1280,1024]{1,0:T(8,128)(2,1)S(1)} %collective-permute-done.2.refs_5_.refs_2_.refs_3_, bf16[288,1280]{1,0:T(8,128)(2,1)S(1)} %get-tuple-element.36.refs_3_.refs_0_.refs_5_), custom_call_target="tpu_custom_call" | custom-call | flops 30000001024 | bytes 7389184 | tf_op jit(solution)/shard_map/base_mate/pallas_call | solution.py:218
  48.9 1.1 collective-permute-start.9
  50.2 0.5 collective-permute-start.10
  50.7 2.7 %base_own.1.refs_5_ = f32[288,1024]{1,0:T(8,128)S(1)} custom-call(bf16[288,1280]{1,0:T(8,128)(2,1)S(1)} %get-tuple-element.36.refs_3_.refs_0_.refs_5_, bf16[1280,1024]{1,0:T(8,128)(2,1)S(1)} %copy-done.1, bf16[288,1408]{1,0:T(8,128)(2,1)S(1)} %get-tuple-element.35.refs_2_.refs_1_.refs_6_, ...), custom_call_target="tpu_custom_call" | custom-call | flops 30000001024 | bytes 7970816 | tf_op jit(solution)/shard_map/base_own/pallas_call | solution.py:218
  53.4 2.6 %low_mate.1 = (f32[288,128]{1,0:T(8,128)S(1)}, bf16[288,1408]{1,0:T(8,128)(2,1)S(1)}) custom-call(bf16[2,304,1280]{2,1,0:T(8,128)(2,1)S(1)} %collective-permute-done.4.refs_0_.refs_4_, bf16[1792,128]{1,0:T(8,128)(2,1)S(1)} %weights.1.refs_1_.refs_2_, bf16[3,1792,128]{2,1,0:T(8,128)(2,1)S(1)} %pad_maximum_fusion.refs_4_.refs_2_.refs_3_, ...), custom_call_target="tpu_custom_call" | custom-call | flops 1 | bytes 1 | tf_op jit(solution)/shard_map/low_mate/pallas_call | solution.py:218
  56.0 1.1 collective-permute-start.8
  57.1 2.7 %low_own.1 = (f32[288,128]{1,0:T(8,128)S(1)}, bf16[512,1024]{1,0:T(8,128)(2,1)S(1)}) custom-call(bf16[288,1280]{1,0:T(8,128)(2,1)S(1)} %get-tuple-element.36.refs_3_.refs_0_.refs_5_, bf16[288,1408]{1,0:T(8,128)(2,1)S(1)} %get-tuple-element.35.refs_2_.refs_1_.refs_6_, bf16[1792,128]{1,0:T(8,128)(2,1)S(1)} %weights.1.refs_1_.refs_2_, ...), custom_call_target="tpu_custom_call" | custom-call | flops 1 | bytes 1 | tf_op jit(solution)/shard_map/low_own/pallas_call | solution.py:218
  59.8 5.2 %collective-permute-done.9.refs_6_ = bf16[288,1024]{1,0:T(8,128)(2,1)S(1)} collective-permute-done((bf16[288,1024]{1,0:T(8,128)(2,1)S(1)}, bf16[288,1024]{1,0:T(8,128)(2,1)S(1)}, u32[]{:S(2)}, u32[]{:S(2)}) %collective-permute-start.9) | collective-permute-done | bytes 589856 | tf_op jit(solution)/shard_map/ppermute | solution.py:527
  65.0 1.6 %collective-permute-done.8.refs_3_ = f32[288,128]{1,0:T(8,128)S(1)} collective-permute-done((f32[288,128]{1,0:T(8,128)S(1)}, f32[288,128]{1,0:T(8,128)S(1)}, u32[]{:S(2)}, u32[]{:S(2)}) %collective-permute-start.8) | collective-permute-done | bytes 147488 | tf_op jit(solution)/shard_map/ppermute | solution.py:527
  66.6 4.2 %keys.1 = (bf16[288,128]{1,0:T(8,128)(2,1)S(1)}, f32[2,4,32,1024]{3,2,1,0:T(8,128)S(1)}, f32[2,4,32,1024]{3,2,1,0:T(8,128)S(1)}) custom-call(s32[4]{0:T(128)S(1)} %copy-done.11, bf16[288,1408]{1,0:T(8,128)(2,1)S(1)} %get-tuple-element.35.refs_2_.refs_1_.refs_6_, f32[288,128]{1,0:T(8,128)S(1)} %get-tuple-element.41.refs_2_, ...), custom_call_target="tpu_custom_call" | custom-call | flops 30000001024 | bytes 6685200 | tf_op jit(solution)/shard_map/keys/pallas_call | solution.py:218
  70.8 1.5 %collective-permute-start.11 = (bf16[288,128]{1,0:T(8,128)(2,1)S(1)}, bf16[288,128]{1,0:T(8,128)(2,1)S(1)}, u32[]{:S(2)}, u32[]{:S(2)}) collective-permute-start(bf16[288,128]{1,0:T(8,128)(2,1)S(1)} %get-tuple-element.44.refs_0_), channel_id=1, source_target_pairs={{0,2},{1,3},{2,0},{3,1},{4,6},{5,7},{6,4},{7,5},{8,10},{9,11},{10,... | collective-permute-start | bytes 221192 | tf_op jit(solution)/shard_map/ppermute | solution.py:527
  72.5 0.3 collective-permute-start.12
  72.8 2.7 %collective-permute-done.11.refs_1_ = bf16[288,128]{1,0:T(8,128)(2,1)S(1)} collective-permute-done((bf16[288,128]{1,0:T(8,128)(2,1)S(1)}, bf16[288,128]{1,0:T(8,128)(2,1)S(1)}, u32[]{:S(2)}, u32[]{:S(2)}) %collective-permute-start.11) | collective-permute-done | bytes 73760 | tf_op jit(solution)/shard_map/ppermute | solution.py:527
  75.8 1.5 %collective-permute-start.19 = (bf16[4,32,1024]{2,1,0:T(8,128)(2,1)S(1)}, bf16[4,32,1024]{2,1,0:T(8,128)(2,1)S(1)}, u32[]{:S(2)}, u32[]{:S(2)}) collective-permute-start(bf16[4,32,1024]{2,1,0:T(8,128)(2,1)S(1)} %get-tuple-element.53), channel_id=1, source_target_pairs={{0,2},{1,3},{2,0},{3,1},{4,6},{5,7},{6,4},{7,5},{8,10},{9,11},{10,... | collective-permute-start | bytes 786440 | tf_op jit(solution)/shard_map/ppermute | solution.py:527
  77.3 4.0 %down.1 = (f32[128,1280]{1,0:T(8,128)S(1)}, bf16[128,1280]{1,0:T(8,128)(2,1)S(1)}, bf16[128,1280]{1,0:T(8,128)(2,1)S(1)}, bf16[128,1280]{1,0:T(8,128)(2,1)S(1)}) custom-call(bf16[288,128]{1,0:T(8,128)(2,1)S(1)} %get-tuple-element.44.refs_0_, bf16[288,128]{1,0:T(8,128)(2,1)S(1)} %collective-permute-done.11.refs_1_, ...), custom_call_target="tpu_custom_call" | custom-call | flops 30000001024 | bytes 6660096 | tf_op jit(solution)/shard_map/down/pallas_call | solution.py:218
  81.3 1.6 %collective-permute-start.16 = (bf16[128,1280]{1,0:T(8,128)(2,1)S(1)}, bf16[128,1280]{1,0:T(8,128)(2,1)S(1)}, u32[]{:S(2)}, u32[]{:S(2)}) collective-permute-start(bf16[128,1280]{1,0:T(8,128)(2,1)S(1)} %get-tuple-element.50.refs_2_), channel_id=1, source_target_pairs={{0,4},{4,0},{8,12},{12,8},{1,5},{5,1},{9,13},{13,9},{2,6},{6,2},{1... | collective-permute-start | bytes 983048 | tf_op jit(solution)/shard_map/ppermute | solution.py:530
  83.0 2.6 %collective-permute-start.17 = (bf16[128,1280]{1,0:T(8,128)(2,1)S(1)}, bf16[128,1280]{1,0:T(8,128)(2,1)S(1)}, u32[]{:S(2)}, u32[]{:S(2)}) collective-permute-start(bf16[128,1280]{1,0:T(8,128)(2,1)S(1)} %get-tuple-element.51), channel_id=1, source_target_pairs={{0,8},{4,12},{8,0},{12,4},{1,9},{5,13},{9,1},{13,5},{2,10},{6,14},... | collective-permute-start | bytes 983048 | tf_op jit(solution)/shard_map/ppermute | solution.py:530
  86.0 0.7 collective-permute-start.20
  86.7 3.5 %collective-permute-start.21 = (bf16[32,1024]{1,0:T(8,128)(2,1)S(1)}, bf16[32,1024]{1,0:T(8,128)(2,1)S(1)}, u32[]{:S(2)}, u32[]{:S(2)}) collective-permute-start(bf16[32,1024]{1,0:T(8,128)(2,1)S(1)} %get-tuple-element.56), channel_id=1, source_target_pairs={{0,8},{4,12},{8,0},{12,4},{1,9},{5,13},{9,1},{13,5},{2,10},{6,14},... | collective-permute-start | bytes 196616 | tf_op jit(solution)/shard_map/ppermute | solution.py:530
  90.2 16.4 %collective-permute-done.20.refs_8_ = bf16[32,1024]{1,0:T(8,128)(2,1)S(1)} collective-permute-done((bf16[32,1024]{1,0:T(8,128)(2,1)S(1)}, bf16[32,1024]{1,0:T(8,128)(2,1)S(1)}, u32[]{:S(2)}, u32[]{:S(2)}) %collective-permute-start.20) | collective-permute-done | bytes 65568 | tf_op jit(solution)/shard_map/ppermute | solution.py:530
  106.6 2.9 %collective-permute-start.22 = (bf16[32,1024]{1,0:T(8,128)(2,1)S(1)}, bf16[32,1024]{1,0:T(8,128)(2,1)S(1)}, u32[]{:S(2)}, u32[]{:S(2)}) collective-permute-start(bf16[32,1024]{1,0:T(8,128)(2,1)S(1)} %get-tuple-element.57), channel_id=1, source_target_pairs={{0,12},{4,8},{8,4},{12,0},{1,13},{5,9},{9,5},{13,1},{2,14},{6,10},... | collective-permute-start | bytes 196616 | tf_op jit(solution)/shard_map/ppermute | solution.py:530
  109.5 9.9 %collective-permute-done.21.refs_9_ = bf16[32,1024]{1,0:T(8,128)(2,1)S(1)} collective-permute-done((bf16[32,1024]{1,0:T(8,128)(2,1)S(1)}, bf16[32,1024]{1,0:T(8,128)(2,1)S(1)}, u32[]{:S(2)}, u32[]{:S(2)}) %collective-permute-start.21) | collective-permute-done | bytes 65568 | tf_op jit(solution)/shard_map/ppermute | solution.py:530
  119.5 4.5 %update.1 = (f32[1280,128]{1,0:T(8,128)}, f32[1280,128]{1,0:T(8,128)}, f32[1280,128]{1,0:T(8,128)}, f32[32,1024]{1,0:T(8,128)}, f32[32,1024]{1,0:T(8,128)}, /*index=5*/f32[32,1024]{1,0:T(8,128)}) custom-call(f32[128,1280]{1,0:T(8,128)S(1)} %get-tuple-element.49.refs_0_, bf16[128,1280]{1,0:T(8,128)(2,1)S(1)} %collective-permute-done.16.refs_1_, ...), custom_call_target="tpu_custom_call" | custom-call | flops 30000001024 | bytes 6684672 | tf_op jit(solution)/shard_map/update/pallas_call | solution.py:218
  (53 shorter events, 1.5 us)
Async XLA Ops:
  0.6 7.4 %copy-start.3 = (f32[1,1280,128]{2,1,0:T(8,128)S(1)}, f32[1,1280,128]{2,1,0:T(8,128)}, u32[]{:S(2)}) copy-start(f32[1,1280,128]{2,1,0:T(8,128)} %param.20) | copy-start | bytes 1966084
  0.6 7.4 %copy-start.6 = (f32[1,32,1024]{2,1,0:T(8,128)S(1)}, f32[1,32,1024]{2,1,0:T(8,128)}, u32[]{:S(2)}) copy-start(f32[1,32,1024]{2,1,0:T(8,128)} %param.21) | copy-start | bytes 393220
  0.7 7.4 %copy-start.11 = (s32[4]{0:T(128)S(1)}, s32[4]{0:T(128)}, u32[]{:S(2)}) copy-start(s32[4]{0:T(128)} %refs_0_.7) | copy-start | bytes 52
  0.7 7.3 %collective-permute-start = (f32[32,1024]{1,0:T(8,128)}, f32[32,1024]{1,0:T(8,128)S(1)}, u32[]{:S(2)}, u32[]{:S(2)}) collective-permute-start(f32[32,1024]{1,0:T(8,128)} %bitcast.20), channel_id=1, source_target_pairs={{0,2},{1,3},{2,0},{3,1},{4,6},{5,7},{6,4},{7,5},{8,10},{9,11},{10,... | collective-permute-start | bytes 393224 | tf_op jit(solution)/shard_map/ppermute | solution.py:527
  3.7 11.3 %collective-permute-start.2 = (bf16[1280,1024]{1,0:T(8,128)(2,1)}, bf16[1280,1024]{1,0:T(8,128)(2,1)S(1)}, u32[]{:S(2)}, u32[]{:S(2)}) collective-permute-start(bf16[1280,1024]{1,0:T(8,128)(2,1)} %refs_1_.7), channel_id=1, source_target_pairs={{0,1},{1,0},{2,3},{3,2},{4,5},{5,4},{6,7},{7,6},{8,9},{9,8},{10,11... | collective-permute-start | bytes 7864328 | tf_op jit(solution)/shard_map/ppermute | solution.py:524
  9.3 36.8 %copy-start.1 = (bf16[1280,1024]{1,0:T(8,128)(2,1)S(1)}, bf16[1280,1024]{1,0:T(8,128)(2,1)}, u32[]{:S(2)}) copy-start(bf16[1280,1024]{1,0:T(8,128)(2,1)} %refs_1_.7) | copy-start | bytes 7864324
  9.3 5.4 %collective-permute-start.1 = (bf16[1792,128]{1,0:T(8,128)(2,1)S(1)}, bf16[1792,128]{1,0:T(8,128)(2,1)S(1)}, u32[]{:S(2)}, u32[]{:S(2)}) collective-permute-start(bf16[1792,128]{1,0:T(8,128)(2,1)S(1)} %weights.1.refs_1_.refs_2_), channel_id=1, source_target_pairs={{0,1},{1,0},{2,3},{3,2},{4,5},{5,4},{6,7},{7,6},{8,9},{9,8},{10,11... | collective-permute-start | bytes 1376264 | tf_op jit(solution)/shard_map/ppermute | solution.py:524
  9.9 36.2 %collective-permute-start.4 = (bf16[2,304,1280]{2,1,0:T(8,128)(2,1)}, bf16[2,304,1280]{2,1,0:T(8,128)(2,1)S(1)}, u32[]{:S(2)}, u32[]{:S(2)}) collective-permute-start(bf16[2,304,1280]{2,1,0:T(8,128)(2,1)} %pack_sent.1.refs_4_), channel_id=1, source_target_pairs={{0,2},{1,3},{2,0},{3,1},{4,6},{5,7},{6,4},{7,5},{8,10},{9,11},{10,... | collective-permute-start | bytes 4669448 | tf_op jit(solution)/shard_map/ppermute | solution.py:527
  10.5 39.4 %collective-permute-start.3 = (bf16[1792,128]{1,0:T(8,128)(2,1)S(1)}, bf16[1792,128]{1,0:T(8,128)(2,1)S(1)}, u32[]{:S(2)}, u32[]{:S(2)}) collective-permute-start(bf16[1792,128]{1,0:T(8,128)(2,1)S(1)} %weights.1.refs_1_.refs_2_), channel_id=1, source_target_pairs={{0,4},{4,0},{8,12},{12,8},{1,5},{5,1},{9,13},{13,9},{2,6},{6,2},{1... | collective-permute-start | bytes 1376264 | tf_op jit(solution)/shard_map/ppermute | solution.py:530
  12.1 37.8 %collective-permute-start.5 = (bf16[1792,128]{1,0:T(8,128)(2,1)S(1)}, bf16[1792,128]{1,0:T(8,128)(2,1)S(1)}, u32[]{:S(2)}, u32[]{:S(2)}) collective-permute-start(bf16[1792,128]{1,0:T(8,128)(2,1)S(1)} %weights.1.refs_1_.refs_2_), channel_id=1, source_target_pairs={{0,8},{4,12},{8,0},{12,4},{1,9},{5,13},{9,1},{13,5},{2,10},{6,14},... | collective-permute-start | bytes 1376264 | tf_op jit(solution)/shard_map/ppermute | solution.py:530
  14.7 35.3 %collective-permute-start.6 = (bf16[1792,128]{1,0:T(8,128)(2,1)S(1)}, bf16[1792,128]{1,0:T(8,128)(2,1)S(1)}, u32[]{:S(2)}, u32[]{:S(2)}) collective-permute-start(bf16[1792,128]{1,0:T(8,128)(2,1)S(1)} %weights.1.refs_1_.refs_2_), channel_id=1, source_target_pairs={{0,12},{4,8},{8,4},{12,0},{1,13},{5,9},{9,5},{13,1},{2,14},{6,10},... | collective-permute-start | bytes 1376264 | tf_op jit(solution)/shard_map/ppermute | solution.py:530
  48.9 16.1 %collective-permute-start.9 = (bf16[288,1024]{1,0:T(8,128)(2,1)S(1)}, bf16[288,1024]{1,0:T(8,128)(2,1)S(1)}, u32[]{:S(2)}, u32[]{:S(2)}) collective-permute-start(bf16[288,1024]{1,0:T(8,128)(2,1)S(1)} %base_mate.1), channel_id=1, source_target_pairs={{0,2},{1,3},{2,0},{3,1},{4,6},{5,7},{6,4},{7,5},{8,10},{9,11},{10,... | collective-permute-start | bytes 1769480 | tf_op jit(solution)/shard_map/ppermute | solution.py:527
  50.1 3.3 %collective-permute-start.7 = (bf16[3,1792,128]{2,1,0:T(8,128)(2,1)S(1)}, bf16[3,1792,128]{2,1,0:T(8,128)(2,1)S(1)}, u32[]{:S(2)}, u32[]{:S(2)}) collective-permute-start(bf16[3,1792,128]{2,1,0:T(8,128)(2,1)S(1)} %pad_maximum_fusion.refs_4_.refs_2_.refs_3_), channel_id=1, source_target_pairs={{0,1},{1,0},{2,3},{3,2},{4,5},{5,4},{6,7},{7,6},{8,9},{9,8},{10,11... | collective-permute-start | bytes 4128776 | tf_op jit(solution)/shard_map/ppermute | solution.py:524
  50.2 14.8 %collective-permute-start.10 = (bf16[288,1408]{1,0:T(8,128)(2,1)S(1)}, bf16[288,1408]{1,0:T(8,128)(2,1)S(1)}, u32[]{:S(2)}, u32[]{:S(2)}) collective-permute-start(bf16[288,1408]{1,0:T(8,128)(2,1)S(1)} %get-tuple-element.35.refs_2_.refs_1_.refs_6_), channel_id=1, source_target_pairs={{0,1},{1,0},{2,3},{3,2},{4,5},{5,4},{6,7},{7,6},{8,9},{9,8},{10,11... | collective-permute-start | bytes 2433032 | tf_op jit(solution)/shard_map/ppermute | solution.py:524
  56.0 10.5 %copy-start.12 = (f32[128]{0:T(128)S(1)}, f32[128]{0:T(128)}, u32[]{:S(2)}) copy-start(f32[128]{0:T(128)} %param.19) | copy-start | bytes 1540
  56.0 10.5 %collective-permute-start.8 = (f32[288,128]{1,0:T(8,128)S(1)}, f32[288,128]{1,0:T(8,128)S(1)}, u32[]{:S(2)}, u32[]{:S(2)}) collective-permute-start(f32[288,128]{1,0:T(8,128)S(1)} %get-tuple-element.40.refs_6_), channel_id=1, source_target_pairs={{0,2},{1,3},{2,0},{3,1},{4,6},{5,7},{6,4},{7,5},{8,10},{9,11},{10,... | collective-permute-start | bytes 442376 | tf_op jit(solution)/shard_map/ppermute | solution.py:527
  70.7 4.8 %collective-permute-start.15 = (f32[2,4,32,1024]{3,2,1,0:T(8,128)S(1)}, f32[2,4,32,1024]{3,2,1,0:T(8,128)S(1)}, u32[]{:S(2)}, u32[]{:S(2)}) collective-permute-start(f32[2,4,32,1024]{3,2,1,0:T(8,128)S(1)} %get-tuple-element.47), channel_id=1, source_target_pairs={{0,1},{1,0},{2,3},{3,2},{4,5},{5,4},{6,7},{7,6},{8,9},{9,8},{10,11... | collective-permute-start | bytes 3145736 | tf_op jit(solution)/shard_map/ppermute | solution.py:524
  70.8 4.7 %collective-permute-start.11 = (bf16[288,128]{1,0:T(8,128)(2,1)S(1)}, bf16[288,128]{1,0:T(8,128)(2,1)S(1)}, u32[]{:S(2)}, u32[]{:S(2)}) collective-permute-start(bf16[288,128]{1,0:T(8,128)(2,1)S(1)} %get-tuple-element.44.refs_0_), channel_id=1, source_target_pairs={{0,2},{1,3},{2,0},{3,1},{4,6},{5,7},{6,4},{7,5},{8,10},{9,11},{10,... | collective-permute-start | bytes 221192 | tf_op jit(solution)/shard_map/ppermute | solution.py:527
  72.3 5.0 %collective-permute-start.14 = (bf16[288,1408]{1,0:T(8,128)(2,1)S(1)}, bf16[288,1408]{1,0:T(8,128)(2,1)S(1)}, u32[]{:S(2)}, u32[]{:S(2)}) collective-permute-start(bf16[288,1408]{1,0:T(8,128)(2,1)S(1)} %get-tuple-element.45), channel_id=1, source_target_pairs={{0,1},{1,0},{2,3},{3,2},{4,5},{5,4},{6,7},{7,6},{8,9},{9,8},{10,11... | collective-permute-start | bytes 2433032 | tf_op jit(solution)/shard_map/ppermute | solution.py:524
  72.5 4.8 %collective-permute-start.12 = (bf16[288,128]{1,0:T(8,128)(2,1)S(1)}, bf16[288,128]{1,0:T(8,128)(2,1)S(1)}, u32[]{:S(2)}, u32[]{:S(2)}) collective-permute-start(bf16[288,128]{1,0:T(8,128)(2,1)S(1)} %get-tuple-element.44.refs_0_), channel_id=1, source_target_pairs={{0,1},{1,0},{2,3},{3,2},{4,5},{5,4},{6,7},{7,6},{8,9},{9,8},{10,11... | collective-permute-start | bytes 221192 | tf_op jit(solution)/shard_map/ppermute | solution.py:524
  75.5 1.8 %collective-permute-start.13 = (bf16[288,128]{1,0:T(8,128)(2,1)S(1)}, bf16[288,128]{1,0:T(8,128)(2,1)S(1)}, u32[]{:S(2)}, u32[]{:S(2)}) collective-permute-start(bf16[288,128]{1,0:T(8,128)(2,1)S(1)} %collective-permute-done.11.refs_1_), channel_id=1, source_target_pairs={{0,1},{1,0},{2,3},{3,2},{4,5},{5,4},{6,7},{7,6},{8,9},{9,8},{10,11... | collective-permute-start | bytes 221192 | tf_op jit(solution)/shard_map/ppermute | solution.py:524
  75.8 10.1 %collective-permute-start.19 = (bf16[4,32,1024]{2,1,0:T(8,128)(2,1)S(1)}, bf16[4,32,1024]{2,1,0:T(8,128)(2,1)S(1)}, u32[]{:S(2)}, u32[]{:S(2)}) collective-permute-start(bf16[4,32,1024]{2,1,0:T(8,128)(2,1)S(1)} %get-tuple-element.53), channel_id=1, source_target_pairs={{0,2},{1,3},{2,0},{3,1},{4,6},{5,7},{6,4},{7,5},{8,10},{9,11},{10,... | collective-permute-start | bytes 786440 | tf_op jit(solution)/shard_map/ppermute | solution.py:527
  81.3 38.1 %collective-permute-start.16 = (bf16[128,1280]{1,0:T(8,128)(2,1)S(1)}, bf16[128,1280]{1,0:T(8,128)(2,1)S(1)}, u32[]{:S(2)}, u32[]{:S(2)}) collective-permute-start(bf16[128,1280]{1,0:T(8,128)(2,1)S(1)} %get-tuple-element.50.refs_2_), channel_id=1, source_target_pairs={{0,4},{4,0},{8,12},{12,8},{1,5},{5,1},{9,13},{13,9},{2,6},{6,2},{1... | collective-permute-start | bytes 983048 | tf_op jit(solution)/shard_map/ppermute | solution.py:530
  83.0 36.5 %collective-permute-start.17 = (bf16[128,1280]{1,0:T(8,128)(2,1)S(1)}, bf16[128,1280]{1,0:T(8,128)(2,1)S(1)}, u32[]{:S(2)}, u32[]{:S(2)}) collective-permute-start(bf16[128,1280]{1,0:T(8,128)(2,1)S(1)} %get-tuple-element.51), channel_id=1, source_target_pairs={{0,8},{4,12},{8,0},{12,4},{1,9},{5,13},{9,1},{13,5},{2,10},{6,14},... | collective-permute-start | bytes 983048 | tf_op jit(solution)/shard_map/ppermute | solution.py:530
  85.6 33.9 %copy-start.4 = (f32[1,1280,128]{2,1,0:T(8,128)S(1)}, f32[1,1280,128]{2,1,0:T(8,128)}, u32[]{:S(2)}) copy-start(f32[1,1280,128]{2,1,0:T(8,128)} %param.22) | copy-start | bytes 1966084
  85.6 33.9 %copy-start.5 = (f32[1,1280,128]{2,1,0:T(8,128)S(1)}, f32[1,1280,128]{2,1,0:T(8,128)}, u32[]{:S(2)}) copy-start(f32[1,1280,128]{2,1,0:T(8,128)} %param.24) | copy-start | bytes 1966084
  85.6 33.9 %copy-start.7 = (f32[1,32,1024]{2,1,0:T(8,128)S(1)}, f32[1,32,1024]{2,1,0:T(8,128)}, u32[]{:S(2)}) copy-start(f32[1,32,1024]{2,1,0:T(8,128)} %param.23) | copy-start | bytes 393220
  85.6 34.0 %copy-start.8 = (f32[1,32,1024]{2,1,0:T(8,128)S(1)}, f32[1,32,1024]{2,1,0:T(8,128)}, u32[]{:S(2)}) copy-start(f32[1,32,1024]{2,1,0:T(8,128)} %param.25) | copy-start | bytes 393220
  85.6 33.9 %collective-permute-start.18 = (bf16[128,1280]{1,0:T(8,128)(2,1)S(1)}, bf16[128,1280]{1,0:T(8,128)(2,1)S(1)}, u32[]{:S(2)}, u32[]{:S(2)}) collective-permute-start(bf16[128,1280]{1,0:T(8,128)(2,1)S(1)} %get-tuple-element.52), channel_id=1, source_target_pairs={{0,12},{4,8},{8,4},{12,0},{1,13},{5,9},{9,5},{13,1},{2,14},{6,10},... | collective-permute-start | bytes 983048 | tf_op jit(solution)/shard_map/ppermute | solution.py:530
  86.0 20.6 %collective-permute-start.20 = (bf16[32,1024]{1,0:T(8,128)(2,1)S(1)}, bf16[32,1024]{1,0:T(8,128)(2,1)S(1)}, u32[]{:S(2)}, u32[]{:S(2)}) collective-permute-start(bf16[32,1024]{1,0:T(8,128)(2,1)S(1)} %get-tuple-element.55), channel_id=1, source_target_pairs={{0,4},{4,0},{8,12},{12,8},{1,5},{5,1},{9,13},{13,9},{2,6},{6,2},{1... | collective-permute-start | bytes 196616 | tf_op jit(solution)/shard_map/ppermute | solution.py:530
  86.7 32.7 %collective-permute-start.21 = (bf16[32,1024]{1,0:T(8,128)(2,1)S(1)}, bf16[32,1024]{1,0:T(8,128)(2,1)S(1)}, u32[]{:S(2)}, u32[]{:S(2)}) collective-permute-start(bf16[32,1024]{1,0:T(8,128)(2,1)S(1)} %get-tuple-element.56), channel_id=1, source_target_pairs={{0,8},{4,12},{8,0},{12,4},{1,9},{5,13},{9,1},{13,5},{2,10},{6,14},... | collective-permute-start | bytes 196616 | tf_op jit(solution)/shard_map/ppermute | solution.py:530
  106.6 12.9 %collective-permute-start.22 = (bf16[32,1024]{1,0:T(8,128)(2,1)S(1)}, bf16[32,1024]{1,0:T(8,128)(2,1)S(1)}, u32[]{:S(2)}, u32[]{:S(2)}) collective-permute-start(bf16[32,1024]{1,0:T(8,128)(2,1)S(1)} %get-tuple-element.57), channel_id=1, source_target_pairs={{0,12},{4,8},{8,4},{12,0},{1,13},{5,9},{9,5},{13,1},{2,14},{6,10},... | collective-permute-start | bytes 196616 | tf_op jit(solution)/shard_map/ppermute | solution.py:530
  (4 other events, 27.5 us)

commit v4 on v3

--- a/solution.py
+++ b/solution.py
@@ -202,7 +202,7 @@
         return self.target
 
 
-def call(kernel, name, scalars, late, outs, plain=(), order=(), scratch=(), vmem=36, light=False):
+def call(kernel, name, scalars, late, outs, plain=(), order=(), scratch=(), vmem=36, light=False, out_spec=VMEM):
     n, m, p, d, o = len(scalars), len(late), len(plain), len(order), len(outs)
 
     def body(*refs):
@@ -219,7 +219,7 @@
         body,
         name=name,
         in_specs=[SMEM] * n + [HBM] * (m + p + d),
-        out_specs=tuple(VMEM for _ in outs),
+        out_specs=tuple(out_spec for _ in outs),
         out_shape=tuple(outs),
         scratch_shapes=[pltpu.VMEM(a.shape, a.dtype) for a in late]
         + [pltpu.SemaphoreType.DMA((max(m, 1),))]
@@ -335,9 +335,8 @@
     out[...] = (total + mm(rows.get()[1, :LIVE], mate.get()[...])).astype(bf16)
 
 
-def down_factors(own, others):
-    parts = [own.get()[:QUARTER]] + [others.get()[j, :QUARTER] for j in range(3)]
-    return jnp.concatenate(parts, axis=1)
+def down_factors(weights):
+    return jnp.concatenate([weights.get()[j, :QUARTER] for j in range(4)], axis=1)
 
 
 def mate_places(rows):
@@ -353,14 +352,14 @@
     return total
 
 
-def low_mate_kernel(rows, own, others, core_own, core_others, out, core_out):
+def low_mate_kernel(rows, weights, weights_core, out, core_out):
     held = rows.get()
     places = mate_places(held)
     core_out[:, :QUARTER] = held[1, :LIVE]
     core_out[:, QUARTER:] = places
-    every = mm(held[0, :LIVE], down_factors(own, others))
-    every = every + mm(held[1, :LIVE], down_factors(core_own, core_others))
-    out[...] = own_adapter(every, places)
+    every = mm(held[0, :LIVE], down_factors(weights))
+    every = every + mm(held[1, :LIVE], down_factors(weights_core))
+    out[...] = own_adapter(every, places).astype(bf16)
 
 
 def base_own_kernel(near, own, far, mate, out):
@@ -368,21 +367,20 @@
     out[...] = total + mm(far.get()[:, :QUARTER], mate.get()[...])
 
 
-def low_own_kernel(near, far, own, others, core_own, core_others, out, up):
+def low_own_kernel(near, far, weights, weights_core, out, up):
     f = lax.axis_index("fsdp")
     c, x = f % 2, f // 2
     held = far.get()
-    every = mm(near.get()[...], down_factors(own, others))
-    every = every + mm(held[:, :QUARTER], down_factors(core_own, core_others))
+    every = mm(near.get()[...], down_factors(weights))
+    every = every + mm(held[:, :QUARTER], down_factors(weights_core))
     out[...] = own_adapter(every, held[:, QUARTER:])
     for j in range(4):
         for part in range(2):
-            for first, rest, side in ((own, others, c), (core_own, core_others, 1 - c)):
-                source = rest.get().at[j - 1] if j else first.get()
+            for source, side in ((weights, c), (weights_core, 1 - c)):
                 target = pl.multiple_of(128 * j + 64 * (x ^ part) + 32 * side, 32)
                 for k in range(8):
                     at = QUARTER + 64 * k + 32 * part
-                    up[pl.ds(target, 32), 128 * k : 128 * k + 128] = source[at : at + 32, :]
+                    up[pl.ds(target, 32), 128 * k : 128 * k + 128] = source.get()[j, at : at + 32]
 
 
 def identity():
@@ -413,7 +411,7 @@
     scale = jnp.zeros((LIVE, HEAD), f32)
     for j in range(4):
         scale = jnp.where(adapter == j, scales[j], scale)
-    lowrank = (low.get()[...] + low_mate.get()[...]).astype(bf16).astype(f32)
+    lowrank = (low.get()[...] + low_mate.get()[...].astype(f32)).astype(bf16).astype(f32)
     wide = spread(lowrank, ids, range(4))
     added = mm(wide, up[...])
     parts = []
@@ -481,20 +479,34 @@
 
 def update_kernel(*refs):
     own, one, two, three, down, moment, variance = refs[:7]
-    outs = refs[14:]
-    for start in range(0, QUARTER, 128):
-        part = slice(start, start + 128)
+    outs, held, sems = refs[14:20], refs[20:26], refs[26]
+    step = 256
+    copies = []
+
+    def leave(n, rows):
+        copies.append(pltpu.make_async_copy(held[n].at[rows], outs[n].at[rows], sems.at[len(copies)]))
+        copies[-1].start()
+
+    for start in range(0, QUARTER, step):
+        rows = pl.ds(start, step)
+        part = slice(start, start + step)
         total = own.get()[:, part] + one.get()[:, part].astype(f32)
         total = total + (two.get()[:, part].astype(f32) + three.get()[:, part].astype(f32))
-        outs[0][part], outs[1][part], outs[2][part] = optimizer_update(
+        held[0][part], held[1][part], held[2][part] = optimizer_update(
             down.get()[part], total.T, moment.get()[part], variance.get()[part]
         )
+        for n in range(3):
+            leave(n, rows)
     own, one, two, three, up, moment, variance = refs[7:14]
     total = own.get()[...] + one.get()[...].astype(f32)
     total = total + (two.get()[...].astype(f32) + three.get()[...].astype(f32))
-    outs[3][...], outs[4][...], outs[5][...] = optimizer_update(
+    held[3][...], held[4][...], held[5][...] = optimizer_update(
         up.get()[...], total, moment.get()[...], variance.get()[...]
     )
+    for n in range(3, 6):
+        leave(n, pl.ds(0, 32))
+    for copy in copies:
+        copy.wait()
 
 
 def after(value, *others):
@@ -549,10 +561,9 @@
         [ranks],
         [adapter_down_factor[0], adapter_up_factor[0], up_mate],
         [shape((QUARTER + 512, PADDED_RANK), bf16)],
-        order=[sent],
+        order=[sent, frozen_core],
     )
     arrived = [along(message, j) for j in (1, 2, 3)]
-    message_core = core(message)
 
     near, far, grads = call(
         lambda *refs: pack_kept_kernel(slots, *refs),
@@ -565,7 +576,7 @@
             shape((LIVE, KEY_WIDTH), bf16),
         ],
         [tokens],
-        order=[message_core, frozen_core],
+        order=[message],
         scratch=[pltpu.VMEM((2, tokens.shape[0], QUARTER), bf16), pltpu.SemaphoreType.DMA((2,))],
     )
     far_core = core(far)
@@ -579,23 +590,22 @@
         order=[near],
     )
     base_mate = across(partial)
-    others = jnp.stack([after(w, partial) for w in arrived])
-    others_core = core(others)
+    weights = jnp.stack([message] + [after(w, partial) for w in arrived])
+    weights_core = core(weights)
     (base,) = call(
         base_own_kernel,
         "base_own",
         [],
         [near, frozen, far, frozen_core],
         [shape((LIVE, KEY_WIDTH), f32)],
-        order=[others],
-    )
-    weights = [message, others, message_core, others_core]
+        order=[weights],
+    )
     low_sent, cross = call(
         low_mate_kernel,
         "low_mate",
         [],
-        [rows, *weights],
-        [shape((LIVE, PADDED_RANK), f32), shape((LIVE, QUARTER + 128), bf16)],
+        [rows, weights, weights_core],
+        [shape((LIVE, PADDED_RANK), bf16), shape((LIVE, QUARTER + 128), bf16)],
         order=[base],
         light=True,
     )
@@ -604,7 +614,7 @@
         low_own_kernel,
         "low_own",
         [],
-        [near, far, *weights],
+        [near, far, weights, weights_core],
         [shape((LIVE, PADDED_RANK), f32), shape((512, KEY_WIDTH), bf16)],
         order=[low_sent],
         light=True,
@@ -626,13 +636,6 @@
     dlow_cross = core(dlow_mate)
     up_core_in = core(up_core)
 
-    up_total, up_sent = call(
-        up_core_kernel,
-        "up_core",
-        [],
-        [up_kept, up_core_in],
-        [shape((4, 32, KEY_WIDTH), f32), shape((4, 32, KEY_WIDTH), bf16)],
-    )
     own, one, two, three = call(
         down_kernel,
         "down",
@@ -640,7 +643,6 @@
         [dlow, dlow_mate, dlow_core, dlow_cross, rows],
         [shape((PADDED_RANK, QUARTER), t) for t in (f32, bf16, bf16, bf16)],
         [near, far, far_core, cross_core],
-        order=[up_total],
         scratch=[
             pltpu.VMEM((4 * LIVE, QUARTER), bf16),
             pltpu.VMEM((4 * LIVE, HEAD), bf16),
@@ -649,6 +651,14 @@
     )
     three_in, two_in, one_in = along(three, 3), along(two, 2), along(one, 1)
 
+    up_total, up_sent = call(
+        up_core_kernel,
+        "up_core",
+        [],
+        [up_kept, up_core_in],
+        [shape((4, 32, KEY_WIDTH), f32), shape((4, 32, KEY_WIDTH), bf16)],
+        order=[three],
+    )
     up_parts = call(
         up_across_kernel,
         "up_across",
@@ -657,7 +667,7 @@
         [shape((32, KEY_WIDTH), t) for t in (f32, bf16, bf16, bf16)],
         order=[one],
     )
-    up_in = [up_parts[0]] + [along(up_parts[j], j) for j in (1, 2, 3)]
+    up_in = [up_parts[0]] + [along(up_parts[j], j) for j in (3, 2, 1)]
 
     new_down, down_first, down_second, new_up, up_first, up_second = call(
         update_kernel,
@@ -666,6 +676,10 @@
         [own, one_in, two_in, three_in, adapter_down_factor[0], down_first_moment[0], down_second_moment[0]]
         + [*up_in, adapter_up_factor[0], up_first_moment[0], up_second_moment[0]],
         [shape(adapter_down_factor.shape[1:], f32)] * 3 + [shape(adapter_up_factor.shape[1:], f32)] * 3,
+        scratch=[pltpu.VMEM(adapter_down_factor.shape[1:], f32)] * 3
+        + [pltpu.VMEM(adapter_up_factor.shape[1:], f32)] * 3
+        + [pltpu.SemaphoreType.DMA((18,))],
+        out_spec=HBM,
     )
     return tuple(o[None] for o in (new_down, new_up, down_first, up_first, down_second, up_second))
 

time: 124 us -> 121 us (0.976)
  Pallas kernels: 32.4 us -> 30.5 us
  starting transfers between devices: 26.6 us -> 25 us
  waiting for transfers between devices: 63.8 us -> 62.4 us
  local copies, waits for them, and re-layouts: 0.07 us -> 1.45 us
    ppermute x9, waiting for transfers between devices: 26.3 us -> 23.3 us  [along(): return lax.ppermute(value, 'dp', [(i, i ^ distance) for i in range(4)])]
    ppermute x6, starting transfers between devices: 8.81 us -> 6.59 us  [across(): return lax.ppermute(value, 'fsdp', [(i, i ^ 2) for i in range(4)])]
    ppermute x8 -> x7, waiting for transfers between devices: 0.02 us -> 2.14 us  [core(): return lax.ppermute(value, 'fsdp', [(i, i ^ 1) for i in range(4)])]
    pallas_call x12, Pallas kernels: 32.4 us -> 30.5 us  [call(): pl.pallas_call(body, name=name, in_specs=[SMEM] * n + [HBM] * (m + p + d)...]
    unnamed x26 -> x28, local copies, waits for them, and re-layouts: 0.07 us -> 1.45 us
  transfers between devices with their start and end apart: 23 -> 22, of which waited for: 6 -> 10; matrix products, arithmetic and copies ran while one was open for 0% -> 0% of each run, Pallas kernels for 19% -> 22%
where the time goes in v4:
time: 121 us
  waiting for transfers between devices  62.4 us (52%)
  Pallas kernels  30.5 us (25%)
  starting transfers between devices  25 us (21%)
  local copies, waits for them, and re-layouts  1.45 us (1%)
    ppermute x6, waiting for transfers between devices, across(): return lax.ppermute(value, 'fsdp', [(i, i ^ 2) for i in range(4)])  37 us
    pallas_call x12, Pallas kernels, call(): pl.pallas_call(body, name=name, in_specs=[SMEM] * n + [HBM] * (m + p + d)...  30.5 us
    ppermute x9, waiting for transfers between devices, along(): return lax.ppermute(value, 'dp', [(i, i ^ distance) for i in range(4)])  23.3 us
    ppermute x9, starting transfers between devices, along(): return lax.ppermute(value, 'dp', [(i, i ^ distance) for i in range(4)])  16.8 us
    ppermute x6, starting transfers between devices, across(): return lax.ppermute(value, 'fsdp', [(i, i ^ 2) for i in range(4)])  6.59 us
  transfers between devices with their start and end apart: 22, of which 10 were waited for; matrix products, arithmetic and copies ran while one was open for 0% of the time, Pallas kernels for 22%

profile of v4, /device:TPU:0, one launch (start us, length us, event | category | flops | bytes accessed | tf_op | source)
XLA Modules:
  0.0 120.6 jit_solution(3333507827550925029)
XLA Ops:
  1.2 2.6 %collective-permute-start = (f32[32,1024]{1,0:T(8,128)}, f32[32,1024]{1,0:T(8,128)S(1)}, u32[]{:S(2)}, u32[]{:S(2)}) collective-permute-start(f32[32,1024]{1,0:T(8,128)} %bitcast.22), channel_id=1, source_target_pairs={{0,2},{1,3},{2,0},{3,1},{4,6},{5,7},{6,4},{7,5},{8,10},{9,11},{10,... | collective-permute-start | bytes 393224 | tf_op jit(solution)/shard_map/ppermute | solution.py:539
  3.7 4.3 %pack_sent.1.refs_4_ = bf16[2,304,1280]{2,1,0:T(8,128)(2,1)} custom-call(s32[1,12]{1,0:T(1,128)} %refs_0_.6, s32[1,12]{1,0:T(1,128)} %refs_1_.5, bf16[384,5120]{1,0:T(8,128)(2,1)} %refs_3_.1), custom_call_target="tpu_custom_call" | custom-call | flops 30000001024 | bytes 5488736 | tf_op jit(solution)/shard_map/pack_sent/pallas_call | solution.py:218
  8.3 1.4 %copy-done.2 = bf16[2,304,1280]{2,1,0:T(8,128)(2,1)S(1)} copy-done((bf16[2,304,1280]{2,1,0:T(8,128)(2,1)S(1)}, bf16[2,304,1280]{2,1,0:T(8,128)(2,1)}, u32[]{:S(2)}) %copy-start.2) | copy-done | bytes 1556504
  9.7 1.2 weights.1.refs_4_
  10.9 2.0 %collective-permute-start.2 = (bf16[1792,128]{1,0:T(8,128)(2,1)S(1)}, bf16[1792,128]{1,0:T(8,128)(2,1)S(1)}, u32[]{:S(2)}, u32[]{:S(2)}) collective-permute-start(bf16[1792,128]{1,0:T(8,128)(2,1)S(1)} %weights.1.refs_4_), channel_id=1, source_target_pairs={{0,4},{4,0},{8,12},{12,8},{1,5},{5,1},{9,13},{13,9},{2,6},{6,2},{1... | collective-permute-start | bytes 1376264 | tf_op jit(solution)/shard_map/ppermute | solution.py:542
  13.0 2.6 %collective-permute-start.4 = (bf16[1792,128]{1,0:T(8,128)(2,1)S(1)}, bf16[1792,128]{1,0:T(8,128)(2,1)S(1)}, u32[]{:S(2)}, u32[]{:S(2)}) collective-permute-start(bf16[1792,128]{1,0:T(8,128)(2,1)S(1)} %weights.1.refs_4_), channel_id=1, source_target_pairs={{0,8},{4,12},{8,0},{12,4},{1,9},{5,13},{9,1},{13,5},{2,10},{6,14},... | collective-permute-start | bytes 1376264 | tf_op jit(solution)/shard_map/ppermute | solution.py:542
  15.6 3.1 %pack_kept.1 = (bf16[288,1280]{1,0:T(8,128)(2,1)S(1)}, bf16[288,1408]{1,0:T(8,128)(2,1)S(1)}, bf16[288,1024]{1,0:T(8,128)(2,1)S(1)}) custom-call(s32[1,12]{1,0:T(1,128)S(1)} %copy-done.10, s32[1,12]{1,0:T(1,128)S(1)} %copy-done.11, bf16[384,1024]{1,0:T(8,128)(2,1)S(1)} %copy-done.3, bf16[384,5120]{1,0:T(8,128)(2,1)S(1)} %copy-done, ...), custom_call_target="tpu_custom_call" | custom-call | flops 30000001024 | bytes 6856800 | tf_op jit(solution)/shard_map/pack_kept/pallas_call | solution.py:218
  18.7 25.8 %collective-permute-done.3.refs_0_.refs_4_ = bf16[2,304,1280]{2,1,0:T(8,128)(2,1)S(1)} collective-permute-done((bf16[2,304,1280]{2,1,0:T(8,128)(2,1)}, bf16[2,304,1280]{2,1,0:T(8,128)(2,1)S(1)}, u32[]{:S(2)}, u32[]{:S(2)}) %collective-permute-start.3) | collective-permute-done | bytes 1556512 | tf_op jit(solution)/shard_map/ppermute | solution.py:539
  44.5 2.7 %base_mate.1 = bf16[288,1024]{1,0:T(8,128)(2,1)S(1)} custom-call(bf16[2,304,1280]{2,1,0:T(8,128)(2,1)S(1)} %collective-permute-done.3.refs_0_.refs_4_, bf16[1280,1024]{1,0:T(8,128)(2,1)S(1)} %copy-done.1, bf16[1280,1024]{1,0:T(8,128)(2,1)S(1)} %collective-permute-done.1.refs_5_.refs_2_.refs_3_, bf16[288,1280]{1,0:T(8,128)(2,1)S(1)} %get-tuple-element.36.refs_3_.refs_0_.refs_5_), custom_call_target="tpu_custom_call" | custom-call | flops 30000001024 | bytes 7389184 | tf_op jit(solution)/shard_map/base_mate/pallas_call | solution.py:218
  48.5 2.7 %base_own.1.refs_3_.refs_5_ = f32[288,1024]{1,0:T(8,128)S(1)} custom-call(bf16[288,1280]{1,0:T(8,128)(2,1)S(1)} %get-tuple-element.36.refs_3_.refs_0_.refs_5_, bf16[1280,1024]{1,0:T(8,128)(2,1)S(1)} %copy-done.1, bf16[288,1408]{1,0:T(8,128)(2,1)S(1)} %get-tuple-element.35.refs_2_.refs_1_.refs_6_, ...), custom_call_target="tpu_custom_call" | custom-call | flops 30000001024 | bytes 7970816 | tf_op jit(solution)/shard_map/base_own/pallas_call | solution.py:218
  51.3 1.4 %collective-permute-done.6.refs_2_.refs_3_ = bf16[4,1792,128]{2,1,0:T(8,128)(2,1)S(1)} collective-permute-done((bf16[4,1792,128]{2,1,0:T(8,128)(2,1)S(1)}, bf16[4,1792,128]{2,1,0:T(8,128)(2,1)S(1)}, u32[]{:S(2)}, u32[]{:S(2)}) %collective-permute-start.6) | collective-permute-done | bytes 1835040 | tf_op jit(solution)/shard_map/ppermute | solution.py:536
  52.6 1.8 %low_mate.1 = (bf16[288,128]{1,0:T(8,128)(2,1)S(1)}, bf16[288,1408]{1,0:T(8,128)(2,1)S(1)}) custom-call(bf16[2,304,1280]{2,1,0:T(8,128)(2,1)S(1)} %collective-permute-done.3.refs_0_.refs_4_, bf16[4,1792,128]{2,1,0:T(8,128)(2,1)S(1)} %pad_maximum_fusion.refs_4_.refs_1_.refs_2_, bf16[4,1792,128]{2,1,0:T(8,128)(2,1)S(1)} %collective-permute-done.6.refs_2_.refs_3_, ...), custom_call_target="tpu_custom_call" | custom-call | flops 1 | bytes 1 | tf_op jit(solution)/shard_map/low_mate/pallas_call | solution.py:218
  54.5 1.7 %collective-permute-start.7 = (bf16[288,128]{1,0:T(8,128)(2,1)S(1)}, bf16[288,128]{1,0:T(8,128)(2,1)S(1)}, u32[]{:S(2)}, u32[]{:S(2)}) collective-permute-start(bf16[288,128]{1,0:T(8,128)(2,1)S(1)} %get-tuple-element.40.refs_4_), channel_id=1, source_target_pairs={{0,2},{1,3},{2,0},{3,1},{4,6},{5,7},{6,4},{7,5},{8,10},{9,11},{10,... | collective-permute-start | bytes 221192 | tf_op jit(solution)/shard_map/ppermute | solution.py:539
  56.2 2.0 %low_own.1 = (f32[288,128]{1,0:T(8,128)S(1)}, bf16[512,1024]{1,0:T(8,128)(2,1)S(1)}) custom-call(bf16[288,1280]{1,0:T(8,128)(2,1)S(1)} %get-tuple-element.36.refs_3_.refs_0_.refs_5_, bf16[288,1408]{1,0:T(8,128)(2,1)S(1)} %get-tuple-element.35.refs_2_.refs_1_.refs_6_, bf16[4,1792,128]{2,1,0:T(8,128)(2,1)S(1)} %pad_maximum_fusion.refs_4_.refs_1_.refs_2_, ...), custom_call_target="tpu_custom_call" | custom-call | flops 1 | bytes 1 | tf_op jit(solution)/shard_map/low_own/pallas_call | solution.py:218
  58.1 4.5 %collective-permute-done.8.refs_6_ = bf16[288,1024]{1,0:T(8,128)(2,1)S(1)} collective-permute-done((bf16[288,1024]{1,0:T(8,128)(2,1)S(1)}, bf16[288,1024]{1,0:T(8,128)(2,1)S(1)}, u32[]{:S(2)}, u32[]{:S(2)}) %collective-permute-start.8) | collective-permute-done | bytes 589856 | tf_op jit(solution)/shard_map/ppermute | solution.py:539
  62.6 0.8 collective-permute-done.7.refs_3_
  63.4 4.1 %keys.1 = (bf16[288,128]{1,0:T(8,128)(2,1)S(1)}, f32[2,4,32,1024]{3,2,1,0:T(8,128)S(1)}, f32[2,4,32,1024]{3,2,1,0:T(8,128)S(1)}) custom-call(s32[4]{0:T(128)S(1)} %copy-done.12, bf16[288,1408]{1,0:T(8,128)(2,1)S(1)} %get-tuple-element.35.refs_2_.refs_1_.refs_6_, f32[288,128]{1,0:T(8,128)S(1)} %get-tuple-element.41.refs_2_, ...), custom_call_target="tpu_custom_call" | custom-call | flops 30000001024 | bytes 6611472 | tf_op jit(solution)/shard_map/keys/pallas_call | solution.py:218
  67.5 0.8 collective-permute-start.10
  68.3 3.6 %collective-permute-done.10.refs_1_ = bf16[288,128]{1,0:T(8,128)(2,1)S(1)} collective-permute-done((bf16[288,128]{1,0:T(8,128)(2,1)S(1)}, bf16[288,128]{1,0:T(8,128)(2,1)S(1)}, u32[]{:S(2)}, u32[]{:S(2)}) %collective-permute-start.10) | collective-permute-done | bytes 73760 | tf_op jit(solution)/shard_map/ppermute | solution.py:539
  72.4 0.8 collective-permute-done.12.refs_3_
  73.2 4.0 %down.1 = (f32[128,1280]{1,0:T(8,128)S(1)}, bf16[128,1280]{1,0:T(8,128)(2,1)S(1)}, bf16[128,1280]{1,0:T(8,128)(2,1)S(1)}, bf16[128,1280]{1,0:T(8,128)(2,1)S(1)}) custom-call(bf16[288,128]{1,0:T(8,128)(2,1)S(1)} %get-tuple-element.44.refs_0_, bf16[288,128]{1,0:T(8,128)(2,1)S(1)} %collective-permute-done.10.refs_1_, ...), custom_call_target="tpu_custom_call" | custom-call | flops 30000001024 | bytes 6660096 | tf_op jit(solution)/shard_map/down/pallas_call | solution.py:218
  77.5 0.8 collective-permute-start.18
  78.3 3.4 %collective-permute-start.16 = (bf16[128,1280]{1,0:T(8,128)(2,1)S(1)}, bf16[128,1280]{1,0:T(8,128)(2,1)S(1)}, u32[]{:S(2)}, u32[]{:S(2)}) collective-permute-start(bf16[128,1280]{1,0:T(8,128)(2,1)S(1)} %get-tuple-element.49.refs_2_), channel_id=1, source_target_pairs={{0,12},{4,8},{8,4},{12,0},{1,13},{5,9},{9,5},{13,1},{2,14},{6,10},... | collective-permute-start | bytes 983048 | tf_op jit(solution)/shard_map/ppermute | solution.py:542
  81.7 1.9 %collective-permute-start.14 = (bf16[128,1280]{1,0:T(8,128)(2,1)S(1)}, bf16[128,1280]{1,0:T(8,128)(2,1)S(1)}, u32[]{:S(2)}, u32[]{:S(2)}) collective-permute-start(bf16[128,1280]{1,0:T(8,128)(2,1)S(1)} %get-tuple-element.47.refs_2_), channel_id=1, source_target_pairs={{0,4},{4,0},{8,12},{12,8},{1,5},{5,1},{9,13},{13,9},{2,6},{6,2},{1... | collective-permute-start | bytes 983048 | tf_op jit(solution)/shard_map/ppermute | solution.py:542
  83.6 2.4 %collective-permute-done.18.refs_1_ = bf16[4,32,1024]{2,1,0:T(8,128)(2,1)S(1)} collective-permute-done((bf16[4,32,1024]{2,1,0:T(8,128)(2,1)S(1)}, bf16[4,32,1024]{2,1,0:T(8,128)(2,1)S(1)}, u32[]{:S(2)}, u32[]{:S(2)}) %collective-permute-start.18) | collective-permute-done | bytes 262176 | tf_op jit(solution)/shard_map/ppermute | solution.py:539
  86.0 3.7 %collective-permute-start.19 = (bf16[32,1024]{1,0:T(8,128)(2,1)S(1)}, bf16[32,1024]{1,0:T(8,128)(2,1)S(1)}, u32[]{:S(2)}, u32[]{:S(2)}) collective-permute-start(bf16[32,1024]{1,0:T(8,128)(2,1)S(1)} %get-tuple-element.55), channel_id=1, source_target_pairs={{0,12},{4,8},{8,4},{12,0},{1,13},{5,9},{9,5},{13,1},{2,14},{6,10},... | collective-permute-start | bytes 196616 | tf_op jit(solution)/shard_map/ppermute | solution.py:542
  89.7 0.8 collective-permute-start.20
  90.5 6.3 %collective-permute-done.14.refs_1_ = bf16[128,1280]{1,0:T(8,128)(2,1)S(1)} collective-permute-done((bf16[128,1280]{1,0:T(8,128)(2,1)S(1)}, bf16[128,1280]{1,0:T(8,128)(2,1)S(1)}, u32[]{:S(2)}, u32[]{:S(2)}) %collective-permute-start.14) | collective-permute-done | bytes 327712 | tf_op jit(solution)/shard_map/ppermute | solution.py:542
  96.9 2.5 %collective-permute-start.21 = (bf16[32,1024]{1,0:T(8,128)(2,1)S(1)}, bf16[32,1024]{1,0:T(8,128)(2,1)S(1)}, u32[]{:S(2)}, u32[]{:S(2)}) collective-permute-start(bf16[32,1024]{1,0:T(8,128)(2,1)S(1)} %get-tuple-element.57), channel_id=1, source_target_pairs={{0,4},{4,0},{8,12},{12,8},{1,5},{5,1},{9,13},{13,9},{2,6},{6,2},{1... | collective-permute-start | bytes 196616 | tf_op jit(solution)/shard_map/ppermute | solution.py:542
  99.3 14.2 %collective-permute-done.15.refs_2_ = bf16[128,1280]{1,0:T(8,128)(2,1)S(1)} collective-permute-done((bf16[128,1280]{1,0:T(8,128)(2,1)S(1)}, bf16[128,1280]{1,0:T(8,128)(2,1)S(1)}, u32[]{:S(2)}, u32[]{:S(2)}) %collective-permute-start.15) | collective-permute-done | bytes 327712 | tf_op jit(solution)/shard_map/ppermute | solution.py:542
  113.5 2.7 %collective-permute-done.20.refs_9_ = bf16[32,1024]{1,0:T(8,128)(2,1)S(1)} collective-permute-done((bf16[32,1024]{1,0:T(8,128)(2,1)S(1)}, bf16[32,1024]{1,0:T(8,128)(2,1)S(1)}, u32[]{:S(2)}, u32[]{:S(2)}) %collective-permute-start.20) | collective-permute-done | bytes 65568 | tf_op jit(solution)/shard_map/ppermute | solution.py:542
  116.3 4.2 %update.1 = (f32[1280,128]{1,0:T(8,128)}, f32[1280,128]{1,0:T(8,128)}, f32[1280,128]{1,0:T(8,128)}, f32[32,1024]{1,0:T(8,128)}, f32[32,1024]{1,0:T(8,128)}, /*index=5*/f32[32,1024]{1,0:T(8,128)}) custom-call(f32[128,1280]{1,0:T(8,128)S(1)} %get-tuple-element.46.refs_0_, bf16[128,1280]{1,0:T(8,128)(2,1)S(1)} %collective-permute-done.14.refs_1_, ...), custom_call_target="tpu_custom_call" | custom-call | flops 30000001024 | bytes 6684672 | tf_op jit(solution)/shard_map/update/pallas_call | solution.py:218
  (53 shorter events, 3.0 us)
Async XLA Ops:
  0.6 7.7 %collective-permute-start.1 = (bf16[1280,1024]{1,0:T(8,128)(2,1)}, bf16[1280,1024]{1,0:T(8,128)(2,1)S(1)}, u32[]{:S(2)}, u32[]{:S(2)}) collective-permute-start(bf16[1280,1024]{1,0:T(8,128)(2,1)} %refs_1_.7), channel_id=1, source_target_pairs={{0,1},{1,0},{2,3},{3,2},{4,5},{5,4},{6,7},{7,6},{8,9},{9,8},{10,11... | collective-permute-start | bytes 7864328 | tf_op jit(solution)/shard_map/ppermute | solution.py:536
  1.2 7.2 %copy-start.4 = (f32[1,1280,128]{2,1,0:T(8,128)S(1)}, f32[1,1280,128]{2,1,0:T(8,128)}, u32[]{:S(2)}) copy-start(f32[1,1280,128]{2,1,0:T(8,128)} %param.20) | copy-start | bytes 1966084
  1.2 7.2 %copy-start.7 = (f32[1,32,1024]{2,1,0:T(8,128)S(1)}, f32[1,32,1024]{2,1,0:T(8,128)}, u32[]{:S(2)}) copy-start(f32[1,32,1024]{2,1,0:T(8,128)} %param.21) | copy-start | bytes 393220
  1.2 7.2 %copy-start.12 = (s32[4]{0:T(128)S(1)}, s32[4]{0:T(128)}, u32[]{:S(2)}) copy-start(s32[4]{0:T(128)} %refs_0_.7) | copy-start | bytes 52
  1.2 7.1 %collective-permute-start = (f32[32,1024]{1,0:T(8,128)}, f32[32,1024]{1,0:T(8,128)S(1)}, u32[]{:S(2)}, u32[]{:S(2)}) collective-permute-start(f32[32,1024]{1,0:T(8,128)} %bitcast.22), channel_id=1, source_target_pairs={{0,2},{1,3},{2,0},{3,1},{4,6},{5,7},{6,4},{7,5},{8,10},{9,11},{10,... | collective-permute-start | bytes 393224 | tf_op jit(solution)/shard_map/ppermute | solution.py:539
  8.1 36.4 %collective-permute-start.3 = (bf16[2,304,1280]{2,1,0:T(8,128)(2,1)}, bf16[2,304,1280]{2,1,0:T(8,128)(2,1)S(1)}, u32[]{:S(2)}, u32[]{:S(2)}) collective-permute-start(bf16[2,304,1280]{2,1,0:T(8,128)(2,1)} %pack_sent.1.refs_4_), channel_id=1, source_target_pairs={{0,2},{1,3},{2,0},{3,1},{4,6},{5,7},{6,4},{7,5},{8,10},{9,11},{10,... | collective-permute-start | bytes 4669448 | tf_op jit(solution)/shard_map/ppermute | solution.py:539
  9.7 5.8 %copy-start.11 = (s32[1,12]{1,0:T(1,128)S(1)}, s32[1,12]{1,0:T(1,128)}, u32[]{:S(2)}) copy-start(s32[1,12]{1,0:T(1,128)} %refs_1_.5) | copy-start | bytes 148
  10.9 33.5 %copy-start.1 = (bf16[1280,1024]{1,0:T(8,128)(2,1)S(1)}, bf16[1280,1024]{1,0:T(8,128)(2,1)}, u32[]{:S(2)}) copy-start(bf16[1280,1024]{1,0:T(8,128)(2,1)} %refs_1_.7) | copy-start | bytes 7864324
  10.9 36.8 %collective-permute-start.2 = (bf16[1792,128]{1,0:T(8,128)(2,1)S(1)}, bf16[1792,128]{1,0:T(8,128)(2,1)S(1)}, u32[]{:S(2)}, u32[]{:S(2)}) collective-permute-start(bf16[1792,128]{1,0:T(8,128)(2,1)S(1)} %weights.1.refs_4_), channel_id=1, source_target_pairs={{0,4},{4,0},{8,12},{12,8},{1,5},{5,1},{9,13},{13,9},{2,6},{6,2},{1... | collective-permute-start | bytes 1376264 | tf_op jit(solution)/shard_map/ppermute | solution.py:542
  13.0 34.7 %collective-permute-start.4 = (bf16[1792,128]{1,0:T(8,128)(2,1)S(1)}, bf16[1792,128]{1,0:T(8,128)(2,1)S(1)}, u32[]{:S(2)}, u32[]{:S(2)}) collective-permute-start(bf16[1792,128]{1,0:T(8,128)(2,1)S(1)} %weights.1.refs_4_), channel_id=1, source_target_pairs={{0,8},{4,12},{8,0},{12,4},{1,9},{5,13},{9,1},{13,5},{2,10},{6,14},... | collective-permute-start | bytes 1376264 | tf_op jit(solution)/shard_map/ppermute | solution.py:542
  15.6 32.1 %collective-permute-start.5 = (bf16[1792,128]{1,0:T(8,128)(2,1)S(1)}, bf16[1792,128]{1,0:T(8,128)(2,1)S(1)}, u32[]{:S(2)}, u32[]{:S(2)}) collective-permute-start(bf16[1792,128]{1,0:T(8,128)(2,1)S(1)} %weights.1.refs_4_), channel_id=1, source_target_pairs={{0,12},{4,8},{8,4},{12,0},{1,13},{5,9},{9,5},{13,1},{2,14},{6,10},... | collective-permute-start | bytes 1376264 | tf_op jit(solution)/shard_map/ppermute | solution.py:542
  47.2 15.4 %collective-permute-start.8 = (bf16[288,1024]{1,0:T(8,128)(2,1)S(1)}, bf16[288,1024]{1,0:T(8,128)(2,1)S(1)}, u32[]{:S(2)}, u32[]{:S(2)}) collective-permute-start(bf16[288,1024]{1,0:T(8,128)(2,1)S(1)} %base_mate.1), channel_id=1, source_target_pairs={{0,2},{1,3},{2,0},{3,1},{4,6},{5,7},{6,4},{7,5},{8,10},{9,11},{10,... | collective-permute-start | bytes 1769480 | tf_op jit(solution)/shard_map/ppermute | solution.py:539
  47.7 14.9 %collective-permute-start.9 = (bf16[288,1408]{1,0:T(8,128)(2,1)S(1)}, bf16[288,1408]{1,0:T(8,128)(2,1)S(1)}, u32[]{:S(2)}, u32[]{:S(2)}) collective-permute-start(bf16[288,1408]{1,0:T(8,128)(2,1)S(1)} %get-tuple-element.35.refs_2_.refs_1_.refs_6_), channel_id=1, source_target_pairs={{0,1},{1,0},{2,3},{3,2},{4,5},{5,4},{6,7},{7,6},{8,9},{9,8},{10,11... | collective-permute-start | bytes 2433032 | tf_op jit(solution)/shard_map/ppermute | solution.py:536
  48.0 4.7 %collective-permute-start.6 = (bf16[4,1792,128]{2,1,0:T(8,128)(2,1)S(1)}, bf16[4,1792,128]{2,1,0:T(8,128)(2,1)S(1)}, u32[]{:S(2)}, u32[]{:S(2)}) collective-permute-start(bf16[4,1792,128]{2,1,0:T(8,128)(2,1)S(1)} %pad_maximum_fusion.refs_4_.refs_1_.refs_2_), channel_id=1, source_target_pairs={{0,1},{1,0},{2,3},{3,2},{4,5},{5,4},{6,7},{7,6},{8,9},{9,8},{10,11... | collective-permute-start | bytes 5505032 | tf_op jit(solution)/shard_map/ppermute | solution.py:536
  54.5 8.9 %collective-permute-start.7 = (bf16[288,128]{1,0:T(8,128)(2,1)S(1)}, bf16[288,128]{1,0:T(8,128)(2,1)S(1)}, u32[]{:S(2)}, u32[]{:S(2)}) collective-permute-start(bf16[288,128]{1,0:T(8,128)(2,1)S(1)} %get-tuple-element.40.refs_4_), channel_id=1, source_target_pairs={{0,2},{1,3},{2,0},{3,1},{4,6},{5,7},{6,4},{7,5},{8,10},{9,11},{10,... | collective-permute-start | bytes 221192 | tf_op jit(solution)/shard_map/ppermute | solution.py:539
  56.2 7.2 %copy-start.13 = (f32[128]{0:T(128)S(1)}, f32[128]{0:T(128)}, u32[]{:S(2)}) copy-start(f32[128]{0:T(128)} %param.19) | copy-start | bytes 1540
  56.2 17.0 %collective-permute-start.13 = (bf16[288,1408]{1,0:T(8,128)(2,1)S(1)}, bf16[288,1408]{1,0:T(8,128)(2,1)S(1)}, u32[]{:S(2)}, u32[]{:S(2)}) collective-permute-start(bf16[288,1408]{1,0:T(8,128)(2,1)S(1)} %get-tuple-element.45), channel_id=1, source_target_pairs={{0,1},{1,0},{2,3},{3,2},{4,5},{5,4},{6,7},{7,6},{8,9},{9,8},{10,11... | collective-permute-start | bytes 2433032 | tf_op jit(solution)/shard_map/ppermute | solution.py:536
  67.5 4.4 %collective-permute-start.10 = (bf16[288,128]{1,0:T(8,128)(2,1)S(1)}, bf16[288,128]{1,0:T(8,128)(2,1)S(1)}, u32[]{:S(2)}, u32[]{:S(2)}) collective-permute-start(bf16[288,128]{1,0:T(8,128)(2,1)S(1)} %get-tuple-element.44.refs_0_), channel_id=1, source_target_pairs={{0,2},{1,3},{2,0},{3,1},{4,6},{5,7},{6,4},{7,5},{8,10},{9,11},{10,... | collective-permute-start | bytes 221192 | tf_op jit(solution)/shard_map/ppermute | solution.py:539
  68.3 4.1 %collective-permute-start.11 = (bf16[288,128]{1,0:T(8,128)(2,1)S(1)}, bf16[288,128]{1,0:T(8,128)(2,1)S(1)}, u32[]{:S(2)}, u32[]{:S(2)}) collective-permute-start(bf16[288,128]{1,0:T(8,128)(2,1)S(1)} %get-tuple-element.44.refs_0_), channel_id=1, source_target_pairs={{0,1},{1,0},{2,3},{3,2},{4,5},{5,4},{6,7},{7,6},{8,9},{9,8},{10,11... | collective-permute-start | bytes 221192 | tf_op jit(solution)/shard_map/ppermute | solution.py:536
  71.9 1.3 %collective-permute-start.12 = (bf16[288,128]{1,0:T(8,128)(2,1)S(1)}, bf16[288,128]{1,0:T(8,128)(2,1)S(1)}, u32[]{:S(2)}, u32[]{:S(2)}) collective-permute-start(bf16[288,128]{1,0:T(8,128)(2,1)S(1)} %collective-permute-done.10.refs_1_), channel_id=1, source_target_pairs={{0,1},{1,0},{2,3},{3,2},{4,5},{5,4},{6,7},{7,6},{8,9},{9,8},{10,11... | collective-permute-start | bytes 221192 | tf_op jit(solution)/shard_map/ppermute | solution.py:536
  71.9 5.3 %collective-permute-start.17 = (f32[2,4,32,1024]{3,2,1,0:T(8,128)S(1)}, f32[2,4,32,1024]{3,2,1,0:T(8,128)S(1)}, u32[]{:S(2)}, u32[]{:S(2)}) collective-permute-start(f32[2,4,32,1024]{3,2,1,0:T(8,128)S(1)} %get-tuple-element.51), channel_id=1, source_target_pairs={{0,1},{1,0},{2,3},{3,2},{4,5},{5,4},{6,7},{7,6},{8,9},{9,8},{10,11... | collective-permute-start | bytes 3145736 | tf_op jit(solution)/shard_map/ppermute | solution.py:536
  77.5 8.4 %collective-permute-start.18 = (bf16[4,32,1024]{2,1,0:T(8,128)(2,1)S(1)}, bf16[4,32,1024]{2,1,0:T(8,128)(2,1)S(1)}, u32[]{:S(2)}, u32[]{:S(2)}) collective-permute-start(bf16[4,32,1024]{2,1,0:T(8,128)(2,1)S(1)} %get-tuple-element.53), channel_id=1, source_target_pairs={{0,2},{1,3},{2,0},{3,1},{4,6},{5,7},{6,4},{7,5},{8,10},{9,11},{10,... | collective-permute-start | bytes 786440 | tf_op jit(solution)/shard_map/ppermute | solution.py:539
  78.3 35.3 %collective-permute-start.16 = (bf16[128,1280]{1,0:T(8,128)(2,1)S(1)}, bf16[128,1280]{1,0:T(8,128)(2,1)S(1)}, u32[]{:S(2)}, u32[]{:S(2)}) collective-permute-start(bf16[128,1280]{1,0:T(8,128)(2,1)S(1)} %get-tuple-element.49.refs_2_), channel_id=1, source_target_pairs={{0,12},{4,8},{8,4},{12,0},{1,13},{5,9},{9,5},{13,1},{2,14},{6,10},... | collective-permute-start | bytes 983048 | tf_op jit(solution)/shard_map/ppermute | solution.py:542
  81.7 15.2 %collective-permute-start.14 = (bf16[128,1280]{1,0:T(8,128)(2,1)S(1)}, bf16[128,1280]{1,0:T(8,128)(2,1)S(1)}, u32[]{:S(2)}, u32[]{:S(2)}) collective-permute-start(bf16[128,1280]{1,0:T(8,128)(2,1)S(1)} %get-tuple-element.47.refs_2_), channel_id=1, source_target_pairs={{0,4},{4,0},{8,12},{12,8},{1,5},{5,1},{9,13},{13,9},{2,6},{6,2},{1... | collective-permute-start | bytes 983048 | tf_op jit(solution)/shard_map/ppermute | solution.py:542
  83.5 30.0 %collective-permute-start.15 = (bf16[128,1280]{1,0:T(8,128)(2,1)S(1)}, bf16[128,1280]{1,0:T(8,128)(2,1)S(1)}, u32[]{:S(2)}, u32[]{:S(2)}) collective-permute-start(bf16[128,1280]{1,0:T(8,128)(2,1)S(1)} %get-tuple-element.48), channel_id=1, source_target_pairs={{0,8},{4,12},{8,0},{12,4},{1,9},{5,13},{9,1},{13,5},{2,10},{6,14},... | collective-permute-start | bytes 983048 | tf_op jit(solution)/shard_map/ppermute | solution.py:542
  85.9 30.4 %copy-start.5 = (f32[1,1280,128]{2,1,0:T(8,128)S(1)}, f32[1,1280,128]{2,1,0:T(8,128)}, u32[]{:S(2)}) copy-start(f32[1,1280,128]{2,1,0:T(8,128)} %param.22) | copy-start | bytes 1966084
  85.9 30.4 %copy-start.6 = (f32[1,1280,128]{2,1,0:T(8,128)S(1)}, f32[1,1280,128]{2,1,0:T(8,128)}, u32[]{:S(2)}) copy-start(f32[1,1280,128]{2,1,0:T(8,128)} %param.24) | copy-start | bytes 1966084
  85.9 30.4 %copy-start.8 = (f32[1,32,1024]{2,1,0:T(8,128)S(1)}, f32[1,32,1024]{2,1,0:T(8,128)}, u32[]{:S(2)}) copy-start(f32[1,32,1024]{2,1,0:T(8,128)} %param.23) | copy-start | bytes 393220
  85.9 30.4 %copy-start.9 = (f32[1,32,1024]{2,1,0:T(8,128)S(1)}, f32[1,32,1024]{2,1,0:T(8,128)}, u32[]{:S(2)}) copy-start(f32[1,32,1024]{2,1,0:T(8,128)} %param.25) | copy-start | bytes 393220
  86.0 27.5 %collective-permute-start.19 = (bf16[32,1024]{1,0:T(8,128)(2,1)S(1)}, bf16[32,1024]{1,0:T(8,128)(2,1)S(1)}, u32[]{:S(2)}, u32[]{:S(2)}) collective-permute-start(bf16[32,1024]{1,0:T(8,128)(2,1)S(1)} %get-tuple-element.55), channel_id=1, source_target_pairs={{0,12},{4,8},{8,4},{12,0},{1,13},{5,9},{9,5},{13,1},{2,14},{6,10},... | collective-permute-start | bytes 196616 | tf_op jit(solution)/shard_map/ppermute | solution.py:542
  89.7 26.5 %collective-permute-start.20 = (bf16[32,1024]{1,0:T(8,128)(2,1)S(1)}, bf16[32,1024]{1,0:T(8,128)(2,1)S(1)}, u32[]{:S(2)}, u32[]{:S(2)}) collective-permute-start(bf16[32,1024]{1,0:T(8,128)(2,1)S(1)} %get-tuple-element.56), channel_id=1, source_target_pairs={{0,8},{4,12},{8,0},{12,4},{1,9},{5,13},{9,1},{13,5},{2,10},{6,14},... | collective-permute-start | bytes 196616 | tf_op jit(solution)/shard_map/ppermute | solution.py:542
  96.9 19.4 %collective-permute-start.21 = (bf16[32,1024]{1,0:T(8,128)(2,1)S(1)}, bf16[32,1024]{1,0:T(8,128)(2,1)S(1)}, u32[]{:S(2)}, u32[]{:S(2)}) collective-permute-start(bf16[32,1024]{1,0:T(8,128)(2,1)S(1)} %get-tuple-element.57), channel_id=1, source_target_pairs={{0,4},{4,0},{8,12},{12,8},{1,5},{5,1},{9,13},{13,9},{2,6},{6,2},{1... | collective-permute-start | bytes 196616 | tf_op jit(solution)/shard_map/ppermute | solution.py:542
  (4 other events, 18.9 us)

commit v5 on v4

--- a/solution.py
+++ b/solution.py
@@ -292,7 +292,7 @@
     return copies
 
 
-def pack_sent_kernel(slots, lengths, adapters, tokens, out, held, sems):
+def pack_sent_kernel(slots, lengths, adapters, tokens, out, held, packed, sems):
     copies = quarter_copies(tokens, held, sems, (2, 3))
     found = slot_places(lengths, adapters, slots)
     chosen = packing(*found, slots)
@@ -300,9 +300,13 @@
     for q in range(2):
         for b in range(10):
             at = min(16 * (10 * q + b), LIVE - 16)
-            out[q, LIVE:, 128 * b : 128 * b + 128] = ids[at : at + 16]
+            packed[q, LIVE:, 128 * b : 128 * b + 128] = ids[at : at + 16]
         copies[q].wait()
-        out[q, :LIVE] = mm(chosen, held[q]).astype(bf16)
+        packed[q, :LIVE] = mm(chosen, held[q]).astype(bf16)
+        copies.append(pltpu.make_async_copy(packed.at[q], out.at[q], sems.at[2 + q]))
+        copies[-1].start()
+    for copy in copies[2:]:
+        copy.wait()
 
 
 def pack_kept_kernel(slots, lengths, adapters, cotangent, tokens, near_out, far_out, grads_out, held, sems):
@@ -400,7 +404,7 @@
 
 
 def keys_kernel(ranks, far, low, low_mate, up_late, base, base_mate, grads, gain, *refs):
-    dlow_out, kept_out, sent_out, total = refs
+    dlow_out, key_grads_out, wide_out = refs
     up = up_late.get()
     dp = lax.axis_index("dp")
     f = lax.axis_index("fsdp")
@@ -430,7 +434,16 @@
     for j in range(4):
         picked = jnp.where(adapter == j, every[:, 128 * j : 128 * j + 128], picked)
     dlow_out[...] = (scale * picked).astype(bf16)
-    total[...] = mm(transposed(wide), key_grads)
+    key_grads_out[...] = key_grads
+    wide_out[...] = wide
+
+
+def up_sums_kernel(ranks, wide, key_grads, kept_out, sent_out, total):
+    dp = lax.axis_index("dp")
+    f = lax.axis_index("fsdp")
+    c, x = f % 2, f // 2
+    scales = [adapter_alpha_scale / jnp.full((1, HEAD), ranks[dp ^ j], i32).astype(f32) for j in range(4)]
+    total[...] = mm(transposed(wide.get()[...]), key_grads.get()[...])
     for j in range(4):
         scale_j = scales[j][0:1, 0:1]
         for part in range(2):
@@ -450,8 +463,8 @@
         out[...] = (own.get()[j] + arrived.get()[j].astype(f32)).astype(out.dtype)
 
 
-def down_kernel(dlow, dlow_mate, dlow_core, dlow_cross, rows, near, far, far_core, cross, *refs):
-    outs, (held, ids, sems) = refs[:4], refs[4:]
+def down_kernel(places, dlow, dlow_mate, dlow_core, dlow_cross, rows, near, far, far_core, cross, *refs):
+    outs, (held, ids, sems) = refs[:2], refs[2:]
     copies = [pltpu.make_async_copy(far.at[:, pl.ds(QUARTER, 128)], ids.at[pl.ds(0, LIVE), :], sems.at[0])]
     copies.append(
         pltpu.make_async_copy(far_core.at[:, pl.ds(QUARTER, 128)], ids.at[pl.ds(2 * LIVE, LIVE), :], sems.at[1])
@@ -470,11 +483,12 @@
     for copy in copies[:3]:
         copy.wait()
     lows = jnp.concatenate([d.get()[...] for d in (dlow, dlow_mate, dlow_core, dlow_cross)], axis=0)
-    wide = transposed(spread(lows, ids[...], range(4)))
+    wide = transposed(spread(lows, ids[...], places))
     for copy in copies[3:]:
         copy.wait()
-    for j, out in enumerate(outs):
-        out[...] = mm(wide[128 * j : 128 * j + 128], held[...]).astype(out.dtype)
+    total = mm(wide, held[...])
+    for n, out in enumerate(outs):
+        out[...] = total[128 * n : 128 * n + 128].astype(out.dtype)
 
 
 def update_kernel(*refs):
@@ -550,8 +564,13 @@
         [],
         [shape((2, LIVE + 16, QUARTER), bf16)],
         [tokens],
-        scratch=[pltpu.VMEM((2, tokens.shape[0], QUARTER), bf16), pltpu.SemaphoreType.DMA((2,))],
+        scratch=[
+            pltpu.VMEM((2, tokens.shape[0], QUARTER), bf16),
+            pltpu.VMEM((2, LIVE + 16, QUARTER), bf16),
+            pltpu.SemaphoreType.DMA((4,)),
+        ],
         vmem=60,
+        out_spec=HBM,
     )
     rows = across(sent)
 
@@ -619,37 +638,49 @@
         order=[low_sent],
         light=True,
     )
-    dlow, up_kept, up_core = call(
+    dlow, key_grads, wide = call(
         keys_kernel,
         "keys",
         [ranks],
         [far, low, low_mate, up, base, base_mate, grads, key_norm_weight[None, :]],
         [
             shape((LIVE, PADDED_RANK), bf16),
-            shape((2, 4, 32, KEY_WIDTH), f32),
-            shape((2, 4, 32, KEY_WIDTH), f32),
+            shape((LIVE, KEY_WIDTH), bf16),
+            shape((LIVE, 512), bf16),
         ],
         order=[far_core],
+    )
+    up_kept, up_core = call(
+        up_sums_kernel,
+        "up_sums",
+        [ranks],
+        [wide, key_grads],
+        [shape((2, 4, 32, KEY_WIDTH), f32)] * 2,
         scratch=[pltpu.VMEM((512, KEY_WIDTH), f32)],
     )
     dlow_mate, dlow_core = across(dlow), core(dlow)
+    dlow_mate = after(dlow_mate, up_kept)
     dlow_cross = core(dlow_mate)
     up_core_in = core(up_core)
 
-    own, one, two, three = call(
-        down_kernel,
-        "down",
-        [],
-        [dlow, dlow_mate, dlow_core, dlow_cross, rows],
-        [shape((PADDED_RANK, QUARTER), t) for t in (f32, bf16, bf16, bf16)],
-        [near, far, far_core, cross_core],
-        scratch=[
-            pltpu.VMEM((4 * LIVE, QUARTER), bf16),
-            pltpu.VMEM((4 * LIVE, HEAD), bf16),
-            pltpu.SemaphoreType.DMA((7,)),
-        ],
-    )
-    three_in, two_in, one_in = along(three, 3), along(two, 2), along(one, 1)
+    def down(places, types, order):
+        return call(
+            lambda *refs: down_kernel(places, *refs),
+            "down",
+            [],
+            [dlow, dlow_mate, dlow_core, dlow_cross, rows],
+            [shape((PADDED_RANK, QUARTER), t) for t in types],
+            [near, far, far_core, cross_core],
+            order=order,
+            scratch=[
+                pltpu.VMEM((4 * LIVE, QUARTER), bf16),
+                pltpu.VMEM((4 * LIVE, HEAD), bf16),
+                pltpu.SemaphoreType.DMA((7,)),
+            ],
+        )
+
+    three, two = down((3, 2), (bf16, bf16), [])
+    three_in, two_in = along(three, 3), along(two, 2)
 
     up_total, up_sent = call(
         up_core_kernel,
@@ -659,15 +690,18 @@
         [shape((4, 32, KEY_WIDTH), f32), shape((4, 32, KEY_WIDTH), bf16)],
         order=[three],
     )
+    up_arrived = across(up_sent)
+    own, one = down((0, 1), (f32, bf16), [up_arrived])
+    one_in = along(one, 1)
     up_parts = call(
         up_across_kernel,
         "up_across",
         [],
-        [up_total, across(up_sent)],
+        [up_total, up_arrived],
         [shape((32, KEY_WIDTH), t) for t in (f32, bf16, bf16, bf16)],
         order=[one],
     )
-    up_in = [up_parts[0]] + [along(up_parts[j], j) for j in (3, 2, 1)]
+    up_in = [up_parts[0], along(up_parts[3], 3), along(up_parts[2], 2), along(after(up_parts[1], one_in), 1)]
 
     new_down, down_first, down_second, new_up, up_first, up_second = call(
         update_kernel,

time: 121 us -> 119 us (0.983)
  waiting for transfers between devices: 62.4 us -> 56.8 us
  Pallas kernels: 30.5 us -> 33.2 us
    ppermute x9, waiting for transfers between devices: 23.3 us -> 19.4 us  [along(): return lax.ppermute(value, 'dp', [(i, i ^ distance) for i in range(4)])]
    pallas_call x12 -> x14, Pallas kernels: 30.5 us -> 33.2 us  [call(): pl.pallas_call(body, name=name, in_specs=[SMEM] * n + [HBM] * (m + p + d)...]
    ppermute x6, waiting for transfers between devices: 37 us -> 35.3 us  [across(): return lax.ppermute(value, 'fsdp', [(i, i ^ 2) for i in range(4)])]
  transfers between devices with their start and end apart: 22 -> 22, of which waited for: 10 -> 10; matrix products, arithmetic and copies ran while one was open for 0% -> 0% of each run, Pallas kernels for 22% -> 24%
where the time goes in v5:
time: 119 us
  waiting for transfers between devices  56.8 us (48%)
  Pallas kernels  33.2 us (28%)
  starting transfers between devices  25.9 us (22%)
  local copies, waits for them, and re-layouts  1.47 us (1%)
    ppermute x6, waiting for transfers between devices, across(): return lax.ppermute(value, 'fsdp', [(i, i ^ 2) for i in range(4)])  35.3 us
    pallas_call x14, Pallas kernels, call(): pl.pallas_call(body, name=name, in_specs=[SMEM] * n + [HBM] * (m + p + d)...  33.2 us
    ppermute x9, waiting for transfers between devices, along(): return lax.ppermute(value, 'dp', [(i, i ^ distance) for i in range(4)])  19.4 us
    ppermute x9, starting transfers between devices, along(): return lax.ppermute(value, 'dp', [(i, i ^ distance) for i in range(4)])  17.7 us
    ppermute x6, starting transfers between devices, across(): return lax.ppermute(value, 'fsdp', [(i, i ^ 2) for i in range(4)])  6.6 us
  transfers between devices with their start and end apart: 22, of which 10 were waited for; matrix products, arithmetic and copies ran while one was open for 0% of the time, Pallas kernels for 24%

profile of v5, /device:TPU:0, one launch (start us, length us, event | category | flops | bytes accessed | tf_op | source)
XLA Modules:
  0.0 118.6 jit_solution(7611103897112532776)
XLA Ops:
  1.2 2.6 %collective-permute-start = (f32[32,1024]{1,0:T(8,128)}, f32[32,1024]{1,0:T(8,128)S(1)}, u32[]{:S(2)}, u32[]{:S(2)}) collective-permute-start(f32[32,1024]{1,0:T(8,128)} %bitcast.22), channel_id=1, source_target_pairs={{0,2},{1,3},{2,0},{3,1},{4,6},{5,7},{6,4},{7,5},{8,10},{9,11},{10,... | collective-permute-start | bytes 393224 | tf_op jit(solution)/shard_map/ppermute | solution.py:553
  3.7 4.1 %pack_sent.1.refs_4_ = bf16[2,304,1280]{2,1,0:T(8,128)(2,1)} custom-call(s32[1,12]{1,0:T(1,128)} %refs_0_.7, s32[1,12]{1,0:T(1,128)} %refs_1_.5, bf16[384,5120]{1,0:T(8,128)(2,1)} %refs_3_.1), custom_call_target="tpu_custom_call" | custom-call | flops 30000001024 | bytes 5488736 | tf_op jit(solution)/shard_map/pack_sent/pallas_call | solution.py:218
  8.1 1.4 %copy-done.2 = bf16[2,304,1280]{2,1,0:T(8,128)(2,1)S(1)} copy-done((bf16[2,304,1280]{2,1,0:T(8,128)(2,1)S(1)}, bf16[2,304,1280]{2,1,0:T(8,128)(2,1)}, u32[]{:S(2)}) %copy-start.2) | copy-done | bytes 1556504
  9.5 1.2 weights.1.refs_4_
  10.7 2.0 %collective-permute-start.2 = (bf16[1792,128]{1,0:T(8,128)(2,1)S(1)}, bf16[1792,128]{1,0:T(8,128)(2,1)S(1)}, u32[]{:S(2)}, u32[]{:S(2)}) collective-permute-start(bf16[1792,128]{1,0:T(8,128)(2,1)S(1)} %weights.1.refs_4_), channel_id=1, source_target_pairs={{0,4},{4,0},{8,12},{12,8},{1,5},{5,1},{9,13},{13,9},{2,6},{6,2},{1... | collective-permute-start | bytes 1376264 | tf_op jit(solution)/shard_map/ppermute | solution.py:556
  12.7 2.6 %collective-permute-start.4 = (bf16[1792,128]{1,0:T(8,128)(2,1)S(1)}, bf16[1792,128]{1,0:T(8,128)(2,1)S(1)}, u32[]{:S(2)}, u32[]{:S(2)}) collective-permute-start(bf16[1792,128]{1,0:T(8,128)(2,1)S(1)} %weights.1.refs_4_), channel_id=1, source_target_pairs={{0,8},{4,12},{8,0},{12,4},{1,9},{5,13},{9,1},{13,5},{2,10},{6,14},... | collective-permute-start | bytes 1376264 | tf_op jit(solution)/shard_map/ppermute | solution.py:556
  15.3 3.0 %pack_kept.1 = (bf16[288,1280]{1,0:T(8,128)(2,1)S(1)}, bf16[288,1408]{1,0:T(8,128)(2,1)S(1)}, bf16[288,1024]{1,0:T(8,128)(2,1)S(1)}) custom-call(s32[1,12]{1,0:T(1,128)S(1)} %copy-done.10, s32[1,12]{1,0:T(1,128)S(1)} %copy-done.11, bf16[384,1024]{1,0:T(8,128)(2,1)S(1)} %copy-done.3, bf16[384,5120]{1,0:T(8,128)(2,1)S(1)} %copy-done, ...), custom_call_target="tpu_custom_call" | custom-call | flops 30000001024 | bytes 6856800 | tf_op jit(solution)/shard_map/pack_kept/pallas_call | solution.py:218
  18.4 25.8 %collective-permute-done.3.refs_0_.refs_4_ = bf16[2,304,1280]{2,1,0:T(8,128)(2,1)S(1)} collective-permute-done((bf16[2,304,1280]{2,1,0:T(8,128)(2,1)}, bf16[2,304,1280]{2,1,0:T(8,128)(2,1)S(1)}, u32[]{:S(2)}, u32[]{:S(2)}) %collective-permute-start.3) | collective-permute-done | bytes 1556512 | tf_op jit(solution)/shard_map/ppermute | solution.py:553
  44.2 2.7 %base_mate.1 = bf16[288,1024]{1,0:T(8,128)(2,1)S(1)} custom-call(bf16[2,304,1280]{2,1,0:T(8,128)(2,1)S(1)} %collective-permute-done.3.refs_0_.refs_4_, bf16[1280,1024]{1,0:T(8,128)(2,1)S(1)} %copy-done.1, bf16[1280,1024]{1,0:T(8,128)(2,1)S(1)} %collective-permute-done.1.refs_5_.refs_2_.refs_3_, bf16[288,1280]{1,0:T(8,128)(2,1)S(1)} %get-tuple-element.40.refs_3_.refs_0_.refs_5_), custom_call_target="tpu_custom_call" | custom-call | flops 30000001024 | bytes 7389184 | tf_op jit(solution)/shard_map/base_mate/pallas_call | solution.py:218
  48.3 2.7 %base_own.1.refs_3_.refs_5_ = f32[288,1024]{1,0:T(8,128)S(1)} custom-call(bf16[288,1280]{1,0:T(8,128)(2,1)S(1)} %get-tuple-element.40.refs_3_.refs_0_.refs_5_, bf16[1280,1024]{1,0:T(8,128)(2,1)S(1)} %copy-done.1, bf16[288,1408]{1,0:T(8,128)(2,1)S(1)} %get-tuple-element.39.refs_2_.refs_1_.refs_6_, ...), custom_call_target="tpu_custom_call" | custom-call | flops 30000001024 | bytes 7970816 | tf_op jit(solution)/shard_map/base_own/pallas_call | solution.py:218
  51.0 1.4 %collective-permute-done.6.refs_2_.refs_3_ = bf16[4,1792,128]{2,1,0:T(8,128)(2,1)S(1)} collective-permute-done((bf16[4,1792,128]{2,1,0:T(8,128)(2,1)S(1)}, bf16[4,1792,128]{2,1,0:T(8,128)(2,1)S(1)}, u32[]{:S(2)}, u32[]{:S(2)}) %collective-permute-start.6) | collective-permute-done | bytes 1835040 | tf_op jit(solution)/shard_map/ppermute | solution.py:550
  52.4 1.8 %low_mate.1 = (bf16[288,128]{1,0:T(8,128)(2,1)S(1)}, bf16[288,1408]{1,0:T(8,128)(2,1)S(1)}) custom-call(bf16[2,304,1280]{2,1,0:T(8,128)(2,1)S(1)} %collective-permute-done.3.refs_0_.refs_4_, bf16[4,1792,128]{2,1,0:T(8,128)(2,1)S(1)} %pad_maximum_fusion.refs_4_.refs_1_.refs_2_, bf16[4,1792,128]{2,1,0:T(8,128)(2,1)S(1)} %collective-permute-done.6.refs_2_.refs_3_, ...), custom_call_target="tpu_custom_call" | custom-call | flops 1 | bytes 1 | tf_op jit(solution)/shard_map/low_mate/pallas_call | solution.py:218
  54.2 1.7 %collective-permute-start.7 = (bf16[288,128]{1,0:T(8,128)(2,1)S(1)}, bf16[288,128]{1,0:T(8,128)(2,1)S(1)}, u32[]{:S(2)}, u32[]{:S(2)}) collective-permute-start(bf16[288,128]{1,0:T(8,128)(2,1)S(1)} %get-tuple-element.44.refs_4_), channel_id=1, source_target_pairs={{0,2},{1,3},{2,0},{3,1},{4,6},{5,7},{6,4},{7,5},{8,10},{9,11},{10,... | collective-permute-start | bytes 221192 | tf_op jit(solution)/shard_map/ppermute | solution.py:553
  55.9 2.0 %low_own.1 = (f32[288,128]{1,0:T(8,128)S(1)}, bf16[512,1024]{1,0:T(8,128)(2,1)S(1)}) custom-call(bf16[288,1280]{1,0:T(8,128)(2,1)S(1)} %get-tuple-element.40.refs_3_.refs_0_.refs_5_, bf16[288,1408]{1,0:T(8,128)(2,1)S(1)} %get-tuple-element.39.refs_2_.refs_1_.refs_6_, bf16[4,1792,128]{2,1,0:T(8,128)(2,1)S(1)} %pad_maximum_fusion.refs_4_.refs_1_.refs_2_, ...), custom_call_target="tpu_custom_call" | custom-call | flops 1 | bytes 1 | tf_op jit(solution)/shard_map/low_own/pallas_call | solution.py:218
  57.9 4.5 %collective-permute-done.8.refs_6_ = bf16[288,1024]{1,0:T(8,128)(2,1)S(1)} collective-permute-done((bf16[288,1024]{1,0:T(8,128)(2,1)S(1)}, bf16[288,1024]{1,0:T(8,128)(2,1)S(1)}, u32[]{:S(2)}, u32[]{:S(2)}) %collective-permute-start.8) | collective-permute-done | bytes 589856 | tf_op jit(solution)/shard_map/ppermute | solution.py:553
  63.1 3.3 %keys.1 = (bf16[288,128]{1,0:T(8,128)(2,1)S(1)}, bf16[288,1024]{1,0:T(8,128)(2,1)S(1)}, bf16[288,512]{1,0:T(8,128)(2,1)S(1)}) custom-call(s32[4]{0:T(128)S(1)} %copy-done.13, bf16[288,1408]{1,0:T(8,128)(2,1)S(1)} %get-tuple-element.39.refs_2_.refs_1_.refs_6_, f32[288,128]{1,0:T(8,128)S(1)} %get-tuple-element.45.refs_2_, ...), custom_call_target="tpu_custom_call" | custom-call | flops 30000001024 | bytes 5399056 | tf_op jit(solution)/shard_map/keys/pallas_call | solution.py:218
  66.5 0.8 collective-permute-start.10
  67.3 1.9 %up_sums.1 = (f32[2,4,32,1024]{3,2,1,0:T(8,128)S(1)}, f32[2,4,32,1024]{3,2,1,0:T(8,128)S(1)}) custom-call(s32[4]{0:T(128)S(1)} %copy-done.13, bf16[288,512]{1,0:T(8,128)(2,1)S(1)} %get-tuple-element.49.refs_1_, bf16[288,1024]{1,0:T(8,128)(2,1)S(1)} %get-tuple-element.50.refs_2_), custom_call_target="tpu_custom_call" | custom-call | flops 30000001024 | bytes 2981904 | tf_op jit(solution)/shard_map/up_sums/pallas_call | solution.py:218
  69.2 1.7 %collective-permute-done.10.refs_1_ = bf16[288,128]{1,0:T(8,128)(2,1)S(1)} collective-permute-done((bf16[288,128]{1,0:T(8,128)(2,1)S(1)}, bf16[288,128]{1,0:T(8,128)(2,1)S(1)}, u32[]{:S(2)}, u32[]{:S(2)}) %collective-permute-start.10) | collective-permute-done | bytes 73760 | tf_op jit(solution)/shard_map/ppermute | solution.py:553
  72.2 3.0 %down.2 = (bf16[128,1280]{1,0:T(8,128)(2,1)S(1)}, bf16[128,1280]{1,0:T(8,128)(2,1)S(1)}) custom-call(bf16[288,128]{1,0:T(8,128)(2,1)S(1)} %get-tuple-element.48.refs_0_, bf16[288,128]{1,0:T(8,128)(2,1)S(1)} %collective-permute-done.10.refs_1_, bf16[288,128]{1,0:T(8,128)(2,1)S(1)} %collective-permute-done.11.refs_2_, ...), custom_call_target="tpu_custom_call" | custom-call | flops 30000001024 | bytes 5677056 | tf_op jit(solution)/shard_map/down/pallas_call | solution.py:218
  75.5 0.8 collective-permute-start.15
  76.3 3.4 %collective-permute-start.18 = (bf16[128,1280]{1,0:T(8,128)(2,1)S(1)}, bf16[128,1280]{1,0:T(8,128)(2,1)S(1)}, u32[]{:S(2)}, u32[]{:S(2)}) collective-permute-start(bf16[128,1280]{1,0:T(8,128)(2,1)S(1)} %get-tuple-element.55.refs_2_), channel_id=1, source_target_pairs={{0,12},{4,8},{8,4},{12,0},{1,13},{5,9},{9,5},{13,1},{2,14},{6,10},... | collective-permute-start | bytes 983048 | tf_op jit(solution)/shard_map/ppermute | solution.py:556
  79.7 1.8 %collective-permute-start.17 = (bf16[128,1280]{1,0:T(8,128)(2,1)S(1)}, bf16[128,1280]{1,0:T(8,128)(2,1)S(1)}, u32[]{:S(2)}, u32[]{:S(2)}) collective-permute-start(bf16[128,1280]{1,0:T(8,128)(2,1)S(1)} %get-tuple-element.59), channel_id=1, source_target_pairs={{0,8},{4,12},{8,0},{12,4},{1,9},{5,13},{9,1},{13,5},{2,10},{6,14},... | collective-permute-start | bytes 983048 | tf_op jit(solution)/shard_map/ppermute | solution.py:556
  81.4 2.5 %collective-permute-done.15.refs_9_.refs_1_ = bf16[4,32,1024]{2,1,0:T(8,128)(2,1)S(1)} collective-permute-done((bf16[4,32,1024]{2,1,0:T(8,128)(2,1)S(1)}, bf16[4,32,1024]{2,1,0:T(8,128)(2,1)S(1)}, u32[]{:S(2)}, u32[]{:S(2)}) %collective-permute-start.15) | collective-permute-done | bytes 262176 | tf_op jit(solution)/shard_map/ppermute | solution.py:553
  83.9 2.8 %down.3 = (f32[128,1280]{1,0:T(8,128)S(1)}, bf16[128,1280]{1,0:T(8,128)(2,1)S(1)}) custom-call(bf16[288,128]{1,0:T(8,128)(2,1)S(1)} %get-tuple-element.48.refs_0_, bf16[288,128]{1,0:T(8,128)(2,1)S(1)} %collective-permute-done.10.refs_1_, bf16[288,128]{1,0:T(8,128)(2,1)S(1)} %collective-permute-done.11.refs_2_, ...), custom_call_target="tpu_custom_call" | custom-call | flops 30000001024 | bytes 6004736 | tf_op jit(solution)/shard_map/down/pallas_call | solution.py:218
  86.7 3.0 %collective-permute-start.16 = (bf16[128,1280]{1,0:T(8,128)(2,1)S(1)}, bf16[128,1280]{1,0:T(8,128)(2,1)S(1)}, u32[]{:S(2)}, u32[]{:S(2)}) collective-permute-start(bf16[128,1280]{1,0:T(8,128)(2,1)S(1)} %get-tuple-element.58.refs_2_), channel_id=1, source_target_pairs={{0,4},{4,0},{8,12},{12,8},{1,5},{5,1},{9,13},{13,9},{2,6},{6,2},{1... | collective-permute-start | bytes 983048 | tf_op jit(solution)/shard_map/ppermute | solution.py:556
  89.9 2.5 %collective-permute-start.19 = (bf16[32,1024]{1,0:T(8,128)(2,1)S(1)}, bf16[32,1024]{1,0:T(8,128)(2,1)S(1)}, u32[]{:S(2)}, u32[]{:S(2)}) collective-permute-start(bf16[32,1024]{1,0:T(8,128)(2,1)S(1)} %get-tuple-element.62), channel_id=1, source_target_pairs={{0,12},{4,8},{8,4},{12,0},{1,13},{5,9},{9,5},{13,1},{2,14},{6,10},... | collective-permute-start | bytes 196616 | tf_op jit(solution)/shard_map/ppermute | solution.py:556
  92.4 9.5 %collective-permute-done.16.refs_1_ = bf16[128,1280]{1,0:T(8,128)(2,1)S(1)} collective-permute-done((bf16[128,1280]{1,0:T(8,128)(2,1)S(1)}, bf16[128,1280]{1,0:T(8,128)(2,1)S(1)}, u32[]{:S(2)}, u32[]{:S(2)}) %collective-permute-start.16) | collective-permute-done | bytes 327712 | tf_op jit(solution)/shard_map/ppermute | solution.py:556
  101.9 2.5 %collective-permute-start.21 = (bf16[32,1024]{1,0:T(8,128)(2,1)S(1)}, bf16[32,1024]{1,0:T(8,128)(2,1)S(1)}, u32[]{:S(2)}, u32[]{:S(2)}) collective-permute-start(bf16[32,1024]{1,0:T(8,128)(2,1)S(1)} %get-tuple-element.65), channel_id=1, source_target_pairs={{0,4},{4,0},{8,12},{12,8},{1,5},{5,1},{9,13},{13,9},{2,6},{6,2},{1... | collective-permute-start | bytes 196616 | tf_op jit(solution)/shard_map/ppermute | solution.py:556
  104.4 7.2 %collective-permute-done.17.refs_2_ = bf16[128,1280]{1,0:T(8,128)(2,1)S(1)} collective-permute-done((bf16[128,1280]{1,0:T(8,128)(2,1)S(1)}, bf16[128,1280]{1,0:T(8,128)(2,1)S(1)}, u32[]{:S(2)}, u32[]{:S(2)}) %collective-permute-start.17) | collective-permute-done | bytes 327712 | tf_op jit(solution)/shard_map/ppermute | solution.py:556
  111.6 2.7 %collective-permute-done.20.refs_9_ = bf16[32,1024]{1,0:T(8,128)(2,1)S(1)} collective-permute-done((bf16[32,1024]{1,0:T(8,128)(2,1)S(1)}, bf16[32,1024]{1,0:T(8,128)(2,1)S(1)}, u32[]{:S(2)}, u32[]{:S(2)}) %collective-permute-start.20) | collective-permute-done | bytes 65568 | tf_op jit(solution)/shard_map/ppermute | solution.py:556
  114.3 4.2 %update.1 = (f32[1280,128]{1,0:T(8,128)}, f32[1280,128]{1,0:T(8,128)}, f32[1280,128]{1,0:T(8,128)}, f32[32,1024]{1,0:T(8,128)}, f32[32,1024]{1,0:T(8,128)}, /*index=5*/f32[32,1024]{1,0:T(8,128)}) custom-call(f32[128,1280]{1,0:T(8,128)S(1)} %get-tuple-element.57.refs_0_, bf16[128,1280]{1,0:T(8,128)(2,1)S(1)} %collective-permute-done.16.refs_1_, ...), custom_call_target="tpu_custom_call" | custom-call | flops 30000001024 | bytes 6684672 | tf_op jit(solution)/shard_map/update/pallas_call | solution.py:218
  (55 shorter events, 4.6 us)
Async XLA Ops:
  0.6 7.4 %collective-permute-start.1 = (bf16[1280,1024]{1,0:T(8,128)(2,1)}, bf16[1280,1024]{1,0:T(8,128)(2,1)S(1)}, u32[]{:S(2)}, u32[]{:S(2)}) collective-permute-start(bf16[1280,1024]{1,0:T(8,128)(2,1)} %refs_1_.7), channel_id=1, source_target_pairs={{0,1},{1,0},{2,3},{3,2},{4,5},{5,4},{6,7},{7,6},{8,9},{9,8},{10,11... | collective-permute-start | bytes 7864328 | tf_op jit(solution)/shard_map/ppermute | solution.py:550
  1.2 6.9 %copy-start.4 = (f32[1,1280,128]{2,1,0:T(8,128)S(1)}, f32[1,1280,128]{2,1,0:T(8,128)}, u32[]{:S(2)}) copy-start(f32[1,1280,128]{2,1,0:T(8,128)} %param.20) | copy-start | bytes 1966084
  1.2 6.9 %copy-start.7 = (f32[1,32,1024]{2,1,0:T(8,128)S(1)}, f32[1,32,1024]{2,1,0:T(8,128)}, u32[]{:S(2)}) copy-start(f32[1,32,1024]{2,1,0:T(8,128)} %param.21) | copy-start | bytes 393220
  1.2 6.9 %copy-start.13 = (s32[4]{0:T(128)S(1)}, s32[4]{0:T(128)}, u32[]{:S(2)}) copy-start(s32[4]{0:T(128)} %refs_0_.9) | copy-start | bytes 52
  1.2 6.9 %collective-permute-start = (f32[32,1024]{1,0:T(8,128)}, f32[32,1024]{1,0:T(8,128)S(1)}, u32[]{:S(2)}, u32[]{:S(2)}) collective-permute-start(f32[32,1024]{1,0:T(8,128)} %bitcast.22), channel_id=1, source_target_pairs={{0,2},{1,3},{2,0},{3,1},{4,6},{5,7},{6,4},{7,5},{8,10},{9,11},{10,... | collective-permute-start | bytes 393224 | tf_op jit(solution)/shard_map/ppermute | solution.py:553
  7.8 36.4 %collective-permute-start.3 = (bf16[2,304,1280]{2,1,0:T(8,128)(2,1)}, bf16[2,304,1280]{2,1,0:T(8,128)(2,1)S(1)}, u32[]{:S(2)}, u32[]{:S(2)}) collective-permute-start(bf16[2,304,1280]{2,1,0:T(8,128)(2,1)} %pack_sent.1.refs_4_), channel_id=1, source_target_pairs={{0,2},{1,3},{2,0},{3,1},{4,6},{5,7},{6,4},{7,5},{8,10},{9,11},{10,... | collective-permute-start | bytes 4669448 | tf_op jit(solution)/shard_map/ppermute | solution.py:553
  9.5 5.8 %copy-start.11 = (s32[1,12]{1,0:T(1,128)S(1)}, s32[1,12]{1,0:T(1,128)}, u32[]{:S(2)}) copy-start(s32[1,12]{1,0:T(1,128)} %refs_1_.5) | copy-start | bytes 148
  10.7 33.5 %copy-start.1 = (bf16[1280,1024]{1,0:T(8,128)(2,1)S(1)}, bf16[1280,1024]{1,0:T(8,128)(2,1)}, u32[]{:S(2)}) copy-start(bf16[1280,1024]{1,0:T(8,128)(2,1)} %refs_1_.7) | copy-start | bytes 7864324
  10.7 36.7 %collective-permute-start.2 = (bf16[1792,128]{1,0:T(8,128)(2,1)S(1)}, bf16[1792,128]{1,0:T(8,128)(2,1)S(1)}, u32[]{:S(2)}, u32[]{:S(2)}) collective-permute-start(bf16[1792,128]{1,0:T(8,128)(2,1)S(1)} %weights.1.refs_4_), channel_id=1, source_target_pairs={{0,4},{4,0},{8,12},{12,8},{1,5},{5,1},{9,13},{13,9},{2,6},{6,2},{1... | collective-permute-start | bytes 1376264 | tf_op jit(solution)/shard_map/ppermute | solution.py:556
  12.7 34.7 %collective-permute-start.4 = (bf16[1792,128]{1,0:T(8,128)(2,1)S(1)}, bf16[1792,128]{1,0:T(8,128)(2,1)S(1)}, u32[]{:S(2)}, u32[]{:S(2)}) collective-permute-start(bf16[1792,128]{1,0:T(8,128)(2,1)S(1)} %weights.1.refs_4_), channel_id=1, source_target_pairs={{0,8},{4,12},{8,0},{12,4},{1,9},{5,13},{9,1},{13,5},{2,10},{6,14},... | collective-permute-start | bytes 1376264 | tf_op jit(solution)/shard_map/ppermute | solution.py:556
  15.3 32.1 %collective-permute-start.5 = (bf16[1792,128]{1,0:T(8,128)(2,1)S(1)}, bf16[1792,128]{1,0:T(8,128)(2,1)S(1)}, u32[]{:S(2)}, u32[]{:S(2)}) collective-permute-start(bf16[1792,128]{1,0:T(8,128)(2,1)S(1)} %weights.1.refs_4_), channel_id=1, source_target_pairs={{0,12},{4,8},{8,4},{12,0},{1,13},{5,9},{9,5},{13,1},{2,14},{6,10},... | collective-permute-start | bytes 1376264 | tf_op jit(solution)/shard_map/ppermute | solution.py:556
  46.9 15.4 %collective-permute-start.8 = (bf16[288,1024]{1,0:T(8,128)(2,1)S(1)}, bf16[288,1024]{1,0:T(8,128)(2,1)S(1)}, u32[]{:S(2)}, u32[]{:S(2)}) collective-permute-start(bf16[288,1024]{1,0:T(8,128)(2,1)S(1)} %base_mate.1), channel_id=1, source_target_pairs={{0,2},{1,3},{2,0},{3,1},{4,6},{5,7},{6,4},{7,5},{8,10},{9,11},{10,... | collective-permute-start | bytes 1769480 | tf_op jit(solution)/shard_map/ppermute | solution.py:553
  47.4 14.9 %collective-permute-start.9 = (bf16[288,1408]{1,0:T(8,128)(2,1)S(1)}, bf16[288,1408]{1,0:T(8,128)(2,1)S(1)}, u32[]{:S(2)}, u32[]{:S(2)}) collective-permute-start(bf16[288,1408]{1,0:T(8,128)(2,1)S(1)} %get-tuple-element.39.refs_2_.refs_1_.refs_6_), channel_id=1, source_target_pairs={{0,1},{1,0},{2,3},{3,2},{4,5},{5,4},{6,7},{7,6},{8,9},{9,8},{10,11... | collective-permute-start | bytes 2433032 | tf_op jit(solution)/shard_map/ppermute | solution.py:550
  47.7 4.7 %collective-permute-start.6 = (bf16[4,1792,128]{2,1,0:T(8,128)(2,1)S(1)}, bf16[4,1792,128]{2,1,0:T(8,128)(2,1)S(1)}, u32[]{:S(2)}, u32[]{:S(2)}) collective-permute-start(bf16[4,1792,128]{2,1,0:T(8,128)(2,1)S(1)} %pad_maximum_fusion.refs_4_.refs_1_.refs_2_), channel_id=1, source_target_pairs={{0,1},{1,0},{2,3},{3,2},{4,5},{5,4},{6,7},{7,6},{8,9},{9,8},{10,11... | collective-permute-start | bytes 5505032 | tf_op jit(solution)/shard_map/ppermute | solution.py:550
  54.2 8.9 %collective-permute-start.7 = (bf16[288,128]{1,0:T(8,128)(2,1)S(1)}, bf16[288,128]{1,0:T(8,128)(2,1)S(1)}, u32[]{:S(2)}, u32[]{:S(2)}) collective-permute-start(bf16[288,128]{1,0:T(8,128)(2,1)S(1)} %get-tuple-element.44.refs_4_), channel_id=1, source_target_pairs={{0,2},{1,3},{2,0},{3,1},{4,6},{5,7},{6,4},{7,5},{8,10},{9,11},{10,... | collective-permute-start | bytes 221192 | tf_op jit(solution)/shard_map/ppermute | solution.py:553
  55.9 7.2 %copy-start.12 = (f32[128]{0:T(128)S(1)}, f32[128]{0:T(128)}, u32[]{:S(2)}) copy-start(f32[128]{0:T(128)} %param.19) | copy-start | bytes 1540
  55.9 16.3 %collective-permute-start.13 = (bf16[288,1408]{1,0:T(8,128)(2,1)S(1)}, bf16[288,1408]{1,0:T(8,128)(2,1)S(1)}, u32[]{:S(2)}, u32[]{:S(2)}) collective-permute-start(bf16[288,1408]{1,0:T(8,128)(2,1)S(1)} %get-tuple-element.53), channel_id=1, source_target_pairs={{0,1},{1,0},{2,3},{3,2},{4,5},{5,4},{6,7},{7,6},{8,9},{9,8},{10,11... | collective-permute-start | bytes 2433032 | tf_op jit(solution)/shard_map/ppermute | solution.py:550
  66.5 4.4 %collective-permute-start.10 = (bf16[288,128]{1,0:T(8,128)(2,1)S(1)}, bf16[288,128]{1,0:T(8,128)(2,1)S(1)}, u32[]{:S(2)}, u32[]{:S(2)}) collective-permute-start(bf16[288,128]{1,0:T(8,128)(2,1)S(1)} %get-tuple-element.48.refs_0_), channel_id=1, source_target_pairs={{0,2},{1,3},{2,0},{3,1},{4,6},{5,7},{6,4},{7,5},{8,10},{9,11},{10,... | collective-permute-start | bytes 221192 | tf_op jit(solution)/shard_map/ppermute | solution.py:553
  67.3 4.1 %collective-permute-start.11 = (bf16[288,128]{1,0:T(8,128)(2,1)S(1)}, bf16[288,128]{1,0:T(8,128)(2,1)S(1)}, u32[]{:S(2)}, u32[]{:S(2)}) collective-permute-start(bf16[288,128]{1,0:T(8,128)(2,1)S(1)} %get-tuple-element.48.refs_0_), channel_id=1, source_target_pairs={{0,1},{1,0},{2,3},{3,2},{4,5},{5,4},{6,7},{7,6},{8,9},{9,8},{10,11... | collective-permute-start | bytes 221192 | tf_op jit(solution)/shard_map/ppermute | solution.py:550
  70.9 1.3 %collective-permute-start.12 = (bf16[288,128]{1,0:T(8,128)(2,1)S(1)}, bf16[288,128]{1,0:T(8,128)(2,1)S(1)}, u32[]{:S(2)}, u32[]{:S(2)}) collective-permute-start(bf16[288,128]{1,0:T(8,128)(2,1)S(1)} %collective-permute-done.10.refs_1_), channel_id=1, source_target_pairs={{0,1},{1,0},{2,3},{3,2},{4,5},{5,4},{6,7},{7,6},{8,9},{9,8},{10,11... | collective-permute-start | bytes 221192 | tf_op jit(solution)/shard_map/ppermute | solution.py:550
  70.9 4.3 %collective-permute-start.14 = (f32[2,4,32,1024]{3,2,1,0:T(8,128)S(1)}, f32[2,4,32,1024]{3,2,1,0:T(8,128)S(1)}, u32[]{:S(2)}, u32[]{:S(2)}) collective-permute-start(f32[2,4,32,1024]{3,2,1,0:T(8,128)S(1)} %get-tuple-element.54), channel_id=1, source_target_pairs={{0,1},{1,0},{2,3},{3,2},{4,5},{5,4},{6,7},{7,6},{8,9},{9,8},{10,11... | collective-permute-start | bytes 3145736 | tf_op jit(solution)/shard_map/ppermute | solution.py:550
  75.5 8.4 %collective-permute-start.15 = (bf16[4,32,1024]{2,1,0:T(8,128)(2,1)S(1)}, bf16[4,32,1024]{2,1,0:T(8,128)(2,1)S(1)}, u32[]{:S(2)}, u32[]{:S(2)}) collective-permute-start(bf16[4,32,1024]{2,1,0:T(8,128)(2,1)S(1)} %get-tuple-element.56), channel_id=1, source_target_pairs={{0,2},{1,3},{2,0},{3,1},{4,6},{5,7},{6,4},{7,5},{8,10},{9,11},{10,... | collective-permute-start | bytes 786440 | tf_op jit(solution)/shard_map/ppermute | solution.py:553
  76.3 35.3 %collective-permute-start.18 = (bf16[128,1280]{1,0:T(8,128)(2,1)S(1)}, bf16[128,1280]{1,0:T(8,128)(2,1)S(1)}, u32[]{:S(2)}, u32[]{:S(2)}) collective-permute-start(bf16[128,1280]{1,0:T(8,128)(2,1)S(1)} %get-tuple-element.55.refs_2_), channel_id=1, source_target_pairs={{0,12},{4,8},{8,4},{12,0},{1,13},{5,9},{9,5},{13,1},{2,14},{6,10},... | collective-permute-start | bytes 983048 | tf_op jit(solution)/shard_map/ppermute | solution.py:556
  79.7 31.9 %collective-permute-start.17 = (bf16[128,1280]{1,0:T(8,128)(2,1)S(1)}, bf16[128,1280]{1,0:T(8,128)(2,1)S(1)}, u32[]{:S(2)}, u32[]{:S(2)}) collective-permute-start(bf16[128,1280]{1,0:T(8,128)(2,1)S(1)} %get-tuple-element.59), channel_id=1, source_target_pairs={{0,8},{4,12},{8,0},{12,4},{1,9},{5,13},{9,1},{13,5},{2,10},{6,14},... | collective-permute-start | bytes 983048 | tf_op jit(solution)/shard_map/ppermute | solution.py:556
  86.7 15.2 %collective-permute-start.16 = (bf16[128,1280]{1,0:T(8,128)(2,1)S(1)}, bf16[128,1280]{1,0:T(8,128)(2,1)S(1)}, u32[]{:S(2)}, u32[]{:S(2)}) collective-permute-start(bf16[128,1280]{1,0:T(8,128)(2,1)S(1)} %get-tuple-element.58.refs_2_), channel_id=1, source_target_pairs={{0,4},{4,0},{8,12},{12,8},{1,5},{5,1},{9,13},{13,9},{2,6},{6,2},{1... | collective-permute-start | bytes 983048 | tf_op jit(solution)/shard_map/ppermute | solution.py:556
  89.7 24.5 %copy-start.5 = (f32[1,1280,128]{2,1,0:T(8,128)S(1)}, f32[1,1280,128]{2,1,0:T(8,128)}, u32[]{:S(2)}) copy-start(f32[1,1280,128]{2,1,0:T(8,128)} %param.22) | copy-start | bytes 1966084
  89.7 24.5 %copy-start.6 = (f32[1,1280,128]{2,1,0:T(8,128)S(1)}, f32[1,1280,128]{2,1,0:T(8,128)}, u32[]{:S(2)}) copy-start(f32[1,1280,128]{2,1,0:T(8,128)} %param.24) | copy-start | bytes 1966084
  89.7 24.5 %copy-start.8 = (f32[1,32,1024]{2,1,0:T(8,128)S(1)}, f32[1,32,1024]{2,1,0:T(8,128)}, u32[]{:S(2)}) copy-start(f32[1,32,1024]{2,1,0:T(8,128)} %param.23) | copy-start | bytes 393220
  89.7 24.5 %copy-start.9 = (f32[1,32,1024]{2,1,0:T(8,128)S(1)}, f32[1,32,1024]{2,1,0:T(8,128)}, u32[]{:S(2)}) copy-start(f32[1,32,1024]{2,1,0:T(8,128)} %param.25) | copy-start | bytes 393220
  89.9 21.7 %collective-permute-start.19 = (bf16[32,1024]{1,0:T(8,128)(2,1)S(1)}, bf16[32,1024]{1,0:T(8,128)(2,1)S(1)}, u32[]{:S(2)}, u32[]{:S(2)}) collective-permute-start(bf16[32,1024]{1,0:T(8,128)(2,1)S(1)} %get-tuple-element.62), channel_id=1, source_target_pairs={{0,12},{4,8},{8,4},{12,0},{1,13},{5,9},{9,5},{13,1},{2,14},{6,10},... | collective-permute-start | bytes 196616 | tf_op jit(solution)/shard_map/ppermute | solution.py:556
  92.4 21.9 %collective-permute-start.20 = (bf16[32,1024]{1,0:T(8,128)(2,1)S(1)}, bf16[32,1024]{1,0:T(8,128)(2,1)S(1)}, u32[]{:S(2)}, u32[]{:S(2)}) collective-permute-start(bf16[32,1024]{1,0:T(8,128)(2,1)S(1)} %get-tuple-element.63), channel_id=1, source_target_pairs={{0,8},{4,12},{8,0},{12,4},{1,9},{5,13},{9,1},{13,5},{2,10},{6,14},... | collective-permute-start | bytes 196616 | tf_op jit(solution)/shard_map/ppermute | solution.py:556
  101.9 12.4 %collective-permute-start.21 = (bf16[32,1024]{1,0:T(8,128)(2,1)S(1)}, bf16[32,1024]{1,0:T(8,128)(2,1)S(1)}, u32[]{:S(2)}, u32[]{:S(2)}) collective-permute-start(bf16[32,1024]{1,0:T(8,128)(2,1)S(1)} %get-tuple-element.65), channel_id=1, source_target_pairs={{0,4},{4,0},{8,12},{12,8},{1,5},{5,1},{9,13},{13,9},{2,6},{6,2},{1... | collective-permute-start | bytes 196616 | tf_op jit(solution)/shard_map/ppermute | solution.py:556
  (4 other events, 18.8 us)

commit v6 on v5

--- a/solution.py
+++ b/solution.py
@@ -334,9 +334,9 @@
             out[at : at + 32] = masked[:, 128 * k : 128 * k + 128]
 
 
-def base_mate_kernel(rows, own, mate, out):
-    total = mm(rows.get()[0, :LIVE], own.get()[...])
-    out[...] = (total + mm(rows.get()[1, :LIVE], mate.get()[...])).astype(bf16)
+def base_mate_kernel(lanes, rows, own, mate, out):
+    total = mm(rows.get()[0, :LIVE], own.get()[:, lanes])
+    out[...] = (total + mm(rows.get()[1, :LIVE], mate.get()[:, lanes])).astype(bf16)
 
 
 def down_factors(weights):
@@ -403,7 +403,7 @@
     return jnp.concatenate(parts, axis=0)
 
 
-def keys_kernel(ranks, far, low, low_mate, up_late, base, base_mate, grads, gain, *refs):
+def keys_kernel(ranks, far, low, low_mate, up_late, base, left, right, grads, gain, *refs):
     dlow_out, key_grads_out, wide_out = refs
     up = up_late.get()
     dp = lax.axis_index("dp")
@@ -421,7 +421,8 @@
     parts = []
     for k in range(8):
         lanes = slice(128 * k, 128 * k + 128)
-        held = (base.get()[:, lanes] + base_mate.get()[:, lanes].astype(f32)).astype(bf16).astype(f32)
+        arrived = (left if k < 4 else right).get()[:, 128 * (k % 4) : 128 * (k % 4) + 128].astype(f32)
+        held = (base.get()[:, lanes] + arrived).astype(bf16).astype(f32)
         head = held + scale * added[:, lanes]
         inverse = lax.rsqrt(jnp.mean(head * head, axis=-1, keepdims=True) + norm_epsilon)
         normed = head * inverse
@@ -491,18 +492,11 @@
         out[...] = total[128 * n : 128 * n + 128].astype(out.dtype)
 
 
-def update_kernel(*refs):
-    own, one, two, three, down, moment, variance = refs[:7]
-    outs, held, sems = refs[14:20], refs[20:26], refs[26]
+def update_down_kernel(own, one, two, three, down, moment, variance, *refs):
+    outs, held, sems = refs[:3], refs[3:6], refs[6]
     step = 256
     copies = []
-
-    def leave(n, rows):
-        copies.append(pltpu.make_async_copy(held[n].at[rows], outs[n].at[rows], sems.at[len(copies)]))
-        copies[-1].start()
-
     for start in range(0, QUARTER, step):
-        rows = pl.ds(start, step)
         part = slice(start, start + step)
         total = own.get()[:, part] + one.get()[:, part].astype(f32)
         total = total + (two.get()[:, part].astype(f32) + three.get()[:, part].astype(f32))
@@ -510,17 +504,19 @@
             down.get()[part], total.T, moment.get()[part], variance.get()[part]
         )
         for n in range(3):
-            leave(n, rows)
-    own, one, two, three, up, moment, variance = refs[7:14]
+            rows = pl.ds(start, step)
+            copies.append(pltpu.make_async_copy(held[n].at[rows], outs[n].at[rows], sems.at[len(copies)]))
+            copies[-1].start()
+    for copy in copies:
+        copy.wait()
+
+
+def update_up_kernel(own, one, two, three, up, moment, variance, *outs):
     total = own.get()[...] + one.get()[...].astype(f32)
     total = total + (two.get()[...].astype(f32) + three.get()[...].astype(f32))
-    held[3][...], held[4][...], held[5][...] = optimizer_update(
+    outs[0][...], outs[1][...], outs[2][...] = optimizer_update(
         up.get()[...], total, moment.get()[...], variance.get()[...]
     )
-    for n in range(3, 6):
-        leave(n, pl.ds(0, 32))
-    for copy in copies:
-        copy.wait()
 
 
 def after(value, *others):
@@ -600,15 +596,21 @@
     )
     far_core = core(far)
 
-    (partial,) = call(
-        base_mate_kernel,
-        "base_mate",
-        [],
-        [rows, frozen, frozen_core],
-        [shape((LIVE, KEY_WIDTH), bf16)],
-        order=[near],
-    )
-    base_mate = across(partial)
+    half = KEY_WIDTH // 2
+
+    def base_mate(lanes, order):
+        return call(
+            lambda *refs: base_mate_kernel(lanes, *refs),
+            "base_mate",
+            [],
+            [rows, frozen, frozen_core],
+            [shape((LIVE, half), bf16)],
+            order=order,
+        )[0]
+
+    left = base_mate(slice(0, half), [near])
+    partial = base_mate(slice(half, KEY_WIDTH), [left])
+    mate_left, mate_right = across(left), across(partial)
     weights = jnp.stack([message] + [after(w, partial) for w in arrived])
     weights_core = core(weights)
     (base,) = call(
@@ -642,7 +644,7 @@
         keys_kernel,
         "keys",
         [ranks],
-        [far, low, low_mate, up, base, base_mate, grads, key_norm_weight[None, :]],
+        [far, low, low_mate, up, base, mate_left, mate_right, grads, key_norm_weight[None, :]],
         [
             shape((LIVE, PADDED_RANK), bf16),
             shape((LIVE, KEY_WIDTH), bf16),
@@ -703,17 +705,23 @@
     )
     up_in = [up_parts[0], along(up_parts[3], 3), along(up_parts[2], 2), along(after(up_parts[1], one_in), 1)]
 
-    new_down, down_first, down_second, new_up, up_first, up_second = call(
-        update_kernel,
-        "update",
+    new_down, down_first, down_second = call(
+        update_down_kernel,
+        "update_down",
         [],
-        [own, one_in, two_in, three_in, adapter_down_factor[0], down_first_moment[0], down_second_moment[0]]
-        + [*up_in, adapter_up_factor[0], up_first_moment[0], up_second_moment[0]],
-        [shape(adapter_down_factor.shape[1:], f32)] * 3 + [shape(adapter_up_factor.shape[1:], f32)] * 3,
-        scratch=[pltpu.VMEM(adapter_down_factor.shape[1:], f32)] * 3
-        + [pltpu.VMEM(adapter_up_factor.shape[1:], f32)] * 3
-        + [pltpu.SemaphoreType.DMA((18,))],
+        [own, one_in, two_in, three_in, adapter_down_factor[0], down_first_moment[0], down_second_moment[0]],
+        [shape(adapter_down_factor.shape[1:], f32)] * 3,
+        scratch=[pltpu.VMEM(adapter_down_factor.shape[1:], f32)] * 3 + [pltpu.SemaphoreType.DMA((15,))],
         out_spec=HBM,
+    )
+    new_up, up_first, up_second = call(
+        update_up_kernel,
+        "update_up",
+        [],
+        [*up_in, adapter_up_factor[0], up_first_moment[0], up_second_moment[0]],
+        [shape(adapter_up_factor.shape[1:], f32)] * 3,
+        order=[new_down],
+        vmem=60,
     )
     return tuple(o[None] for o in (new_down, new_up, down_first, up_first, down_second, up_second))
 

time: 119 us -> 117 us (0.983)
  waiting for transfers between devices: 56.8 us -> 50 us
  starting transfers between devices: 25.9 us -> 28.2 us
  Pallas kernels: 33.2 us -> 35.2 us
    ppermute x9, waiting for transfers between devices: 19.4 us -> 15.8 us  [along(): return lax.ppermute(value, 'dp', [(i, i ^ distance) for i in range(4)])]
    ppermute x6 -> x7, waiting for transfers between devices: 35.3 us -> 32 us  [across(): return lax.ppermute(value, 'fsdp', [(i, i ^ 2) for i in range(4)])]
    pallas_call x14 -> x16, Pallas kernels: 33.2 us -> 35.2 us  [call(): pl.pallas_call(body, name=name, in_specs=[SMEM] * n + [HBM] * (m + p + d)...]
    ppermute x9, starting transfers between devices: 17.7 us -> 19.5 us  [along(): return lax.ppermute(value, 'dp', [(i, i ^ distance) for i in range(4)])]
    ppermute x6 -> x7, starting transfers between devices: 6.6 us -> 7.09 us  [across(): return lax.ppermute(value, 'fsdp', [(i, i ^ 2) for i in range(4)])]
  transfers between devices with their start and end apart: 22 -> 23, of which waited for: 10 -> 9; matrix products, arithmetic and copies ran while one was open for 0% -> 0% of each run, Pallas kernels for 24% -> 28%
where the time goes in v6:
time: 117 us
  waiting for transfers between devices  50 us (43%)
  Pallas kernels  35.2 us (30%)
  starting transfers between devices  28.2 us (24%)
  local copies, waits for them, and re-layouts  2.08 us (2%)
    pallas_call x16, Pallas kernels, call(): pl.pallas_call(body, name=name, in_specs=[SMEM] * n + [HBM] * (m + p + d)...  35.2 us
    ppermute x7, waiting for transfers between devices, across(): return lax.ppermute(value, 'fsdp', [(i, i ^ 2) for i in range(4)])  32 us
    ppermute x9, starting transfers between devices, along(): return lax.ppermute(value, 'dp', [(i, i ^ distance) for i in range(4)])  19.5 us
    ppermute x9, waiting for transfers between devices, along(): return lax.ppermute(value, 'dp', [(i, i ^ distance) for i in range(4)])  15.8 us
    ppermute x7, starting transfers between devices, across(): return lax.ppermute(value, 'fsdp', [(i, i ^ 2) for i in range(4)])  7.09 us
  transfers between devices with their start and end apart: 23, of which 9 were waited for; matrix products, arithmetic and copies ran while one was open for 0% of the time, Pallas kernels for 28%

profile of v6, /device:TPU:0, one launch (start us, length us, event | category | flops | bytes accessed | tf_op | source)
XLA Modules:
  0.0 116.7 jit_solution(1073737637544806313)
XLA Ops:
  1.2 2.6 %collective-permute-start = (f32[32,1024]{1,0:T(8,128)}, f32[32,1024]{1,0:T(8,128)S(1)}, u32[]{:S(2)}, u32[]{:S(2)}) collective-permute-start(f32[32,1024]{1,0:T(8,128)} %bitcast.22), channel_id=1, source_target_pairs={{0,2},{1,3},{2,0},{3,1},{4,6},{5,7},{6,4},{7,5},{8,10},{9,11},{10,... | collective-permute-start | bytes 393224 | tf_op jit(solution)/shard_map/ppermute | solution.py:549
  3.7 4.1 %pack_sent.1.refs_4_ = bf16[2,304,1280]{2,1,0:T(8,128)(2,1)} custom-call(s32[1,12]{1,0:T(1,128)} %refs_0_.7, s32[1,12]{1,0:T(1,128)} %refs_1_.6, bf16[384,5120]{1,0:T(8,128)(2,1)} %refs_3_.1), custom_call_target="tpu_custom_call" | custom-call | flops 30000001024 | bytes 5488736 | tf_op jit(solution)/shard_map/pack_sent/pallas_call | solution.py:218
  8.1 1.4 %copy-done.2 = bf16[2,304,1280]{2,1,0:T(8,128)(2,1)S(1)} copy-done((bf16[2,304,1280]{2,1,0:T(8,128)(2,1)S(1)}, bf16[2,304,1280]{2,1,0:T(8,128)(2,1)}, u32[]{:S(2)}) %copy-start.2) | copy-done | bytes 1556504
  9.5 1.2 %weights.1.refs_4_ = bf16[1792,128]{1,0:T(8,128)(2,1)S(1)} custom-call(s32[4]{0:T(128)S(1)} %copy-done.11, f32[1280,128]{1,0:T(8,128)S(1)} %bitcast.18, f32[32,1024]{1,0:T(8,128)S(1)} %bitcast.24, f32[32,1024]{1,0:T(8,128)S(1)} %collective-permute-done.refs_3_, bf16[2,304,1280]{2,1,0:T(8,128)(2,1)S(1)} %copy-done.2, ...), custom_call_target="tpu_custom_call" | custom-call | flops 30000001024 | bytes 1376272 | tf_op jit(solution)/shard_map/weights/pallas_call | solution.py:218
  10.7 2.0 %collective-permute-start.2 = (bf16[1792,128]{1,0:T(8,128)(2,1)S(1)}, bf16[1792,128]{1,0:T(8,128)(2,1)S(1)}, u32[]{:S(2)}, u32[]{:S(2)}) collective-permute-start(bf16[1792,128]{1,0:T(8,128)(2,1)S(1)} %weights.1.refs_4_), channel_id=1, source_target_pairs={{0,4},{4,0},{8,12},{12,8},{1,5},{5,1},{9,13},{13,9},{2,6},{6,2},{1... | collective-permute-start | bytes 1376264 | tf_op jit(solution)/shard_map/ppermute | solution.py:552
  12.7 2.6 %collective-permute-start.4 = (bf16[1792,128]{1,0:T(8,128)(2,1)S(1)}, bf16[1792,128]{1,0:T(8,128)(2,1)S(1)}, u32[]{:S(2)}, u32[]{:S(2)}) collective-permute-start(bf16[1792,128]{1,0:T(8,128)(2,1)S(1)} %weights.1.refs_4_), channel_id=1, source_target_pairs={{0,8},{4,12},{8,0},{12,4},{1,9},{5,13},{9,1},{13,5},{2,10},{6,14},... | collective-permute-start | bytes 1376264 | tf_op jit(solution)/shard_map/ppermute | solution.py:552
  15.3 3.0 %pack_kept.1 = (bf16[288,1280]{1,0:T(8,128)(2,1)S(1)}, bf16[288,1408]{1,0:T(8,128)(2,1)S(1)}, bf16[288,1024]{1,0:T(8,128)(2,1)S(1)}) custom-call(s32[1,12]{1,0:T(1,128)S(1)} %copy-done.8, s32[1,12]{1,0:T(1,128)S(1)} %copy-done.9, bf16[384,1024]{1,0:T(8,128)(2,1)S(1)} %copy-done.3, bf16[384,5120]{1,0:T(8,128)(2,1)S(1)} %copy-done, ...), custom_call_target="tpu_custom_call" | custom-call | flops 30000001024 | bytes 6856800 | tf_op jit(solution)/shard_map/pack_kept/pallas_call | solution.py:218
  18.4 25.8 %collective-permute-done.3.refs_0_.refs_4_ = bf16[2,304,1280]{2,1,0:T(8,128)(2,1)S(1)} collective-permute-done((bf16[2,304,1280]{2,1,0:T(8,128)(2,1)}, bf16[2,304,1280]{2,1,0:T(8,128)(2,1)S(1)}, u32[]{:S(2)}, u32[]{:S(2)}) %collective-permute-start.3) | collective-permute-done | bytes 1556512 | tf_op jit(solution)/shard_map/ppermute | solution.py:549
  44.2 1.9 %base_mate.2.refs_3_ = bf16[288,512]{1,0:T(8,128)(2,1)S(1)} custom-call(bf16[2,304,1280]{2,1,0:T(8,128)(2,1)S(1)} %collective-permute-done.3.refs_0_.refs_4_, bf16[1280,1024]{1,0:T(8,128)(2,1)S(1)} %copy-done.1, bf16[1280,1024]{1,0:T(8,128)(2,1)S(1)} %collective-permute-done.1.refs_5_.refs_2_.refs_3_, ...), custom_call_target="tpu_custom_call" | custom-call | flops 30000001024 | bytes 7094272 | tf_op jit(solution)/shard_map/base_mate/pallas_call | solution.py:218
  46.6 1.9 %base_mate.3 = bf16[288,512]{1,0:T(8,128)(2,1)S(1)} custom-call(bf16[2,304,1280]{2,1,0:T(8,128)(2,1)S(1)} %collective-permute-done.3.refs_0_.refs_4_, bf16[1280,1024]{1,0:T(8,128)(2,1)S(1)} %copy-done.1, bf16[1280,1024]{1,0:T(8,128)(2,1)S(1)} %collective-permute-done.1.refs_5_.refs_2_.refs_3_, bf16[288,512]{1,0:T(8,128)(2,1)S(1)} %base_mate.2.refs_3_), custom_call_target="tpu_custom_call" | custom-call | flops 30000001024 | bytes 7094272 | tf_op jit(solution)/shard_map/base_mate/pallas_call | solution.py:218
  48.5 1.7 %collective-permute-start.9 = (bf16[288,512]{1,0:T(8,128)(2,1)S(1)}, bf16[288,512]{1,0:T(8,128)(2,1)S(1)}, u32[]{:S(2)}, u32[]{:S(2)}) collective-permute-start(bf16[288,512]{1,0:T(8,128)(2,1)S(1)} %base_mate.3), channel_id=1, source_target_pairs={{0,2},{1,3},{2,0},{3,1},{4,6},{5,7},{6,4},{7,5},{8,10},{9,11},{10,... | collective-permute-start | bytes 884744 | tf_op jit(solution)/shard_map/ppermute | solution.py:549
  51.0 2.7 %base_own.1.refs_3_.refs_5_ = f32[288,1024]{1,0:T(8,128)S(1)} custom-call(bf16[288,1280]{1,0:T(8,128)(2,1)S(1)} %get-tuple-element.40.refs_3_.refs_0_.refs_5_, bf16[1280,1024]{1,0:T(8,128)(2,1)S(1)} %copy-done.1, bf16[288,1408]{1,0:T(8,128)(2,1)S(1)} %get-tuple-element.39.refs_2_.refs_1_.refs_6_, ...), custom_call_target="tpu_custom_call" | custom-call | flops 30000001024 | bytes 7970816 | tf_op jit(solution)/shard_map/base_own/pallas_call | solution.py:218
  53.7 1.4 %collective-permute-done.6.refs_2_.refs_3_ = bf16[4,1792,128]{2,1,0:T(8,128)(2,1)S(1)} collective-permute-done((bf16[4,1792,128]{2,1,0:T(8,128)(2,1)S(1)}, bf16[4,1792,128]{2,1,0:T(8,128)(2,1)S(1)}, u32[]{:S(2)}, u32[]{:S(2)}) %collective-permute-start.6) | collective-permute-done | bytes 1835040 | tf_op jit(solution)/shard_map/ppermute | solution.py:546
  55.1 1.8 %low_mate.1 = (bf16[288,128]{1,0:T(8,128)(2,1)S(1)}, bf16[288,1408]{1,0:T(8,128)(2,1)S(1)}) custom-call(bf16[2,304,1280]{2,1,0:T(8,128)(2,1)S(1)} %collective-permute-done.3.refs_0_.refs_4_, bf16[4,1792,128]{2,1,0:T(8,128)(2,1)S(1)} %pad_maximum_fusion.refs_4_.refs_1_.refs_2_, bf16[4,1792,128]{2,1,0:T(8,128)(2,1)S(1)} %collective-permute-done.6.refs_2_.refs_3_, ...), custom_call_target="tpu_custom_call" | custom-call | flops 1 | bytes 1 | tf_op jit(solution)/shard_map/low_mate/pallas_call | solution.py:218
  57.5 2.0 %low_own.1 = (f32[288,128]{1,0:T(8,128)S(1)}, bf16[512,1024]{1,0:T(8,128)(2,1)S(1)}) custom-call(bf16[288,1280]{1,0:T(8,128)(2,1)S(1)} %get-tuple-element.40.refs_3_.refs_0_.refs_5_, bf16[288,1408]{1,0:T(8,128)(2,1)S(1)} %get-tuple-element.39.refs_2_.refs_1_.refs_6_, bf16[4,1792,128]{2,1,0:T(8,128)(2,1)S(1)} %pad_maximum_fusion.refs_4_.refs_1_.refs_2_, ...), custom_call_target="tpu_custom_call" | custom-call | flops 1 | bytes 1 | tf_op jit(solution)/shard_map/low_own/pallas_call | solution.py:218
  59.4 2.1 %collective-permute-done.9.refs_7_ = bf16[288,512]{1,0:T(8,128)(2,1)S(1)} collective-permute-done((bf16[288,512]{1,0:T(8,128)(2,1)S(1)}, bf16[288,512]{1,0:T(8,128)(2,1)S(1)}, u32[]{:S(2)}, u32[]{:S(2)}) %collective-permute-start.9) | collective-permute-done | bytes 294944 | tf_op jit(solution)/shard_map/ppermute | solution.py:549
  62.3 3.5 %keys.1 = (bf16[288,128]{1,0:T(8,128)(2,1)S(1)}, bf16[288,1024]{1,0:T(8,128)(2,1)S(1)}, bf16[288,512]{1,0:T(8,128)(2,1)S(1)}) custom-call(s32[4]{0:T(128)S(1)} %copy-done.11, bf16[288,1408]{1,0:T(8,128)(2,1)S(1)} %get-tuple-element.39.refs_2_.refs_1_.refs_6_, f32[288,128]{1,0:T(8,128)S(1)} %get-tuple-element.45.refs_2_, ...), custom_call_target="tpu_custom_call" | custom-call | flops 30000001024 | bytes 5399056 | tf_op jit(solution)/shard_map/keys/pallas_call | solution.py:218
  65.8 0.8 collective-permute-start.11
  66.6 1.9 %up_sums.1 = (f32[2,4,32,1024]{3,2,1,0:T(8,128)S(1)}, f32[2,4,32,1024]{3,2,1,0:T(8,128)S(1)}) custom-call(s32[4]{0:T(128)S(1)} %copy-done.11, bf16[288,512]{1,0:T(8,128)(2,1)S(1)} %get-tuple-element.49.refs_1_, bf16[288,1024]{1,0:T(8,128)(2,1)S(1)} %get-tuple-element.50.refs_2_), custom_call_target="tpu_custom_call" | custom-call | flops 30000001024 | bytes 2981904 | tf_op jit(solution)/shard_map/up_sums/pallas_call | solution.py:218
  68.5 1.7 %collective-permute-done.11.refs_1_ = bf16[288,128]{1,0:T(8,128)(2,1)S(1)} collective-permute-done((bf16[288,128]{1,0:T(8,128)(2,1)S(1)}, bf16[288,128]{1,0:T(8,128)(2,1)S(1)}, u32[]{:S(2)}, u32[]{:S(2)}) %collective-permute-start.11) | collective-permute-done | bytes 73760 | tf_op jit(solution)/shard_map/ppermute | solution.py:549
  71.5 3.0 %down.2 = (bf16[128,1280]{1,0:T(8,128)(2,1)S(1)}, bf16[128,1280]{1,0:T(8,128)(2,1)S(1)}) custom-call(bf16[288,128]{1,0:T(8,128)(2,1)S(1)} %get-tuple-element.48.refs_0_, bf16[288,128]{1,0:T(8,128)(2,1)S(1)} %collective-permute-done.11.refs_1_, bf16[288,128]{1,0:T(8,128)(2,1)S(1)} %collective-permute-done.12.refs_2_, ...), custom_call_target="tpu_custom_call" | custom-call | flops 30000001024 | bytes 5677056 | tf_op jit(solution)/shard_map/down/pallas_call | solution.py:218
  75.6 3.4 %collective-permute-start.19 = (bf16[128,1280]{1,0:T(8,128)(2,1)S(1)}, bf16[128,1280]{1,0:T(8,128)(2,1)S(1)}, u32[]{:S(2)}, u32[]{:S(2)}) collective-permute-start(bf16[128,1280]{1,0:T(8,128)(2,1)S(1)} %get-tuple-element.55.refs_2_), channel_id=1, source_target_pairs={{0,12},{4,8},{8,4},{12,0},{1,13},{5,9},{9,5},{13,1},{2,14},{6,10},... | collective-permute-start | bytes 983048 | tf_op jit(solution)/shard_map/ppermute | solution.py:552
  79.0 2.6 %collective-permute-start.18 = (bf16[128,1280]{1,0:T(8,128)(2,1)S(1)}, bf16[128,1280]{1,0:T(8,128)(2,1)S(1)}, u32[]{:S(2)}, u32[]{:S(2)}) collective-permute-start(bf16[128,1280]{1,0:T(8,128)(2,1)S(1)} %get-tuple-element.59), channel_id=1, source_target_pairs={{0,8},{4,12},{8,0},{12,4},{1,9},{5,13},{9,1},{13,5},{2,10},{6,14},... | collective-permute-start | bytes 983048 | tf_op jit(solution)/shard_map/ppermute | solution.py:552
  81.6 1.6 %collective-permute-done.16.refs_9_.refs_1_ = bf16[4,32,1024]{2,1,0:T(8,128)(2,1)S(1)} collective-permute-done((bf16[4,32,1024]{2,1,0:T(8,128)(2,1)S(1)}, bf16[4,32,1024]{2,1,0:T(8,128)(2,1)S(1)}, u32[]{:S(2)}, u32[]{:S(2)}) %collective-permute-start.16) | collective-permute-done | bytes 262176 | tf_op jit(solution)/shard_map/ppermute | solution.py:549
  83.2 2.8 %down.3 = (f32[128,1280]{1,0:T(8,128)S(1)}, bf16[128,1280]{1,0:T(8,128)(2,1)S(1)}) custom-call(bf16[288,128]{1,0:T(8,128)(2,1)S(1)} %get-tuple-element.48.refs_0_, bf16[288,128]{1,0:T(8,128)(2,1)S(1)} %collective-permute-done.11.refs_1_, bf16[288,128]{1,0:T(8,128)(2,1)S(1)} %collective-permute-done.12.refs_2_, ...), custom_call_target="tpu_custom_call" | custom-call | flops 30000001024 | bytes 6004736 | tf_op jit(solution)/shard_map/down/pallas_call | solution.py:218
  86.0 3.8 %collective-permute-start.17 = (bf16[128,1280]{1,0:T(8,128)(2,1)S(1)}, bf16[128,1280]{1,0:T(8,128)(2,1)S(1)}, u32[]{:S(2)}, u32[]{:S(2)}) collective-permute-start(bf16[128,1280]{1,0:T(8,128)(2,1)S(1)} %get-tuple-element.58.refs_2_), channel_id=1, source_target_pairs={{0,4},{4,0},{8,12},{12,8},{1,5},{5,1},{9,13},{13,9},{2,6},{6,2},{1... | collective-permute-start | bytes 983048 | tf_op jit(solution)/shard_map/ppermute | solution.py:552
  90.0 2.5 %collective-permute-start.20 = (bf16[32,1024]{1,0:T(8,128)(2,1)S(1)}, bf16[32,1024]{1,0:T(8,128)(2,1)S(1)}, u32[]{:S(2)}, u32[]{:S(2)}) collective-permute-start(bf16[32,1024]{1,0:T(8,128)(2,1)S(1)} %get-tuple-element.63), channel_id=1, source_target_pairs={{0,12},{4,8},{8,4},{12,0},{1,13},{5,9},{9,5},{13,1},{2,14},{6,10},... | collective-permute-start | bytes 196616 | tf_op jit(solution)/shard_map/ppermute | solution.py:552
  92.6 8.6 %collective-permute-done.17.refs_1_ = bf16[128,1280]{1,0:T(8,128)(2,1)S(1)} collective-permute-done((bf16[128,1280]{1,0:T(8,128)(2,1)S(1)}, bf16[128,1280]{1,0:T(8,128)(2,1)S(1)}, u32[]{:S(2)}, u32[]{:S(2)}) %collective-permute-start.17) | collective-permute-done | bytes 327712 | tf_op jit(solution)/shard_map/ppermute | solution.py:552
  101.2 2.5 %collective-permute-start.22 = (bf16[32,1024]{1,0:T(8,128)(2,1)S(1)}, bf16[32,1024]{1,0:T(8,128)(2,1)S(1)}, u32[]{:S(2)}, u32[]{:S(2)}) collective-permute-start(bf16[32,1024]{1,0:T(8,128)(2,1)S(1)} %get-tuple-element.66), channel_id=1, source_target_pairs={{0,4},{4,0},{8,12},{12,8},{1,5},{5,1},{9,13},{13,9},{2,6},{6,2},{1... | collective-permute-start | bytes 196616 | tf_op jit(solution)/shard_map/ppermute | solution.py:552
  103.7 7.2 %collective-permute-done.18.refs_2_ = bf16[128,1280]{1,0:T(8,128)(2,1)S(1)} collective-permute-done((bf16[128,1280]{1,0:T(8,128)(2,1)S(1)}, bf16[128,1280]{1,0:T(8,128)(2,1)S(1)}, u32[]{:S(2)}, u32[]{:S(2)}) %collective-permute-start.18) | collective-permute-done | bytes 327712 | tf_op jit(solution)/shard_map/ppermute | solution.py:552
  110.9 2.9 %update_down.1 = (f32[1280,128]{1,0:T(8,128)}, f32[1280,128]{1,0:T(8,128)}, f32[1280,128]{1,0:T(8,128)}) custom-call(f32[128,1280]{1,0:T(8,128)S(1)} %get-tuple-element.57.refs_0_, bf16[128,1280]{1,0:T(8,128)(2,1)S(1)} %collective-permute-done.17.refs_1_, bf16[128,1280]{1,0:T(8,128)(2,1)S(1)} %collective-permute-done.18.refs_2_, ...), custom_call_target="tpu_custom_call" | custom-call | flops 30000001024 | bytes 5570560 | tf_op jit(solution)/shard_map/update_down/pallas_call | solution.py:218
  114.5 2.0 %update_up.1 = (f32[32,1024]{1,0:T(8,128)}, f32[32,1024]{1,0:T(8,128)}, f32[32,1024]{1,0:T(8,128)}) custom-call(f32[32,1024]{1,0:T(8,128)} %copy-done.12, bf16[32,1024]{1,0:T(8,128)(2,1)} %copy-done.13, bf16[32,1024]{1,0:T(8,128)(2,1)} %copy-done.14, bf16[32,1024]{1,0:T(8,128)(2,1)} %copy-done.15, f32[32,1024]{1,0:T(8,128)} %bitcast.23, ...), custom_call_target="tpu_custom_call" | custom-call | flops 30000001024 | bytes 1114112 | tf_op jit(solution)/shard_map/update_up/pallas_call | solution.py:218
  (63 shorter events, 6.5 us)
Async XLA Ops:
  0.6 7.4 %collective-permute-start.1 = (bf16[1280,1024]{1,0:T(8,128)(2,1)}, bf16[1280,1024]{1,0:T(8,128)(2,1)S(1)}, u32[]{:S(2)}, u32[]{:S(2)}) collective-permute-start(bf16[1280,1024]{1,0:T(8,128)(2,1)} %refs_1_.9), channel_id=1, source_target_pairs={{0,1},{1,0},{2,3},{3,2},{4,5},{5,4},{6,7},{7,6},{8,9},{9,8},{10,11... | collective-permute-start | bytes 7864328 | tf_op jit(solution)/shard_map/ppermute | solution.py:546
  1.1 6.9 %copy-start.4 = (f32[1,1280,128]{2,1,0:T(8,128)S(1)}, f32[1,1280,128]{2,1,0:T(8,128)}, u32[]{:S(2)}) copy-start(f32[1,1280,128]{2,1,0:T(8,128)} %param.20) | copy-start | bytes 1966084
  1.2 6.9 %copy-start.7 = (f32[1,32,1024]{2,1,0:T(8,128)S(1)}, f32[1,32,1024]{2,1,0:T(8,128)}, u32[]{:S(2)}) copy-start(f32[1,32,1024]{2,1,0:T(8,128)} %param.21) | copy-start | bytes 393220
  1.2 6.9 %copy-start.11 = (s32[4]{0:T(128)S(1)}, s32[4]{0:T(128)}, u32[]{:S(2)}) copy-start(s32[4]{0:T(128)} %refs_0_.9) | copy-start | bytes 52
  1.2 6.9 %collective-permute-start = (f32[32,1024]{1,0:T(8,128)}, f32[32,1024]{1,0:T(8,128)S(1)}, u32[]{:S(2)}, u32[]{:S(2)}) collective-permute-start(f32[32,1024]{1,0:T(8,128)} %bitcast.22), channel_id=1, source_target_pairs={{0,2},{1,3},{2,0},{3,1},{4,6},{5,7},{6,4},{7,5},{8,10},{9,11},{10,... | collective-permute-start | bytes 393224 | tf_op jit(solution)/shard_map/ppermute | solution.py:549
  7.8 36.4 %collective-permute-start.3 = (bf16[2,304,1280]{2,1,0:T(8,128)(2,1)}, bf16[2,304,1280]{2,1,0:T(8,128)(2,1)S(1)}, u32[]{:S(2)}, u32[]{:S(2)}) collective-permute-start(bf16[2,304,1280]{2,1,0:T(8,128)(2,1)} %pack_sent.1.refs_4_), channel_id=1, source_target_pairs={{0,2},{1,3},{2,0},{3,1},{4,6},{5,7},{6,4},{7,5},{8,10},{9,11},{10,... | collective-permute-start | bytes 4669448 | tf_op jit(solution)/shard_map/ppermute | solution.py:549
  9.5 5.8 %copy-start.8 = (s32[1,12]{1,0:T(1,128)S(1)}, s32[1,12]{1,0:T(1,128)}, u32[]{:S(2)}) copy-start(s32[1,12]{1,0:T(1,128)} %refs_0_.7) | copy-start | bytes 148
  9.5 5.8 %copy-start.9 = (s32[1,12]{1,0:T(1,128)S(1)}, s32[1,12]{1,0:T(1,128)}, u32[]{:S(2)}) copy-start(s32[1,12]{1,0:T(1,128)} %refs_1_.6) | copy-start | bytes 148
  10.7 33.5 %copy-start.1 = (bf16[1280,1024]{1,0:T(8,128)(2,1)S(1)}, bf16[1280,1024]{1,0:T(8,128)(2,1)}, u32[]{:S(2)}) copy-start(bf16[1280,1024]{1,0:T(8,128)(2,1)} %refs_1_.9) | copy-start | bytes 7864324
  10.7 39.5 %collective-permute-start.2 = (bf16[1792,128]{1,0:T(8,128)(2,1)S(1)}, bf16[1792,128]{1,0:T(8,128)(2,1)S(1)}, u32[]{:S(2)}, u32[]{:S(2)}) collective-permute-start(bf16[1792,128]{1,0:T(8,128)(2,1)S(1)} %weights.1.refs_4_), channel_id=1, source_target_pairs={{0,4},{4,0},{8,12},{12,8},{1,5},{5,1},{9,13},{13,9},{2,6},{6,2},{1... | collective-permute-start | bytes 1376264 | tf_op jit(solution)/shard_map/ppermute | solution.py:552
  12.7 37.4 %collective-permute-start.4 = (bf16[1792,128]{1,0:T(8,128)(2,1)S(1)}, bf16[1792,128]{1,0:T(8,128)(2,1)S(1)}, u32[]{:S(2)}, u32[]{:S(2)}) collective-permute-start(bf16[1792,128]{1,0:T(8,128)(2,1)S(1)} %weights.1.refs_4_), channel_id=1, source_target_pairs={{0,8},{4,12},{8,0},{12,4},{1,9},{5,13},{9,1},{13,5},{2,10},{6,14},... | collective-permute-start | bytes 1376264 | tf_op jit(solution)/shard_map/ppermute | solution.py:552
  15.3 34.9 %collective-permute-start.5 = (bf16[1792,128]{1,0:T(8,128)(2,1)S(1)}, bf16[1792,128]{1,0:T(8,128)(2,1)S(1)}, u32[]{:S(2)}, u32[]{:S(2)}) collective-permute-start(bf16[1792,128]{1,0:T(8,128)(2,1)S(1)} %weights.1.refs_4_), channel_id=1, source_target_pairs={{0,12},{4,8},{8,4},{12,0},{1,13},{5,9},{9,5},{13,1},{2,14},{6,10},... | collective-permute-start | bytes 1376264 | tf_op jit(solution)/shard_map/ppermute | solution.py:552
  46.1 15.4 %collective-permute-start.8 = (bf16[288,512]{1,0:T(8,128)(2,1)S(1)}, bf16[288,512]{1,0:T(8,128)(2,1)S(1)}, u32[]{:S(2)}, u32[]{:S(2)}) collective-permute-start(bf16[288,512]{1,0:T(8,128)(2,1)S(1)} %base_mate.2.refs_3_), channel_id=1, source_target_pairs={{0,2},{1,3},{2,0},{3,1},{4,6},{5,7},{6,4},{7,5},{8,10},{9,11},{10,... | collective-permute-start | bytes 884744 | tf_op jit(solution)/shard_map/ppermute | solution.py:549
  48.5 13.0 %collective-permute-start.9 = (bf16[288,512]{1,0:T(8,128)(2,1)S(1)}, bf16[288,512]{1,0:T(8,128)(2,1)S(1)}, u32[]{:S(2)}, u32[]{:S(2)}) collective-permute-start(bf16[288,512]{1,0:T(8,128)(2,1)S(1)} %base_mate.3), channel_id=1, source_target_pairs={{0,2},{1,3},{2,0},{3,1},{4,6},{5,7},{6,4},{7,5},{8,10},{9,11},{10,... | collective-permute-start | bytes 884744 | tf_op jit(solution)/shard_map/ppermute | solution.py:549
  50.2 11.4 %collective-permute-start.10 = (bf16[288,1408]{1,0:T(8,128)(2,1)S(1)}, bf16[288,1408]{1,0:T(8,128)(2,1)S(1)}, u32[]{:S(2)}, u32[]{:S(2)}) collective-permute-start(bf16[288,1408]{1,0:T(8,128)(2,1)S(1)} %get-tuple-element.39.refs_2_.refs_1_.refs_6_), channel_id=1, source_target_pairs={{0,1},{1,0},{2,3},{3,2},{4,5},{5,4},{6,7},{7,6},{8,9},{9,8},{10,11... | collective-permute-start | bytes 2433032 | tf_op jit(solution)/shard_map/ppermute | solution.py:546
  50.4 4.7 %collective-permute-start.6 = (bf16[4,1792,128]{2,1,0:T(8,128)(2,1)S(1)}, bf16[4,1792,128]{2,1,0:T(8,128)(2,1)S(1)}, u32[]{:S(2)}, u32[]{:S(2)}) collective-permute-start(bf16[4,1792,128]{2,1,0:T(8,128)(2,1)S(1)} %pad_maximum_fusion.refs_4_.refs_1_.refs_2_), channel_id=1, source_target_pairs={{0,1},{1,0},{2,3},{3,2},{4,5},{5,4},{6,7},{7,6},{8,9},{9,8},{10,11... | collective-permute-start | bytes 5505032 | tf_op jit(solution)/shard_map/ppermute | solution.py:546
  57.0 5.3 %collective-permute-start.7 = (bf16[288,128]{1,0:T(8,128)(2,1)S(1)}, bf16[288,128]{1,0:T(8,128)(2,1)S(1)}, u32[]{:S(2)}, u32[]{:S(2)}) collective-permute-start(bf16[288,128]{1,0:T(8,128)(2,1)S(1)} %get-tuple-element.44.refs_4_), channel_id=1, source_target_pairs={{0,2},{1,3},{2,0},{3,1},{4,6},{5,7},{6,4},{7,5},{8,10},{9,11},{10,... | collective-permute-start | bytes 221192 | tf_op jit(solution)/shard_map/ppermute | solution.py:549
  57.5 14.0 %collective-permute-start.14 = (bf16[288,1408]{1,0:T(8,128)(2,1)S(1)}, bf16[288,1408]{1,0:T(8,128)(2,1)S(1)}, u32[]{:S(2)}, u32[]{:S(2)}) collective-permute-start(bf16[288,1408]{1,0:T(8,128)(2,1)S(1)} %get-tuple-element.53), channel_id=1, source_target_pairs={{0,1},{1,0},{2,3},{3,2},{4,5},{5,4},{6,7},{7,6},{8,9},{9,8},{10,11... | collective-permute-start | bytes 2433032 | tf_op jit(solution)/shard_map/ppermute | solution.py:546
  65.8 4.4 %collective-permute-start.11 = (bf16[288,128]{1,0:T(8,128)(2,1)S(1)}, bf16[288,128]{1,0:T(8,128)(2,1)S(1)}, u32[]{:S(2)}, u32[]{:S(2)}) collective-permute-start(bf16[288,128]{1,0:T(8,128)(2,1)S(1)} %get-tuple-element.48.refs_0_), channel_id=1, source_target_pairs={{0,2},{1,3},{2,0},{3,1},{4,6},{5,7},{6,4},{7,5},{8,10},{9,11},{10,... | collective-permute-start | bytes 221192 | tf_op jit(solution)/shard_map/ppermute | solution.py:549
  66.6 4.1 %collective-permute-start.12 = (bf16[288,128]{1,0:T(8,128)(2,1)S(1)}, bf16[288,128]{1,0:T(8,128)(2,1)S(1)}, u32[]{:S(2)}, u32[]{:S(2)}) collective-permute-start(bf16[288,128]{1,0:T(8,128)(2,1)S(1)} %get-tuple-element.48.refs_0_), channel_id=1, source_target_pairs={{0,1},{1,0},{2,3},{3,2},{4,5},{5,4},{6,7},{7,6},{8,9},{9,8},{10,11... | collective-permute-start | bytes 221192 | tf_op jit(solution)/shard_map/ppermute | solution.py:546
  70.2 1.3 %collective-permute-start.13 = (bf16[288,128]{1,0:T(8,128)(2,1)S(1)}, bf16[288,128]{1,0:T(8,128)(2,1)S(1)}, u32[]{:S(2)}, u32[]{:S(2)}) collective-permute-start(bf16[288,128]{1,0:T(8,128)(2,1)S(1)} %collective-permute-done.11.refs_1_), channel_id=1, source_target_pairs={{0,1},{1,0},{2,3},{3,2},{4,5},{5,4},{6,7},{7,6},{8,9},{9,8},{10,11... | collective-permute-start | bytes 221192 | tf_op jit(solution)/shard_map/ppermute | solution.py:546
  70.2 4.3 %collective-permute-start.15 = (f32[2,4,32,1024]{3,2,1,0:T(8,128)S(1)}, f32[2,4,32,1024]{3,2,1,0:T(8,128)S(1)}, u32[]{:S(2)}, u32[]{:S(2)}) collective-permute-start(f32[2,4,32,1024]{3,2,1,0:T(8,128)S(1)} %get-tuple-element.54), channel_id=1, source_target_pairs={{0,1},{1,0},{2,3},{3,2},{4,5},{5,4},{6,7},{7,6},{8,9},{9,8},{10,11... | collective-permute-start | bytes 3145736 | tf_op jit(solution)/shard_map/ppermute | solution.py:546
  74.8 8.4 %collective-permute-start.16 = (bf16[4,32,1024]{2,1,0:T(8,128)(2,1)S(1)}, bf16[4,32,1024]{2,1,0:T(8,128)(2,1)S(1)}, u32[]{:S(2)}, u32[]{:S(2)}) collective-permute-start(bf16[4,32,1024]{2,1,0:T(8,128)(2,1)S(1)} %get-tuple-element.56), channel_id=1, source_target_pairs={{0,2},{1,3},{2,0},{3,1},{4,6},{5,7},{6,4},{7,5},{8,10},{9,11},{10,... | collective-permute-start | bytes 786440 | tf_op jit(solution)/shard_map/ppermute | solution.py:549
  75.6 35.3 %collective-permute-start.19 = (bf16[128,1280]{1,0:T(8,128)(2,1)S(1)}, bf16[128,1280]{1,0:T(8,128)(2,1)S(1)}, u32[]{:S(2)}, u32[]{:S(2)}) collective-permute-start(bf16[128,1280]{1,0:T(8,128)(2,1)S(1)} %get-tuple-element.55.refs_2_), channel_id=1, source_target_pairs={{0,12},{4,8},{8,4},{12,0},{1,13},{5,9},{9,5},{13,1},{2,14},{6,10},... | collective-permute-start | bytes 983048 | tf_op jit(solution)/shard_map/ppermute | solution.py:552
  79.0 31.9 %collective-permute-start.18 = (bf16[128,1280]{1,0:T(8,128)(2,1)S(1)}, bf16[128,1280]{1,0:T(8,128)(2,1)S(1)}, u32[]{:S(2)}, u32[]{:S(2)}) collective-permute-start(bf16[128,1280]{1,0:T(8,128)(2,1)S(1)} %get-tuple-element.59), channel_id=1, source_target_pairs={{0,8},{4,12},{8,0},{12,4},{1,9},{5,13},{9,1},{13,5},{2,10},{6,14},... | collective-permute-start | bytes 983048 | tf_op jit(solution)/shard_map/ppermute | solution.py:552
  86.0 15.1 %collective-permute-start.17 = (bf16[128,1280]{1,0:T(8,128)(2,1)S(1)}, bf16[128,1280]{1,0:T(8,128)(2,1)S(1)}, u32[]{:S(2)}, u32[]{:S(2)}) collective-permute-start(bf16[128,1280]{1,0:T(8,128)(2,1)S(1)} %get-tuple-element.58.refs_2_), channel_id=1, source_target_pairs={{0,4},{4,0},{8,12},{12,8},{1,5},{5,1},{9,13},{13,9},{2,6},{6,2},{1... | collective-permute-start | bytes 983048 | tf_op jit(solution)/shard_map/ppermute | solution.py:552
  89.9 21.0 %copy-start.5 = (f32[1,1280,128]{2,1,0:T(8,128)S(1)}, f32[1,1280,128]{2,1,0:T(8,128)}, u32[]{:S(2)}) copy-start(f32[1,1280,128]{2,1,0:T(8,128)} %param.22) | copy-start | bytes 1966084
  89.9 21.0 %copy-start.6 = (f32[1,1280,128]{2,1,0:T(8,128)S(1)}, f32[1,1280,128]{2,1,0:T(8,128)}, u32[]{:S(2)}) copy-start(f32[1,1280,128]{2,1,0:T(8,128)} %param.24) | copy-start | bytes 1966084
  90.0 23.8 %copy-start.12 = (f32[32,1024]{1,0:T(8,128)}, f32[32,1024]{1,0:T(8,128)S(1)}, u32[]{:S(2)}) copy-start(f32[32,1024]{1,0:T(8,128)S(1)} %get-tuple-element.62.refs_0_) | copy-start | bytes 393220
  90.0 23.8 %collective-permute-start.20 = (bf16[32,1024]{1,0:T(8,128)(2,1)S(1)}, bf16[32,1024]{1,0:T(8,128)(2,1)S(1)}, u32[]{:S(2)}, u32[]{:S(2)}) collective-permute-start(bf16[32,1024]{1,0:T(8,128)(2,1)S(1)} %get-tuple-element.63), channel_id=1, source_target_pairs={{0,12},{4,8},{8,4},{12,0},{1,13},{5,9},{9,5},{13,1},{2,14},{6,10},... | collective-permute-start | bytes 196616 | tf_op jit(solution)/shard_map/ppermute | solution.py:552
  92.6 21.3 %collective-permute-start.21 = (bf16[32,1024]{1,0:T(8,128)(2,1)S(1)}, bf16[32,1024]{1,0:T(8,128)(2,1)S(1)}, u32[]{:S(2)}, u32[]{:S(2)}) collective-permute-start(bf16[32,1024]{1,0:T(8,128)(2,1)S(1)} %get-tuple-element.64), channel_id=1, source_target_pairs={{0,8},{4,12},{8,0},{12,4},{1,9},{5,13},{9,1},{13,5},{2,10},{6,14},... | collective-permute-start | bytes 196616 | tf_op jit(solution)/shard_map/ppermute | solution.py:552
  101.2 12.7 %collective-permute-start.22 = (bf16[32,1024]{1,0:T(8,128)(2,1)S(1)}, bf16[32,1024]{1,0:T(8,128)(2,1)S(1)}, u32[]{:S(2)}, u32[]{:S(2)}) collective-permute-start(bf16[32,1024]{1,0:T(8,128)(2,1)S(1)} %get-tuple-element.66), channel_id=1, source_target_pairs={{0,4},{4,0},{8,12},{12,8},{1,5},{5,1},{9,13},{13,9},{2,6},{6,2},{1... | collective-permute-start | bytes 196616 | tf_op jit(solution)/shard_map/ppermute | solution.py:552
  (7 other events, 19.8 us)

commit v7 on v6

--- a/solution.py
+++ b/solution.py
@@ -551,7 +551,6 @@
     def along(value, distance):
         return lax.ppermute(value, "dp", [(i, i ^ distance) for i in range(4)])
 
-    frozen_core = core(frozen)
     up_mate = across(adapter_up_factor[0])
     (sent,) = call(
         lambda *refs: pack_sent_kernel(slots, *refs),
@@ -569,6 +568,7 @@
         out_spec=HBM,
     )
     rows = across(sent)
+    frozen_core = core(after(frozen, sent))
 
     (message,) = call(
         weights_kernel,
@@ -576,7 +576,7 @@
         [ranks],
         [adapter_down_factor[0], adapter_up_factor[0], up_mate],
         [shape((QUARTER + 512, PADDED_RANK), bf16)],
-        order=[sent, frozen_core],
+        order=[sent],
     )
     arrived = [along(message, j) for j in (1, 2, 3)]
 
@@ -591,7 +591,7 @@
             shape((LIVE, KEY_WIDTH), bf16),
         ],
         [tokens],
-        order=[message],
+        order=[message, frozen_core],
         scratch=[pltpu.VMEM((2, tokens.shape[0], QUARTER), bf16), pltpu.SemaphoreType.DMA((2,))],
     )
     far_core = core(far)

time: 117 us -> 116 us (level)
  waiting for transfers between devices: 50 us -> 44.8 us
  starting transfers between devices: 28.2 us -> 32 us
    ppermute x9, starting transfers between devices: 19.5 us -> 23 us  [along(): return lax.ppermute(value, 'dp', [(i, i ^ distance) for i in range(4)])]
    ppermute x7, waiting for transfers between devices: 32 us -> 29.6 us  [across(): return lax.ppermute(value, 'fsdp', [(i, i ^ 2) for i in range(4)])]
    ppermute x9, waiting for transfers between devices: 15.8 us -> 14 us  [along(): return lax.ppermute(value, 'dp', [(i, i ^ distance) for i in range(4)])]
  transfers between devices with their start and end apart: 23 -> 23, of which waited for: 9 -> 8; matrix products, arithmetic and copies ran while one was open for 0% -> 0% of each run, Pallas kernels for 28% -> 28%
where the time goes in v7:
time: 116 us
  waiting for transfers between devices  44.8 us (39%)
  Pallas kernels  35.2 us (30%)
  starting transfers between devices  32 us (28%)
  local copies, waits for them, and re-layouts  2.11 us (2%)
    pallas_call x16, Pallas kernels, call(): pl.pallas_call(body, name=name, in_specs=[SMEM] * n + [HBM] * (m + p + d)...  35.2 us
    ppermute x7, waiting for transfers between devices, across(): return lax.ppermute(value, 'fsdp', [(i, i ^ 2) for i in range(4)])  29.6 us
    ppermute x9, starting transfers between devices, along(): return lax.ppermute(value, 'dp', [(i, i ^ distance) for i in range(4)])  23 us
    ppermute x9, waiting for transfers between devices, along(): return lax.ppermute(value, 'dp', [(i, i ^ distance) for i in range(4)])  14 us
    ppermute x7, starting transfers between devices, across(): return lax.ppermute(value, 'fsdp', [(i, i ^ 2) for i in range(4)])  7.92 us
  transfers between devices with their start and end apart: 23, of which 8 were waited for; matrix products, arithmetic and copies ran while one was open for 0% of the time, Pallas kernels for 28%

profile of v7, /device:TPU:0, one launch (start us, length us, event | category | flops | bytes accessed | tf_op | source)
XLA Modules:
  0.0 115.6 jit_solution(12144897341831985875)
XLA Ops:
  0.7 3.0 %collective-permute-start = (f32[32,1024]{1,0:T(8,128)}, f32[32,1024]{1,0:T(8,128)S(1)}, u32[]{:S(2)}, u32[]{:S(2)}) collective-permute-start(f32[32,1024]{1,0:T(8,128)} %bitcast.22), channel_id=1, source_target_pairs={{0,2},{1,3},{2,0},{3,1},{4,6},{5,7},{6,4},{7,5},{8,10},{9,11},{10,... | collective-permute-start | bytes 393224 | tf_op jit(solution)/shard_map/ppermute | solution.py:549
  3.7 4.1 %pack_sent.1.refs_4_ = bf16[2,304,1280]{2,1,0:T(8,128)(2,1)} custom-call(s32[1,12]{1,0:T(1,128)} %refs_0_.7, s32[1,12]{1,0:T(1,128)} %refs_1_.6, bf16[384,5120]{1,0:T(8,128)(2,1)} %refs_3_.1), custom_call_target="tpu_custom_call" | custom-call | flops 30000001024 | bytes 5488736 | tf_op jit(solution)/shard_map/pack_sent/pallas_call | solution.py:218
  8.1 1.4 %copy-done.2 = bf16[2,304,1280]{2,1,0:T(8,128)(2,1)S(1)} copy-done((bf16[2,304,1280]{2,1,0:T(8,128)(2,1)S(1)}, bf16[2,304,1280]{2,1,0:T(8,128)(2,1)}, u32[]{:S(2)}) %copy-start.2) | copy-done | bytes 1556504
  9.6 1.2 %weights.1.refs_4_ = bf16[1792,128]{1,0:T(8,128)(2,1)S(1)} custom-call(s32[4]{0:T(128)S(1)} %copy-done.11, f32[1280,128]{1,0:T(8,128)S(1)} %bitcast.18, f32[32,1024]{1,0:T(8,128)S(1)} %bitcast.24, f32[32,1024]{1,0:T(8,128)S(1)} %collective-permute-done.refs_3_, bf16[2,304,1280]{2,1,0:T(8,128)(2,1)S(1)} %copy-done.2), custom_call_target="tpu_custom_call" | custom-call | flops 30000001024 | bytes 1376272 | tf_op jit(solution)/shard_map/weights/pallas_call | solution.py:218
  10.8 2.1 %collective-permute-start.2 = (bf16[1792,128]{1,0:T(8,128)(2,1)S(1)}, bf16[1792,128]{1,0:T(8,128)(2,1)S(1)}, u32[]{:S(2)}, u32[]{:S(2)}) collective-permute-start(bf16[1792,128]{1,0:T(8,128)(2,1)S(1)} %weights.1.refs_4_), channel_id=1, source_target_pairs={{0,4},{4,0},{8,12},{12,8},{1,5},{5,1},{9,13},{13,9},{2,6},{6,2},{1... | collective-permute-start | bytes 1376264 | tf_op jit(solution)/shard_map/ppermute | solution.py:552
  12.8 2.6 %collective-permute-start.4 = (bf16[1792,128]{1,0:T(8,128)(2,1)S(1)}, bf16[1792,128]{1,0:T(8,128)(2,1)S(1)}, u32[]{:S(2)}, u32[]{:S(2)}) collective-permute-start(bf16[1792,128]{1,0:T(8,128)(2,1)S(1)} %weights.1.refs_4_), channel_id=1, source_target_pairs={{0,8},{4,12},{8,0},{12,4},{1,9},{5,13},{9,1},{13,5},{2,10},{6,14},... | collective-permute-start | bytes 1376264 | tf_op jit(solution)/shard_map/ppermute | solution.py:552
  15.4 3.1 %pack_kept.1 = (bf16[288,1280]{1,0:T(8,128)(2,1)S(1)}, bf16[288,1408]{1,0:T(8,128)(2,1)S(1)}, bf16[288,1024]{1,0:T(8,128)(2,1)S(1)}) custom-call(s32[1,12]{1,0:T(1,128)S(1)} %copy-done.8, s32[1,12]{1,0:T(1,128)S(1)} %copy-done.9, bf16[384,1024]{1,0:T(8,128)(2,1)S(1)} %copy-done.3, bf16[384,5120]{1,0:T(8,128)(2,1)S(1)} %copy-done, ...), custom_call_target="tpu_custom_call" | custom-call | flops 30000001024 | bytes 6856800 | tf_op jit(solution)/shard_map/pack_kept/pallas_call | solution.py:218
  18.5 25.0 %collective-permute-done.3.refs_0_.refs_4_ = bf16[2,304,1280]{2,1,0:T(8,128)(2,1)S(1)} collective-permute-done((bf16[2,304,1280]{2,1,0:T(8,128)(2,1)}, bf16[2,304,1280]{2,1,0:T(8,128)(2,1)S(1)}, u32[]{:S(2)}, u32[]{:S(2)}) %collective-permute-start.3) | collective-permute-done | bytes 1556512 | tf_op jit(solution)/shard_map/ppermute | solution.py:549
  43.5 1.9 %base_mate.2.refs_3_ = bf16[288,512]{1,0:T(8,128)(2,1)S(1)} custom-call(bf16[2,304,1280]{2,1,0:T(8,128)(2,1)S(1)} %collective-permute-done.3.refs_0_.refs_4_, bf16[1280,1024]{1,0:T(8,128)(2,1)S(1)} %copy-done.1, bf16[1280,1024]{1,0:T(8,128)(2,1)S(1)} %collective-permute-done.1.refs_5_.refs_2_.refs_3_, ...), custom_call_target="tpu_custom_call" | custom-call | flops 30000001024 | bytes 7094272 | tf_op jit(solution)/shard_map/base_mate/pallas_call | solution.py:218
  46.0 1.9 %base_mate.3 = bf16[288,512]{1,0:T(8,128)(2,1)S(1)} custom-call(bf16[2,304,1280]{2,1,0:T(8,128)(2,1)S(1)} %collective-permute-done.3.refs_0_.refs_4_, bf16[1280,1024]{1,0:T(8,128)(2,1)S(1)} %copy-done.1, bf16[1280,1024]{1,0:T(8,128)(2,1)S(1)} %collective-permute-done.1.refs_5_.refs_2_.refs_3_, bf16[288,512]{1,0:T(8,128)(2,1)S(1)} %base_mate.2.refs_3_), custom_call_target="tpu_custom_call" | custom-call | flops 30000001024 | bytes 7094272 | tf_op jit(solution)/shard_map/base_mate/pallas_call | solution.py:218
  47.9 1.6 %collective-permute-start.9 = (bf16[288,512]{1,0:T(8,128)(2,1)S(1)}, bf16[288,512]{1,0:T(8,128)(2,1)S(1)}, u32[]{:S(2)}, u32[]{:S(2)}) collective-permute-start(bf16[288,512]{1,0:T(8,128)(2,1)S(1)} %base_mate.3), channel_id=1, source_target_pairs={{0,2},{1,3},{2,0},{3,1},{4,6},{5,7},{6,4},{7,5},{8,10},{9,11},{10,... | collective-permute-start | bytes 884744 | tf_op jit(solution)/shard_map/ppermute | solution.py:549
  50.3 2.7 %base_own.1.refs_3_.refs_5_ = f32[288,1024]{1,0:T(8,128)S(1)} custom-call(bf16[288,1280]{1,0:T(8,128)(2,1)S(1)} %get-tuple-element.42.refs_3_.refs_0_.refs_5_, bf16[1280,1024]{1,0:T(8,128)(2,1)S(1)} %copy-done.1, bf16[288,1408]{1,0:T(8,128)(2,1)S(1)} %get-tuple-element.41.refs_2_.refs_1_.refs_6_, ...), custom_call_target="tpu_custom_call" | custom-call | flops 30000001024 | bytes 7970816 | tf_op jit(solution)/shard_map/base_own/pallas_call | solution.py:218
  53.6 1.8 %low_mate.1 = (bf16[288,128]{1,0:T(8,128)(2,1)S(1)}, bf16[288,1408]{1,0:T(8,128)(2,1)S(1)}) custom-call(bf16[2,304,1280]{2,1,0:T(8,128)(2,1)S(1)} %collective-permute-done.3.refs_0_.refs_4_, bf16[4,1792,128]{2,1,0:T(8,128)(2,1)S(1)} %pad_maximum_fusion.refs_4_.refs_1_.refs_2_, bf16[4,1792,128]{2,1,0:T(8,128)(2,1)S(1)} %collective-permute-done.6.refs_2_.refs_3_, ...), custom_call_target="tpu_custom_call" | custom-call | flops 1 | bytes 1 | tf_op jit(solution)/shard_map/low_mate/pallas_call | solution.py:218
  56.0 2.0 %low_own.1 = (f32[288,128]{1,0:T(8,128)S(1)}, bf16[512,1024]{1,0:T(8,128)(2,1)S(1)}) custom-call(bf16[288,1280]{1,0:T(8,128)(2,1)S(1)} %get-tuple-element.42.refs_3_.refs_0_.refs_5_, bf16[288,1408]{1,0:T(8,128)(2,1)S(1)} %get-tuple-element.41.refs_2_.refs_1_.refs_6_, bf16[4,1792,128]{2,1,0:T(8,128)(2,1)S(1)} %pad_maximum_fusion.refs_4_.refs_1_.refs_2_, ...), custom_call_target="tpu_custom_call" | custom-call | flops 1 | bytes 1 | tf_op jit(solution)/shard_map/low_own/pallas_call | solution.py:218
  58.0 2.1 %collective-permute-done.9.refs_7_ = bf16[288,512]{1,0:T(8,128)(2,1)S(1)} collective-permute-done((bf16[288,512]{1,0:T(8,128)(2,1)S(1)}, bf16[288,512]{1,0:T(8,128)(2,1)S(1)}, u32[]{:S(2)}, u32[]{:S(2)}) %collective-permute-start.9) | collective-permute-done | bytes 294944 | tf_op jit(solution)/shard_map/ppermute | solution.py:549
  60.2 0.8 collective-permute-done.7.refs_3_
  61.0 3.5 %keys.1 = (bf16[288,128]{1,0:T(8,128)(2,1)S(1)}, bf16[288,1024]{1,0:T(8,128)(2,1)S(1)}, bf16[288,512]{1,0:T(8,128)(2,1)S(1)}) custom-call(s32[4]{0:T(128)S(1)} %copy-done.11, bf16[288,1408]{1,0:T(8,128)(2,1)S(1)} %get-tuple-element.41.refs_2_.refs_1_.refs_6_, f32[288,128]{1,0:T(8,128)S(1)} %get-tuple-element.47.refs_2_, ...), custom_call_target="tpu_custom_call" | custom-call | flops 30000001024 | bytes 5399056 | tf_op jit(solution)/shard_map/keys/pallas_call | solution.py:218
  64.4 0.9 collective-permute-start.11
  65.4 1.9 %up_sums.1 = (f32[2,4,32,1024]{3,2,1,0:T(8,128)S(1)}, f32[2,4,32,1024]{3,2,1,0:T(8,128)S(1)}) custom-call(s32[4]{0:T(128)S(1)} %copy-done.11, bf16[288,512]{1,0:T(8,128)(2,1)S(1)} %get-tuple-element.51.refs_1_, bf16[288,1024]{1,0:T(8,128)(2,1)S(1)} %get-tuple-element.52.refs_2_), custom_call_target="tpu_custom_call" | custom-call | flops 30000001024 | bytes 2981904 | tf_op jit(solution)/shard_map/up_sums/pallas_call | solution.py:218
  67.3 1.6 %collective-permute-done.11.refs_1_ = bf16[288,128]{1,0:T(8,128)(2,1)S(1)} collective-permute-done((bf16[288,128]{1,0:T(8,128)(2,1)S(1)}, bf16[288,128]{1,0:T(8,128)(2,1)S(1)}, u32[]{:S(2)}, u32[]{:S(2)}) %collective-permute-start.11) | collective-permute-done | bytes 73760 | tf_op jit(solution)/shard_map/ppermute | solution.py:549
  70.1 3.0 %down.2 = (bf16[128,1280]{1,0:T(8,128)(2,1)S(1)}, bf16[128,1280]{1,0:T(8,128)(2,1)S(1)}) custom-call(bf16[288,128]{1,0:T(8,128)(2,1)S(1)} %get-tuple-element.50.refs_0_, bf16[288,128]{1,0:T(8,128)(2,1)S(1)} %collective-permute-done.11.refs_1_, bf16[288,128]{1,0:T(8,128)(2,1)S(1)} %collective-permute-done.12.refs_2_, ...), custom_call_target="tpu_custom_call" | custom-call | flops 30000001024 | bytes 5677056 | tf_op jit(solution)/shard_map/down/pallas_call | solution.py:218
  73.4 0.9 collective-permute-start.16
  74.4 3.4 %collective-permute-start.19 = (bf16[128,1280]{1,0:T(8,128)(2,1)S(1)}, bf16[128,1280]{1,0:T(8,128)(2,1)S(1)}, u32[]{:S(2)}, u32[]{:S(2)}) collective-permute-start(bf16[128,1280]{1,0:T(8,128)(2,1)S(1)} %get-tuple-element.57.refs_2_), channel_id=1, source_target_pairs={{0,12},{4,8},{8,4},{12,0},{1,13},{5,9},{9,5},{13,1},{2,14},{6,10},... | collective-permute-start | bytes 983048 | tf_op jit(solution)/shard_map/ppermute | solution.py:552
  77.8 4.4 %collective-permute-start.18 = (bf16[128,1280]{1,0:T(8,128)(2,1)S(1)}, bf16[128,1280]{1,0:T(8,128)(2,1)S(1)}, u32[]{:S(2)}, u32[]{:S(2)}) collective-permute-start(bf16[128,1280]{1,0:T(8,128)(2,1)S(1)} %get-tuple-element.61), channel_id=1, source_target_pairs={{0,8},{4,12},{8,0},{12,4},{1,9},{5,13},{9,1},{13,5},{2,10},{6,14},... | collective-permute-start | bytes 983048 | tf_op jit(solution)/shard_map/ppermute | solution.py:552
  82.2 2.8 %down.3 = (f32[128,1280]{1,0:T(8,128)S(1)}, bf16[128,1280]{1,0:T(8,128)(2,1)S(1)}) custom-call(bf16[288,128]{1,0:T(8,128)(2,1)S(1)} %get-tuple-element.50.refs_0_, bf16[288,128]{1,0:T(8,128)(2,1)S(1)} %collective-permute-done.11.refs_1_, bf16[288,128]{1,0:T(8,128)(2,1)S(1)} %collective-permute-done.12.refs_2_, ...), custom_call_target="tpu_custom_call" | custom-call | flops 30000001024 | bytes 6004736 | tf_op jit(solution)/shard_map/down/pallas_call | solution.py:218
  85.0 5.6 %collective-permute-start.17 = (bf16[128,1280]{1,0:T(8,128)(2,1)S(1)}, bf16[128,1280]{1,0:T(8,128)(2,1)S(1)}, u32[]{:S(2)}, u32[]{:S(2)}) collective-permute-start(bf16[128,1280]{1,0:T(8,128)(2,1)S(1)} %get-tuple-element.60.refs_2_), channel_id=1, source_target_pairs={{0,4},{4,0},{8,12},{12,8},{1,5},{5,1},{9,13},{13,9},{2,6},{6,2},{1... | collective-permute-start | bytes 983048 | tf_op jit(solution)/shard_map/ppermute | solution.py:552
  90.7 2.5 %collective-permute-start.20 = (bf16[32,1024]{1,0:T(8,128)(2,1)S(1)}, bf16[32,1024]{1,0:T(8,128)(2,1)S(1)}, u32[]{:S(2)}, u32[]{:S(2)}) collective-permute-start(bf16[32,1024]{1,0:T(8,128)(2,1)S(1)} %get-tuple-element.65), channel_id=1, source_target_pairs={{0,12},{4,8},{8,4},{12,0},{1,13},{5,9},{9,5},{13,1},{2,14},{6,10},... | collective-permute-start | bytes 196616 | tf_op jit(solution)/shard_map/ppermute | solution.py:552
  93.3 6.7 %collective-permute-done.17.refs_1_ = bf16[128,1280]{1,0:T(8,128)(2,1)S(1)} collective-permute-done((bf16[128,1280]{1,0:T(8,128)(2,1)S(1)}, bf16[128,1280]{1,0:T(8,128)(2,1)S(1)}, u32[]{:S(2)}, u32[]{:S(2)}) %collective-permute-start.17) | collective-permute-done | bytes 327712 | tf_op jit(solution)/shard_map/ppermute | solution.py:552
  100.0 2.5 %collective-permute-start.22 = (bf16[32,1024]{1,0:T(8,128)(2,1)S(1)}, bf16[32,1024]{1,0:T(8,128)(2,1)S(1)}, u32[]{:S(2)}, u32[]{:S(2)}) collective-permute-start(bf16[32,1024]{1,0:T(8,128)(2,1)S(1)} %get-tuple-element.68), channel_id=1, source_target_pairs={{0,4},{4,0},{8,12},{12,8},{1,5},{5,1},{9,13},{13,9},{2,6},{6,2},{1... | collective-permute-start | bytes 196616 | tf_op jit(solution)/shard_map/ppermute | solution.py:552
  102.5 7.2 %collective-permute-done.18.refs_2_ = bf16[128,1280]{1,0:T(8,128)(2,1)S(1)} collective-permute-done((bf16[128,1280]{1,0:T(8,128)(2,1)S(1)}, bf16[128,1280]{1,0:T(8,128)(2,1)S(1)}, u32[]{:S(2)}, u32[]{:S(2)}) %collective-permute-start.18) | collective-permute-done | bytes 327712 | tf_op jit(solution)/shard_map/ppermute | solution.py:552
  109.7 2.9 %update_down.1 = (f32[1280,128]{1,0:T(8,128)}, f32[1280,128]{1,0:T(8,128)}, f32[1280,128]{1,0:T(8,128)}) custom-call(f32[128,1280]{1,0:T(8,128)S(1)} %get-tuple-element.59.refs_0_, bf16[128,1280]{1,0:T(8,128)(2,1)S(1)} %collective-permute-done.17.refs_1_, bf16[128,1280]{1,0:T(8,128)(2,1)S(1)} %collective-permute-done.18.refs_2_, ...), custom_call_target="tpu_custom_call" | custom-call | flops 30000001024 | bytes 5570560 | tf_op jit(solution)/shard_map/update_down/pallas_call | solution.py:218
  113.4 2.0 %update_up.1 = (f32[32,1024]{1,0:T(8,128)}, f32[32,1024]{1,0:T(8,128)}, f32[32,1024]{1,0:T(8,128)}) custom-call(f32[32,1024]{1,0:T(8,128)} %copy-done.12, bf16[32,1024]{1,0:T(8,128)(2,1)} %copy-done.13, bf16[32,1024]{1,0:T(8,128)(2,1)} %copy-done.14, bf16[32,1024]{1,0:T(8,128)(2,1)} %copy-done.15, f32[32,1024]{1,0:T(8,128)} %bitcast.23, ...), custom_call_target="tpu_custom_call" | custom-call | flops 30000001024 | bytes 1114112 | tf_op jit(solution)/shard_map/update_up/pallas_call | solution.py:218
  (63 shorter events, 5.3 us)
Async XLA Ops:
  0.6 7.5 %copy-start.1 = (bf16[1280,1024]{1,0:T(8,128)(2,1)S(1)}, bf16[1280,1024]{1,0:T(8,128)(2,1)}, u32[]{:S(2)}) copy-start(bf16[1280,1024]{1,0:T(8,128)(2,1)} %refs_1_.9) | copy-start | bytes 7864324
  0.6 7.5 %copy-start.4 = (f32[1,1280,128]{2,1,0:T(8,128)S(1)}, f32[1,1280,128]{2,1,0:T(8,128)}, u32[]{:S(2)}) copy-start(f32[1,1280,128]{2,1,0:T(8,128)} %param.20) | copy-start | bytes 1966084
  0.7 7.5 %copy-start.7 = (f32[1,32,1024]{2,1,0:T(8,128)S(1)}, f32[1,32,1024]{2,1,0:T(8,128)}, u32[]{:S(2)}) copy-start(f32[1,32,1024]{2,1,0:T(8,128)} %param.21) | copy-start | bytes 393220
  0.7 7.5 %copy-start.11 = (s32[4]{0:T(128)S(1)}, s32[4]{0:T(128)}, u32[]{:S(2)}) copy-start(s32[4]{0:T(128)} %refs_0_.9) | copy-start | bytes 52
  0.7 7.4 %collective-permute-start = (f32[32,1024]{1,0:T(8,128)}, f32[32,1024]{1,0:T(8,128)S(1)}, u32[]{:S(2)}, u32[]{:S(2)}) collective-permute-start(f32[32,1024]{1,0:T(8,128)} %bitcast.22), channel_id=1, source_target_pairs={{0,2},{1,3},{2,0},{3,1},{4,6},{5,7},{6,4},{7,5},{8,10},{9,11},{10,... | collective-permute-start | bytes 393224 | tf_op jit(solution)/shard_map/ppermute | solution.py:549
  7.8 35.8 %collective-permute-start.3 = (bf16[2,304,1280]{2,1,0:T(8,128)(2,1)}, bf16[2,304,1280]{2,1,0:T(8,128)(2,1)S(1)}, u32[]{:S(2)}, u32[]{:S(2)}) collective-permute-start(bf16[2,304,1280]{2,1,0:T(8,128)(2,1)} %pack_sent.1.refs_4_), channel_id=1, source_target_pairs={{0,2},{1,3},{2,0},{3,1},{4,6},{5,7},{6,4},{7,5},{8,10},{9,11},{10,... | collective-permute-start | bytes 4669448 | tf_op jit(solution)/shard_map/ppermute | solution.py:549
  8.1 7.3 %collective-permute-start.1 = (bf16[1280,1024]{1,0:T(8,128)(2,1)S(1)}, bf16[1280,1024]{1,0:T(8,128)(2,1)S(1)}, u32[]{:S(2)}, u32[]{:S(2)}) collective-permute-start(bf16[1280,1024]{1,0:T(8,128)(2,1)S(1)} %copy-done.1), channel_id=1, source_target_pairs={{0,1},{1,0},{2,3},{3,2},{4,5},{5,4},{6,7},{7,6},{8,9},{9,8},{10,11... | collective-permute-start | bytes 7864328 | tf_op jit(solution)/shard_map/ppermute | solution.py:546
  9.6 5.9 %copy-start.8 = (s32[1,12]{1,0:T(1,128)S(1)}, s32[1,12]{1,0:T(1,128)}, u32[]{:S(2)}) copy-start(s32[1,12]{1,0:T(1,128)} %refs_0_.7) | copy-start | bytes 148
  9.6 5.9 %copy-start.9 = (s32[1,12]{1,0:T(1,128)S(1)}, s32[1,12]{1,0:T(1,128)}, u32[]{:S(2)}) copy-start(s32[1,12]{1,0:T(1,128)} %refs_1_.6) | copy-start | bytes 148
  10.8 38.7 %collective-permute-start.2 = (bf16[1792,128]{1,0:T(8,128)(2,1)S(1)}, bf16[1792,128]{1,0:T(8,128)(2,1)S(1)}, u32[]{:S(2)}, u32[]{:S(2)}) collective-permute-start(bf16[1792,128]{1,0:T(8,128)(2,1)S(1)} %weights.1.refs_4_), channel_id=1, source_target_pairs={{0,4},{4,0},{8,12},{12,8},{1,5},{5,1},{9,13},{13,9},{2,6},{6,2},{1... | collective-permute-start | bytes 1376264 | tf_op jit(solution)/shard_map/ppermute | solution.py:552
  12.8 36.7 %collective-permute-start.4 = (bf16[1792,128]{1,0:T(8,128)(2,1)S(1)}, bf16[1792,128]{1,0:T(8,128)(2,1)S(1)}, u32[]{:S(2)}, u32[]{:S(2)}) collective-permute-start(bf16[1792,128]{1,0:T(8,128)(2,1)S(1)} %weights.1.refs_4_), channel_id=1, source_target_pairs={{0,8},{4,12},{8,0},{12,4},{1,9},{5,13},{9,1},{13,5},{2,10},{6,14},... | collective-permute-start | bytes 1376264 | tf_op jit(solution)/shard_map/ppermute | solution.py:552
  15.4 34.1 %collective-permute-start.5 = (bf16[1792,128]{1,0:T(8,128)(2,1)S(1)}, bf16[1792,128]{1,0:T(8,128)(2,1)S(1)}, u32[]{:S(2)}, u32[]{:S(2)}) collective-permute-start(bf16[1792,128]{1,0:T(8,128)(2,1)S(1)} %weights.1.refs_4_), channel_id=1, source_target_pairs={{0,12},{4,8},{8,4},{12,0},{1,13},{5,9},{9,5},{13,1},{2,14},{6,10},... | collective-permute-start | bytes 1376264 | tf_op jit(solution)/shard_map/ppermute | solution.py:552
  45.4 14.7 %collective-permute-start.8 = (bf16[288,512]{1,0:T(8,128)(2,1)S(1)}, bf16[288,512]{1,0:T(8,128)(2,1)S(1)}, u32[]{:S(2)}, u32[]{:S(2)}) collective-permute-start(bf16[288,512]{1,0:T(8,128)(2,1)S(1)} %base_mate.2.refs_3_), channel_id=1, source_target_pairs={{0,2},{1,3},{2,0},{3,1},{4,6},{5,7},{6,4},{7,5},{8,10},{9,11},{10,... | collective-permute-start | bytes 884744 | tf_op jit(solution)/shard_map/ppermute | solution.py:549
  47.9 12.2 %collective-permute-start.9 = (bf16[288,512]{1,0:T(8,128)(2,1)S(1)}, bf16[288,512]{1,0:T(8,128)(2,1)S(1)}, u32[]{:S(2)}, u32[]{:S(2)}) collective-permute-start(bf16[288,512]{1,0:T(8,128)(2,1)S(1)} %base_mate.3), channel_id=1, source_target_pairs={{0,2},{1,3},{2,0},{3,1},{4,6},{5,7},{6,4},{7,5},{8,10},{9,11},{10,... | collective-permute-start | bytes 884744 | tf_op jit(solution)/shard_map/ppermute | solution.py:549
  49.7 3.9 %collective-permute-start.6 = (bf16[4,1792,128]{2,1,0:T(8,128)(2,1)S(1)}, bf16[4,1792,128]{2,1,0:T(8,128)(2,1)S(1)}, u32[]{:S(2)}, u32[]{:S(2)}) collective-permute-start(bf16[4,1792,128]{2,1,0:T(8,128)(2,1)S(1)} %pad_maximum_fusion.refs_4_.refs_1_.refs_2_), channel_id=1, source_target_pairs={{0,1},{1,0},{2,3},{3,2},{4,5},{5,4},{6,7},{7,6},{8,9},{9,8},{10,11... | collective-permute-start | bytes 5505032 | tf_op jit(solution)/shard_map/ppermute | solution.py:546
  49.8 10.4 %collective-permute-start.10 = (bf16[288,1408]{1,0:T(8,128)(2,1)S(1)}, bf16[288,1408]{1,0:T(8,128)(2,1)S(1)}, u32[]{:S(2)}, u32[]{:S(2)}) collective-permute-start(bf16[288,1408]{1,0:T(8,128)(2,1)S(1)} %get-tuple-element.41.refs_2_.refs_1_.refs_6_), channel_id=1, source_target_pairs={{0,1},{1,0},{2,3},{3,2},{4,5},{5,4},{6,7},{7,6},{8,9},{9,8},{10,11... | collective-permute-start | bytes 2433032 | tf_op jit(solution)/shard_map/ppermute | solution.py:546
  55.4 5.5 %collective-permute-start.7 = (bf16[288,128]{1,0:T(8,128)(2,1)S(1)}, bf16[288,128]{1,0:T(8,128)(2,1)S(1)}, u32[]{:S(2)}, u32[]{:S(2)}) collective-permute-start(bf16[288,128]{1,0:T(8,128)(2,1)S(1)} %get-tuple-element.46.refs_4_), channel_id=1, source_target_pairs={{0,2},{1,3},{2,0},{3,1},{4,6},{5,7},{6,4},{7,5},{8,10},{9,11},{10,... | collective-permute-start | bytes 221192 | tf_op jit(solution)/shard_map/ppermute | solution.py:549
  56.0 14.1 %collective-permute-start.14 = (bf16[288,1408]{1,0:T(8,128)(2,1)S(1)}, bf16[288,1408]{1,0:T(8,128)(2,1)S(1)}, u32[]{:S(2)}, u32[]{:S(2)}) collective-permute-start(bf16[288,1408]{1,0:T(8,128)(2,1)S(1)} %get-tuple-element.55), channel_id=1, source_target_pairs={{0,1},{1,0},{2,3},{3,2},{4,5},{5,4},{6,7},{7,6},{8,9},{9,8},{10,11... | collective-permute-start | bytes 2433032 | tf_op jit(solution)/shard_map/ppermute | solution.py:546
  64.4 4.4 %collective-permute-start.11 = (bf16[288,128]{1,0:T(8,128)(2,1)S(1)}, bf16[288,128]{1,0:T(8,128)(2,1)S(1)}, u32[]{:S(2)}, u32[]{:S(2)}) collective-permute-start(bf16[288,128]{1,0:T(8,128)(2,1)S(1)} %get-tuple-element.50.refs_0_), channel_id=1, source_target_pairs={{0,2},{1,3},{2,0},{3,1},{4,6},{5,7},{6,4},{7,5},{8,10},{9,11},{10,... | collective-permute-start | bytes 221192 | tf_op jit(solution)/shard_map/ppermute | solution.py:549
  65.4 4.0 %collective-permute-start.12 = (bf16[288,128]{1,0:T(8,128)(2,1)S(1)}, bf16[288,128]{1,0:T(8,128)(2,1)S(1)}, u32[]{:S(2)}, u32[]{:S(2)}) collective-permute-start(bf16[288,128]{1,0:T(8,128)(2,1)S(1)} %get-tuple-element.50.refs_0_), channel_id=1, source_target_pairs={{0,1},{1,0},{2,3},{3,2},{4,5},{5,4},{6,7},{7,6},{8,9},{9,8},{10,11... | collective-permute-start | bytes 221192 | tf_op jit(solution)/shard_map/ppermute | solution.py:546
  68.9 1.3 %collective-permute-start.13 = (bf16[288,128]{1,0:T(8,128)(2,1)S(1)}, bf16[288,128]{1,0:T(8,128)(2,1)S(1)}, u32[]{:S(2)}, u32[]{:S(2)}) collective-permute-start(bf16[288,128]{1,0:T(8,128)(2,1)S(1)} %collective-permute-done.11.refs_1_), channel_id=1, source_target_pairs={{0,1},{1,0},{2,3},{3,2},{4,5},{5,4},{6,7},{7,6},{8,9},{9,8},{10,11... | collective-permute-start | bytes 221192 | tf_op jit(solution)/shard_map/ppermute | solution.py:546
  68.9 4.3 %collective-permute-start.15 = (f32[2,4,32,1024]{3,2,1,0:T(8,128)S(1)}, f32[2,4,32,1024]{3,2,1,0:T(8,128)S(1)}, u32[]{:S(2)}, u32[]{:S(2)}) collective-permute-start(f32[2,4,32,1024]{3,2,1,0:T(8,128)S(1)} %get-tuple-element.56), channel_id=1, source_target_pairs={{0,1},{1,0},{2,3},{3,2},{4,5},{5,4},{6,7},{7,6},{8,9},{9,8},{10,11... | collective-permute-start | bytes 3145736 | tf_op jit(solution)/shard_map/ppermute | solution.py:546
  73.4 8.7 %collective-permute-start.16 = (bf16[4,32,1024]{2,1,0:T(8,128)(2,1)S(1)}, bf16[4,32,1024]{2,1,0:T(8,128)(2,1)S(1)}, u32[]{:S(2)}, u32[]{:S(2)}) collective-permute-start(bf16[4,32,1024]{2,1,0:T(8,128)(2,1)S(1)} %get-tuple-element.58), channel_id=1, source_target_pairs={{0,2},{1,3},{2,0},{3,1},{4,6},{5,7},{6,4},{7,5},{8,10},{9,11},{10,... | collective-permute-start | bytes 786440 | tf_op jit(solution)/shard_map/ppermute | solution.py:549
  74.4 35.3 %collective-permute-start.19 = (bf16[128,1280]{1,0:T(8,128)(2,1)S(1)}, bf16[128,1280]{1,0:T(8,128)(2,1)S(1)}, u32[]{:S(2)}, u32[]{:S(2)}) collective-permute-start(bf16[128,1280]{1,0:T(8,128)(2,1)S(1)} %get-tuple-element.57.refs_2_), channel_id=1, source_target_pairs={{0,12},{4,8},{8,4},{12,0},{1,13},{5,9},{9,5},{13,1},{2,14},{6,10},... | collective-permute-start | bytes 983048 | tf_op jit(solution)/shard_map/ppermute | solution.py:552
  77.8 31.9 %collective-permute-start.18 = (bf16[128,1280]{1,0:T(8,128)(2,1)S(1)}, bf16[128,1280]{1,0:T(8,128)(2,1)S(1)}, u32[]{:S(2)}, u32[]{:S(2)}) collective-permute-start(bf16[128,1280]{1,0:T(8,128)(2,1)S(1)} %get-tuple-element.61), channel_id=1, source_target_pairs={{0,8},{4,12},{8,0},{12,4},{1,9},{5,13},{9,1},{13,5},{2,10},{6,14},... | collective-permute-start | bytes 983048 | tf_op jit(solution)/shard_map/ppermute | solution.py:552
  85.0 15.0 %collective-permute-start.17 = (bf16[128,1280]{1,0:T(8,128)(2,1)S(1)}, bf16[128,1280]{1,0:T(8,128)(2,1)S(1)}, u32[]{:S(2)}, u32[]{:S(2)}) collective-permute-start(bf16[128,1280]{1,0:T(8,128)(2,1)S(1)} %get-tuple-element.60.refs_2_), channel_id=1, source_target_pairs={{0,4},{4,0},{8,12},{12,8},{1,5},{5,1},{9,13},{13,9},{2,6},{6,2},{1... | collective-permute-start | bytes 983048 | tf_op jit(solution)/shard_map/ppermute | solution.py:552
  90.6 19.1 %copy-start.5 = (f32[1,1280,128]{2,1,0:T(8,128)S(1)}, f32[1,1280,128]{2,1,0:T(8,128)}, u32[]{:S(2)}) copy-start(f32[1,1280,128]{2,1,0:T(8,128)} %param.22) | copy-start | bytes 1966084
  90.6 19.1 %copy-start.6 = (f32[1,1280,128]{2,1,0:T(8,128)S(1)}, f32[1,1280,128]{2,1,0:T(8,128)}, u32[]{:S(2)}) copy-start(f32[1,1280,128]{2,1,0:T(8,128)} %param.24) | copy-start | bytes 1966084
  90.7 21.9 %copy-start.12 = (f32[32,1024]{1,0:T(8,128)}, f32[32,1024]{1,0:T(8,128)S(1)}, u32[]{:S(2)}) copy-start(f32[32,1024]{1,0:T(8,128)S(1)} %get-tuple-element.64.refs_0_) | copy-start | bytes 393220
  90.7 21.9 %collective-permute-start.20 = (bf16[32,1024]{1,0:T(8,128)(2,1)S(1)}, bf16[32,1024]{1,0:T(8,128)(2,1)S(1)}, u32[]{:S(2)}, u32[]{:S(2)}) collective-permute-start(bf16[32,1024]{1,0:T(8,128)(2,1)S(1)} %get-tuple-element.65), channel_id=1, source_target_pairs={{0,12},{4,8},{8,4},{12,0},{1,13},{5,9},{9,5},{13,1},{2,14},{6,10},... | collective-permute-start | bytes 196616 | tf_op jit(solution)/shard_map/ppermute | solution.py:552
  93.3 19.4 %collective-permute-start.21 = (bf16[32,1024]{1,0:T(8,128)(2,1)S(1)}, bf16[32,1024]{1,0:T(8,128)(2,1)S(1)}, u32[]{:S(2)}, u32[]{:S(2)}) collective-permute-start(bf16[32,1024]{1,0:T(8,128)(2,1)S(1)} %get-tuple-element.66), channel_id=1, source_target_pairs={{0,8},{4,12},{8,0},{12,4},{1,9},{5,13},{9,1},{13,5},{2,10},{6,14},... | collective-permute-start | bytes 196616 | tf_op jit(solution)/shard_map/ppermute | solution.py:552
  100.0 12.7 %collective-permute-start.22 = (bf16[32,1024]{1,0:T(8,128)(2,1)S(1)}, bf16[32,1024]{1,0:T(8,128)(2,1)S(1)}, u32[]{:S(2)}, u32[]{:S(2)}) collective-permute-start(bf16[32,1024]{1,0:T(8,128)(2,1)S(1)} %get-tuple-element.68), channel_id=1, source_target_pairs={{0,4},{4,0},{8,12},{12,8},{1,5},{5,1},{9,13},{13,9},{2,6},{6,2},{1... | collective-permute-start | bytes 196616 | tf_op jit(solution)/shard_map/ppermute | solution.py:552
  (7 other events, 20.0 us)

commit v8 on v7

--- a/solution.py
+++ b/solution.py
@@ -371,13 +371,14 @@
     out[...] = total + mm(far.get()[:, :QUARTER], mate.get()[...])
 
 
-def low_own_kernel(near, far, weights, weights_core, out, up):
+def low_own_kernel(near, far, weights, weights_core, out, up, places_out):
     f = lax.axis_index("fsdp")
     c, x = f % 2, f // 2
     held = far.get()
     every = mm(near.get()[...], down_factors(weights))
     every = every + mm(held[:, :QUARTER], down_factors(weights_core))
     out[...] = own_adapter(every, held[:, QUARTER:])
+    places_out[...] = held[:, QUARTER:]
     for j in range(4):
         for part in range(2):
             for source, side in ((weights, c), (weights_core, 1 - c)):
@@ -403,13 +404,13 @@
     return jnp.concatenate(parts, axis=0)
 
 
-def keys_kernel(ranks, far, low, low_mate, up_late, base, left, right, grads, gain, *refs):
+def keys_kernel(ranks, places, low, low_mate, up_late, base, left, right, grads, gain, *refs):
     dlow_out, key_grads_out, wide_out = refs
     up = up_late.get()
     dp = lax.axis_index("dp")
     f = lax.axis_index("fsdp")
     c, x = f % 2, f // 2
-    ids = far.get()[:, QUARTER:]
+    ids = places.get()[...]
     adapter = ids.astype(f32)
     scales = [adapter_alpha_scale / jnp.full((1, HEAD), ranks[dp ^ j], i32).astype(f32) for j in range(4)]
     scale = jnp.zeros((LIVE, HEAD), f32)
@@ -631,12 +632,12 @@
         light=True,
     )
     low_mate, cross_core = across(low_sent), core(cross)
-    low, up = call(
+    low, up, places = call(
         low_own_kernel,
         "low_own",
         [],
         [near, far, weights, weights_core],
-        [shape((LIVE, PADDED_RANK), f32), shape((512, KEY_WIDTH), bf16)],
+        [shape((LIVE, PADDED_RANK), f32), shape((512, KEY_WIDTH), bf16), shape((LIVE, HEAD), bf16)],
         order=[low_sent],
         light=True,
     )
@@ -644,7 +645,7 @@
         keys_kernel,
         "keys",
         [ranks],
-        [far, low, low_mate, up, base, mate_left, mate_right, grads, key_norm_weight[None, :]],
+        [places, low, low_mate, up, base, mate_left, mate_right, grads, key_norm_weight[None, :]],
         [
             shape((LIVE, PADDED_RANK), bf16),
             shape((LIVE, KEY_WIDTH), bf16),

time: 116 us -> 116 us (level)
  no operation moved by 1% of the time
where the time goes in v8:
time: 116 us
  waiting for transfers between devices  44.8 us (39%)
  Pallas kernels  35.2 us (30%)
  starting transfers between devices  32.1 us (28%)
  local copies, waits for them, and re-layouts  2.11 us (2%)
    pallas_call x16, Pallas kernels, call(): pl.pallas_call(body, name=name, in_specs=[SMEM] * n + [HBM] * (m + p + d)...  35.2 us
    ppermute x7, waiting for transfers between devices, across(): return lax.ppermute(value, 'fsdp', [(i, i ^ 2) for i in range(4)])  29.6 us
    ppermute x9, starting transfers between devices, along(): return lax.ppermute(value, 'dp', [(i, i ^ distance) for i in range(4)])  23 us
    ppermute x9, waiting for transfers between devices, along(): return lax.ppermute(value, 'dp', [(i, i ^ distance) for i in range(4)])  14 us
    ppermute x7, starting transfers between devices, across(): return lax.ppermute(value, 'fsdp', [(i, i ^ 2) for i in range(4)])  7.92 us
  transfers between devices with their start and end apart: 23, of which 8 were waited for; matrix products, arithmetic and copies ran while one was open for 0% of the time, Pallas kernels for 28%

profile of v8, /device:TPU:0, one launch (start us, length us, event | category | flops | bytes accessed | tf_op | source)
XLA Modules:
  0.0 115.6 jit_solution(8307194515373713940)
XLA Ops:
  0.7 3.0 %collective-permute-start = (f32[32,1024]{1,0:T(8,128)}, f32[32,1024]{1,0:T(8,128)S(1)}, u32[]{:S(2)}, u32[]{:S(2)}) collective-permute-start(f32[32,1024]{1,0:T(8,128)} %bitcast.22), channel_id=1, source_target_pairs={{0,2},{1,3},{2,0},{3,1},{4,6},{5,7},{6,4},{7,5},{8,10},{9,11},{10,... | collective-permute-start | bytes 393224 | tf_op jit(solution)/shard_map/ppermute | solution.py:550
  3.7 4.1 %pack_sent.1.refs_4_ = bf16[2,304,1280]{2,1,0:T(8,128)(2,1)} custom-call(s32[1,12]{1,0:T(1,128)} %refs_0_.7, s32[1,12]{1,0:T(1,128)} %refs_1_.6, bf16[384,5120]{1,0:T(8,128)(2,1)} %refs_3_.1), custom_call_target="tpu_custom_call" | custom-call | flops 30000001024 | bytes 5488736 | tf_op jit(solution)/shard_map/pack_sent/pallas_call | solution.py:218
  8.1 1.4 %copy-done.2 = bf16[2,304,1280]{2,1,0:T(8,128)(2,1)S(1)} copy-done((bf16[2,304,1280]{2,1,0:T(8,128)(2,1)S(1)}, bf16[2,304,1280]{2,1,0:T(8,128)(2,1)}, u32[]{:S(2)}) %copy-start.2) | copy-done | bytes 1556504
  9.6 1.2 %weights.1.refs_4_ = bf16[1792,128]{1,0:T(8,128)(2,1)S(1)} custom-call(s32[4]{0:T(128)S(1)} %copy-done.11, f32[1280,128]{1,0:T(8,128)S(1)} %bitcast.18, f32[32,1024]{1,0:T(8,128)S(1)} %bitcast.24, f32[32,1024]{1,0:T(8,128)S(1)} %collective-permute-done.refs_3_, bf16[2,304,1280]{2,1,0:T(8,128)(2,1)S(1)} %copy-done.2), custom_call_target="tpu_custom_call" | custom-call | flops 30000001024 | bytes 1376272 | tf_op jit(solution)/shard_map/weights/pallas_call | solution.py:218
  10.8 2.1 %collective-permute-start.2 = (bf16[1792,128]{1,0:T(8,128)(2,1)S(1)}, bf16[1792,128]{1,0:T(8,128)(2,1)S(1)}, u32[]{:S(2)}, u32[]{:S(2)}) collective-permute-start(bf16[1792,128]{1,0:T(8,128)(2,1)S(1)} %weights.1.refs_4_), channel_id=1, source_target_pairs={{0,4},{4,0},{8,12},{12,8},{1,5},{5,1},{9,13},{13,9},{2,6},{6,2},{1... | collective-permute-start | bytes 1376264 | tf_op jit(solution)/shard_map/ppermute | solution.py:553
  12.8 2.6 %collective-permute-start.4 = (bf16[1792,128]{1,0:T(8,128)(2,1)S(1)}, bf16[1792,128]{1,0:T(8,128)(2,1)S(1)}, u32[]{:S(2)}, u32[]{:S(2)}) collective-permute-start(bf16[1792,128]{1,0:T(8,128)(2,1)S(1)} %weights.1.refs_4_), channel_id=1, source_target_pairs={{0,8},{4,12},{8,0},{12,4},{1,9},{5,13},{9,1},{13,5},{2,10},{6,14},... | collective-permute-start | bytes 1376264 | tf_op jit(solution)/shard_map/ppermute | solution.py:553
  15.4 3.1 %pack_kept.1 = (bf16[288,1280]{1,0:T(8,128)(2,1)S(1)}, bf16[288,1408]{1,0:T(8,128)(2,1)S(1)}, bf16[288,1024]{1,0:T(8,128)(2,1)S(1)}) custom-call(s32[1,12]{1,0:T(1,128)S(1)} %copy-done.8, s32[1,12]{1,0:T(1,128)S(1)} %copy-done.9, bf16[384,1024]{1,0:T(8,128)(2,1)S(1)} %copy-done.3, bf16[384,5120]{1,0:T(8,128)(2,1)S(1)} %copy-done, ...), custom_call_target="tpu_custom_call" | custom-call | flops 30000001024 | bytes 6856800 | tf_op jit(solution)/shard_map/pack_kept/pallas_call | solution.py:218
  18.5 25.0 %collective-permute-done.3.refs_0_.refs_4_ = bf16[2,304,1280]{2,1,0:T(8,128)(2,1)S(1)} collective-permute-done((bf16[2,304,1280]{2,1,0:T(8,128)(2,1)}, bf16[2,304,1280]{2,1,0:T(8,128)(2,1)S(1)}, u32[]{:S(2)}, u32[]{:S(2)}) %collective-permute-start.3) | collective-permute-done | bytes 1556512 | tf_op jit(solution)/shard_map/ppermute | solution.py:550
  43.5 1.9 %base_mate.2.refs_3_ = bf16[288,512]{1,0:T(8,128)(2,1)S(1)} custom-call(bf16[2,304,1280]{2,1,0:T(8,128)(2,1)S(1)} %collective-permute-done.3.refs_0_.refs_4_, bf16[1280,1024]{1,0:T(8,128)(2,1)S(1)} %copy-done.1, bf16[1280,1024]{1,0:T(8,128)(2,1)S(1)} %collective-permute-done.1.refs_5_.refs_2_.refs_3_, ...), custom_call_target="tpu_custom_call" | custom-call | flops 30000001024 | bytes 7094272 | tf_op jit(solution)/shard_map/base_mate/pallas_call | solution.py:218
  46.0 1.9 %base_mate.3 = bf16[288,512]{1,0:T(8,128)(2,1)S(1)} custom-call(bf16[2,304,1280]{2,1,0:T(8,128)(2,1)S(1)} %collective-permute-done.3.refs_0_.refs_4_, bf16[1280,1024]{1,0:T(8,128)(2,1)S(1)} %copy-done.1, bf16[1280,1024]{1,0:T(8,128)(2,1)S(1)} %collective-permute-done.1.refs_5_.refs_2_.refs_3_, bf16[288,512]{1,0:T(8,128)(2,1)S(1)} %base_mate.2.refs_3_), custom_call_target="tpu_custom_call" | custom-call | flops 30000001024 | bytes 7094272 | tf_op jit(solution)/shard_map/base_mate/pallas_call | solution.py:218
  47.9 1.6 %collective-permute-start.9 = (bf16[288,512]{1,0:T(8,128)(2,1)S(1)}, bf16[288,512]{1,0:T(8,128)(2,1)S(1)}, u32[]{:S(2)}, u32[]{:S(2)}) collective-permute-start(bf16[288,512]{1,0:T(8,128)(2,1)S(1)} %base_mate.3), channel_id=1, source_target_pairs={{0,2},{1,3},{2,0},{3,1},{4,6},{5,7},{6,4},{7,5},{8,10},{9,11},{10,... | collective-permute-start | bytes 884744 | tf_op jit(solution)/shard_map/ppermute | solution.py:550
  50.3 2.7 %base_own.1.refs_3_.refs_5_ = f32[288,1024]{1,0:T(8,128)S(1)} custom-call(bf16[288,1280]{1,0:T(8,128)(2,1)S(1)} %get-tuple-element.42.refs_3_.refs_0_.refs_5_, bf16[1280,1024]{1,0:T(8,128)(2,1)S(1)} %copy-done.1, bf16[288,1408]{1,0:T(8,128)(2,1)S(1)} %get-tuple-element.43.refs_2_.refs_1_.refs_6_, ...), custom_call_target="tpu_custom_call" | custom-call | flops 30000001024 | bytes 7970816 | tf_op jit(solution)/shard_map/base_own/pallas_call | solution.py:218
  53.6 1.8 %low_mate.1 = (bf16[288,128]{1,0:T(8,128)(2,1)S(1)}, bf16[288,1408]{1,0:T(8,128)(2,1)S(1)}) custom-call(bf16[2,304,1280]{2,1,0:T(8,128)(2,1)S(1)} %collective-permute-done.3.refs_0_.refs_4_, bf16[4,1792,128]{2,1,0:T(8,128)(2,1)S(1)} %pad_maximum_fusion.refs_4_.refs_1_.refs_2_, bf16[4,1792,128]{2,1,0:T(8,128)(2,1)S(1)} %collective-permute-done.6.refs_2_.refs_3_, ...), custom_call_target="tpu_custom_call" | custom-call | flops 1 | bytes 1 | tf_op jit(solution)/shard_map/low_mate/pallas_call | solution.py:218
  56.0 2.0 %low_own.1 = (f32[288,128]{1,0:T(8,128)S(1)}, bf16[512,1024]{1,0:T(8,128)(2,1)S(1)}, bf16[288,128]{1,0:T(8,128)(2,1)S(1)}) custom-call(bf16[288,1280]{1,0:T(8,128)(2,1)S(1)} %get-tuple-element.42.refs_3_.refs_0_.refs_5_, bf16[288,1408]{1,0:T(8,128)(2,1)S(1)} %get-tuple-element.43.refs_2_.refs_1_.refs_6_, ...), custom_call_target="tpu_custom_call" | custom-call | flops 1 | bytes 1 | tf_op jit(solution)/shard_map/low_own/pallas_call | solution.py:218
  58.0 2.1 %collective-permute-done.9.refs_7_ = bf16[288,512]{1,0:T(8,128)(2,1)S(1)} collective-permute-done((bf16[288,512]{1,0:T(8,128)(2,1)S(1)}, bf16[288,512]{1,0:T(8,128)(2,1)S(1)}, u32[]{:S(2)}, u32[]{:S(2)}) %collective-permute-start.9) | collective-permute-done | bytes 294944 | tf_op jit(solution)/shard_map/ppermute | solution.py:550
  60.2 0.8 collective-permute-done.7.refs_3_
  61.0 3.5 %keys.1 = (bf16[288,128]{1,0:T(8,128)(2,1)S(1)}, bf16[288,1024]{1,0:T(8,128)(2,1)S(1)}, bf16[288,512]{1,0:T(8,128)(2,1)S(1)}) custom-call(s32[4]{0:T(128)S(1)} %copy-done.11, bf16[288,128]{1,0:T(8,128)(2,1)S(1)} %get-tuple-element.48.refs_1_, f32[288,128]{1,0:T(8,128)S(1)} %get-tuple-element.49.refs_2_, bf16[288,128]{1,0:T(8,128)(2,1)S(1)} %collective-permute-done.7.refs_3_, ...), custom_call_target="tpu_custom_call" | custom-call | flops 30000001024 | bytes 4661776 | tf_op jit(solution)/shard_map/keys/pallas_call | solution.py:218
  64.4 0.9 collective-permute-start.11
  65.4 1.9 %up_sums.1 = (f32[2,4,32,1024]{3,2,1,0:T(8,128)S(1)}, f32[2,4,32,1024]{3,2,1,0:T(8,128)S(1)}) custom-call(s32[4]{0:T(128)S(1)} %copy-done.11, bf16[288,512]{1,0:T(8,128)(2,1)S(1)} %get-tuple-element.53.refs_1_, bf16[288,1024]{1,0:T(8,128)(2,1)S(1)} %get-tuple-element.54.refs_2_), custom_call_target="tpu_custom_call" | custom-call | flops 30000001024 | bytes 2981904 | tf_op jit(solution)/shard_map/up_sums/pallas_call | solution.py:218
  67.3 1.6 %collective-permute-done.11.refs_1_ = bf16[288,128]{1,0:T(8,128)(2,1)S(1)} collective-permute-done((bf16[288,128]{1,0:T(8,128)(2,1)S(1)}, bf16[288,128]{1,0:T(8,128)(2,1)S(1)}, u32[]{:S(2)}, u32[]{:S(2)}) %collective-permute-start.11) | collective-permute-done | bytes 73760 | tf_op jit(solution)/shard_map/ppermute | solution.py:550
  70.1 3.0 %down.2 = (bf16[128,1280]{1,0:T(8,128)(2,1)S(1)}, bf16[128,1280]{1,0:T(8,128)(2,1)S(1)}) custom-call(bf16[288,128]{1,0:T(8,128)(2,1)S(1)} %get-tuple-element.52.refs_0_, bf16[288,128]{1,0:T(8,128)(2,1)S(1)} %collective-permute-done.11.refs_1_, bf16[288,128]{1,0:T(8,128)(2,1)S(1)} %collective-permute-done.12.refs_2_, ...), custom_call_target="tpu_custom_call" | custom-call | flops 30000001024 | bytes 5677056 | tf_op jit(solution)/shard_map/down/pallas_call | solution.py:218
  73.5 0.9 collective-permute-start.16
  74.4 3.4 %collective-permute-start.19 = (bf16[128,1280]{1,0:T(8,128)(2,1)S(1)}, bf16[128,1280]{1,0:T(8,128)(2,1)S(1)}, u32[]{:S(2)}, u32[]{:S(2)}) collective-permute-start(bf16[128,1280]{1,0:T(8,128)(2,1)S(1)} %get-tuple-element.59.refs_2_), channel_id=1, source_target_pairs={{0,12},{4,8},{8,4},{12,0},{1,13},{5,9},{9,5},{13,1},{2,14},{6,10},... | collective-permute-start | bytes 983048 | tf_op jit(solution)/shard_map/ppermute | solution.py:553
  77.8 4.4 %collective-permute-start.18 = (bf16[128,1280]{1,0:T(8,128)(2,1)S(1)}, bf16[128,1280]{1,0:T(8,128)(2,1)S(1)}, u32[]{:S(2)}, u32[]{:S(2)}) collective-permute-start(bf16[128,1280]{1,0:T(8,128)(2,1)S(1)} %get-tuple-element.63), channel_id=1, source_target_pairs={{0,8},{4,12},{8,0},{12,4},{1,9},{5,13},{9,1},{13,5},{2,10},{6,14},... | collective-permute-start | bytes 983048 | tf_op jit(solution)/shard_map/ppermute | solution.py:553
  82.2 2.8 %down.3 = (f32[128,1280]{1,0:T(8,128)S(1)}, bf16[128,1280]{1,0:T(8,128)(2,1)S(1)}) custom-call(bf16[288,128]{1,0:T(8,128)(2,1)S(1)} %get-tuple-element.52.refs_0_, bf16[288,128]{1,0:T(8,128)(2,1)S(1)} %collective-permute-done.11.refs_1_, bf16[288,128]{1,0:T(8,128)(2,1)S(1)} %collective-permute-done.12.refs_2_, ...), custom_call_target="tpu_custom_call" | custom-call | flops 30000001024 | bytes 6004736 | tf_op jit(solution)/shard_map/down/pallas_call | solution.py:218
  85.0 5.6 %collective-permute-start.17 = (bf16[128,1280]{1,0:T(8,128)(2,1)S(1)}, bf16[128,1280]{1,0:T(8,128)(2,1)S(1)}, u32[]{:S(2)}, u32[]{:S(2)}) collective-permute-start(bf16[128,1280]{1,0:T(8,128)(2,1)S(1)} %get-tuple-element.62.refs_2_), channel_id=1, source_target_pairs={{0,4},{4,0},{8,12},{12,8},{1,5},{5,1},{9,13},{13,9},{2,6},{6,2},{1... | collective-permute-start | bytes 983048 | tf_op jit(solution)/shard_map/ppermute | solution.py:553
  90.7 2.5 %collective-permute-start.20 = (bf16[32,1024]{1,0:T(8,128)(2,1)S(1)}, bf16[32,1024]{1,0:T(8,128)(2,1)S(1)}, u32[]{:S(2)}, u32[]{:S(2)}) collective-permute-start(bf16[32,1024]{1,0:T(8,128)(2,1)S(1)} %get-tuple-element.67), channel_id=1, source_target_pairs={{0,12},{4,8},{8,4},{12,0},{1,13},{5,9},{9,5},{13,1},{2,14},{6,10},... | collective-permute-start | bytes 196616 | tf_op jit(solution)/shard_map/ppermute | solution.py:553
  93.3 6.7 %collective-permute-done.17.refs_1_ = bf16[128,1280]{1,0:T(8,128)(2,1)S(1)} collective-permute-done((bf16[128,1280]{1,0:T(8,128)(2,1)S(1)}, bf16[128,1280]{1,0:T(8,128)(2,1)S(1)}, u32[]{:S(2)}, u32[]{:S(2)}) %collective-permute-start.17) | collective-permute-done | bytes 327712 | tf_op jit(solution)/shard_map/ppermute | solution.py:553
  100.0 2.5 %collective-permute-start.22 = (bf16[32,1024]{1,0:T(8,128)(2,1)S(1)}, bf16[32,1024]{1,0:T(8,128)(2,1)S(1)}, u32[]{:S(2)}, u32[]{:S(2)}) collective-permute-start(bf16[32,1024]{1,0:T(8,128)(2,1)S(1)} %get-tuple-element.70), channel_id=1, source_target_pairs={{0,4},{4,0},{8,12},{12,8},{1,5},{5,1},{9,13},{13,9},{2,6},{6,2},{1... | collective-permute-start | bytes 196616 | tf_op jit(solution)/shard_map/ppermute | solution.py:553
  102.5 7.2 %collective-permute-done.18.refs_2_ = bf16[128,1280]{1,0:T(8,128)(2,1)S(1)} collective-permute-done((bf16[128,1280]{1,0:T(8,128)(2,1)S(1)}, bf16[128,1280]{1,0:T(8,128)(2,1)S(1)}, u32[]{:S(2)}, u32[]{:S(2)}) %collective-permute-start.18) | collective-permute-done | bytes 327712 | tf_op jit(solution)/shard_map/ppermute | solution.py:553
  109.7 2.9 %update_down.1 = (f32[1280,128]{1,0:T(8,128)}, f32[1280,128]{1,0:T(8,128)}, f32[1280,128]{1,0:T(8,128)}) custom-call(f32[128,1280]{1,0:T(8,128)S(1)} %get-tuple-element.61.refs_0_, bf16[128,1280]{1,0:T(8,128)(2,1)S(1)} %collective-permute-done.17.refs_1_, bf16[128,1280]{1,0:T(8,128)(2,1)S(1)} %collective-permute-done.18.refs_2_, ...), custom_call_target="tpu_custom_call" | custom-call | flops 30000001024 | bytes 5570560 | tf_op jit(solution)/shard_map/update_down/pallas_call | solution.py:218
  113.4 2.0 %update_up.1 = (f32[32,1024]{1,0:T(8,128)}, f32[32,1024]{1,0:T(8,128)}, f32[32,1024]{1,0:T(8,128)}) custom-call(f32[32,1024]{1,0:T(8,128)} %copy-done.12, bf16[32,1024]{1,0:T(8,128)(2,1)} %copy-done.13, bf16[32,1024]{1,0:T(8,128)(2,1)} %copy-done.14, bf16[32,1024]{1,0:T(8,128)(2,1)} %copy-done.15, f32[32,1024]{1,0:T(8,128)} %bitcast.23, ...), custom_call_target="tpu_custom_call" | custom-call | flops 30000001024 | bytes 1114112 | tf_op jit(solution)/shard_map/update_up/pallas_call | solution.py:218
  (63 shorter events, 5.3 us)
Async XLA Ops:
  0.6 7.5 %copy-start.1 = (bf16[1280,1024]{1,0:T(8,128)(2,1)S(1)}, bf16[1280,1024]{1,0:T(8,128)(2,1)}, u32[]{:S(2)}) copy-start(bf16[1280,1024]{1,0:T(8,128)(2,1)} %refs_1_.9) | copy-start | bytes 7864324
  0.6 7.5 %copy-start.4 = (f32[1,1280,128]{2,1,0:T(8,128)S(1)}, f32[1,1280,128]{2,1,0:T(8,128)}, u32[]{:S(2)}) copy-start(f32[1,1280,128]{2,1,0:T(8,128)} %param.20) | copy-start | bytes 1966084
  0.7 7.5 %copy-start.7 = (f32[1,32,1024]{2,1,0:T(8,128)S(1)}, f32[1,32,1024]{2,1,0:T(8,128)}, u32[]{:S(2)}) copy-start(f32[1,32,1024]{2,1,0:T(8,128)} %param.21) | copy-start | bytes 393220
  0.7 7.5 %copy-start.11 = (s32[4]{0:T(128)S(1)}, s32[4]{0:T(128)}, u32[]{:S(2)}) copy-start(s32[4]{0:T(128)} %refs_0_.9) | copy-start | bytes 52
  0.7 7.4 %collective-permute-start = (f32[32,1024]{1,0:T(8,128)}, f32[32,1024]{1,0:T(8,128)S(1)}, u32[]{:S(2)}, u32[]{:S(2)}) collective-permute-start(f32[32,1024]{1,0:T(8,128)} %bitcast.22), channel_id=1, source_target_pairs={{0,2},{1,3},{2,0},{3,1},{4,6},{5,7},{6,4},{7,5},{8,10},{9,11},{10,... | collective-permute-start | bytes 393224 | tf_op jit(solution)/shard_map/ppermute | solution.py:550
  7.8 35.8 %collective-permute-start.3 = (bf16[2,304,1280]{2,1,0:T(8,128)(2,1)}, bf16[2,304,1280]{2,1,0:T(8,128)(2,1)S(1)}, u32[]{:S(2)}, u32[]{:S(2)}) collective-permute-start(bf16[2,304,1280]{2,1,0:T(8,128)(2,1)} %pack_sent.1.refs_4_), channel_id=1, source_target_pairs={{0,2},{1,3},{2,0},{3,1},{4,6},{5,7},{6,4},{7,5},{8,10},{9,11},{10,... | collective-permute-start | bytes 4669448 | tf_op jit(solution)/shard_map/ppermute | solution.py:550
  8.1 7.3 %collective-permute-start.1 = (bf16[1280,1024]{1,0:T(8,128)(2,1)S(1)}, bf16[1280,1024]{1,0:T(8,128)(2,1)S(1)}, u32[]{:S(2)}, u32[]{:S(2)}) collective-permute-start(bf16[1280,1024]{1,0:T(8,128)(2,1)S(1)} %copy-done.1), channel_id=1, source_target_pairs={{0,1},{1,0},{2,3},{3,2},{4,5},{5,4},{6,7},{7,6},{8,9},{9,8},{10,11... | collective-permute-start | bytes 7864328 | tf_op jit(solution)/shard_map/ppermute | solution.py:547
  9.6 5.9 %copy-start.8 = (s32[1,12]{1,0:T(1,128)S(1)}, s32[1,12]{1,0:T(1,128)}, u32[]{:S(2)}) copy-start(s32[1,12]{1,0:T(1,128)} %refs_0_.7) | copy-start | bytes 148
  9.6 5.9 %copy-start.9 = (s32[1,12]{1,0:T(1,128)S(1)}, s32[1,12]{1,0:T(1,128)}, u32[]{:S(2)}) copy-start(s32[1,12]{1,0:T(1,128)} %refs_1_.6) | copy-start | bytes 148
  10.8 38.7 %collective-permute-start.2 = (bf16[1792,128]{1,0:T(8,128)(2,1)S(1)}, bf16[1792,128]{1,0:T(8,128)(2,1)S(1)}, u32[]{:S(2)}, u32[]{:S(2)}) collective-permute-start(bf16[1792,128]{1,0:T(8,128)(2,1)S(1)} %weights.1.refs_4_), channel_id=1, source_target_pairs={{0,4},{4,0},{8,12},{12,8},{1,5},{5,1},{9,13},{13,9},{2,6},{6,2},{1... | collective-permute-start | bytes 1376264 | tf_op jit(solution)/shard_map/ppermute | solution.py:553
  12.8 36.7 %collective-permute-start.4 = (bf16[1792,128]{1,0:T(8,128)(2,1)S(1)}, bf16[1792,128]{1,0:T(8,128)(2,1)S(1)}, u32[]{:S(2)}, u32[]{:S(2)}) collective-permute-start(bf16[1792,128]{1,0:T(8,128)(2,1)S(1)} %weights.1.refs_4_), channel_id=1, source_target_pairs={{0,8},{4,12},{8,0},{12,4},{1,9},{5,13},{9,1},{13,5},{2,10},{6,14},... | collective-permute-start | bytes 1376264 | tf_op jit(solution)/shard_map/ppermute | solution.py:553
  15.4 34.1 %collective-permute-start.5 = (bf16[1792,128]{1,0:T(8,128)(2,1)S(1)}, bf16[1792,128]{1,0:T(8,128)(2,1)S(1)}, u32[]{:S(2)}, u32[]{:S(2)}) collective-permute-start(bf16[1792,128]{1,0:T(8,128)(2,1)S(1)} %weights.1.refs_4_), channel_id=1, source_target_pairs={{0,12},{4,8},{8,4},{12,0},{1,13},{5,9},{9,5},{13,1},{2,14},{6,10},... | collective-permute-start | bytes 1376264 | tf_op jit(solution)/shard_map/ppermute | solution.py:553
  45.4 14.7 %collective-permute-start.8 = (bf16[288,512]{1,0:T(8,128)(2,1)S(1)}, bf16[288,512]{1,0:T(8,128)(2,1)S(1)}, u32[]{:S(2)}, u32[]{:S(2)}) collective-permute-start(bf16[288,512]{1,0:T(8,128)(2,1)S(1)} %base_mate.2.refs_3_), channel_id=1, source_target_pairs={{0,2},{1,3},{2,0},{3,1},{4,6},{5,7},{6,4},{7,5},{8,10},{9,11},{10,... | collective-permute-start | bytes 884744 | tf_op jit(solution)/shard_map/ppermute | solution.py:550
  47.9 12.2 %collective-permute-start.9 = (bf16[288,512]{1,0:T(8,128)(2,1)S(1)}, bf16[288,512]{1,0:T(8,128)(2,1)S(1)}, u32[]{:S(2)}, u32[]{:S(2)}) collective-permute-start(bf16[288,512]{1,0:T(8,128)(2,1)S(1)} %base_mate.3), channel_id=1, source_target_pairs={{0,2},{1,3},{2,0},{3,1},{4,6},{5,7},{6,4},{7,5},{8,10},{9,11},{10,... | collective-permute-start | bytes 884744 | tf_op jit(solution)/shard_map/ppermute | solution.py:550
  49.7 3.9 %collective-permute-start.6 = (bf16[4,1792,128]{2,1,0:T(8,128)(2,1)S(1)}, bf16[4,1792,128]{2,1,0:T(8,128)(2,1)S(1)}, u32[]{:S(2)}, u32[]{:S(2)}) collective-permute-start(bf16[4,1792,128]{2,1,0:T(8,128)(2,1)S(1)} %pad_maximum_fusion.refs_4_.refs_1_.refs_2_), channel_id=1, source_target_pairs={{0,1},{1,0},{2,3},{3,2},{4,5},{5,4},{6,7},{7,6},{8,9},{9,8},{10,11... | collective-permute-start | bytes 5505032 | tf_op jit(solution)/shard_map/ppermute | solution.py:547
  49.8 10.4 %collective-permute-start.10 = (bf16[288,1408]{1,0:T(8,128)(2,1)S(1)}, bf16[288,1408]{1,0:T(8,128)(2,1)S(1)}, u32[]{:S(2)}, u32[]{:S(2)}) collective-permute-start(bf16[288,1408]{1,0:T(8,128)(2,1)S(1)} %get-tuple-element.43.refs_2_.refs_1_.refs_6_), channel_id=1, source_target_pairs={{0,1},{1,0},{2,3},{3,2},{4,5},{5,4},{6,7},{7,6},{8,9},{9,8},{10,11... | collective-permute-start | bytes 2433032 | tf_op jit(solution)/shard_map/ppermute | solution.py:547
  55.4 5.5 %collective-permute-start.7 = (bf16[288,128]{1,0:T(8,128)(2,1)S(1)}, bf16[288,128]{1,0:T(8,128)(2,1)S(1)}, u32[]{:S(2)}, u32[]{:S(2)}) collective-permute-start(bf16[288,128]{1,0:T(8,128)(2,1)S(1)} %get-tuple-element.47.refs_4_), channel_id=1, source_target_pairs={{0,2},{1,3},{2,0},{3,1},{4,6},{5,7},{6,4},{7,5},{8,10},{9,11},{10,... | collective-permute-start | bytes 221192 | tf_op jit(solution)/shard_map/ppermute | solution.py:550
  56.0 14.1 %collective-permute-start.14 = (bf16[288,1408]{1,0:T(8,128)(2,1)S(1)}, bf16[288,1408]{1,0:T(8,128)(2,1)S(1)}, u32[]{:S(2)}, u32[]{:S(2)}) collective-permute-start(bf16[288,1408]{1,0:T(8,128)(2,1)S(1)} %get-tuple-element.57), channel_id=1, source_target_pairs={{0,1},{1,0},{2,3},{3,2},{4,5},{5,4},{6,7},{7,6},{8,9},{9,8},{10,11... | collective-permute-start | bytes 2433032 | tf_op jit(solution)/shard_map/ppermute | solution.py:547
  64.4 4.4 %collective-permute-start.11 = (bf16[288,128]{1,0:T(8,128)(2,1)S(1)}, bf16[288,128]{1,0:T(8,128)(2,1)S(1)}, u32[]{:S(2)}, u32[]{:S(2)}) collective-permute-start(bf16[288,128]{1,0:T(8,128)(2,1)S(1)} %get-tuple-element.52.refs_0_), channel_id=1, source_target_pairs={{0,2},{1,3},{2,0},{3,1},{4,6},{5,7},{6,4},{7,5},{8,10},{9,11},{10,... | collective-permute-start | bytes 221192 | tf_op jit(solution)/shard_map/ppermute | solution.py:550
  65.4 4.0 %collective-permute-start.12 = (bf16[288,128]{1,0:T(8,128)(2,1)S(1)}, bf16[288,128]{1,0:T(8,128)(2,1)S(1)}, u32[]{:S(2)}, u32[]{:S(2)}) collective-permute-start(bf16[288,128]{1,0:T(8,128)(2,1)S(1)} %get-tuple-element.52.refs_0_), channel_id=1, source_target_pairs={{0,1},{1,0},{2,3},{3,2},{4,5},{5,4},{6,7},{7,6},{8,9},{9,8},{10,11... | collective-permute-start | bytes 221192 | tf_op jit(solution)/shard_map/ppermute | solution.py:547
  68.9 1.3 %collective-permute-start.13 = (bf16[288,128]{1,0:T(8,128)(2,1)S(1)}, bf16[288,128]{1,0:T(8,128)(2,1)S(1)}, u32[]{:S(2)}, u32[]{:S(2)}) collective-permute-start(bf16[288,128]{1,0:T(8,128)(2,1)S(1)} %collective-permute-done.11.refs_1_), channel_id=1, source_target_pairs={{0,1},{1,0},{2,3},{3,2},{4,5},{5,4},{6,7},{7,6},{8,9},{9,8},{10,11... | collective-permute-start | bytes 221192 | tf_op jit(solution)/shard_map/ppermute | solution.py:547
  68.9 4.3 %collective-permute-start.15 = (f32[2,4,32,1024]{3,2,1,0:T(8,128)S(1)}, f32[2,4,32,1024]{3,2,1,0:T(8,128)S(1)}, u32[]{:S(2)}, u32[]{:S(2)}) collective-permute-start(f32[2,4,32,1024]{3,2,1,0:T(8,128)S(1)} %get-tuple-element.58), channel_id=1, source_target_pairs={{0,1},{1,0},{2,3},{3,2},{4,5},{5,4},{6,7},{7,6},{8,9},{9,8},{10,11... | collective-permute-start | bytes 3145736 | tf_op jit(solution)/shard_map/ppermute | solution.py:547
  73.5 8.7 %collective-permute-start.16 = (bf16[4,32,1024]{2,1,0:T(8,128)(2,1)S(1)}, bf16[4,32,1024]{2,1,0:T(8,128)(2,1)S(1)}, u32[]{:S(2)}, u32[]{:S(2)}) collective-permute-start(bf16[4,32,1024]{2,1,0:T(8,128)(2,1)S(1)} %get-tuple-element.60), channel_id=1, source_target_pairs={{0,2},{1,3},{2,0},{3,1},{4,6},{5,7},{6,4},{7,5},{8,10},{9,11},{10,... | collective-permute-start | bytes 786440 | tf_op jit(solution)/shard_map/ppermute | solution.py:550
  74.4 35.3 %collective-permute-start.19 = (bf16[128,1280]{1,0:T(8,128)(2,1)S(1)}, bf16[128,1280]{1,0:T(8,128)(2,1)S(1)}, u32[]{:S(2)}, u32[]{:S(2)}) collective-permute-start(bf16[128,1280]{1,0:T(8,128)(2,1)S(1)} %get-tuple-element.59.refs_2_), channel_id=1, source_target_pairs={{0,12},{4,8},{8,4},{12,0},{1,13},{5,9},{9,5},{13,1},{2,14},{6,10},... | collective-permute-start | bytes 983048 | tf_op jit(solution)/shard_map/ppermute | solution.py:553
  77.8 31.9 %collective-permute-start.18 = (bf16[128,1280]{1,0:T(8,128)(2,1)S(1)}, bf16[128,1280]{1,0:T(8,128)(2,1)S(1)}, u32[]{:S(2)}, u32[]{:S(2)}) collective-permute-start(bf16[128,1280]{1,0:T(8,128)(2,1)S(1)} %get-tuple-element.63), channel_id=1, source_target_pairs={{0,8},{4,12},{8,0},{12,4},{1,9},{5,13},{9,1},{13,5},{2,10},{6,14},... | collective-permute-start | bytes 983048 | tf_op jit(solution)/shard_map/ppermute | solution.py:553
  85.0 15.0 %collective-permute-start.17 = (bf16[128,1280]{1,0:T(8,128)(2,1)S(1)}, bf16[128,1280]{1,0:T(8,128)(2,1)S(1)}, u32[]{:S(2)}, u32[]{:S(2)}) collective-permute-start(bf16[128,1280]{1,0:T(8,128)(2,1)S(1)} %get-tuple-element.62.refs_2_), channel_id=1, source_target_pairs={{0,4},{4,0},{8,12},{12,8},{1,5},{5,1},{9,13},{13,9},{2,6},{6,2},{1... | collective-permute-start | bytes 983048 | tf_op jit(solution)/shard_map/ppermute | solution.py:553
  90.6 19.1 %copy-start.5 = (f32[1,1280,128]{2,1,0:T(8,128)S(1)}, f32[1,1280,128]{2,1,0:T(8,128)}, u32[]{:S(2)}) copy-start(f32[1,1280,128]{2,1,0:T(8,128)} %param.22) | copy-start | bytes 1966084
  90.6 19.1 %copy-start.6 = (f32[1,1280,128]{2,1,0:T(8,128)S(1)}, f32[1,1280,128]{2,1,0:T(8,128)}, u32[]{:S(2)}) copy-start(f32[1,1280,128]{2,1,0:T(8,128)} %param.24) | copy-start | bytes 1966084
  90.7 21.9 %copy-start.12 = (f32[32,1024]{1,0:T(8,128)}, f32[32,1024]{1,0:T(8,128)S(1)}, u32[]{:S(2)}) copy-start(f32[32,1024]{1,0:T(8,128)S(1)} %get-tuple-element.66.refs_0_) | copy-start | bytes 393220
  90.7 21.9 %collective-permute-start.20 = (bf16[32,1024]{1,0:T(8,128)(2,1)S(1)}, bf16[32,1024]{1,0:T(8,128)(2,1)S(1)}, u32[]{:S(2)}, u32[]{:S(2)}) collective-permute-start(bf16[32,1024]{1,0:T(8,128)(2,1)S(1)} %get-tuple-element.67), channel_id=1, source_target_pairs={{0,12},{4,8},{8,4},{12,0},{1,13},{5,9},{9,5},{13,1},{2,14},{6,10},... | collective-permute-start | bytes 196616 | tf_op jit(solution)/shard_map/ppermute | solution.py:553
  93.3 19.4 %collective-permute-start.21 = (bf16[32,1024]{1,0:T(8,128)(2,1)S(1)}, bf16[32,1024]{1,0:T(8,128)(2,1)S(1)}, u32[]{:S(2)}, u32[]{:S(2)}) collective-permute-start(bf16[32,1024]{1,0:T(8,128)(2,1)S(1)} %get-tuple-element.68), channel_id=1, source_target_pairs={{0,8},{4,12},{8,0},{12,4},{1,9},{5,13},{9,1},{13,5},{2,10},{6,14},... | collective-permute-start | bytes 196616 | tf_op jit(solution)/shard_map/ppermute | solution.py:553
  100.0 12.7 %collective-permute-start.22 = (bf16[32,1024]{1,0:T(8,128)(2,1)S(1)}, bf16[32,1024]{1,0:T(8,128)(2,1)S(1)}, u32[]{:S(2)}, u32[]{:S(2)}) collective-permute-start(bf16[32,1024]{1,0:T(8,128)(2,1)S(1)} %get-tuple-element.70), channel_id=1, source_target_pairs={{0,4},{4,0},{8,12},{12,8},{1,5},{5,1},{9,13},{13,9},{2,6},{6,2},{1... | collective-permute-start | bytes 196616 | tf_op jit(solution)/shard_map/ppermute | solution.py:553
  (7 other events, 20.0 us)
